TPU v7x, 128 devices: a whole 4x4x4 slice. The times are simulated.
128 devices in a mesh: dp: 2 (over z_lo), tm: 4 (over z_hi, core), height: 16 (over y, x).
Axes of the slice: x: 4, y: 4, z: 4 (z_hi: 2, z_lo: 2; z = z_hi * 2 + z_lo), core: 2. Of those that a mesh axis runs over, the one named last changes fastest.
Arguments:
- clip: bfloat16 [2, 12, 64, 128, 128], P('dp', 'tm', 'height'), may hold values from -6 to 6
- first_weight: bfloat16 [3, 3, 3, 128, 128], replicated, may hold values from -0.109375 to 0.109375
- second_weight: bfloat16 [3, 3, 3, 128, 128], replicated, may hold values from -0.109375 to 0.109375
- cotangent: bfloat16 [2, 12, 64, 128, 128], P('dp', 'tm', 'height'), may hold values from -6 to 6
Outputs:
- output: bfloat16 [2, 12, 64, 128, 128], P('dp', 'tm', 'height')
- clip_grad: bfloat16 [2, 12, 64, 128, 128], P('dp', 'tm', 'height')
- first_grad: float32 [3, 3, 3, 128, 128], replicated
- second_grad: float32 [3, 3, 3, 128, 128], replicated
All inputs are finite; a program needn't handle non-finite values.
Results may differ from a plain program's by a relative error of at most 0.0085.
Values may be sent and summed in bfloat16 or wider, within the bound.
No kernel may reach another device: no remote copies, remote signals or barrier semaphores. Data moves between devices by JAX's collectives and lax.ppermute only.
A program may use at most 128 MiB of HBM per device.

v0:
```python
import functools
import math

import jax
import jax.numpy as jnp
from jax import lax
from jax.experimental import pallas as pl
from jax.experimental.pallas import tpu as pltpu
from jax.sharding import PartitionSpec as P

ALL = ("dp", "tm", "height")
PARAMS = pltpu.CompilerParams(vmem_limit_bytes=48 * 1024 * 1024)
VMEM = pl.BlockSpec(memory_space=pltpu.VMEM)
TAPS = [(a, b) for a in range(3) for b in range(3)]


def call(kernel, outs, scratch, flops, *args):
    moved = sum(x.size * x.dtype.itemsize for x in (*args, *outs))
    return pl.pallas_call(
        kernel,
        out_shape=outs,
        in_specs=[VMEM] * len(args),
        out_specs=[VMEM] * len(outs),
        scratch_shapes=scratch,
        compiler_params=PARAMS,
        cost_estimate=pl.CostEstimate(flops=flops, bytes_accessed=moved, transcendentals=0),
    )(*args)


def lay(pad, centre, time, low, high, ahead):
    frames, rows = centre.shape[:2]
    first = 0 if ahead else 2
    pad[first : first + frames, 1 : 1 + rows] = centre[...]
    first = frames if ahead else 0
    pad[first : first + 2, 1 : 1 + rows] = time[...]
    pad[:, 0:1] = low[...]
    pad[:, 1 + rows :] = high[...]


def down(value, columns):
    row = lax.broadcasted_iota(jnp.int32, value.shape, 0) % columns
    return jnp.where(row == 0, 0.0, pltpu.roll(value, 1, 0))


def up(value, columns):
    row = lax.broadcasted_iota(jnp.int32, value.shape, 0) % columns
    return jnp.where(row == columns - 1, 0.0, pltpu.roll(value, value.shape[0] - 1, 0))


def convolve(pad, taps, frame, rows, transposed):
    columns, channels = pad.shape[2:]
    parts = []
    for a, b in TAPS:
        t, h = (frame + 2 - a, 2 - b) if transposed else (frame + a, b)
        parts.append(pad[t, h : h + rows].reshape(rows * columns, channels))
    stacked = jnp.concatenate(parts, axis=1)
    dims = (((1,), (1 if transposed else 0,)), ((), ()))
    product = lax.dot_general(stacked, taps[...], dims, preferred_element_type=jnp.float32)
    left, middle, right = (product[:, c * channels : (c + 1) * channels] for c in range(3))
    if transposed:
        left, right = right, left
    return down(left, columns) + middle + up(right, columns)


def lay_taps(taps, kernel, transposed):
    c_in, c_out = kernel.shape[3:]
    for place, (a, b) in enumerate(TAPS):
        for c in range(3):
            if transposed:
                taps[c * c_in : (c + 1) * c_in, place * c_out : (place + 1) * c_out] = kernel[a, b, c]
            else:
                taps[place * c_in : (place + 1) * c_in, c * c_out : (c + 1) * c_out] = kernel[a, b, c]


def first_kernel(centre, time, low, high, kernel, slope, hidden, pad, taps):
    lay(pad, centre, time, low, high, False)
    lay_taps(taps, kernel, False)
    frames, rows = centre.shape[:2]
    for t in range(frames):
        z = convolve(pad, taps, t, rows, False)
        s = jax.nn.sigmoid(z)
        slope[t] = (s * (1.0 + z * (1.0 - s))).reshape(slope.shape[1:])
        hidden[t] = (z * s).astype(jnp.bfloat16).reshape(hidden.shape[1:])


def second_kernel(centre, time, low, high, kernel, cotangent, output, grad, pad, taps):
    lay(pad, centre, time, low, high, False)
    lay_taps(taps, kernel, False)
    frames, rows = centre.shape[:2]
    for t in range(frames):
        z = convolve(pad, taps, t, rows, False)
        s = jax.nn.sigmoid(z)
        output[t] = (z * s).astype(jnp.bfloat16).reshape(output.shape[1:])
        steep = (s * (1.0 + z * (1.0 - s))).reshape(grad.shape[1:])
        grad[t] = (cotangent[t].astype(jnp.float32) * steep).astype(jnp.bfloat16)


def back_kernel(centre, time, low, high, kernel, *rest):
    slope, (grad, pad, taps) = rest[:-3], rest[-3:]
    lay(pad, centre, time, low, high, True)
    lay_taps(taps, kernel, True)
    frames, rows = centre.shape[:2]
    for t in range(frames):
        z = convolve(pad, taps, t, rows, True).reshape(grad.shape[1:])
        if slope:
            z = z * slope[0][t]
        grad[t] = z.astype(jnp.bfloat16)


def weight_kernel(centre, time, low, high, grad, out, pad, moved):
    lay(pad, centre, time, low, high, False)
    frames, rows, columns, channels = centre.shape
    cells = frames * rows * columns
    wide = grad[...].reshape(cells, channels).astype(jnp.float32)
    moved[:, :channels] = up(wide, columns).astype(jnp.bfloat16)
    moved[:, channels : 2 * channels] = grad[...].reshape(cells, channels)
    moved[:, 2 * channels :] = down(wide, columns).astype(jnp.bfloat16)
    dims = (((0,), (0,)), ((), ()))
    for a, b in TAPS:
        block = pad[a : a + frames, b : b + rows].reshape(cells, channels)
        product = lax.dot_general(block, moved[...], dims, preferred_element_type=jnp.float32)
        for c in range(3):
            out[a, b, c] = product[:, c * channels : (c + 1) * channels].astype(out.dtype)


def edges(block, ahead):
    count, line = lax.axis_size("tm"), lax.axis_size("height")
    step = -1 if ahead else 1
    route = [(i, i + step) for i in range(count) if 0 <= i + step < count]
    time = lax.ppermute(block[:2] if ahead else block[-2:], "tm", route)
    whole = jnp.concatenate([block, time] if ahead else [time, block], axis=0)
    forward = [(i, i + 1) for i in range(line - 1)]
    backward = [(j, i) for i, j in forward]
    low = lax.ppermute(whole[:, -1:], "height", forward)
    high = lax.ppermute(whole[:, :1], "height", backward)
    return time, low, high


def body(clip, first_weight, second_weight, cotangent):
    _, frames, rows, columns, channels = clip.shape
    cells = frames * rows * columns
    clip, cotangent = clip[0], cotangent[0]
    flops = 2 * cells * 27 * channels * channels
    shape = (frames, rows, columns, channels)
    bf16 = jax.ShapeDtypeStruct(shape, jnp.bfloat16)
    f32 = jax.ShapeDtypeStruct(shape, jnp.float32)
    raw = jax.ShapeDtypeStruct((3, 3, 3, channels, channels), jnp.bfloat16)
    pad = pltpu.VMEM((frames + 2, rows + 2, columns, channels), jnp.bfloat16)
    taps = pltpu.VMEM((9 * channels, 3 * channels), jnp.bfloat16)
    back_taps = pltpu.VMEM((3 * channels, 9 * channels), jnp.bfloat16)
    moved = pltpu.VMEM((cells, 3 * channels), jnp.bfloat16)

    clip_edges = edges(clip, False)
    slope, hidden = call(first_kernel, [f32, bf16], [pad, taps], flops, clip, *clip_edges, first_weight)
    hidden_edges = edges(hidden, False)
    output, grad_two = call(
        second_kernel, [bf16, bf16], [pad, taps], flops, hidden, *hidden_edges, second_weight, cotangent
    )
    two_edges = edges(grad_two, True)
    (second_raw,) = call(weight_kernel, [raw], [pad, moved], flops, hidden, *hidden_edges, grad_two)
    (grad_one,) = call(back_kernel, [bf16], [pad, back_taps], flops, grad_two, *two_edges, second_weight, slope)
    one_edges = edges(grad_one, True)
    (first_raw,) = call(weight_kernel, [raw], [pad, moved], flops, clip, *clip_edges, grad_one)
    (clip_grad,) = call(back_kernel, [bf16], [pad, back_taps], flops, grad_one, *one_edges, first_weight)

    devices = lax.axis_size(ALL)
    scale = 1.0 / math.sqrt(cells * devices)
    both = jnp.stack([first_raw, second_raw]).reshape(devices, -1, channels)
    terms = lax.all_to_all(both, ALL, 0, 0, tiled=True)
    total = jnp.sum(terms.astype(jnp.float32), axis=0).astype(jnp.bfloat16)
    spread = jnp.broadcast_to(total[None], both.shape)
    sums = lax.all_to_all(spread, ALL, 0, 0, tiled=True).reshape(2, *raw.shape)
    sums = sums.astype(jnp.float32) * scale
    return output[None], clip_grad[None], sums[0], sums[1]


def solution(mesh):
    block = P("dp", "tm", "height", None, None)
    return jax.shard_map(
        body,
        mesh=mesh,
        in_specs=(block, P(), P(), block),
        out_specs=(block, block, P(), P()),
        check_vma=False,
    )
```

profile of v0, /device:TPU:25, one launch (start us, length us, event | category | flops | bytes accessed | tf_op | source)
XLA Modules:
  0.0 167.4 jit_solution(16005972591217244284)
XLA Ops:
  1.6 6.1 %collective-permute-start = (bf16[2,4,128,128]{3,2,1,0:T(8,128)(2,1)S(1)}, bf16[2,4,128,128]{3,2,1,0:T(8,128)(2,1)S(1)}, u32[]{:S(2)}, u32[]{:S(2)}) collective-permute-start(bf16[2,4,128,128]{3,2,1,0:T(8,128)(2,1)S(1)} %slice_bitcast_fusion), channel_id=1, source_target_pairs={{0,16},{16,32},{32,48},{1,17},{17,33},{33,49},{2,18},{18,34},{34,5... | collective-permute-start | bytes 786440 | tf_op jit(solution)/shard_map/ppermute | solution.py:130
  7.7 3.3 %collective-permute-done.time = bf16[2,4,128,128]{3,2,1,0:T(8,128)(2,1)S(1)} collective-permute-done((bf16[2,4,128,128]{3,2,1,0:T(8,128)(2,1)S(1)}, bf16[2,4,128,128]{3,2,1,0:T(8,128)(2,1)S(1)}, u32[]{:S(2)}, u32[]{:S(2)}) %collective-permute-start) | collective-permute-done | bytes 262176 | tf_op jit(solution)/shard_map/ppermute | solution.py:130
  11.9 4.6 %collective-permute-start.2 = (bf16[5,1,128,128]{3,2,1,0:T(8,128)(2,1)S(1)}, bf16[5,1,128,128]{3,2,1,0:T(8,128)(2,1)S(1)}, u32[]{:S(2)}, u32[]{:S(2)}) collective-permute-start(bf16[5,1,128,128]{3,2,1,0:T(8,128)(2,1)S(1)} %get-tuple-element.20), channel_id=1, source_target_pairs={{1,0},{2,1},{3,2},{4,3},{5,4},{6,5},{7,6},{8,7},{9,8},{10,9},{11,1... | collective-permute-start | bytes 491528 | tf_op jit(solution)/shard_map/ppermute | solution.py:135
  16.5 1.9 %collective-permute-start.1 = (bf16[5,1,128,128]{3,2,1,0:T(8,128)(2,1)S(1)}, bf16[5,1,128,128]{3,2,1,0:T(8,128)(2,1)S(1)}, u32[]{:S(2)}, u32[]{:S(2)}) collective-permute-start(bf16[5,1,128,128]{3,2,1,0:T(8,128)(2,1)S(1)} %get-tuple-element.21), channel_id=1, source_target_pairs={{0,1},{1,2},{2,3},{3,4},{4,5},{5,6},{6,7},{7,8},{8,9},{9,10},{10,1... | collective-permute-start | bytes 491528 | tf_op jit(solution)/shard_map/ppermute | solution.py:134
  18.8 5.9 %collective-permute-done.1.low = bf16[5,1,128,128]{3,2,1,0:T(8,128)(2,1)S(1)} collective-permute-done((bf16[5,1,128,128]{3,2,1,0:T(8,128)(2,1)S(1)}, bf16[5,1,128,128]{3,2,1,0:T(8,128)(2,1)S(1)}, u32[]{:S(2)}, u32[]{:S(2)}) %collective-permute-start.1) | collective-permute-done | bytes 163872 | tf_op jit(solution)/shard_map/ppermute | solution.py:134
  26.9 2.2 %shard_map.75 = (f32[3,4,128,128]{3,2,1,0:T(8,128)S(1)}, bf16[3,4,128,128]{3,2,1,0:T(8,128)(2,1)S(1)}) custom-call(bf16[3,4,128,128]{3,2,1,0:T(8,128)(2,1)S(1)} %bitcast.11, bf16[2,4,128,128]{3,2,1,0:T(8,128)(2,1)S(1)} %collective-permute-done.time, bf16[5,1,128,128]{3,2,1,0:T(8,128)(2,1)S(1)} %collective-permute-done.1.low, ...), custom_call_target="tpu_custom_call" | custom-call | flops 1358954496 | bytes 3047424 | tf_op jit(solution)/shard_map/pallas_call | solution.py:19
  29.2 7.5 %collective-permute-start.3 = (bf16[2,4,128,128]{3,2,1,0:T(8,128)(2,1)S(1)}, bf16[2,4,128,128]{3,2,1,0:T(8,128)(2,1)S(1)}, u32[]{:S(2)}, u32[]{:S(2)}) collective-permute-start(bf16[2,4,128,128]{3,2,1,0:T(8,128)(2,1)S(1)} %slice.51), channel_id=1, source_target_pairs={{0,16},{16,32},{32,48},{1,17},{17,33},{33,49},{2,18},{18,34},{34,5... | collective-permute-start | bytes 786440 | tf_op jit(solution)/shard_map/ppermute | solution.py:130
  36.6 3.3 %collective-permute-done.3.time = bf16[2,4,128,128]{3,2,1,0:T(8,128)(2,1)S(1)} collective-permute-done((bf16[2,4,128,128]{3,2,1,0:T(8,128)(2,1)S(1)}, bf16[2,4,128,128]{3,2,1,0:T(8,128)(2,1)S(1)}, u32[]{:S(2)}, u32[]{:S(2)}) %collective-permute-start.3) | collective-permute-done | bytes 262176 | tf_op jit(solution)/shard_map/ppermute | solution.py:130
  40.0 1.9 %collective-permute-start.5 = (bf16[5,1,128,128]{3,2,1,0:T(8,128)(2,1)S(1)}, bf16[5,1,128,128]{3,2,1,0:T(8,128)(2,1)S(1)}, u32[]{:S(2)}, u32[]{:S(2)}) collective-permute-start(bf16[5,1,128,128]{3,2,1,0:T(8,128)(2,1)S(1)} %get-tuple-element.18), channel_id=1, source_target_pairs={{1,0},{2,1},{3,2},{4,3},{5,4},{6,5},{7,6},{8,7},{9,8},{10,9},{11,1... | collective-permute-start | bytes 491528 | tf_op jit(solution)/shard_map/ppermute | solution.py:135
  42.0 3.4 %collective-permute-start.4 = (bf16[5,1,128,128]{3,2,1,0:T(8,128)(2,1)S(1)}, bf16[5,1,128,128]{3,2,1,0:T(8,128)(2,1)S(1)}, u32[]{:S(2)}, u32[]{:S(2)}) collective-permute-start(bf16[5,1,128,128]{3,2,1,0:T(8,128)(2,1)S(1)} %get-tuple-element.19), channel_id=1, source_target_pairs={{0,1},{1,2},{2,3},{3,4},{4,5},{5,6},{6,7},{7,8},{8,9},{9,10},{10,1... | collective-permute-start | bytes 491528 | tf_op jit(solution)/shard_map/ppermute | solution.py:134
  46.1 4.0 %collective-permute-done.4.low = bf16[5,1,128,128]{3,2,1,0:T(8,128)(2,1)S(1)} collective-permute-done((bf16[5,1,128,128]{3,2,1,0:T(8,128)(2,1)S(1)}, bf16[5,1,128,128]{3,2,1,0:T(8,128)(2,1)S(1)}, u32[]{:S(2)}, u32[]{:S(2)}) %collective-permute-start.4) | collective-permute-done | bytes 163872 | tf_op jit(solution)/shard_map/ppermute | solution.py:134
  50.1 3.0 %shard_map.76 = (bf16[3,4,128,128]{3,2,1,0:T(8,128)(2,1)}, bf16[3,4,128,128]{3,2,1,0:T(8,128)(2,1)S(1)}) custom-call(bf16[3,4,128,128]{3,2,1,0:T(8,128)(2,1)S(1)} %get-tuple-element.8.centre, bf16[2,4,128,128]{3,2,1,0:T(8,128)(2,1)S(1)} %collective-permute-done.3.time, bf16[5,1,128,128]{3,2,1,0:T(8,128)(2,1)S(1)} %collective-permute-done.4.low, ...), custom_call_target="tpu_custom_call" | custom-call | flops 1358954496 | bytes 3047424 | tf_op jit(solution)/shard_map/pallas_call | solution.py:19
  53.2 1.9 %collective-permute-start.6 = (bf16[2,4,128,128]{3,2,1,0:T(8,128)(2,1)S(1)}, bf16[2,4,128,128]{3,2,1,0:T(8,128)(2,1)S(1)}, u32[]{:S(2)}, u32[]{:S(2)}) collective-permute-start(bf16[2,4,128,128]{3,2,1,0:T(8,128)(2,1)S(1)} %slice.54), channel_id=1, source_target_pairs={{16,0},{32,16},{48,32},{17,1},{33,17},{49,33},{18,2},{34,18},{50,3... | collective-permute-start | bytes 786440 | tf_op jit(solution)/shard_map/ppermute | solution.py:130
  55.1 9.1 %collective-permute-done.6.time = bf16[2,4,128,128]{3,2,1,0:T(8,128)(2,1)S(1)} collective-permute-done((bf16[2,4,128,128]{3,2,1,0:T(8,128)(2,1)S(1)}, bf16[2,4,128,128]{3,2,1,0:T(8,128)(2,1)S(1)}, u32[]{:S(2)}, u32[]{:S(2)}) %collective-permute-start.6) | collective-permute-done | bytes 262176 | tf_op jit(solution)/shard_map/ppermute | solution.py:130
  64.3 1.9 %collective-permute-start.8 = (bf16[5,1,128,128]{3,2,1,0:T(8,128)(2,1)S(1)}, bf16[5,1,128,128]{3,2,1,0:T(8,128)(2,1)S(1)}, u32[]{:S(2)}, u32[]{:S(2)}) collective-permute-start(bf16[5,1,128,128]{3,2,1,0:T(8,128)(2,1)S(1)} %get-tuple-element.16), channel_id=1, source_target_pairs={{1,0},{2,1},{3,2},{4,3},{5,4},{6,5},{7,6},{8,7},{9,8},{10,9},{11,1... | collective-permute-start | bytes 491528 | tf_op jit(solution)/shard_map/ppermute | solution.py:135
  66.3 3.4 %collective-permute-start.7 = (bf16[5,1,128,128]{3,2,1,0:T(8,128)(2,1)S(1)}, bf16[5,1,128,128]{3,2,1,0:T(8,128)(2,1)S(1)}, u32[]{:S(2)}, u32[]{:S(2)}) collective-permute-start(bf16[5,1,128,128]{3,2,1,0:T(8,128)(2,1)S(1)} %get-tuple-element.17), channel_id=1, source_target_pairs={{0,1},{1,2},{2,3},{3,4},{4,5},{5,6},{6,7},{7,8},{8,9},{9,10},{10,1... | collective-permute-start | bytes 491528 | tf_op jit(solution)/shard_map/ppermute | solution.py:134
  69.6 2.2 %shard_map.80 = bf16[3,3,3,128,128]{4,3,2,1,0:T(8,128)(2,1)S(1)} custom-call(bf16[3,4,128,128]{3,2,1,0:T(8,128)(2,1)S(1)} %get-tuple-element.8.centre, bf16[2,4,128,128]{3,2,1,0:T(8,128)(2,1)S(1)} %collective-permute-done.3.time, bf16[5,1,128,128]{3,2,1,0:T(8,128)(2,1)S(1)} %collective-permute-done.4.low, ...), custom_call_target="tpu_custom_call" | custom-call | flops 1358954496 | bytes 2260992 | tf_op jit(solution)/shard_map/pallas_call | solution.py:19
  71.9 2.6 %collective-permute-done.7.low = bf16[5,1,128,128]{3,2,1,0:T(8,128)(2,1)S(1)} collective-permute-done((bf16[5,1,128,128]{3,2,1,0:T(8,128)(2,1)S(1)}, bf16[5,1,128,128]{3,2,1,0:T(8,128)(2,1)S(1)}, u32[]{:S(2)}, u32[]{:S(2)}) %collective-permute-start.7) | collective-permute-done | bytes 163872 | tf_op jit(solution)/shard_map/ppermute | solution.py:134
  74.4 2.2 %shard_map.77.centre.grad = bf16[3,4,128,128]{3,2,1,0:T(8,128)(2,1)S(1)} custom-call(bf16[3,4,128,128]{3,2,1,0:T(8,128)(2,1)S(1)} %get-tuple-element.10.centre.grad, bf16[2,4,128,128]{3,2,1,0:T(8,128)(2,1)S(1)} %collective-permute-done.6.time, bf16[5,1,128,128]{3,2,1,0:T(8,128)(2,1)S(1)} %collective-permute-done.7.low, ...), custom_call_target="tpu_custom_call" | custom-call | flops 1358954496 | bytes 3047424 | tf_op jit(solution)/shard_map/pallas_call | solution.py:19
  76.7 2.2 %shard_map.79 = bf16[3,3,3,128,128]{4,3,2,1,0:T(8,128)(2,1)S(1)} custom-call(bf16[3,4,128,128]{3,2,1,0:T(8,128)(2,1)S(1)} %bitcast.12, bf16[2,4,128,128]{3,2,1,0:T(8,128)(2,1)S(1)} %collective-permute-done.time, bf16[5,1,128,128]{3,2,1,0:T(8,128)(2,1)S(1)} %collective-permute-done.1.low, bf16[5,1,128,128]{3,2,1,0:T(8,128)(2,1)S(1)} %collective-permute-done.2.high, ...), custom_call_target="tpu_custom_call" | custom-call | flops 1358954496 | bytes 2260992 | tf_op jit(solution)/shard_map/pallas_call | solution.py:19
  79.1 1.5 reshape.21
  80.6 31.0 %all_to_all.10 = bf16[128,54,128]{2,1,0:T(8,128)(2,1)S(1)} all-to-all(bf16[128,54,128]{2,1,0:T(8,128)(2,1)} %reshape.21), channel_id=1, replica_groups=mesh['dp'=2,'tm'=4,'height'=16] {'dp','tm','height'}, dimensions={0} | all-to-all | bytes 3538944 | tf_op jit(solution)/shard_map/all_to_all | solution.py:169
  111.9 1.5 broadcast_in_dim.14
  113.4 5.6 %all-to-all-start.1 = ((bf16[128,54,128]{2,1,0:T(8,128)(2,1)}), bf16[128,54,128]{2,1,0:T(8,128)(2,1)S(1)}, u32[]{:S(2)}, u32[]{:S(2)}) async-start(bf16[128,54,128]{2,1,0:T(8,128)(2,1)} %broadcast_in_dim.14), calls=%async_computation.1 | async-start | bytes 3670016 | tf_op jit(solution)/shard_map/all_to_all | solution.py:172
  119.0 2.3 %collective-permute-start.9 = (bf16[2,4,128,128]{3,2,1,0:T(8,128)(2,1)S(1)}, bf16[2,4,128,128]{3,2,1,0:T(8,128)(2,1)S(1)}, u32[]{:S(2)}, u32[]{:S(2)}) collective-permute-start(bf16[2,4,128,128]{3,2,1,0:T(8,128)(2,1)S(1)} %slice.66), channel_id=1, source_target_pairs={{16,0},{32,16},{48,32},{17,1},{33,17},{49,33},{18,2},{34,18},{50,3... | collective-permute-start | bytes 786440 | tf_op jit(solution)/shard_map/ppermute | solution.py:130
  121.3 25.0 %collective-permute-done.9.time = bf16[2,4,128,128]{3,2,1,0:T(8,128)(2,1)S(1)} collective-permute-done((bf16[2,4,128,128]{3,2,1,0:T(8,128)(2,1)S(1)}, bf16[2,4,128,128]{3,2,1,0:T(8,128)(2,1)S(1)}, u32[]{:S(2)}, u32[]{:S(2)}) %collective-permute-start.9) | collective-permute-done | bytes 262176 | tf_op jit(solution)/shard_map/ppermute | solution.py:130
  146.4 4.2 %collective-permute-start.11 = (bf16[5,1,128,128]{3,2,1,0:T(8,128)(2,1)S(1)}, bf16[5,1,128,128]{3,2,1,0:T(8,128)(2,1)S(1)}, u32[]{:S(2)}, u32[]{:S(2)}) collective-permute-start(bf16[5,1,128,128]{3,2,1,0:T(8,128)(2,1)S(1)} %get-tuple-element.14), channel_id=1, source_target_pairs={{1,0},{2,1},{3,2},{4,3},{5,4},{6,5},{7,6},{8,7},{9,8},{10,9},{11,1... | collective-permute-start | bytes 491528 | tf_op jit(solution)/shard_map/ppermute | solution.py:135
  150.6 1.9 %collective-permute-start.10 = (bf16[5,1,128,128]{3,2,1,0:T(8,128)(2,1)S(1)}, bf16[5,1,128,128]{3,2,1,0:T(8,128)(2,1)S(1)}, u32[]{:S(2)}, u32[]{:S(2)}) collective-permute-start(bf16[5,1,128,128]{3,2,1,0:T(8,128)(2,1)S(1)} %get-tuple-element.15), channel_id=1, source_target_pairs={{0,1},{1,2},{2,3},{3,4},{4,5},{5,6},{6,7},{7,8},{8,9},{9,10},{10,1... | collective-permute-start | bytes 491528 | tf_op jit(solution)/shard_map/ppermute | solution.py:134
  152.8 5.9 %collective-permute-done.10.low = bf16[5,1,128,128]{3,2,1,0:T(8,128)(2,1)S(1)} collective-permute-done((bf16[5,1,128,128]{3,2,1,0:T(8,128)(2,1)S(1)}, bf16[5,1,128,128]{3,2,1,0:T(8,128)(2,1)S(1)}, u32[]{:S(2)}, u32[]{:S(2)}) %collective-permute-start.10) | collective-permute-done | bytes 163872 | tf_op jit(solution)/shard_map/ppermute | solution.py:134
  158.8 3.0 %shard_map.78 = bf16[3,4,128,128]{3,2,1,0:T(8,128)(2,1)} custom-call(bf16[3,4,128,128]{3,2,1,0:T(8,128)(2,1)S(1)} %shard_map.77.centre.grad, bf16[2,4,128,128]{3,2,1,0:T(8,128)(2,1)S(1)} %collective-permute-done.9.time, bf16[5,1,128,128]{3,2,1,0:T(8,128)(2,1)S(1)} %collective-permute-done.10.low, bf16[5,1,128,128]{3,2,1,0:T(8,128)(2,1)S(1)} %collective-permute-done.11.high, ...), custom_call_target="tpu_custom_call" | custom-call | flops 1358954496 | bytes 2260992 | tf_op jit(solution)/shard_map/pallas_call | solution.py:19
  162.1 1.5 fusion
  163.6 2.5 %squeeze.15 = f32[3,3,3,128,128]{4,3,2,1,0:T(8,128)} reshape(f32[64,54,128]{2,1,0:T(8,128)} %get-tuple-element.12) | data formatting | bytes 3538944 | tf_op jit(solution)/shard_map/squeeze | solution.py:174
  (33 shorter events, 7.9 us)
Async XLA Ops:
  1.6 9.4 %collective-permute-start = (bf16[2,4,128,128]{3,2,1,0:T(8,128)(2,1)S(1)}, bf16[2,4,128,128]{3,2,1,0:T(8,128)(2,1)S(1)}, u32[]{:S(2)}, u32[]{:S(2)}) collective-permute-start(bf16[2,4,128,128]{3,2,1,0:T(8,128)(2,1)S(1)} %slice_bitcast_fusion), channel_id=1, source_target_pairs={{0,16},{16,32},{32,48},{1,17},{17,33},{33,49},{2,18},{18,34},{34,5... | collective-permute-start | bytes 786440 | tf_op jit(solution)/shard_map/ppermute | solution.py:130
  11.9 6.8 %collective-permute-start.2 = (bf16[5,1,128,128]{3,2,1,0:T(8,128)(2,1)S(1)}, bf16[5,1,128,128]{3,2,1,0:T(8,128)(2,1)S(1)}, u32[]{:S(2)}, u32[]{:S(2)}) collective-permute-start(bf16[5,1,128,128]{3,2,1,0:T(8,128)(2,1)S(1)} %get-tuple-element.20), channel_id=1, source_target_pairs={{1,0},{2,1},{3,2},{4,3},{5,4},{6,5},{7,6},{8,7},{9,8},{10,9},{11,1... | collective-permute-start | bytes 491528 | tf_op jit(solution)/shard_map/ppermute | solution.py:135
  16.5 8.2 %collective-permute-start.1 = (bf16[5,1,128,128]{3,2,1,0:T(8,128)(2,1)S(1)}, bf16[5,1,128,128]{3,2,1,0:T(8,128)(2,1)S(1)}, u32[]{:S(2)}, u32[]{:S(2)}) collective-permute-start(bf16[5,1,128,128]{3,2,1,0:T(8,128)(2,1)S(1)} %get-tuple-element.21), channel_id=1, source_target_pairs={{0,1},{1,2},{2,3},{3,4},{4,5},{5,6},{6,7},{7,8},{8,9},{9,10},{10,1... | collective-permute-start | bytes 491528 | tf_op jit(solution)/shard_map/ppermute | solution.py:134
  24.7 1.0 copy-start
  25.7 1.2 copy-start.3
  29.1 21.0 %copy-start.2 = (bf16[3,3,3,128,128]{4,3,2,1,0:T(8,128)(2,1)S(1)}, bf16[3,3,3,128,128]{4,3,2,1,0:T(8,128)(2,1)}, u32[]{:S(2)}) copy-start(bf16[3,3,3,128,128]{4,3,2,1,0:T(8,128)(2,1)} %kernel.6) | copy-start | bytes 2654212
  29.1 21.0 %copy-start.5 = (bf16[1,3,4,128,128]{4,3,2,1,0:T(8,128)(2,1)S(1)}, bf16[1,3,4,128,128]{4,3,2,1,0:T(8,128)(2,1)}, u32[]{:S(2)}) copy-start(bf16[1,3,4,128,128]{4,3,2,1,0:T(8,128)(2,1)} %param.7) | copy-start | bytes 1179652
  29.2 10.8 %collective-permute-start.3 = (bf16[2,4,128,128]{3,2,1,0:T(8,128)(2,1)S(1)}, bf16[2,4,128,128]{3,2,1,0:T(8,128)(2,1)S(1)}, u32[]{:S(2)}, u32[]{:S(2)}) collective-permute-start(bf16[2,4,128,128]{3,2,1,0:T(8,128)(2,1)S(1)} %slice.51), channel_id=1, source_target_pairs={{0,16},{16,32},{32,48},{1,17},{17,33},{33,49},{2,18},{18,34},{34,5... | collective-permute-start | bytes 786440 | tf_op jit(solution)/shard_map/ppermute | solution.py:130
  40.0 6.1 %collective-permute-start.5 = (bf16[5,1,128,128]{3,2,1,0:T(8,128)(2,1)S(1)}, bf16[5,1,128,128]{3,2,1,0:T(8,128)(2,1)S(1)}, u32[]{:S(2)}, u32[]{:S(2)}) collective-permute-start(bf16[5,1,128,128]{3,2,1,0:T(8,128)(2,1)S(1)} %get-tuple-element.18), channel_id=1, source_target_pairs={{1,0},{2,1},{3,2},{4,3},{5,4},{6,5},{7,6},{8,7},{9,8},{10,9},{11,1... | collective-permute-start | bytes 491528 | tf_op jit(solution)/shard_map/ppermute | solution.py:135
  42.0 8.2 %collective-permute-start.4 = (bf16[5,1,128,128]{3,2,1,0:T(8,128)(2,1)S(1)}, bf16[5,1,128,128]{3,2,1,0:T(8,128)(2,1)S(1)}, u32[]{:S(2)}, u32[]{:S(2)}) collective-permute-start(bf16[5,1,128,128]{3,2,1,0:T(8,128)(2,1)S(1)} %get-tuple-element.19), channel_id=1, source_target_pairs={{0,1},{1,2},{2,3},{3,4},{4,5},{5,6},{6,7},{7,8},{8,9},{9,10},{10,1... | collective-permute-start | bytes 491528 | tf_op jit(solution)/shard_map/ppermute | solution.py:134
  53.2 11.1 %collective-permute-start.6 = (bf16[2,4,128,128]{3,2,1,0:T(8,128)(2,1)S(1)}, bf16[2,4,128,128]{3,2,1,0:T(8,128)(2,1)S(1)}, u32[]{:S(2)}, u32[]{:S(2)}) collective-permute-start(bf16[2,4,128,128]{3,2,1,0:T(8,128)(2,1)S(1)} %slice.54), channel_id=1, source_target_pairs={{16,0},{32,16},{48,32},{17,1},{33,17},{49,33},{18,2},{34,18},{50,3... | collective-permute-start | bytes 786440 | tf_op jit(solution)/shard_map/ppermute | solution.py:130
  64.3 7.5 %collective-permute-start.8 = (bf16[5,1,128,128]{3,2,1,0:T(8,128)(2,1)S(1)}, bf16[5,1,128,128]{3,2,1,0:T(8,128)(2,1)S(1)}, u32[]{:S(2)}, u32[]{:S(2)}) collective-permute-start(bf16[5,1,128,128]{3,2,1,0:T(8,128)(2,1)S(1)} %get-tuple-element.16), channel_id=1, source_target_pairs={{1,0},{2,1},{3,2},{4,3},{5,4},{6,5},{7,6},{8,7},{9,8},{10,9},{11,1... | collective-permute-start | bytes 491528 | tf_op jit(solution)/shard_map/ppermute | solution.py:135
  66.3 8.2 %collective-permute-start.7 = (bf16[5,1,128,128]{3,2,1,0:T(8,128)(2,1)S(1)}, bf16[5,1,128,128]{3,2,1,0:T(8,128)(2,1)S(1)}, u32[]{:S(2)}, u32[]{:S(2)}) collective-permute-start(bf16[5,1,128,128]{3,2,1,0:T(8,128)(2,1)S(1)} %get-tuple-element.17), channel_id=1, source_target_pairs={{0,1},{1,2},{2,3},{3,4},{4,5},{5,6},{6,7},{7,8},{8,9},{9,10},{10,1... | collective-permute-start | bytes 491528 | tf_op jit(solution)/shard_map/ppermute | solution.py:134
  74.4 2.2 %copy-start.1 = (bf16[1,3,4,128,128]{4,3,2,1,0:T(8,128)(2,1)S(1)}, bf16[1,3,4,128,128]{4,3,2,1,0:T(8,128)(2,1)}, u32[]{:S(2)}) copy-start(bf16[1,3,4,128,128]{4,3,2,1,0:T(8,128)(2,1)} %param.4) | copy-start | bytes 1179652
  113.4 45.3 %copy-start.4 = (bf16[3,3,3,128,128]{4,3,2,1,0:T(8,128)(2,1)S(1)}, bf16[3,3,3,128,128]{4,3,2,1,0:T(8,128)(2,1)}, u32[]{:S(2)}) copy-start(bf16[3,3,3,128,128]{4,3,2,1,0:T(8,128)(2,1)} %kernel.7) | copy-start | bytes 2654212
  113.4 48.3 %all-to-all-start.1 = ((bf16[128,54,128]{2,1,0:T(8,128)(2,1)}), bf16[128,54,128]{2,1,0:T(8,128)(2,1)S(1)}, u32[]{:S(2)}, u32[]{:S(2)}) async-start(bf16[128,54,128]{2,1,0:T(8,128)(2,1)} %broadcast_in_dim.14), calls=%async_computation.1 | async-start | bytes 3670016 | tf_op jit(solution)/shard_map/all_to_all | solution.py:172
  119.0 27.3 %collective-permute-start.9 = (bf16[2,4,128,128]{3,2,1,0:T(8,128)(2,1)S(1)}, bf16[2,4,128,128]{3,2,1,0:T(8,128)(2,1)S(1)}, u32[]{:S(2)}, u32[]{:S(2)}) collective-permute-start(bf16[2,4,128,128]{3,2,1,0:T(8,128)(2,1)S(1)} %slice.66), channel_id=1, source_target_pairs={{16,0},{32,16},{48,32},{17,1},{33,17},{49,33},{18,2},{34,18},{50,3... | collective-permute-start | bytes 786440 | tf_op jit(solution)/shard_map/ppermute | solution.py:130
  146.4 6.5 %collective-permute-start.11 = (bf16[5,1,128,128]{3,2,1,0:T(8,128)(2,1)S(1)}, bf16[5,1,128,128]{3,2,1,0:T(8,128)(2,1)S(1)}, u32[]{:S(2)}, u32[]{:S(2)}) collective-permute-start(bf16[5,1,128,128]{3,2,1,0:T(8,128)(2,1)S(1)} %get-tuple-element.14), channel_id=1, source_target_pairs={{1,0},{2,1},{3,2},{4,3},{5,4},{6,5},{7,6},{8,7},{9,8},{10,9},{11,1... | collective-permute-start | bytes 491528 | tf_op jit(solution)/shard_map/ppermute | solution.py:135
  150.6 8.2 %collective-permute-start.10 = (bf16[5,1,128,128]{3,2,1,0:T(8,128)(2,1)S(1)}, bf16[5,1,128,128]{3,2,1,0:T(8,128)(2,1)S(1)}, u32[]{:S(2)}, u32[]{:S(2)}) collective-permute-start(bf16[5,1,128,128]{3,2,1,0:T(8,128)(2,1)S(1)} %get-tuple-element.15), channel_id=1, source_target_pairs={{0,1},{1,2},{2,3},{3,4},{4,5},{5,6},{6,7},{7,8},{8,9},{9,10},{10,1... | collective-permute-start | bytes 491528 | tf_op jit(solution)/shard_map/ppermute | solution.py:134
where the time goes:
time: 168 us; the launch traced here: 167 us
  waiting for transfers between devices  60.6 us (36%)
  starting transfers between devices  46.5 us (28%)
  blocking collectives  31 us (18%)
  Pallas kernels  14.9 us (9%)
  local copies, waits for them, and re-layouts  11.8 us (7%)
  other arithmetic  1.81 us (1%)
    ppermute x4, waiting for transfers between devices, edges(): time = lax.ppermute(block[:2] if ahead else block[-2:], 'tm', route)  40.7 us
    all_to_all x1, blocking collectives, body(): terms = lax.all_to_all(both, ALL, 0, 0, tiled=True)  31 us
    ppermute x4, waiting for transfers between devices, edges(): low = lax.ppermute(whole[:, -1:], 'height', forward)  18.5 us
    ppermute x4, starting transfers between devices, edges(): time = lax.ppermute(block[:2] if ahead else block[-2:], 'tm', route)  17.7 us
    pallas_call x6, Pallas kernels, call(): pl.pallas_call(kernel, out_shape=outs, in_specs=[VMEM] * len(args), out_s...  14.9 us
    ppermute x4, starting transfers between devices, edges(): high = lax.ppermute(whole[:, :1], 'height', backward)  12.6 us
    ppermute x4, starting transfers between devices, edges(): low = lax.ppermute(whole[:, -1:], 'height', forward)  10.6 us
    all_to_all x1, starting transfers between devices, body(): sums = lax.all_to_all(spread, ALL, 0, 0, tiled=True).reshape(2, *raw.shape)  5.56 us
  transfers between devices with their start and end apart: 13, of which 11 were waited for; matrix products, arithmetic and copies ran while one was open for 0% of the time, Pallas kernels for 3%

commit v1 on v0

v1 whole, which is shorter than its diff:
```python
import functools
import math

import jax
import jax.numpy as jnp
from jax import lax
from jax.experimental import pallas as pl
from jax.experimental.pallas import tpu as pltpu
from jax.sharding import PartitionSpec as P

ALL = ("dp", "tm", "height")
PARAMS = pltpu.CompilerParams(vmem_limit_bytes=48 * 1024 * 1024)
VMEM = pl.BlockSpec(memory_space=pltpu.VMEM)
TAPS = [(a, b) for a in range(3) for b in range(3)]


def call(kernel, outs, scratch, flops, *args):
    moved = sum(x.size * x.dtype.itemsize for x in (*args, *outs))
    return pl.pallas_call(
        kernel,
        out_shape=outs,
        in_specs=[VMEM] * len(args),
        out_specs=[VMEM] * len(outs),
        scratch_shapes=scratch,
        compiler_params=PARAMS,
        cost_estimate=pl.CostEstimate(flops=flops, bytes_accessed=moved, transcendentals=0),
    )(*args)


def lay(pad, centre, time, near, far, corners, ahead):
    frames, rows = centre.shape[:2]
    place, above = near_row(rows + 2), far_row(rows + 2)
    own = pl.ds(0 if ahead else 2, frames)
    beyond = pl.ds(frames if ahead else 0, 2)
    pad[own, 1 : 1 + rows] = centre[...]
    pad[own, pl.ds(place, 1)] = near[...]
    pad[own, pl.ds(above, 1)] = far[...]
    pad[beyond, 1 : 1 + rows] = time[...]
    pad[beyond, pl.ds(place, 1)] = corners[:, 0:1]
    pad[beyond, pl.ds(above, 1)] = corners[:, 1:2]

    def clear(at):
        pad[at] = jnp.zeros_like(pad[at])

    line, tm = lax.axis_index("height"), lax.axis_index("tm")
    pl.when(line == 0)(lambda: clear((slice(None), slice(0, 1))))
    pl.when(line == lax.axis_size("height") - 1)(lambda: clear((slice(None), slice(rows + 1, rows + 2))))
    pl.when(tm == (lax.axis_size("tm") - 1 if ahead else 0))(lambda: clear((beyond,)))


def near_row(rows):
    return (1 - lax.axis_index("height") % 2) * (rows - 1)


def far_row(rows):
    return lax.axis_index("height") % 2 * (rows - 1)


def strips(block, last, near, far, ahead):
    frames, rows = block.shape[:2]
    last[...] = block[0:2] if ahead else block[frames - 2 :]
    near[...] = block[:, pl.ds(near_row(rows), 1)]
    far[...] = block[:, pl.ds(far_row(rows), 1)]


def down(value, columns):
    row = lax.broadcasted_iota(jnp.int32, value.shape, 0) % columns
    return jnp.where(row == 0, 0.0, pltpu.roll(value, 1, 0))


def up(value, columns):
    row = lax.broadcasted_iota(jnp.int32, value.shape, 0) % columns
    return jnp.where(row == columns - 1, 0.0, pltpu.roll(value, value.shape[0] - 1, 0))


def convolve(pad, taps, frame, rows, transposed):
    columns, channels = pad.shape[2:]
    parts = []
    for a, b in TAPS:
        t, h = (frame + 2 - a, 2 - b) if transposed else (frame + a, b)
        parts.append(pad[t, h : h + rows].reshape(rows * columns, channels))
    stacked = jnp.concatenate(parts, axis=1)
    dims = (((1,), (1 if transposed else 0,)), ((), ()))
    product = lax.dot_general(stacked, taps[...], dims, preferred_element_type=jnp.float32)
    left, middle, right = (product[:, c * channels : (c + 1) * channels] for c in range(3))
    if transposed:
        left, right = right, left
    return down(left, columns) + middle + up(right, columns)


def lay_taps(taps, kernel, transposed):
    c_in, c_out = kernel.shape[3:]
    for place, (a, b) in enumerate(TAPS):
        for c in range(3):
            if transposed:
                taps[c * c_in : (c + 1) * c_in, place * c_out : (place + 1) * c_out] = kernel[a, b, c]
            else:
                taps[place * c_in : (place + 1) * c_in, c * c_out : (c + 1) * c_out] = kernel[a, b, c]


def first_kernel(centre, time, near, far, corners, kernel, slope, hidden, last, near_out, far_out, pad, taps):
    lay(pad, centre, time, near, far, corners, False)
    lay_taps(taps, kernel, False)
    frames, rows = centre.shape[:2]
    for t in range(frames):
        z = convolve(pad, taps, t, rows, False)
        s = jax.nn.sigmoid(z)
        slope[t] = (s * (1.0 + z * (1.0 - s))).reshape(slope.shape[1:])
        hidden[t] = (z * s).astype(jnp.bfloat16).reshape(hidden.shape[1:])
    strips(hidden, last, near_out, far_out, False)


def second_kernel(
    centre, time, near, far, corners, kernel, cotangent, output, grad, last, near_out, far_out, pad, taps
):
    lay(pad, centre, time, near, far, corners, False)
    lay_taps(taps, kernel, False)
    frames, rows = centre.shape[:2]
    for t in range(frames):
        z = convolve(pad, taps, t, rows, False)
        s = jax.nn.sigmoid(z)
        output[t] = (z * s).astype(jnp.bfloat16).reshape(output.shape[1:])
        steep = (s * (1.0 + z * (1.0 - s))).reshape(grad.shape[1:])
        grad[t] = (cotangent[t].astype(jnp.float32) * steep).astype(jnp.bfloat16)
    strips(grad, last, near_out, far_out, True)


def back_kernel(centre, time, near, far, corners, kernel, grad, pad, taps):
    lay(pad, centre, time, near, far, corners, True)
    lay_taps(taps, kernel, True)
    frames, rows = centre.shape[:2]
    for t in range(frames):
        z = convolve(pad, taps, t, rows, True)
        grad[t] = z.astype(jnp.bfloat16).reshape(grad.shape[1:])


def back_slope_kernel(
    centre, time, near, far, corners, kernel, slope, grad, last, near_out, far_out, pad, taps
):
    lay(pad, centre, time, near, far, corners, True)
    lay_taps(taps, kernel, True)
    frames, rows = centre.shape[:2]
    for t in range(frames):
        z = convolve(pad, taps, t, rows, True).reshape(grad.shape[1:])
        grad[t] = (z * slope[t]).astype(jnp.bfloat16)
    strips(grad, last, near_out, far_out, True)


def weight_kernel(centre, time, near, far, corners, grad, keep, send, pad, moved):
    lay(pad, centre, time, near, far, corners, False)
    frames, rows, columns, channels = centre.shape
    cells = frames * rows * columns
    core = lax.axis_index("tm") % 2
    wide = grad[...].reshape(cells, channels).astype(jnp.float32)
    moved[:, :channels] = up(wide, columns).astype(jnp.bfloat16)
    moved[:, channels : 2 * channels] = grad[...].reshape(cells, channels)
    moved[:, 2 * channels :] = down(wide, columns).astype(jnp.bfloat16)
    dims = (((0,), (0,)), ((), ()))
    half = channels // 2
    for place, (a, b) in enumerate(TAPS):
        block = pad[a : a + frames, b : b + rows].reshape(cells, channels)
        product = lax.dot_general(block, moved[...], dims, preferred_element_type=jnp.float32)
        for c in range(3):
            part = product[:, c * channels : (c + 1) * channels]
            mine = jnp.where(core == 0, part[:half], part[half:])
            other = jnp.where(core == 0, part[half:], part[:half])
            keep[:, 3 * place + c] = mine.reshape(4, -1, channels)
            send[:, 3 * place + c] = other.astype(jnp.bfloat16).reshape(4, -1, channels)
    for out in (keep, send):
        out[:, 27:] = jnp.zeros_like(out[:, 27:])


def first_scatter_kernel(keep_one, came_one, keep_two, came_two, mine, *sent):
    x = lax.axis_index("height") % 4
    for d, out in enumerate((mine, *sent)):
        for first, keep, came in ((0, keep_one, came_one), (2, keep_two, came_two)):
            total = keep[x ^ d] + came[x ^ d].astype(jnp.float32)
            out[first : first + 2] = total.reshape(2, -1, *total.shape[1:]).astype(out.dtype)


def second_scatter_kernel(own, one, two, three, mine, *sent):
    y = lax.axis_index("height") // 4
    for d, out in enumerate((mine, *sent)):
        own_part, *parts = (ref[y ^ d].astype(jnp.float32) for ref in (own, one, two, three))
        out[...] = ((own_part + parts[0]) + (parts[1] + parts[2])).astype(out.dtype)


def add_kernel(own, one, two, three, out):
    own, one, two, three = (ref[...].astype(jnp.float32) for ref in (own, one, two, three))
    out[...] = ((own + one) + (two + three)).astype(out.dtype)


def join_kernel(own, one, two, three, out):
    y = lax.axis_index("height") // 4
    for d, part in enumerate((own, one, two, three)):
        out[y ^ d] = part[...]


def gather_kernel(scale, *refs):
    outs = refs[-2:]
    x, core = lax.axis_index("height") % 4, lax.axis_index("tm") % 2
    taps = outs[0].shape[0]
    for d in range(4):
        for half in range(2):
            for k, out in enumerate(outs):
                block = refs[4 * half + d][2 * k : 2 * k + 2].astype(jnp.float32) * scale
                block = block.reshape(-1, *block.shape[2:])[:taps]
                out[:, pl.ds((core ^ half) * 4 + (x ^ d), 1)] = block[:, None]


def swap(value, mask):
    return lax.ppermute(value, ALL, [(i, i ^ mask) for i in range(lax.axis_size(ALL))])


def summed(one, two, scale):
    _, taps, part, channels = one[0].shape
    quarter = (taps // 2, part, channels)
    size = 8 * taps * part * channels

    def shapes(shape):
        return [jax.ShapeDtypeStruct(shape, jnp.float32)] + 3 * [jax.ShapeDtypeStruct(shape, jnp.bfloat16)]

    mine, *sent = call(first_scatter_kernel, shapes((4, *quarter)), [], size, *one, *two)
    terms = [mine] + [swap(value, d) for d, value in enumerate(sent, 1)]
    mine, *sent = call(second_scatter_kernel, shapes(quarter), [], size, *terms)
    terms = [mine] + [swap(value, 4 * d) for d, value in enumerate(sent, 1)]
    small = jax.ShapeDtypeStruct(quarter, jnp.bfloat16)
    (total,) = call(add_kernel, [small], [], size // 4, *terms)
    terms = [total] + [swap(total, mask) for mask in (64, 32, 96)]
    (total,) = call(add_kernel, [small], [], size // 4, *terms)
    terms = [total] + [swap(total, 4 * d) for d in (1, 2, 3)]
    (total,) = call(join_kernel, [jax.ShapeDtypeStruct((4, *quarter), jnp.bfloat16)], [], size, *terms)
    parts = [total] + [swap(total, d) for d in (1, 2, 3)]
    parts += [swap(value, 16) for value in parts]
    whole = jax.ShapeDtypeStruct((27, 8, part, channels), jnp.float32)
    outs = call(functools.partial(gather_kernel, scale), [whole, whole], [], 8 * size, *parts)
    return [out.reshape(3, 3, 3, channels, channels) for out in outs]


def edges(last, near, far, ahead):
    count, line = lax.axis_size("tm"), lax.axis_size("height")
    step = -1 if ahead else 1
    route = [(i, (i + step) % count) for i in range(count)]
    time = lax.ppermute(last, "tm", route)
    near = lax.ppermute(near, "height", [(i, i ^ 1) for i in range(line)])
    far = lax.ppermute(far, "height", [(i, (i - 1 if i % 2 == 0 else i + 1) % line) for i in range(line)])
    rows = jnp.concatenate([near, far], axis=1)
    corners = lax.ppermute(rows[:2] if ahead else rows[-2:], "tm", route)
    return time, near, far, corners


def body(clip, first_weight, second_weight, cotangent):
    _, frames, rows, columns, channels = clip.shape
    cells = frames * rows * columns
    clip, cotangent = clip[0], cotangent[0]
    flops = 2 * cells * 27 * channels * channels
    shape = (frames, rows, columns, channels)
    bf16 = jax.ShapeDtypeStruct(shape, jnp.bfloat16)
    f32 = jax.ShapeDtypeStruct(shape, jnp.float32)
    last = jax.ShapeDtypeStruct((2, *shape[1:]), jnp.bfloat16)
    line = jax.ShapeDtypeStruct((frames, 1, *shape[2:]), jnp.bfloat16)
    quarters = (4, 28, channels // 8, channels)
    keep = jax.ShapeDtypeStruct(quarters, jnp.float32)
    send = jax.ShapeDtypeStruct(quarters, jnp.bfloat16)
    pad = pltpu.VMEM((frames + 2, rows + 2, columns, channels), jnp.bfloat16)
    taps = pltpu.VMEM((9 * channels, 3 * channels), jnp.bfloat16)
    back_taps = pltpu.VMEM((3 * channels, 9 * channels), jnp.bfloat16)
    moved = pltpu.VMEM((cells, 3 * channels), jnp.bfloat16)
    scale = 1.0 / math.sqrt(cells * lax.axis_size(ALL))

    even = lax.axis_index("height") % 2 == 0
    top, bottom = clip[:, :1], clip[:, -1:]
    clip_edges = edges(clip[-2:], jnp.where(even, bottom, top), jnp.where(even, top, bottom), False)
    slope, hidden, *cut = call(
        first_kernel, [f32, bf16, last, line, line], [pad, taps], flops, clip, *clip_edges, first_weight
    )
    hidden_edges = edges(*cut, False)
    output, grad_two, *cut = call(
        second_kernel,
        [bf16, bf16, last, line, line],
        [pad, taps],
        flops,
        hidden,
        *hidden_edges,
        second_weight,
        cotangent,
    )
    two_edges = edges(*cut, True)
    mine, other = call(weight_kernel, [keep, send], [pad, moved], flops, hidden, *hidden_edges, grad_two)
    second_terms = (mine, swap(other, 16))
    grad_one, *cut = call(
        back_slope_kernel,
        [bf16, last, line, line],
        [pad, back_taps],
        flops,
        grad_two,
        *two_edges,
        second_weight,
        slope,
    )
    one_edges = edges(*cut, True)
    mine, other = call(weight_kernel, [keep, send], [pad, moved], flops, clip, *clip_edges, grad_one)
    first_grad, second_grad = summed((mine, swap(other, 16)), second_terms, scale)
    (clip_grad,) = call(back_kernel, [bf16], [pad, back_taps], flops, grad_one, *one_edges, first_weight)
    return output[None], clip_grad[None], first_grad, second_grad


def solution(mesh):
    block = P("dp", "tm", "height", None, None)
    return jax.shard_map(
        body,
        mesh=mesh,
        in_specs=(block, P(), P(), block),
        out_specs=(block, block, P(), P()),
        check_vma=False,
    )
```

time: 168 us -> 121 us (0.72)
  the two profiles are of different devices: /device:TPU:25 before, /device:TPU:1 now
where the time goes in v1:
time: 121 us
  starting transfers between devices  61 us (50%)
  waiting for transfers between devices  36.8 us (30%)
  Pallas kernels  18.2 us (15%)
  local copies, waits for them, and re-layouts  3.15 us (3%)
    ppermute x21, waiting for transfers between devices, swap(): lax.ppermute(value, ALL, [(i, i ^ mask) for i in range(lax.axis_size(ALL))])  20.8 us
    ppermute x21, starting transfers between devices, swap(): lax.ppermute(value, ALL, [(i, i ^ mask) for i in range(lax.axis_size(ALL))])  19.7 us
    pallas_call x12, Pallas kernels, call(): pl.pallas_call(kernel, out_shape=outs, in_specs=[VMEM] * len(args), out_s...  18.2 us
    ppermute x4, starting transfers between devices, edges(): time = lax.ppermute(last, 'tm', route)  14.5 us
    ppermute x4, starting transfers between devices, edges(): corners = lax.ppermute(rows[:2] if ahead else rows[-2:], 'tm', route)  13 us
    ppermute x4, starting transfers between devices, edges(): lax.ppermute(far, 'height', [(i, (i - 1 if i % 2 == 0 else i + 1) % line)...  12.9 us
    ppermute x4, waiting for transfers between devices, edges(): corners = lax.ppermute(rows[:2] if ahead else rows[-2:], 'tm', route)  11.6 us
    ppermute x4, waiting for transfers between devices, edges(): lax.ppermute(far, 'height', [(i, (i - 1 if i % 2 == 0 else i + 1) % line)...  3.58 us
  transfers between devices with their start and end apart: 37, of which 15 were waited for; matrix products, arithmetic and copies ran while one was open for 1% of the time, Pallas kernels for 8%

profile of v1, /device:TPU:1, one launch (start us, length us, event | category | flops | bytes accessed | tf_op | source)
XLA Modules:
  0.0 120.9 jit_solution(14337268294741599682)
XLA Ops:
  1.6 5.8 %collective-permute-start.2 = (bf16[3,1,128,128]{3,2,1,0:T(8,128)(2,1)S(1)}, bf16[3,1,128,128]{3,2,1,0:T(8,128)(2,1)S(1)}, u32[]{:S(2)}, u32[]{:S(2)}) collective-permute-start(bf16[3,1,128,128]{3,2,1,0:T(8,128)(2,1)S(1)} %get-tuple-element.60), channel_id=1, source_target_pairs={{0,15},{1,2},{2,1},{3,4},{4,3},{5,6},{6,5},{7,8},{8,7},{9,10},{10,... | collective-permute-start | bytes 294920 | tf_op jit(solution)/shard_map/ppermute | solution.py:246
  8.4 4.5 %collective-permute-start = (bf16[2,4,128,128]{3,2,1,0:T(8,128)(2,1)S(1)}, bf16[2,4,128,128]{3,2,1,0:T(8,128)(2,1)S(1)}, u32[]{:S(2)}, u32[]{:S(2)}) collective-permute-start(bf16[2,4,128,128]{3,2,1,0:T(8,128)(2,1)S(1)} %slice_bitcast_fusion), channel_id=1, source_target_pairs={{0,16},{16,32},{32,48},{48,0},{1,17},{17,33},{33,49},{49,1},{2,18}... | collective-permute-start | bytes 786440 | tf_op jit(solution)/shard_map/ppermute | solution.py:244
  13.0 3.6 %collective-permute-start.3 = (bf16[2,2,128,128]{3,2,1,0:T(8,128)(2,1)S(1)}, bf16[2,2,128,128]{3,2,1,0:T(8,128)(2,1)S(1)}, u32[]{:S(2)}, u32[]{:S(2)}) collective-permute-start(bf16[2,2,128,128]{3,2,1,0:T(8,128)(2,1)S(1)} %pad_maximum_fusion.3), channel_id=1, source_target_pairs={{0,16},{16,32},{32,48},{48,0},{1,17},{17,33},{33,49},{49,1},{2,18}... | collective-permute-start | bytes 393224 | tf_op jit(solution)/shard_map/ppermute | solution.py:248
  16.6 1.9 %collective-permute-done.3.corners = bf16[2,2,128,128]{3,2,1,0:T(8,128)(2,1)S(1)} collective-permute-done((bf16[2,2,128,128]{3,2,1,0:T(8,128)(2,1)S(1)}, bf16[2,2,128,128]{3,2,1,0:T(8,128)(2,1)S(1)}, u32[]{:S(2)}, u32[]{:S(2)}) %collective-permute-start.3) | collective-permute-done | bytes 131104 | tf_op jit(solution)/shard_map/ppermute | solution.py:248
  20.7 2.4 %shard_map.75 = (f32[3,4,128,128]{3,2,1,0:T(8,128)S(1)}, bf16[3,4,128,128]{3,2,1,0:T(8,128)(2,1)S(1)}, bf16[2,4,128,128]{3,2,1,0:T(8,128)(2,1)S(1)}, bf16[3,1,12...) custom-call(bf16[3,4,128,128]{3,2,1,0:T(8,128)(2,1)S(1)} %bitcast.9, ...), custom_call_target="tpu_custom_call" | custom-call | flops 1358954496 | bytes 3506176 | tf_op jit(solution)/shard_map/pallas_call | solution.py:19
  24.0 2.3 %collective-permute-start.6 = (bf16[3,1,128,128]{3,2,1,0:T(8,128)(2,1)S(1)}, bf16[3,1,128,128]{3,2,1,0:T(8,128)(2,1)S(1)}, u32[]{:S(2)}, u32[]{:S(2)}) collective-permute-start(bf16[3,1,128,128]{3,2,1,0:T(8,128)(2,1)S(1)} %get-tuple-element.35), channel_id=1, source_target_pairs={{0,15},{1,2},{2,1},{3,4},{4,3},{5,6},{6,5},{7,8},{8,7},{9,10},{10,... | collective-permute-start | bytes 294920 | tf_op jit(solution)/shard_map/ppermute | solution.py:246
  26.3 4.2 %collective-permute-start.4 = (bf16[2,4,128,128]{3,2,1,0:T(8,128)(2,1)S(1)}, bf16[2,4,128,128]{3,2,1,0:T(8,128)(2,1)S(1)}, u32[]{:S(2)}, u32[]{:S(2)}) collective-permute-start(bf16[2,4,128,128]{3,2,1,0:T(8,128)(2,1)S(1)} %get-tuple-element.33), channel_id=1, source_target_pairs={{0,16},{16,32},{32,48},{48,0},{1,17},{17,33},{33,49},{49,1},{2,18}... | collective-permute-start | bytes 786440 | tf_op jit(solution)/shard_map/ppermute | solution.py:244
  30.8 5.5 %collective-permute-start.7 = (bf16[2,2,128,128]{3,2,1,0:T(8,128)(2,1)S(1)}, bf16[2,2,128,128]{3,2,1,0:T(8,128)(2,1)S(1)}, u32[]{:S(2)}, u32[]{:S(2)}) collective-permute-start(bf16[2,2,128,128]{3,2,1,0:T(8,128)(2,1)S(1)} %pad_maximum_fusion.2), channel_id=1, source_target_pairs={{0,16},{16,32},{32,48},{48,0},{1,17},{17,33},{33,49},{49,1},{2,18}... | collective-permute-start | bytes 393224 | tf_op jit(solution)/shard_map/ppermute | solution.py:248
  36.3 1.9 %collective-permute-done.7.corners = bf16[2,2,128,128]{3,2,1,0:T(8,128)(2,1)S(1)} collective-permute-done((bf16[2,2,128,128]{3,2,1,0:T(8,128)(2,1)S(1)}, bf16[2,2,128,128]{3,2,1,0:T(8,128)(2,1)S(1)}, u32[]{:S(2)}, u32[]{:S(2)}) %collective-permute-start.7) | collective-permute-done | bytes 131104 | tf_op jit(solution)/shard_map/ppermute | solution.py:248
  38.3 3.2 %shard_map.76 = (bf16[3,4,128,128]{3,2,1,0:T(8,128)(2,1)}, bf16[3,4,128,128]{3,2,1,0:T(8,128)(2,1)S(1)}, bf16[2,4,128,128]{3,2,1,0:T(8,128)(2,1)S(1)}, bf16[3,1,...) custom-call(bf16[3,4,128,128]{3,2,1,0:T(8,128)(2,1)S(1)} %get-tuple-element.32.centre, ...), custom_call_target="tpu_custom_call" | custom-call | flops 1358954496 | bytes 3506176 | tf_op jit(solution)/shard_map/pallas_call | solution.py:19
  41.5 2.0 %collective-permute-start.10 = (bf16[3,1,128,128]{3,2,1,0:T(8,128)(2,1)S(1)}, bf16[3,1,128,128]{3,2,1,0:T(8,128)(2,1)S(1)}, u32[]{:S(2)}, u32[]{:S(2)}) collective-permute-start(bf16[3,1,128,128]{3,2,1,0:T(8,128)(2,1)S(1)} %get-tuple-element.40), channel_id=1, source_target_pairs={{0,15},{1,2},{2,1},{3,4},{4,3},{5,6},{6,5},{7,8},{8,7},{9,10},{10,... | collective-permute-start | bytes 294920 | tf_op jit(solution)/shard_map/ppermute | solution.py:246
  45.3 3.3 %collective-permute-done.10.far = bf16[3,1,128,128]{3,2,1,0:T(8,128)(2,1)S(1)} collective-permute-done((bf16[3,1,128,128]{3,2,1,0:T(8,128)(2,1)S(1)}, bf16[3,1,128,128]{3,2,1,0:T(8,128)(2,1)S(1)}, u32[]{:S(2)}, u32[]{:S(2)}) %collective-permute-start.10) | collective-permute-done | bytes 98336 | tf_op jit(solution)/shard_map/ppermute | solution.py:246
  50.1 2.3 %shard_map.80 = (f32[4,28,16,128]{3,2,1,0:T(8,128)S(1)}, bf16[4,28,16,128]{3,2,1,0:T(8,128)(2,1)S(1)}) custom-call(bf16[3,4,128,128]{3,2,1,0:T(8,128)(2,1)S(1)} %get-tuple-element.32.centre, bf16[2,4,128,128]{3,2,1,0:T(8,128)(2,1)S(1)} %collective-permute-done.4.time, bf16[3,1,128,128]{3,2,1,0:T(8,128)(2,1)S(1)} %collective-permute-done.5.near, ...), custom_call_target="tpu_custom_call" | custom-call | flops 1358954496 | bytes 2752512 | tf_op jit(solution)/shard_map/pallas_call | solution.py:19
  52.5 3.6 %collective-permute-done.11.corners = bf16[2,2,128,128]{3,2,1,0:T(8,128)(2,1)S(1)} collective-permute-done((bf16[2,2,128,128]{3,2,1,0:T(8,128)(2,1)S(1)}, bf16[2,2,128,128]{3,2,1,0:T(8,128)(2,1)S(1)}, u32[]{:S(2)}, u32[]{:S(2)}) %collective-permute-start.11) | collective-permute-done | bytes 131104 | tf_op jit(solution)/shard_map/ppermute | solution.py:248
  56.1 2.6 %shard_map.77 = (bf16[3,4,128,128]{3,2,1,0:T(8,128)(2,1)S(1)}, bf16[2,4,128,128]{3,2,1,0:T(8,128)(2,1)S(1)}, bf16[3,1,128,128]{3,2,1,0:T(8,128)(2,1)S(1)}, bf16[3,1,128,128]{3,2,1,0:T(8,128)(2,1)S(1)}) custom-call(bf16[3,4,128,128]{3,2,1,0:T(8,128)(2,1)S(1)} %get-tuple-element.37.centre.grad, bf16[2,4,128,128]{3,2,1,0:T(8,128)(2,1)S(1)} %collective-permute-done.8.time, ...), custom_call_target="tpu_custom_call" | custom-call | flops 1358954496 | bytes 3506176 | tf_op jit(solution)/shard_map/pallas_call | solution.py:19
  58.7 2.3 %shard_map.79 = (f32[4,28,16,128]{3,2,1,0:T(8,128)S(1)}, bf16[4,28,16,128]{3,2,1,0:T(8,128)(2,1)S(1)}) custom-call(bf16[3,4,128,128]{3,2,1,0:T(8,128)(2,1)S(1)} %bitcast.10, bf16[2,4,128,128]{3,2,1,0:T(8,128)(2,1)S(1)} %collective-permute-done.time, bf16[3,1,128,128]{3,2,1,0:T(8,128)(2,1)S(1)} %collective-permute-done.1.near, ...), custom_call_target="tpu_custom_call" | custom-call | flops 1358954496 | bytes 2752512 | tf_op jit(solution)/shard_map/pallas_call | solution.py:19
  63.2 3.8 %collective-permute-start.20 = (bf16[4,14,16,128]{3,2,1,0:T(8,128)(2,1)S(1)}, bf16[4,14,16,128]{3,2,1,0:T(8,128)(2,1)S(1)}, u32[]{:S(2)}, u32[]{:S(2)}) collective-permute-start(bf16[4,14,16,128]{3,2,1,0:T(8,128)(2,1)S(1)} %get-tuple-element.53), channel_id=1, source_target_pairs={{0,3},{1,2},{2,1},{3,0},{4,7},{5,6},{6,5},{7,4},{8,11},{9,10},{10,... | collective-permute-start | bytes 688136 | tf_op jit(solution)/shard_map/ppermute | solution.py:212
  67.0 3.2 %collective-permute-done.18.one = bf16[4,14,16,128]{3,2,1,0:T(8,128)(2,1)S(1)} collective-permute-done((bf16[4,14,16,128]{3,2,1,0:T(8,128)(2,1)S(1)}, bf16[4,14,16,128]{3,2,1,0:T(8,128)(2,1)S(1)}, u32[]{:S(2)}, u32[]{:S(2)}) %collective-permute-start.18) | collective-permute-done | bytes 229408 | tf_op jit(solution)/shard_map/ppermute | solution.py:212
  70.2 3.0 %collective-permute-done.19.two = bf16[4,14,16,128]{3,2,1,0:T(8,128)(2,1)S(1)} collective-permute-done((bf16[4,14,16,128]{3,2,1,0:T(8,128)(2,1)S(1)}, bf16[4,14,16,128]{3,2,1,0:T(8,128)(2,1)S(1)}, u32[]{:S(2)}, u32[]{:S(2)}) %collective-permute-start.19) | collective-permute-done | bytes 229408 | tf_op jit(solution)/shard_map/ppermute | solution.py:212
  73.2 4.4 %collective-permute-done.20.three = bf16[4,14,16,128]{3,2,1,0:T(8,128)(2,1)S(1)} collective-permute-done((bf16[4,14,16,128]{3,2,1,0:T(8,128)(2,1)S(1)}, bf16[4,14,16,128]{3,2,1,0:T(8,128)(2,1)S(1)}, u32[]{:S(2)}, u32[]{:S(2)}) %collective-permute-start.20) | collective-permute-done | bytes 229408 | tf_op jit(solution)/shard_map/ppermute | solution.py:212
  77.8 2.7 %collective-permute-start.22 = (bf16[14,16,128]{2,1,0:T(8,128)(2,1)S(1)}, bf16[14,16,128]{2,1,0:T(8,128)(2,1)S(1)}, u32[]{:S(2)}, u32[]{:S(2)}) collective-permute-start(bf16[14,16,128]{2,1,0:T(8,128)(2,1)S(1)} %get-tuple-element.56), channel_id=1, source_target_pairs={{0,8},{1,9},{2,10},{3,11},{4,12},{5,13},{6,14},{7,15},{8,0},{9,1},... | collective-permute-start | bytes 172040 | tf_op jit(solution)/shard_map/ppermute | solution.py:212
  82.7 2.7 %collective-permute-done.23.three = bf16[14,16,128]{2,1,0:T(8,128)(2,1)S(1)} collective-permute-done((bf16[14,16,128]{2,1,0:T(8,128)(2,1)S(1)}, bf16[14,16,128]{2,1,0:T(8,128)(2,1)S(1)}, u32[]{:S(2)}, u32[]{:S(2)}) %collective-permute-start.23) | collective-permute-done | bytes 57376 | tf_op jit(solution)/shard_map/ppermute | solution.py:212
  86.0 1.9 %collective-permute-start.25 = (bf16[14,16,128]{2,1,0:T(8,128)(2,1)S(1)}, bf16[14,16,128]{2,1,0:T(8,128)(2,1)S(1)}, u32[]{:S(2)}, u32[]{:S(2)}) collective-permute-start(bf16[14,16,128]{2,1,0:T(8,128)(2,1)S(1)} %shard_map.83.own), channel_id=1, source_target_pairs={{0,32},{1,33},{2,34},{3,35},{4,36},{5,37},{6,38},{7,39},{8,40},{9,... | collective-permute-start | bytes 172040 | tf_op jit(solution)/shard_map/ppermute | solution.py:212
  88.7 2.8 %collective-permute-start.14 = (bf16[3,1,128,128]{3,2,1,0:T(8,128)(2,1)S(1)}, bf16[3,1,128,128]{3,2,1,0:T(8,128)(2,1)S(1)}, u32[]{:S(2)}, u32[]{:S(2)}) collective-permute-start(bf16[3,1,128,128]{3,2,1,0:T(8,128)(2,1)S(1)} %get-tuple-element.45), channel_id=1, source_target_pairs={{0,15},{1,2},{2,1},{3,4},{4,3},{5,6},{6,5},{7,8},{8,7},{9,10},{10,... | collective-permute-start | bytes 294920 | tf_op jit(solution)/shard_map/ppermute | solution.py:246
  92.3 2.6 %collective-permute-start.27 = (bf16[14,16,128]{2,1,0:T(8,128)(2,1)S(1)}, bf16[14,16,128]{2,1,0:T(8,128)(2,1)S(1)}, u32[]{:S(2)}, u32[]{:S(2)}) collective-permute-start(bf16[14,16,128]{2,1,0:T(8,128)(2,1)S(1)} %shard_map.84.own), channel_id=1, source_target_pairs={{0,4},{1,5},{2,6},{3,7},{4,0},{5,1},{6,2},{7,3},{8,12},{9,13},{10,... | collective-permute-start | bytes 172040 | tf_op jit(solution)/shard_map/ppermute | solution.py:212
  96.1 4.8 %collective-permute-start.12 = (bf16[2,4,128,128]{3,2,1,0:T(8,128)(2,1)S(1)}, bf16[2,4,128,128]{3,2,1,0:T(8,128)(2,1)S(1)}, u32[]{:S(2)}, u32[]{:S(2)}) collective-permute-start(bf16[2,4,128,128]{3,2,1,0:T(8,128)(2,1)S(1)} %get-tuple-element.43), channel_id=1, source_target_pairs={{0,48},{16,0},{32,16},{48,32},{1,49},{17,1},{33,17},{49,33},{2,50}... | collective-permute-start | bytes 786440 | tf_op jit(solution)/shard_map/ppermute | solution.py:244
  101.8 2.5 %collective-permute-start.30 = (bf16[4,14,16,128]{3,2,1,0:T(8,128)(2,1)S(1)}, bf16[4,14,16,128]{3,2,1,0:T(8,128)(2,1)S(1)}, u32[]{:S(2)}, u32[]{:S(2)}) collective-permute-start(bf16[4,14,16,128]{3,2,1,0:T(8,128)(2,1)S(1)} %shard_map.85.refs_0_), channel_id=1, source_target_pairs={{0,1},{1,0},{2,3},{3,2},{4,5},{5,4},{6,7},{7,6},{8,9},{9,8},{10,11... | collective-permute-start | bytes 688136 | tf_op jit(solution)/shard_map/ppermute | solution.py:212
  104.3 2.4 %collective-permute-start.15 = (bf16[2,2,128,128]{3,2,1,0:T(8,128)(2,1)S(1)}, bf16[2,2,128,128]{3,2,1,0:T(8,128)(2,1)S(1)}, u32[]{:S(2)}, u32[]{:S(2)}) collective-permute-start(bf16[2,2,128,128]{3,2,1,0:T(8,128)(2,1)S(1)} %pad_maximum_fusion), channel_id=1, source_target_pairs={{0,48},{16,0},{32,16},{48,32},{1,49},{17,1},{33,17},{49,33},{2,50}... | collective-permute-start | bytes 393224 | tf_op jit(solution)/shard_map/ppermute | solution.py:248
  106.7 4.1 %collective-permute-done.15.corners = bf16[2,2,128,128]{3,2,1,0:T(8,128)(2,1)S(1)} collective-permute-done((bf16[2,2,128,128]{3,2,1,0:T(8,128)(2,1)S(1)}, bf16[2,2,128,128]{3,2,1,0:T(8,128)(2,1)S(1)}, u32[]{:S(2)}, u32[]{:S(2)}) %collective-permute-start.15) | collective-permute-done | bytes 131104 | tf_op jit(solution)/shard_map/ppermute | solution.py:248
  110.7 3.4 %collective-permute-done.32.refs_3_ = bf16[4,14,16,128]{3,2,1,0:T(8,128)(2,1)S(1)} collective-permute-done((bf16[4,14,16,128]{3,2,1,0:T(8,128)(2,1)S(1)}, bf16[4,14,16,128]{3,2,1,0:T(8,128)(2,1)S(1)}, u32[]{:S(2)}, u32[]{:S(2)}) %collective-permute-start.32) | collective-permute-done | bytes 229408 | tf_op jit(solution)/shard_map/ppermute | solution.py:212
  115.8 3.1 %shard_map.78 = bf16[3,4,128,128]{3,2,1,0:T(8,128)(2,1)} custom-call(bf16[3,4,128,128]{3,2,1,0:T(8,128)(2,1)S(1)} %get-tuple-element.42.centre.grad, bf16[2,4,128,128]{3,2,1,0:T(8,128)(2,1)S(1)} %collective-permute-done.12.time, bf16[3,1,128,128]{3,2,1,0:T(8,128)(2,1)S(1)} %collective-permute-done.13.near, ...), custom_call_target="tpu_custom_call" | custom-call | flops 1358954496 | bytes 2260992 | tf_op jit(solution)/shard_map/pallas_call | solution.py:19
  118.8 2.1 %shard_map.86 = (f32[27,8,16,128]{3,2,1,0:T(8,128)}, f32[27,8,16,128]{3,2,1,0:T(8,128)}) custom-call(bf16[4,14,16,128]{3,2,1,0:T(8,128)(2,1)S(1)} %shard_map.85.refs_0_, bf16[4,14,16,128]{3,2,1,0:T(8,128)(2,1)S(1)} %collective-permute-done.30.refs_1_, bf16[4,14,16,128]{3,2,1,0:T(8,128)(2,1)S(1)} %collective-permute-done.31.refs_2_, ...), custom_call_target="tpu_custom_call" | custom-call | flops 3670016 | bytes 5373952 | tf_op jit(solution)/shard_map/pallas_call | solution.py:19
  (72 shorter events, 19.2 us)
Async XLA Ops:
  1.6 11.3 %collective-permute-start.2 = (bf16[3,1,128,128]{3,2,1,0:T(8,128)(2,1)S(1)}, bf16[3,1,128,128]{3,2,1,0:T(8,128)(2,1)S(1)}, u32[]{:S(2)}, u32[]{:S(2)}) collective-permute-start(bf16[3,1,128,128]{3,2,1,0:T(8,128)(2,1)S(1)} %get-tuple-element.60), channel_id=1, source_target_pairs={{0,15},{1,2},{2,1},{3,4},{4,3},{5,6},{6,5},{7,8},{8,7},{9,10},{10,... | collective-permute-start | bytes 294920 | tf_op jit(solution)/shard_map/ppermute | solution.py:246
  7.4 5.5 %collective-permute-start.1 = (bf16[3,1,128,128]{3,2,1,0:T(8,128)(2,1)S(1)}, bf16[3,1,128,128]{3,2,1,0:T(8,128)(2,1)S(1)}, u32[]{:S(2)}, u32[]{:S(2)}) collective-permute-start(bf16[3,1,128,128]{3,2,1,0:T(8,128)(2,1)S(1)} %get-tuple-element.61), channel_id=1, source_target_pairs={{0,1},{1,0},{2,3},{3,2},{4,5},{5,4},{6,7},{7,6},{8,9},{9,8},{10,11... | collective-permute-start | bytes 294920 | tf_op jit(solution)/shard_map/ppermute | solution.py:245
  8.4 10.1 %collective-permute-start = (bf16[2,4,128,128]{3,2,1,0:T(8,128)(2,1)S(1)}, bf16[2,4,128,128]{3,2,1,0:T(8,128)(2,1)S(1)}, u32[]{:S(2)}, u32[]{:S(2)}) collective-permute-start(bf16[2,4,128,128]{3,2,1,0:T(8,128)(2,1)S(1)} %slice_bitcast_fusion), channel_id=1, source_target_pairs={{0,16},{16,32},{32,48},{48,0},{1,17},{17,33},{33,49},{49,1},{2,18}... | collective-permute-start | bytes 786440 | tf_op jit(solution)/shard_map/ppermute | solution.py:244
  13.0 5.6 %collective-permute-start.3 = (bf16[2,2,128,128]{3,2,1,0:T(8,128)(2,1)S(1)}, bf16[2,2,128,128]{3,2,1,0:T(8,128)(2,1)S(1)}, u32[]{:S(2)}, u32[]{:S(2)}) collective-permute-start(bf16[2,2,128,128]{3,2,1,0:T(8,128)(2,1)S(1)} %pad_maximum_fusion.3), channel_id=1, source_target_pairs={{0,16},{16,32},{32,48},{48,0},{1,17},{17,33},{33,49},{49,1},{2,18}... | collective-permute-start | bytes 393224 | tf_op jit(solution)/shard_map/ppermute | solution.py:248
  23.1 7.4 %collective-permute-start.5 = (bf16[3,1,128,128]{3,2,1,0:T(8,128)(2,1)S(1)}, bf16[3,1,128,128]{3,2,1,0:T(8,128)(2,1)S(1)}, u32[]{:S(2)}, u32[]{:S(2)}) collective-permute-start(bf16[3,1,128,128]{3,2,1,0:T(8,128)(2,1)S(1)} %get-tuple-element.34), channel_id=1, source_target_pairs={{0,1},{1,0},{2,3},{3,2},{4,5},{5,4},{6,7},{7,6},{8,9},{9,8},{10,11... | collective-permute-start | bytes 294920 | tf_op jit(solution)/shard_map/ppermute | solution.py:245
  24.0 6.8 %collective-permute-start.6 = (bf16[3,1,128,128]{3,2,1,0:T(8,128)(2,1)S(1)}, bf16[3,1,128,128]{3,2,1,0:T(8,128)(2,1)S(1)}, u32[]{:S(2)}, u32[]{:S(2)}) collective-permute-start(bf16[3,1,128,128]{3,2,1,0:T(8,128)(2,1)S(1)} %get-tuple-element.35), channel_id=1, source_target_pairs={{0,15},{1,2},{2,1},{3,4},{4,3},{5,6},{6,5},{7,8},{8,7},{9,10},{10,... | collective-permute-start | bytes 294920 | tf_op jit(solution)/shard_map/ppermute | solution.py:246
  26.3 11.9 %collective-permute-start.4 = (bf16[2,4,128,128]{3,2,1,0:T(8,128)(2,1)S(1)}, bf16[2,4,128,128]{3,2,1,0:T(8,128)(2,1)S(1)}, u32[]{:S(2)}, u32[]{:S(2)}) collective-permute-start(bf16[2,4,128,128]{3,2,1,0:T(8,128)(2,1)S(1)} %get-tuple-element.33), channel_id=1, source_target_pairs={{0,16},{16,32},{32,48},{48,0},{1,17},{17,33},{33,49},{49,1},{2,18}... | collective-permute-start | bytes 786440 | tf_op jit(solution)/shard_map/ppermute | solution.py:244
  30.8 7.4 %collective-permute-start.7 = (bf16[2,2,128,128]{3,2,1,0:T(8,128)(2,1)S(1)}, bf16[2,2,128,128]{3,2,1,0:T(8,128)(2,1)S(1)}, u32[]{:S(2)}, u32[]{:S(2)}) collective-permute-start(bf16[2,2,128,128]{3,2,1,0:T(8,128)(2,1)S(1)} %pad_maximum_fusion.2), channel_id=1, source_target_pairs={{0,16},{16,32},{32,48},{48,0},{1,17},{17,33},{33,49},{49,1},{2,18}... | collective-permute-start | bytes 393224 | tf_op jit(solution)/shard_map/ppermute | solution.py:248
  41.5 7.1 %collective-permute-start.10 = (bf16[3,1,128,128]{3,2,1,0:T(8,128)(2,1)S(1)}, bf16[3,1,128,128]{3,2,1,0:T(8,128)(2,1)S(1)}, u32[]{:S(2)}, u32[]{:S(2)}) collective-permute-start(bf16[3,1,128,128]{3,2,1,0:T(8,128)(2,1)S(1)} %get-tuple-element.40), channel_id=1, source_target_pairs={{0,15},{1,2},{2,1},{3,4},{4,3},{5,6},{6,5},{7,8},{8,7},{9,10},{10,... | collective-permute-start | bytes 294920 | tf_op jit(solution)/shard_map/ppermute | solution.py:246
  43.5 12.7 %collective-permute-start.8 = (bf16[2,4,128,128]{3,2,1,0:T(8,128)(2,1)S(1)}, bf16[2,4,128,128]{3,2,1,0:T(8,128)(2,1)S(1)}, u32[]{:S(2)}, u32[]{:S(2)}) collective-permute-start(bf16[2,4,128,128]{3,2,1,0:T(8,128)(2,1)S(1)} %get-tuple-element.38), channel_id=1, source_target_pairs={{0,48},{16,0},{32,16},{48,32},{1,49},{17,1},{33,17},{49,33},{2,50}... | collective-permute-start | bytes 786440 | tf_op jit(solution)/shard_map/ppermute | solution.py:244
  48.6 7.5 %collective-permute-start.11 = (bf16[2,2,128,128]{3,2,1,0:T(8,128)(2,1)S(1)}, bf16[2,2,128,128]{3,2,1,0:T(8,128)(2,1)S(1)}, u32[]{:S(2)}, u32[]{:S(2)}) collective-permute-start(bf16[2,2,128,128]{3,2,1,0:T(8,128)(2,1)S(1)} %pad_maximum_fusion.1), channel_id=1, source_target_pairs={{0,48},{16,0},{32,16},{48,32},{1,49},{17,1},{33,17},{49,33},{2,50}... | collective-permute-start | bytes 393224 | tf_op jit(solution)/shard_map/ppermute | solution.py:248
  52.3 8.7 %collective-permute-start.17 = (bf16[4,28,16,128]{3,2,1,0:T(8,128)(2,1)S(1)}, bf16[4,28,16,128]{3,2,1,0:T(8,128)(2,1)S(1)}, u32[]{:S(2)}, u32[]{:S(2)}) collective-permute-start(bf16[4,28,16,128]{3,2,1,0:T(8,128)(2,1)S(1)} %get-tuple-element.49), channel_id=1, source_target_pairs={{0,16},{1,17},{2,18},{3,19},{4,20},{5,21},{6,22},{7,23},{8,24},{9,... | collective-permute-start | bytes 1376264 | tf_op jit(solution)/shard_map/ppermute | solution.py:212
  63.0 7.1 %collective-permute-start.18 = (bf16[4,14,16,128]{3,2,1,0:T(8,128)(2,1)S(1)}, bf16[4,14,16,128]{3,2,1,0:T(8,128)(2,1)S(1)}, u32[]{:S(2)}, u32[]{:S(2)}) collective-permute-start(bf16[4,14,16,128]{3,2,1,0:T(8,128)(2,1)S(1)} %get-tuple-element.51), channel_id=1, source_target_pairs={{0,1},{1,0},{2,3},{3,2},{4,5},{5,4},{6,7},{7,6},{8,9},{9,8},{10,11... | collective-permute-start | bytes 688136 | tf_op jit(solution)/shard_map/ppermute | solution.py:212
  63.1 10.1 %collective-permute-start.19 = (bf16[4,14,16,128]{3,2,1,0:T(8,128)(2,1)S(1)}, bf16[4,14,16,128]{3,2,1,0:T(8,128)(2,1)S(1)}, u32[]{:S(2)}, u32[]{:S(2)}) collective-permute-start(bf16[4,14,16,128]{3,2,1,0:T(8,128)(2,1)S(1)} %get-tuple-element.52), channel_id=1, source_target_pairs={{0,2},{1,3},{2,0},{3,1},{4,6},{5,7},{6,4},{7,5},{8,10},{9,11},{10,... | collective-permute-start | bytes 688136 | tf_op jit(solution)/shard_map/ppermute | solution.py:212
  63.2 14.4 %collective-permute-start.20 = (bf16[4,14,16,128]{3,2,1,0:T(8,128)(2,1)S(1)}, bf16[4,14,16,128]{3,2,1,0:T(8,128)(2,1)S(1)}, u32[]{:S(2)}, u32[]{:S(2)}) collective-permute-start(bf16[4,14,16,128]{3,2,1,0:T(8,128)(2,1)S(1)} %get-tuple-element.53), channel_id=1, source_target_pairs={{0,3},{1,2},{2,1},{3,0},{4,7},{5,6},{6,5},{7,4},{8,11},{9,10},{10,... | collective-permute-start | bytes 688136 | tf_op jit(solution)/shard_map/ppermute | solution.py:212
  77.7 3.9 %collective-permute-start.21 = (bf16[14,16,128]{2,1,0:T(8,128)(2,1)S(1)}, bf16[14,16,128]{2,1,0:T(8,128)(2,1)S(1)}, u32[]{:S(2)}, u32[]{:S(2)}) collective-permute-start(bf16[14,16,128]{2,1,0:T(8,128)(2,1)S(1)} %get-tuple-element.55), channel_id=1, source_target_pairs={{0,4},{1,5},{2,6},{3,7},{4,0},{5,1},{6,2},{7,3},{8,12},{9,13},{10,... | collective-permute-start | bytes 172040 | tf_op jit(solution)/shard_map/ppermute | solution.py:212
  77.8 4.9 %collective-permute-start.22 = (bf16[14,16,128]{2,1,0:T(8,128)(2,1)S(1)}, bf16[14,16,128]{2,1,0:T(8,128)(2,1)S(1)}, u32[]{:S(2)}, u32[]{:S(2)}) collective-permute-start(bf16[14,16,128]{2,1,0:T(8,128)(2,1)S(1)} %get-tuple-element.56), channel_id=1, source_target_pairs={{0,8},{1,9},{2,10},{3,11},{4,12},{5,13},{6,14},{7,15},{8,0},{9,1},... | collective-permute-start | bytes 172040 | tf_op jit(solution)/shard_map/ppermute | solution.py:212
  80.5 4.8 %collective-permute-start.23 = (bf16[14,16,128]{2,1,0:T(8,128)(2,1)S(1)}, bf16[14,16,128]{2,1,0:T(8,128)(2,1)S(1)}, u32[]{:S(2)}, u32[]{:S(2)}) collective-permute-start(bf16[14,16,128]{2,1,0:T(8,128)(2,1)S(1)} %get-tuple-element.57), channel_id=1, source_target_pairs={{0,12},{1,13},{2,14},{3,15},{4,8},{5,9},{6,10},{7,11},{8,4},{9,5},... | collective-permute-start | bytes 172040 | tf_op jit(solution)/shard_map/ppermute | solution.py:212
  85.4 6.2 %collective-permute-start.26 = (bf16[14,16,128]{2,1,0:T(8,128)(2,1)S(1)}, bf16[14,16,128]{2,1,0:T(8,128)(2,1)S(1)}, u32[]{:S(2)}, u32[]{:S(2)}) collective-permute-start(bf16[14,16,128]{2,1,0:T(8,128)(2,1)S(1)} %shard_map.83.own), channel_id=1, source_target_pairs={{0,96},{1,97},{2,98},{3,99},{4,100},{5,101},{6,102},{7,103},{8,104... | collective-permute-start | bytes 172040 | tf_op jit(solution)/shard_map/ppermute | solution.py:212
  86.0 5.5 %collective-permute-start.25 = (bf16[14,16,128]{2,1,0:T(8,128)(2,1)S(1)}, bf16[14,16,128]{2,1,0:T(8,128)(2,1)S(1)}, u32[]{:S(2)}, u32[]{:S(2)}) collective-permute-start(bf16[14,16,128]{2,1,0:T(8,128)(2,1)S(1)} %shard_map.83.own), channel_id=1, source_target_pairs={{0,32},{1,33},{2,34},{3,35},{4,36},{5,37},{6,38},{7,39},{8,40},{9,... | collective-permute-start | bytes 172040 | tf_op jit(solution)/shard_map/ppermute | solution.py:212
  88.7 13.1 %collective-permute-start.13 = (bf16[3,1,128,128]{3,2,1,0:T(8,128)(2,1)S(1)}, bf16[3,1,128,128]{3,2,1,0:T(8,128)(2,1)S(1)}, u32[]{:S(2)}, u32[]{:S(2)}) collective-permute-start(bf16[3,1,128,128]{3,2,1,0:T(8,128)(2,1)S(1)} %get-tuple-element.44), channel_id=1, source_target_pairs={{0,1},{1,0},{2,3},{3,2},{4,5},{5,4},{6,7},{7,6},{8,9},{9,8},{10,11... | collective-permute-start | bytes 294920 | tf_op jit(solution)/shard_map/ppermute | solution.py:245
  88.7 15.6 %collective-permute-start.14 = (bf16[3,1,128,128]{3,2,1,0:T(8,128)(2,1)S(1)}, bf16[3,1,128,128]{3,2,1,0:T(8,128)(2,1)S(1)}, u32[]{:S(2)}, u32[]{:S(2)}) collective-permute-start(bf16[3,1,128,128]{3,2,1,0:T(8,128)(2,1)S(1)} %get-tuple-element.45), channel_id=1, source_target_pairs={{0,15},{1,2},{2,1},{3,4},{4,3},{5,6},{6,5},{7,8},{8,7},{9,10},{10,... | collective-permute-start | bytes 294920 | tf_op jit(solution)/shard_map/ppermute | solution.py:246
  91.6 4.5 %collective-permute-start.29 = (bf16[14,16,128]{2,1,0:T(8,128)(2,1)S(1)}, bf16[14,16,128]{2,1,0:T(8,128)(2,1)S(1)}, u32[]{:S(2)}, u32[]{:S(2)}) collective-permute-start(bf16[14,16,128]{2,1,0:T(8,128)(2,1)S(1)} %shard_map.84.own), channel_id=1, source_target_pairs={{0,12},{1,13},{2,14},{3,15},{4,8},{5,9},{6,10},{7,11},{8,4},{9,5},... | collective-permute-start | bytes 172040 | tf_op jit(solution)/shard_map/ppermute | solution.py:212
  92.3 8.7 %collective-permute-start.28 = (bf16[14,16,128]{2,1,0:T(8,128)(2,1)S(1)}, bf16[14,16,128]{2,1,0:T(8,128)(2,1)S(1)}, u32[]{:S(2)}, u32[]{:S(2)}) collective-permute-start(bf16[14,16,128]{2,1,0:T(8,128)(2,1)S(1)} %shard_map.84.own), channel_id=1, source_target_pairs={{0,8},{1,9},{2,10},{3,11},{4,12},{5,13},{6,14},{7,15},{8,0},{9,1},... | collective-permute-start | bytes 172040 | tf_op jit(solution)/shard_map/ppermute | solution.py:212
  92.3 8.7 %collective-permute-start.27 = (bf16[14,16,128]{2,1,0:T(8,128)(2,1)S(1)}, bf16[14,16,128]{2,1,0:T(8,128)(2,1)S(1)}, u32[]{:S(2)}, u32[]{:S(2)}) collective-permute-start(bf16[14,16,128]{2,1,0:T(8,128)(2,1)S(1)} %shard_map.84.own), channel_id=1, source_target_pairs={{0,4},{1,5},{2,6},{3,7},{4,0},{5,1},{6,2},{7,3},{8,12},{9,13},{10,... | collective-permute-start | bytes 172040 | tf_op jit(solution)/shard_map/ppermute | solution.py:212
  96.1 19.7 %collective-permute-start.12 = (bf16[2,4,128,128]{3,2,1,0:T(8,128)(2,1)S(1)}, bf16[2,4,128,128]{3,2,1,0:T(8,128)(2,1)S(1)}, u32[]{:S(2)}, u32[]{:S(2)}) collective-permute-start(bf16[2,4,128,128]{3,2,1,0:T(8,128)(2,1)S(1)} %get-tuple-element.43), channel_id=1, source_target_pairs={{0,48},{16,0},{32,16},{48,32},{1,49},{17,1},{33,17},{49,33},{2,50}... | collective-permute-start | bytes 786440 | tf_op jit(solution)/shard_map/ppermute | solution.py:244
  101.0 13.2 %collective-permute-start.32 = (bf16[4,14,16,128]{3,2,1,0:T(8,128)(2,1)S(1)}, bf16[4,14,16,128]{3,2,1,0:T(8,128)(2,1)S(1)}, u32[]{:S(2)}, u32[]{:S(2)}) collective-permute-start(bf16[4,14,16,128]{3,2,1,0:T(8,128)(2,1)S(1)} %shard_map.85.refs_0_), channel_id=1, source_target_pairs={{0,3},{1,2},{2,1},{3,0},{4,7},{5,6},{6,5},{7,4},{8,11},{9,10},{10,... | collective-permute-start | bytes 688136 | tf_op jit(solution)/shard_map/ppermute | solution.py:212
  101.2 14.0 %collective-permute-start.31 = (bf16[4,14,16,128]{3,2,1,0:T(8,128)(2,1)S(1)}, bf16[4,14,16,128]{3,2,1,0:T(8,128)(2,1)S(1)}, u32[]{:S(2)}, u32[]{:S(2)}) collective-permute-start(bf16[4,14,16,128]{3,2,1,0:T(8,128)(2,1)S(1)} %shard_map.85.refs_0_), channel_id=1, source_target_pairs={{0,2},{1,3},{2,0},{3,1},{4,6},{5,7},{6,4},{7,5},{8,10},{9,11},{10,... | collective-permute-start | bytes 688136 | tf_op jit(solution)/shard_map/ppermute | solution.py:212
  101.8 13.4 %collective-permute-start.30 = (bf16[4,14,16,128]{3,2,1,0:T(8,128)(2,1)S(1)}, bf16[4,14,16,128]{3,2,1,0:T(8,128)(2,1)S(1)}, u32[]{:S(2)}, u32[]{:S(2)}) collective-permute-start(bf16[4,14,16,128]{3,2,1,0:T(8,128)(2,1)S(1)} %shard_map.85.refs_0_), channel_id=1, source_target_pairs={{0,1},{1,0},{2,3},{3,2},{4,5},{5,4},{6,7},{7,6},{8,9},{9,8},{10,11... | collective-permute-start | bytes 688136 | tf_op jit(solution)/shard_map/ppermute | solution.py:212
  104.3 6.4 %collective-permute-start.15 = (bf16[2,2,128,128]{3,2,1,0:T(8,128)(2,1)S(1)}, bf16[2,2,128,128]{3,2,1,0:T(8,128)(2,1)S(1)}, u32[]{:S(2)}, u32[]{:S(2)}) collective-permute-start(bf16[2,2,128,128]{3,2,1,0:T(8,128)(2,1)S(1)} %pad_maximum_fusion), channel_id=1, source_target_pairs={{0,48},{16,0},{32,16},{48,32},{1,49},{17,1},{33,17},{49,33},{2,50}... | collective-permute-start | bytes 393224 | tf_op jit(solution)/shard_map/ppermute | solution.py:248
  110.7 8.1 %collective-permute-start.33 = (bf16[4,14,16,128]{3,2,1,0:T(8,128)(2,1)S(1)}, bf16[4,14,16,128]{3,2,1,0:T(8,128)(2,1)S(1)}, u32[]{:S(2)}, u32[]{:S(2)}) collective-permute-start(bf16[4,14,16,128]{3,2,1,0:T(8,128)(2,1)S(1)} %shard_map.85.refs_0_), channel_id=1, source_target_pairs={{0,16},{1,17},{2,18},{3,19},{4,20},{5,21},{6,22},{7,23},{8,24},{9,... | collective-permute-start | bytes 688136 | tf_op jit(solution)/shard_map/ppermute | solution.py:212
  114.2 4.6 %collective-permute-start.36 = (bf16[4,14,16,128]{3,2,1,0:T(8,128)(2,1)S(1)}, bf16[4,14,16,128]{3,2,1,0:T(8,128)(2,1)S(1)}, u32[]{:S(2)}, u32[]{:S(2)}) collective-permute-start(bf16[4,14,16,128]{3,2,1,0:T(8,128)(2,1)S(1)} %collective-permute-done.32.refs_3_), channel_id=1, source_target_pairs={{0,16},{1,17},{2,18},{3,19},{4,20},{5,21},{6,22},{7,23},{8,24},{9,... | collective-permute-start | bytes 688136 | tf_op jit(solution)/shard_map/ppermute | solution.py:212
  (11 other events, 109.2 us)

commit v2 on v1

--- a/solution.py
+++ b/solution.py
@@ -11,20 +11,51 @@
 ALL = ("dp", "tm", "height")
 PARAMS = pltpu.CompilerParams(vmem_limit_bytes=48 * 1024 * 1024)
 VMEM = pl.BlockSpec(memory_space=pltpu.VMEM)
+HBM = pl.BlockSpec(memory_space=pltpu.HBM)
+ANY = pl.BlockSpec(memory_space=pl.ANY)
 TAPS = [(a, b) for a in range(3) for b in range(3)]
 
 
-def call(kernel, outs, scratch, flops, *args):
+def call(kernel, outs, scratch, flops, *args, after=(), inside=VMEM, outside=()):
     moved = sum(x.size * x.dtype.itemsize for x in (*args, *outs))
+
+    def run(*refs):
+        kernel(*refs[: len(args)], *refs[len(args) + len(after) :])
+
     return pl.pallas_call(
-        kernel,
+        run,
         out_shape=outs,
-        in_specs=[VMEM] * len(args),
-        out_specs=[VMEM] * len(outs),
+        in_specs=[inside] * len(args) + [ANY] * len(after),
+        out_specs=list(outside) + [VMEM] * (len(outs) - len(outside)),
         scratch_shapes=scratch,
         compiler_params=PARAMS,
         cost_estimate=pl.CostEstimate(flops=flops, bytes_accessed=moved, transcendentals=0),
-    )(*args)
+    )(*args, *after)
+
+
+def copied(pairs, sems):
+    copies = [pltpu.make_async_copy(source, target, sems.at[i]) for i, (source, target) in enumerate(pairs)]
+    for copy in copies:
+        copy.start()
+    return copies
+
+
+def cut_kernel(block, whole, last, near, far, sems):
+    frames, rows = block.shape[:2]
+    pairs = [
+        (block.at[:, pl.ds(near_row(rows), 1)], near),
+        (block.at[:, pl.ds(far_row(rows), 1)], far),
+        (block.at[pl.ds(frames - 2, 2)], last),
+        (block, whole),
+    ]
+    for copy in copied(pairs, sems):
+        copy.wait()
+
+
+def taps_kernel(kernel, taps, held, sems):
+    (copy,) = copied([(kernel, held)], sems)
+    copy.wait()
+    lay_taps(taps, held, False)
 
 
 def lay(pad, centre, time, near, far, corners, ahead):
@@ -98,9 +129,8 @@
                 taps[place * c_in : (place + 1) * c_in, c * c_out : (c + 1) * c_out] = kernel[a, b, c]
 
 
-def first_kernel(centre, time, near, far, corners, kernel, slope, hidden, last, near_out, far_out, pad, taps):
+def first_kernel(centre, time, near, far, corners, taps, slope, hidden, last, near_out, far_out, pad):
     lay(pad, centre, time, near, far, corners, False)
-    lay_taps(taps, kernel, False)
     frames, rows = centre.shape[:2]
     for t in range(frames):
         z = convolve(pad, taps, t, rows, False)
@@ -111,7 +141,22 @@
 
 
 def second_kernel(
-    centre, time, near, far, corners, kernel, cotangent, output, grad, last, near_out, far_out, pad, taps
+    centre,
+    time,
+    near,
+    far,
+    corners,
+    kernel,
+    cotangent,
+    output,
+    grad,
+    last,
+    near_out,
+    far_out,
+    pad,
+    taps,
+    held,
+    sems,
 ):
     lay(pad, centre, time, near, far, corners, False)
     lay_taps(taps, kernel, False)
@@ -119,19 +164,26 @@
     for t in range(frames):
         z = convolve(pad, taps, t, rows, False)
         s = jax.nn.sigmoid(z)
-        output[t] = (z * s).astype(jnp.bfloat16).reshape(output.shape[1:])
+        held[t] = (z * s).astype(jnp.bfloat16).reshape(held.shape[1:])
+        pltpu.make_async_copy(held.at[t], output.at[t], sems.at[t]).start()
         steep = (s * (1.0 + z * (1.0 - s))).reshape(grad.shape[1:])
         grad[t] = (cotangent[t].astype(jnp.float32) * steep).astype(jnp.bfloat16)
     strips(grad, last, near_out, far_out, True)
-
-
-def back_kernel(centre, time, near, far, corners, kernel, grad, pad, taps):
+    for t in range(frames):
+        pltpu.make_async_copy(held.at[t], output.at[t], sems.at[t]).wait()
+
+
+def back_kernel(centre, time, near, far, corners, kernel, grad, ended, pad, taps, held, sems):
     lay(pad, centre, time, near, far, corners, True)
     lay_taps(taps, kernel, True)
     frames, rows = centre.shape[:2]
     for t in range(frames):
         z = convolve(pad, taps, t, rows, True)
-        grad[t] = z.astype(jnp.bfloat16).reshape(grad.shape[1:])
+        held[t] = z.astype(jnp.bfloat16).reshape(held.shape[1:])
+        pltpu.make_async_copy(held.at[t], grad.at[t], sems.at[t]).start()
+    ended[...] = jnp.zeros_like(ended)
+    for t in range(frames):
+        pltpu.make_async_copy(held.at[t], grad.at[t], sems.at[t]).wait()
 
 
 def back_slope_kernel(
@@ -173,9 +225,9 @@
 def first_scatter_kernel(keep_one, came_one, keep_two, came_two, mine, *sent):
     x = lax.axis_index("height") % 4
     for d, out in enumerate((mine, *sent)):
-        for first, keep, came in ((0, keep_one, came_one), (2, keep_two, came_two)):
+        for k, (keep, came) in enumerate(((keep_one, came_one), (keep_two, came_two))):
             total = keep[x ^ d] + came[x ^ d].astype(jnp.float32)
-            out[first : first + 2] = total.reshape(2, -1, *total.shape[1:]).astype(out.dtype)
+            out[:, k] = total.reshape(4, -1, *total.shape[1:]).astype(out.dtype)
 
 
 def second_scatter_kernel(own, one, two, three, mine, *sent):
@@ -190,63 +242,107 @@
     out[...] = ((own + one) + (two + three)).astype(out.dtype)
 
 
-def join_kernel(own, one, two, three, out):
+def join_kernel(own, one, three, two, out):
     y = lax.axis_index("height") // 4
     for d, part in enumerate((own, one, two, three)):
         out[y ^ d] = part[...]
 
 
 def gather_kernel(scale, *refs):
-    outs = refs[-2:]
+    pieces, outs, (held, sems) = refs[:8], refs[8:10], refs[10:]
     x, core = lax.axis_index("height") % 4, lax.axis_index("tm") % 2
     taps = outs[0].shape[0]
-    for d in range(4):
-        for half in range(2):
-            for k, out in enumerate(outs):
-                block = refs[4 * half + d][2 * k : 2 * k + 2].astype(jnp.float32) * scale
-                block = block.reshape(-1, *block.shape[2:])[:taps]
-                out[:, pl.ds((core ^ half) * 4 + (x ^ d), 1)] = block[:, None]
+    copies = []
+    for k, out in enumerate(outs):
+        for q in range(4):
+            first, count = 7 * q, min(7, taps - 7 * q)
+            for d in range(4):
+                for half in range(2):
+                    block = pieces[4 * half + d][q, k, :count].astype(jnp.float32) * scale
+                    held[k, pl.ds(first, count), pl.ds((core ^ half) * 4 + (x ^ d), 1)] = block[:, None]
+            part = pl.ds(first, count)
+            copies.append(pltpu.make_async_copy(held.at[k, part], out.at[part], sems.at[4 * k + q]))
+            copies[-1].start()
+    for copy in copies:
+        copy.wait()
 
 
 def swap(value, mask):
     return lax.ppermute(value, ALL, [(i, i ^ mask) for i in range(lax.axis_size(ALL))])
 
 
-def summed(one, two, scale):
+def kinds(shape):
+    return [jax.ShapeDtypeStruct(shape, jnp.float32)] + 3 * [jax.ShapeDtypeStruct(shape, jnp.bfloat16)]
+
+
+def started(one, two):
     _, taps, part, channels = one[0].shape
-    quarter = (taps // 2, part, channels)
-    size = 8 * taps * part * channels
-
-    def shapes(shape):
-        return [jax.ShapeDtypeStruct(shape, jnp.float32)] + 3 * [jax.ShapeDtypeStruct(shape, jnp.bfloat16)]
-
-    mine, *sent = call(first_scatter_kernel, shapes((4, *quarter)), [], size, *one, *two)
-    terms = [mine] + [swap(value, d) for d, value in enumerate(sent, 1)]
-    mine, *sent = call(second_scatter_kernel, shapes(quarter), [], size, *terms)
-    terms = [mine] + [swap(value, 4 * d) for d, value in enumerate(sent, 1)]
+    shape = (4, 2, taps // 4, part, channels)
+    halves = (one[0], swap(one[1], 16), two[0], swap(two[1], 16))
+    return call(first_scatter_kernel, kinds(shape), [], 8 * math.prod(shape), *halves)
+
+
+def summed(mine, sent, edged, ended):
+    quarter = mine.shape[1:]
+    size = math.prod(quarter)
     small = jax.ShapeDtypeStruct(quarter, jnp.bfloat16)
-    (total,) = call(add_kernel, [small], [], size // 4, *terms)
-    terms = [total] + [swap(total, mask) for mask in (64, 32, 96)]
-    (total,) = call(add_kernel, [small], [], size // 4, *terms)
-    terms = [total] + [swap(total, 4 * d) for d in (1, 2, 3)]
-    (total,) = call(join_kernel, [jax.ShapeDtypeStruct((4, *quarter), jnp.bfloat16)], [], size, *terms)
-    parts = [total] + [swap(total, d) for d in (1, 2, 3)]
-    parts += [swap(value, 16) for value in parts]
-    whole = jax.ShapeDtypeStruct((27, 8, part, channels), jnp.float32)
-    outs = call(functools.partial(gather_kernel, scale), [whole, whole], [], 8 * size, *parts)
+    one, two, three = (swap(value, d) for d, value in enumerate(sent, 1))
+    mine, *sent = call(second_scatter_kernel, kinds(quarter), [], 16 * size, mine, two, one, three)
+    one, two, three = (swap(value, 4 * d) for d, value in enumerate(sent, 1))
+    (total,) = call(add_kernel, [small], [], 4 * size, mine, two, one, three, after=edged)
+    one, two, three = (swap(total, mask) for mask in (64, 32, 96))
+    (total,) = call(add_kernel, [small], [], 4 * size, total, one, three, two, after=ended)
+    one, two, three = (swap(total, 4 * d) for d in (1, 2, 3))
+    (total,) = call(
+        join_kernel, [jax.ShapeDtypeStruct((4, *quarter), jnp.bfloat16)], [], 4 * size, total, one, three, two
+    )
+    return total
+
+
+def spread(total, scale):
+    part, channels = total.shape[3:]
+    pieces = [total] + [swap(total, d) for d in (1, 2, 3)]
+    pieces += [swap(value, 16) for value in pieces]
+    whole = (27, 8, part, channels)
+    outs = call(
+        functools.partial(gather_kernel, scale),
+        [jax.ShapeDtypeStruct(whole, jnp.float32)] * 2,
+        [pltpu.VMEM((2, *whole), jnp.float32), pltpu.SemaphoreType.DMA((8,))],
+        16 * total.size,
+        *pieces,
+        outside=(HBM, HBM),
+    )
     return [out.reshape(3, 3, 3, channels, channels) for out in outs]
 
 
-def edges(last, near, far, ahead):
-    count, line = lax.axis_size("tm"), lax.axis_size("height")
+def time_route(ahead):
+    count = lax.axis_size("tm")
     step = -1 if ahead else 1
-    route = [(i, (i + step) % count) for i in range(count)]
-    time = lax.ppermute(last, "tm", route)
+    return [(i, (i + step) % count) for i in range(count)]
+
+
+def pack_kernel(near, far, out, *, first):
+    out[:, 0:1] = near[first : first + 2]
+    out[:, 1:2] = far[first : first + 2]
+
+
+def exchanged(last, near, far, ahead):
+    line = lax.axis_size("height")
+    time = lax.ppermute(last, "tm", time_route(ahead))
     near = lax.ppermute(near, "height", [(i, i ^ 1) for i in range(line)])
     far = lax.ppermute(far, "height", [(i, (i - 1 if i % 2 == 0 else i + 1) % line) for i in range(line)])
-    rows = jnp.concatenate([near, far], axis=1)
-    corners = lax.ppermute(rows[:2] if ahead else rows[-2:], "tm", route)
-    return time, near, far, corners
+    return time, near, far
+
+
+def cornered(time, near, far, ahead, after=()):
+    shape = jax.ShapeDtypeStruct((2, 2, *near.shape[2:]), near.dtype)
+    kernel = functools.partial(pack_kernel, first=0 if ahead else near.shape[0] - 2)
+    if after:
+        (rows,) = call(kernel, [shape], [], 0, near, far, after=after)
+    else:
+        rows = jnp.concatenate([near, far], axis=1)
+        rows = rows[:2] if ahead else rows[-2:]
+    return time, near, far, lax.ppermute(rows, "tm", time_route(ahead))
 
 
 def body(clip, first_weight, second_weight, cotangent):
@@ -266,28 +362,38 @@
     taps = pltpu.VMEM((9 * channels, 3 * channels), jnp.bfloat16)
     back_taps = pltpu.VMEM((3 * channels, 9 * channels), jnp.bfloat16)
     moved = pltpu.VMEM((cells, 3 * channels), jnp.bfloat16)
+    out = pltpu.VMEM(shape, jnp.bfloat16), pltpu.SemaphoreType.DMA((frames,))
     scale = 1.0 / math.sqrt(cells * lax.axis_size(ALL))
 
-    even = lax.axis_index("height") % 2 == 0
-    top, bottom = clip[:, :1], clip[:, -1:]
-    clip_edges = edges(clip[-2:], jnp.where(even, bottom, top), jnp.where(even, top, bottom), False)
+    whole, *cut = call(
+        cut_kernel, [bf16, last, line, line], [pltpu.SemaphoreType.DMA((4,))], 0, clip, inside=HBM
+    )
+    clip_edges = cornered(*exchanged(*cut, False), False)
+    (first_taps,) = call(
+        taps_kernel,
+        [jax.ShapeDtypeStruct(taps.shape, taps.dtype)],
+        [pltpu.VMEM(first_weight.shape, first_weight.dtype), pltpu.SemaphoreType.DMA((1,))],
+        0,
+        first_weight,
+        inside=HBM,
+    )
     slope, hidden, *cut = call(
-        first_kernel, [f32, bf16, last, line, line], [pad, taps], flops, clip, *clip_edges, first_weight
-    )
-    hidden_edges = edges(*cut, False)
+        first_kernel, [f32, bf16, last, line, line], [pad], flops, whole, *clip_edges, first_taps
+    )
+    hidden_edges = cornered(*exchanged(*cut, False), False)
     output, grad_two, *cut = call(
         second_kernel,
         [bf16, bf16, last, line, line],
-        [pad, taps],
+        [pad, taps, *out],
         flops,
         hidden,
         *hidden_edges,
         second_weight,
         cotangent,
-    )
-    two_edges = edges(*cut, True)
-    mine, other = call(weight_kernel, [keep, send], [pad, moved], flops, hidden, *hidden_edges, grad_two)
-    second_terms = (mine, swap(other, 16))
+        outside=(HBM,),
+    )
+    two_edges = cornered(*exchanged(*cut, True), True)
+    second_terms = call(weight_kernel, [keep, send], [pad, moved], flops, hidden, *hidden_edges, grad_two)
     grad_one, *cut = call(
         back_slope_kernel,
         [bf16, last, line, line],
@@ -298,10 +404,22 @@
         second_weight,
         slope,
     )
-    one_edges = edges(*cut, True)
-    mine, other = call(weight_kernel, [keep, send], [pad, moved], flops, clip, *clip_edges, grad_one)
-    first_grad, second_grad = summed((mine, swap(other, 16)), second_terms, scale)
-    (clip_grad,) = call(back_kernel, [bf16], [pad, back_taps], flops, grad_one, *one_edges, first_weight)
+    one_edges = exchanged(*cut, True)
+    first_terms = call(weight_kernel, [keep, send], [pad, moved], flops, whole, *clip_edges, grad_one)
+    mine, *sent = started(first_terms, second_terms)
+    one_edges = cornered(*one_edges, True, after=(mine,))
+    ended = jax.ShapeDtypeStruct((8, 128), jnp.float32)
+    clip_grad, ended = call(
+        back_kernel,
+        [bf16, ended],
+        [pad, back_taps, *out],
+        flops,
+        grad_one,
+        *one_edges,
+        first_weight,
+        outside=(HBM,),
+    )
+    first_grad, second_grad = spread(summed(mine, sent, (one_edges[0], one_edges[3]), (ended,)), scale)
     return output[None], clip_grad[None], first_grad, second_grad
 
 

time: 121 us -> 116 us (0.959)
  waiting for transfers between devices: 36.8 us -> 26.1 us
  starting transfers between devices: 61 us -> 68 us
    ppermute x21, waiting for transfers between devices: 20.8 us -> 6.53 us  [swap(): lax.ppermute(value, ALL, [(i, i ^ mask) for i in range(lax.axis_size(ALL))])]
    ppermute x21, starting transfers between devices: 19.7 us -> 28.2 us  [swap(): lax.ppermute(value, ALL, [(i, i ^ mask) for i in range(lax.axis_size(ALL))])]
    ppermute x16, waiting for transfers between devices: 16 us -> 19.5 us  [the longest x4 11.8 us: exchanged(): lax.ppermute(far, 'height', [(i, (i - 1 if i % 2 == 0 else i + 1) % line)...]
    ppermute x16, starting transfers between devices: 41.3 us -> 39.8 us  [the longest x4 17.2 us: exchanged(): lax.ppermute(far, 'height', [(i, (i - 1 if i % 2 == 0 else i + 1) % line)...]
    pallas_call x12 -> x15, Pallas kernels: 18.2 us -> 18.5 us  [call(): pl.pallas_call(run, out_shape=outs, in_specs=[inside] * len(args) + [ANY]...]
  transfers between devices with their start and end apart: 37 -> 37, of which waited for: 15 -> 13; matrix products, arithmetic and copies ran while one was open for 1% -> 0% of each run, Pallas kernels for 8% -> 9%
where the time goes in v2:
time: 116 us
  starting transfers between devices  68 us (59%)
  waiting for transfers between devices  26.1 us (22%)
  Pallas kernels  18.5 us (16%)
  local copies, waits for them, and re-layouts  2.17 us (2%)
    ppermute x21, starting transfers between devices, swap(): lax.ppermute(value, ALL, [(i, i ^ mask) for i in range(lax.axis_size(ALL))])  28.2 us
    pallas_call x15, Pallas kernels, call(): pl.pallas_call(run, out_shape=outs, in_specs=[inside] * len(args) + [ANY]...  18.5 us
    ppermute x4, starting transfers between devices, exchanged(): lax.ppermute(far, 'height', [(i, (i - 1 if i % 2 == 0 else i + 1) % line)...  17.2 us
    ppermute x4, waiting for transfers between devices, exchanged(): lax.ppermute(far, 'height', [(i, (i - 1 if i % 2 == 0 else i + 1) % line)...  11.8 us
    ppermute x4, starting transfers between devices, exchanged(): time = lax.ppermute(last, 'tm', time_route(ahead))  10.9 us
    ppermute x4, starting transfers between devices, cornered(): return (time, near, far, lax.ppermute(rows, 'tm', time_route(ahead)))  9.33 us
    ppermute x4, waiting for transfers between devices, cornered(): return (time, near, far, lax.ppermute(rows, 'tm', time_route(ahead)))  7.76 us
    ppermute x21, waiting for transfers between devices, swap(): lax.ppermute(value, ALL, [(i, i ^ mask) for i in range(lax.axis_size(ALL))])  6.53 us
  transfers between devices with their start and end apart: 37, of which 13 were waited for; matrix products, arithmetic and copies ran while one was open for 0% of the time, Pallas kernels for 9%

profile of v2, /device:TPU:1, one launch (start us, length us, event | category | flops | bytes accessed | tf_op | source)
XLA Modules:
  0.0 115.7 jit_solution(17510561363858900512)
XLA Ops:
  2.0 2.1 %collective-permute-start.1 = (bf16[3,1,128,128]{3,2,1,0:T(8,128)(2,1)S(1)}, bf16[3,1,128,128]{3,2,1,0:T(8,128)(2,1)S(1)}, u32[]{:S(2)}, u32[]{:S(2)}) collective-permute-start(bf16[3,1,128,128]{3,2,1,0:T(8,128)(2,1)S(1)} %get-tuple-element.40), channel_id=1, source_target_pairs={{0,1},{1,0},{2,3},{3,2},{4,5},{5,4},{6,7},{7,6},{8,9},{9,8},{10,11... | collective-permute-start | bytes 294920 | tf_op jit(solution)/shard_map/ppermute | solution.py:332
  4.1 4.3 %collective-permute-start.2 = (bf16[3,1,128,128]{3,2,1,0:T(8,128)(2,1)S(1)}, bf16[3,1,128,128]{3,2,1,0:T(8,128)(2,1)S(1)}, u32[]{:S(2)}, u32[]{:S(2)}) collective-permute-start(bf16[3,1,128,128]{3,2,1,0:T(8,128)(2,1)S(1)} %get-tuple-element.41), channel_id=1, source_target_pairs={{0,15},{1,2},{2,1},{3,4},{4,3},{5,6},{6,5},{7,8},{8,7},{9,10},{10,... | collective-permute-start | bytes 294920 | tf_op jit(solution)/shard_map/ppermute | solution.py:333
  8.3 4.7 %collective-permute-start = (bf16[2,4,128,128]{3,2,1,0:T(8,128)(2,1)S(1)}, bf16[2,4,128,128]{3,2,1,0:T(8,128)(2,1)S(1)}, u32[]{:S(2)}, u32[]{:S(2)}) collective-permute-start(bf16[2,4,128,128]{3,2,1,0:T(8,128)(2,1)S(1)} %get-tuple-element.39), channel_id=1, source_target_pairs={{0,16},{16,32},{32,48},{48,0},{1,17},{17,33},{33,49},{49,1},{2,18}... | collective-permute-start | bytes 786440 | tf_op jit(solution)/shard_map/ppermute | solution.py:331
  13.1 3.5 %collective-permute-start.3 = (bf16[2,2,128,128]{3,2,1,0:T(8,128)(2,1)S(1)}, bf16[2,2,128,128]{3,2,1,0:T(8,128)(2,1)S(1)}, u32[]{:S(2)}, u32[]{:S(2)}) collective-permute-start(bf16[2,2,128,128]{3,2,1,0:T(8,128)(2,1)S(1)} %pad_maximum_fusion.2), channel_id=1, source_target_pairs={{0,16},{16,32},{32,48},{48,0},{1,17},{17,33},{33,49},{49,1},{2,18}... | collective-permute-start | bytes 393224 | tf_op jit(solution)/shard_map/ppermute | solution.py:345
  18.5 2.3 %shard_map.77 = (f32[3,4,128,128]{3,2,1,0:T(8,128)S(1)}, bf16[3,4,128,128]{3,2,1,0:T(8,128)(2,1)S(1)}, bf16[2,4,128,128]{3,2,1,0:T(8,128)(2,1)S(1)}, bf16[3,1,12...) custom-call(bf16[3,4,128,128]{3,2,1,0:T(8,128)(2,1)S(1)} %get-tuple-element.38.refs_0_, ...), custom_call_target="tpu_custom_call" | custom-call | flops 1358954496 | bytes 3506176 | tf_op jit(solution)/shard_map/pallas_call | solution.py:25
  20.9 4.3 %collective-permute-start.6 = (bf16[3,1,128,128]{3,2,1,0:T(8,128)(2,1)S(1)}, bf16[3,1,128,128]{3,2,1,0:T(8,128)(2,1)S(1)}, u32[]{:S(2)}, u32[]{:S(2)}) collective-permute-start(bf16[3,1,128,128]{3,2,1,0:T(8,128)(2,1)S(1)} %get-tuple-element.45), channel_id=1, source_target_pairs={{0,15},{1,2},{2,1},{3,4},{4,3},{5,6},{6,5},{7,8},{8,7},{9,10},{10,... | collective-permute-start | bytes 294920 | tf_op jit(solution)/shard_map/ppermute | solution.py:333
  25.3 4.2 %collective-permute-start.4 = (bf16[2,4,128,128]{3,2,1,0:T(8,128)(2,1)S(1)}, bf16[2,4,128,128]{3,2,1,0:T(8,128)(2,1)S(1)}, u32[]{:S(2)}, u32[]{:S(2)}) collective-permute-start(bf16[2,4,128,128]{3,2,1,0:T(8,128)(2,1)S(1)} %get-tuple-element.43), channel_id=1, source_target_pairs={{0,16},{16,32},{32,48},{48,0},{1,17},{17,33},{33,49},{49,1},{2,18}... | collective-permute-start | bytes 786440 | tf_op jit(solution)/shard_map/ppermute | solution.py:331
  29.5 3.5 %collective-permute-start.7 = (bf16[2,2,128,128]{3,2,1,0:T(8,128)(2,1)S(1)}, bf16[2,2,128,128]{3,2,1,0:T(8,128)(2,1)S(1)}, u32[]{:S(2)}, u32[]{:S(2)}) collective-permute-start(bf16[2,2,128,128]{3,2,1,0:T(8,128)(2,1)S(1)} %pad_maximum_fusion.1), channel_id=1, source_target_pairs={{0,16},{16,32},{32,48},{48,0},{1,17},{17,33},{33,49},{49,1},{2,18}... | collective-permute-start | bytes 393224 | tf_op jit(solution)/shard_map/ppermute | solution.py:345
  33.0 1.9 %collective-permute-done.7.refs_4_ = bf16[2,2,128,128]{3,2,1,0:T(8,128)(2,1)S(1)} collective-permute-done((bf16[2,2,128,128]{3,2,1,0:T(8,128)(2,1)S(1)}, bf16[2,2,128,128]{3,2,1,0:T(8,128)(2,1)S(1)}, u32[]{:S(2)}, u32[]{:S(2)}) %collective-permute-start.7) | collective-permute-done | bytes 131104 | tf_op jit(solution)/shard_map/ppermute | solution.py:345
  34.9 3.1 %shard_map.78 = (bf16[3,4,128,128]{3,2,1,0:T(8,128)(2,1)}, bf16[3,4,128,128]{3,2,1,0:T(8,128)(2,1)S(1)}, bf16[2,4,128,128]{3,2,1,0:T(8,128)(2,1)S(1)}, bf16[3,1,...) custom-call(bf16[3,4,128,128]{3,2,1,0:T(8,128)(2,1)S(1)} %get-tuple-element.42.refs_0_, ...), custom_call_target="tpu_custom_call" | custom-call | flops 1358954496 | bytes 3506176 | tf_op jit(solution)/shard_map/pallas_call | solution.py:25
  38.1 4.3 %collective-permute-start.10 = (bf16[3,1,128,128]{3,2,1,0:T(8,128)(2,1)S(1)}, bf16[3,1,128,128]{3,2,1,0:T(8,128)(2,1)S(1)}, u32[]{:S(2)}, u32[]{:S(2)}) collective-permute-start(bf16[3,1,128,128]{3,2,1,0:T(8,128)(2,1)S(1)} %get-tuple-element.50), channel_id=1, source_target_pairs={{0,15},{1,2},{2,1},{3,4},{4,3},{5,6},{6,5},{7,8},{8,7},{9,10},{10,... | collective-permute-start | bytes 294920 | tf_op jit(solution)/shard_map/ppermute | solution.py:333
  43.4 1.6 %collective-permute-done.10.refs_3_ = bf16[3,1,128,128]{3,2,1,0:T(8,128)(2,1)S(1)} collective-permute-done((bf16[3,1,128,128]{3,2,1,0:T(8,128)(2,1)S(1)}, bf16[3,1,128,128]{3,2,1,0:T(8,128)(2,1)S(1)}, u32[]{:S(2)}, u32[]{:S(2)}) %collective-permute-start.10) | collective-permute-done | bytes 98336 | tf_op jit(solution)/shard_map/ppermute | solution.py:333
  45.0 1.9 %collective-permute-start.11 = (bf16[2,2,128,128]{3,2,1,0:T(8,128)(2,1)S(1)}, bf16[2,2,128,128]{3,2,1,0:T(8,128)(2,1)S(1)}, u32[]{:S(2)}, u32[]{:S(2)}) collective-permute-start(bf16[2,2,128,128]{3,2,1,0:T(8,128)(2,1)S(1)} %pad_maximum_fusion), channel_id=1, source_target_pairs={{0,48},{16,0},{32,16},{48,32},{1,49},{17,1},{33,17},{49,33},{2,50}... | collective-permute-start | bytes 393224 | tf_op jit(solution)/shard_map/ppermute | solution.py:345
  46.9 2.3 %shard_map.81 = (f32[4,28,16,128]{3,2,1,0:T(8,128)S(1)}, bf16[4,28,16,128]{3,2,1,0:T(8,128)(2,1)S(1)}) custom-call(bf16[3,4,128,128]{3,2,1,0:T(8,128)(2,1)S(1)} %get-tuple-element.42.refs_0_, bf16[2,4,128,128]{3,2,1,0:T(8,128)(2,1)S(1)} %collective-permute-done.4.refs_1_, bf16[3,1,128,128]{3,2,1,0:T(8,128)(2,1)S(1)} %collective-permute-done.5.refs_2_, ...), custom_call_target="tpu_custom_call" | custom-call | flops 1358954496 | bytes 2752512 | tf_op jit(solution)/shard_map/pallas_call | solution.py:25
  49.7 3.1 %collective-permute-done.11.refs_4_ = bf16[2,2,128,128]{3,2,1,0:T(8,128)(2,1)S(1)} collective-permute-done((bf16[2,2,128,128]{3,2,1,0:T(8,128)(2,1)S(1)}, bf16[2,2,128,128]{3,2,1,0:T(8,128)(2,1)S(1)}, u32[]{:S(2)}, u32[]{:S(2)}) %collective-permute-start.11) | collective-permute-done | bytes 131104 | tf_op jit(solution)/shard_map/ppermute | solution.py:345
  52.9 2.6 %shard_map.79 = (bf16[3,4,128,128]{3,2,1,0:T(8,128)(2,1)S(1)}, bf16[2,4,128,128]{3,2,1,0:T(8,128)(2,1)S(1)}, bf16[3,1,128,128]{3,2,1,0:T(8,128)(2,1)S(1)}, bf16[3,1,128,128]{3,2,1,0:T(8,128)(2,1)S(1)}) custom-call(bf16[3,4,128,128]{3,2,1,0:T(8,128)(2,1)S(1)} %get-tuple-element.47.refs_0_.refs_5_, ...), custom_call_target="tpu_custom_call" | custom-call | flops 1358954496 | bytes 3506176 | tf_op jit(solution)/shard_map/pallas_call | solution.py:25
  55.4 2.3 %shard_map.80 = (f32[4,28,16,128]{3,2,1,0:T(8,128)S(1)}, bf16[4,28,16,128]{3,2,1,0:T(8,128)(2,1)S(1)}) custom-call(bf16[3,4,128,128]{3,2,1,0:T(8,128)(2,1)S(1)} %get-tuple-element.38.refs_0_, bf16[2,4,128,128]{3,2,1,0:T(8,128)(2,1)S(1)} %collective-permute-done.refs_1_, bf16[3,1,128,128]{3,2,1,0:T(8,128)(2,1)S(1)} %collective-permute-done.1.refs_2_, ...), custom_call_target="tpu_custom_call" | custom-call | flops 1358954496 | bytes 2752512 | tf_op jit(solution)/shard_map/pallas_call | solution.py:25
  57.9 1.7 %collective-permute-done.15.refs_1_ = bf16[4,28,16,128]{3,2,1,0:T(8,128)(2,1)S(1)} collective-permute-done((bf16[4,28,16,128]{3,2,1,0:T(8,128)(2,1)S(1)}, bf16[4,28,16,128]{3,2,1,0:T(8,128)(2,1)S(1)}, u32[]{:S(2)}, u32[]{:S(2)}) %collective-permute-start.15) | collective-permute-done | bytes 458784 | tf_op jit(solution)/shard_map/ppermute | solution.py:271
  60.0 3.1 %collective-permute-start.20 = (bf16[4,2,7,16,128]{4,3,2,1,0:T(8,128)(2,1)S(1)}, bf16[4,2,7,16,128]{4,3,2,1,0:T(8,128)(2,1)S(1)}, u32[]{:S(2)}, u32[]{:S(2)}) collective-permute-start(bf16[4,2,7,16,128]{4,3,2,1,0:T(8,128)(2,1)S(1)} %get-tuple-element.64), channel_id=1, source_target_pairs={{0,3},{1,2},{2,1},{3,0},{4,7},{5,6},{6,5},{7,4},{8,11},{9,10},{10,... | collective-permute-start | bytes 688136 | tf_op jit(solution)/shard_map/ppermute | solution.py:271
  64.1 4.3 %collective-permute-start.14 = (bf16[3,1,128,128]{3,2,1,0:T(8,128)(2,1)S(1)}, bf16[3,1,128,128]{3,2,1,0:T(8,128)(2,1)S(1)}, u32[]{:S(2)}, u32[]{:S(2)}) collective-permute-start(bf16[3,1,128,128]{3,2,1,0:T(8,128)(2,1)S(1)} %get-tuple-element.55), channel_id=1, source_target_pairs={{0,15},{1,2},{2,1},{3,4},{4,3},{5,6},{6,5},{7,8},{8,7},{9,10},{10,... | collective-permute-start | bytes 294920 | tf_op jit(solution)/shard_map/ppermute | solution.py:333
  68.3 10.2 %collective-permute-done.14.refs_1_.refs_3_ = bf16[3,1,128,128]{3,2,1,0:T(8,128)(2,1)S(1)} collective-permute-done((bf16[3,1,128,128]{3,2,1,0:T(8,128)(2,1)S(1)}, bf16[3,1,128,128]{3,2,1,0:T(8,128)(2,1)S(1)}, u32[]{:S(2)}, u32[]{:S(2)}) %collective-permute-start.14) | collective-permute-done | bytes 98336 | tf_op jit(solution)/shard_map/ppermute | solution.py:333
  79.4 3.1 %collective-permute-start.23 = (bf16[2,7,16,128]{3,2,1,0:T(8,128)(2,1)S(1)}, bf16[2,7,16,128]{3,2,1,0:T(8,128)(2,1)S(1)}, u32[]{:S(2)}, u32[]{:S(2)}) collective-permute-start(bf16[2,7,16,128]{3,2,1,0:T(8,128)(2,1)S(1)} %get-tuple-element.68), channel_id=1, source_target_pairs={{0,12},{1,13},{2,14},{3,15},{4,8},{5,9},{6,10},{7,11},{8,4},{9,5},... | collective-permute-start | bytes 172040 | tf_op jit(solution)/shard_map/ppermute | solution.py:271
  82.6 2.2 %collective-permute-done.17.refs_4_.refs_5_ = bf16[2,2,128,128]{3,2,1,0:T(8,128)(2,1)S(1)} collective-permute-done((bf16[2,2,128,128]{3,2,1,0:T(8,128)(2,1)S(1)}, bf16[2,2,128,128]{3,2,1,0:T(8,128)(2,1)S(1)}, u32[]{:S(2)}, u32[]{:S(2)}) %collective-permute-start.17) | collective-permute-done | bytes 131104 | tf_op jit(solution)/shard_map/ppermute | solution.py:345
  85.8 2.9 %collective-permute-start.25 = (bf16[2,7,16,128]{3,2,1,0:T(8,128)(2,1)S(1)}, bf16[2,7,16,128]{3,2,1,0:T(8,128)(2,1)S(1)}, u32[]{:S(2)}, u32[]{:S(2)}) collective-permute-start(bf16[2,7,16,128]{3,2,1,0:T(8,128)(2,1)S(1)} %shard_map.86.refs_0_), channel_id=1, source_target_pairs={{0,96},{1,97},{2,98},{3,99},{4,100},{5,101},{6,102},{7,103},{8,104... | collective-permute-start | bytes 172040 | tf_op jit(solution)/shard_map/ppermute | solution.py:271
  88.8 3.0 %shard_map.84 = (bf16[3,4,128,128]{3,2,1,0:T(8,128)(2,1)}, f32[8,128]{1,0:T(8,128)S(1)}) custom-call(bf16[3,4,128,128]{3,2,1,0:T(8,128)(2,1)S(1)} %get-tuple-element.52.refs_5_.refs_0_, bf16[2,4,128,128]{3,2,1,0:T(8,128)(2,1)S(1)} %collective-permute-done.12.refs_1_.refs_4_, bf16[3,1,128,128]{3,2,1,0:T(8,128)(2,1)S(1)} %collective-permute-done.13.refs_0_.refs_2_, ...), custom_call_target="tpu_custom_call" | custom-call | flops 1358954496 | bytes 2265088 | tf_op jit(solution)/shard_map/pallas_call | solution.py:25
  93.6 1.4 %collective-permute-start.27 = (bf16[2,7,16,128]{3,2,1,0:T(8,128)(2,1)S(1)}, bf16[2,7,16,128]{3,2,1,0:T(8,128)(2,1)S(1)}, u32[]{:S(2)}, u32[]{:S(2)}) collective-permute-start(bf16[2,7,16,128]{3,2,1,0:T(8,128)(2,1)S(1)} %shard_map.87.refs_0_), channel_id=1, source_target_pairs={{0,4},{1,5},{2,6},{3,7},{4,0},{5,1},{6,2},{7,3},{8,12},{9,13},{10,... | collective-permute-start | bytes 172040 | tf_op jit(solution)/shard_map/ppermute | solution.py:271
  95.0 2.0 %collective-permute-done.29.refs_3_ = bf16[2,7,16,128]{3,2,1,0:T(8,128)(2,1)S(1)} collective-permute-done((bf16[2,7,16,128]{3,2,1,0:T(8,128)(2,1)S(1)}, bf16[2,7,16,128]{3,2,1,0:T(8,128)(2,1)S(1)}, u32[]{:S(2)}, u32[]{:S(2)}) %collective-permute-start.29) | collective-permute-done | bytes 57376 | tf_op jit(solution)/shard_map/ppermute | solution.py:271
  97.3 2.2 %collective-permute-start.32 = (bf16[4,2,7,16,128]{4,3,2,1,0:T(8,128)(2,1)S(1)}, bf16[4,2,7,16,128]{4,3,2,1,0:T(8,128)(2,1)S(1)}, u32[]{:S(2)}, u32[]{:S(2)}) collective-permute-start(bf16[4,2,7,16,128]{4,3,2,1,0:T(8,128)(2,1)S(1)} %shard_map.88.refs_0_), channel_id=1, source_target_pairs={{0,3},{1,2},{2,1},{3,0},{4,7},{5,6},{6,5},{7,4},{8,11},{9,10},{10,... | collective-permute-start | bytes 688136 | tf_op jit(solution)/shard_map/ppermute | solution.py:271
  100.7 5.4 %collective-permute-start.33 = (bf16[4,2,7,16,128]{4,3,2,1,0:T(8,128)(2,1)S(1)}, bf16[4,2,7,16,128]{4,3,2,1,0:T(8,128)(2,1)S(1)}, u32[]{:S(2)}, u32[]{:S(2)}) collective-permute-start(bf16[4,2,7,16,128]{4,3,2,1,0:T(8,128)(2,1)S(1)} %shard_map.88.refs_0_), channel_id=1, source_target_pairs={{0,16},{1,17},{2,18},{3,19},{4,20},{5,21},{6,22},{7,23},{8,24},{9,... | collective-permute-start | bytes 688136 | tf_op jit(solution)/shard_map/ppermute | solution.py:271
  106.0 4.6 %collective-permute-start.36 = (bf16[4,2,7,16,128]{4,3,2,1,0:T(8,128)(2,1)S(1)}, bf16[4,2,7,16,128]{4,3,2,1,0:T(8,128)(2,1)S(1)}, u32[]{:S(2)}, u32[]{:S(2)}) collective-permute-start(bf16[4,2,7,16,128]{4,3,2,1,0:T(8,128)(2,1)S(1)} %collective-permute-done.32.refs_3_), channel_id=1, source_target_pairs={{0,16},{1,17},{2,18},{3,19},{4,20},{5,21},{6,22},{7,23},{8,24},{9,... | collective-permute-start | bytes 688136 | tf_op jit(solution)/shard_map/ppermute | solution.py:271
  110.6 1.5 %collective-permute-start.35 = (bf16[4,2,7,16,128]{4,3,2,1,0:T(8,128)(2,1)S(1)}, bf16[4,2,7,16,128]{4,3,2,1,0:T(8,128)(2,1)S(1)}, u32[]{:S(2)}, u32[]{:S(2)}) collective-permute-start(bf16[4,2,7,16,128]{4,3,2,1,0:T(8,128)(2,1)S(1)} %collective-permute-done.31.refs_2_), channel_id=1, source_target_pairs={{0,16},{1,17},{2,18},{3,19},{4,20},{5,21},{6,22},{7,23},{8,24},{9,... | collective-permute-start | bytes 688136 | tf_op jit(solution)/shard_map/ppermute | solution.py:271
  113.7 1.9 %shard_map.89 = (f32[27,8,16,128]{3,2,1,0:T(8,128)}, f32[27,8,16,128]{3,2,1,0:T(8,128)}) custom-call(bf16[4,2,7,16,128]{4,3,2,1,0:T(8,128)(2,1)S(1)} %shard_map.88.refs_0_, bf16[4,2,7,16,128]{4,3,2,1,0:T(8,128)(2,1)S(1)} %collective-permute-done.30.refs_1_, bf16[4,2,7,16,128]{4,3,2,1,0:T(8,128)(2,1)S(1)} %collective-permute-done.31.refs_2_, ...), custom_call_target="tpu_custom_call" | custom-call | flops 1835008 | bytes 5373952 | tf_op jit(solution)/shard_map/pallas_call | solution.py:25
  (70 shorter events, 13.1 us)
Async XLA Ops:
  2.0 11.1 %collective-permute-start.1 = (bf16[3,1,128,128]{3,2,1,0:T(8,128)(2,1)S(1)}, bf16[3,1,128,128]{3,2,1,0:T(8,128)(2,1)S(1)}, u32[]{:S(2)}, u32[]{:S(2)}) collective-permute-start(bf16[3,1,128,128]{3,2,1,0:T(8,128)(2,1)S(1)} %get-tuple-element.40), channel_id=1, source_target_pairs={{0,1},{1,0},{2,3},{3,2},{4,5},{5,4},{6,7},{7,6},{8,9},{9,8},{10,11... | collective-permute-start | bytes 294920 | tf_op jit(solution)/shard_map/ppermute | solution.py:332
  4.1 9.0 %collective-permute-start.2 = (bf16[3,1,128,128]{3,2,1,0:T(8,128)(2,1)S(1)}, bf16[3,1,128,128]{3,2,1,0:T(8,128)(2,1)S(1)}, u32[]{:S(2)}, u32[]{:S(2)}) collective-permute-start(bf16[3,1,128,128]{3,2,1,0:T(8,128)(2,1)S(1)} %get-tuple-element.41), channel_id=1, source_target_pairs={{0,15},{1,2},{2,1},{3,4},{4,3},{5,6},{6,5},{7,8},{8,7},{9,10},{10,... | collective-permute-start | bytes 294920 | tf_op jit(solution)/shard_map/ppermute | solution.py:333
  8.3 10.1 %collective-permute-start = (bf16[2,4,128,128]{3,2,1,0:T(8,128)(2,1)S(1)}, bf16[2,4,128,128]{3,2,1,0:T(8,128)(2,1)S(1)}, u32[]{:S(2)}, u32[]{:S(2)}) collective-permute-start(bf16[2,4,128,128]{3,2,1,0:T(8,128)(2,1)S(1)} %get-tuple-element.39), channel_id=1, source_target_pairs={{0,16},{16,32},{32,48},{48,0},{1,17},{17,33},{33,49},{49,1},{2,18}... | collective-permute-start | bytes 786440 | tf_op jit(solution)/shard_map/ppermute | solution.py:331
  13.1 5.4 %collective-permute-start.3 = (bf16[2,2,128,128]{3,2,1,0:T(8,128)(2,1)S(1)}, bf16[2,2,128,128]{3,2,1,0:T(8,128)(2,1)S(1)}, u32[]{:S(2)}, u32[]{:S(2)}) collective-permute-start(bf16[2,2,128,128]{3,2,1,0:T(8,128)(2,1)S(1)} %pad_maximum_fusion.2), channel_id=1, source_target_pairs={{0,16},{16,32},{32,48},{48,0},{1,17},{17,33},{33,49},{49,1},{2,18}... | collective-permute-start | bytes 393224 | tf_op jit(solution)/shard_map/ppermute | solution.py:345
  20.8 8.7 %collective-permute-start.5 = (bf16[3,1,128,128]{3,2,1,0:T(8,128)(2,1)S(1)}, bf16[3,1,128,128]{3,2,1,0:T(8,128)(2,1)S(1)}, u32[]{:S(2)}, u32[]{:S(2)}) collective-permute-start(bf16[3,1,128,128]{3,2,1,0:T(8,128)(2,1)S(1)} %get-tuple-element.44), channel_id=1, source_target_pairs={{0,1},{1,0},{2,3},{3,2},{4,5},{5,4},{6,7},{7,6},{8,9},{9,8},{10,11... | collective-permute-start | bytes 294920 | tf_op jit(solution)/shard_map/ppermute | solution.py:332
  20.9 8.6 %collective-permute-start.6 = (bf16[3,1,128,128]{3,2,1,0:T(8,128)(2,1)S(1)}, bf16[3,1,128,128]{3,2,1,0:T(8,128)(2,1)S(1)}, u32[]{:S(2)}, u32[]{:S(2)}) collective-permute-start(bf16[3,1,128,128]{3,2,1,0:T(8,128)(2,1)S(1)} %get-tuple-element.45), channel_id=1, source_target_pairs={{0,15},{1,2},{2,1},{3,4},{4,3},{5,6},{6,5},{7,8},{8,7},{9,10},{10,... | collective-permute-start | bytes 294920 | tf_op jit(solution)/shard_map/ppermute | solution.py:333
  25.3 9.7 %collective-permute-start.4 = (bf16[2,4,128,128]{3,2,1,0:T(8,128)(2,1)S(1)}, bf16[2,4,128,128]{3,2,1,0:T(8,128)(2,1)S(1)}, u32[]{:S(2)}, u32[]{:S(2)}) collective-permute-start(bf16[2,4,128,128]{3,2,1,0:T(8,128)(2,1)S(1)} %get-tuple-element.43), channel_id=1, source_target_pairs={{0,16},{16,32},{32,48},{48,0},{1,17},{17,33},{33,49},{49,1},{2,18}... | collective-permute-start | bytes 786440 | tf_op jit(solution)/shard_map/ppermute | solution.py:331
  29.5 5.4 %collective-permute-start.7 = (bf16[2,2,128,128]{3,2,1,0:T(8,128)(2,1)S(1)}, bf16[2,2,128,128]{3,2,1,0:T(8,128)(2,1)S(1)}, u32[]{:S(2)}, u32[]{:S(2)}) collective-permute-start(bf16[2,2,128,128]{3,2,1,0:T(8,128)(2,1)S(1)} %pad_maximum_fusion.1), channel_id=1, source_target_pairs={{0,16},{16,32},{32,48},{48,0},{1,17},{17,33},{33,49},{49,1},{2,18}... | collective-permute-start | bytes 393224 | tf_op jit(solution)/shard_map/ppermute | solution.py:345
  38.0 5.4 %collective-permute-start.9 = (bf16[3,1,128,128]{3,2,1,0:T(8,128)(2,1)S(1)}, bf16[3,1,128,128]{3,2,1,0:T(8,128)(2,1)S(1)}, u32[]{:S(2)}, u32[]{:S(2)}) collective-permute-start(bf16[3,1,128,128]{3,2,1,0:T(8,128)(2,1)S(1)} %get-tuple-element.49), channel_id=1, source_target_pairs={{0,1},{1,0},{2,3},{3,2},{4,5},{5,4},{6,7},{7,6},{8,9},{9,8},{10,11... | collective-permute-start | bytes 294920 | tf_op jit(solution)/shard_map/ppermute | solution.py:332
  38.1 6.9 %collective-permute-start.10 = (bf16[3,1,128,128]{3,2,1,0:T(8,128)(2,1)S(1)}, bf16[3,1,128,128]{3,2,1,0:T(8,128)(2,1)S(1)}, u32[]{:S(2)}, u32[]{:S(2)}) collective-permute-start(bf16[3,1,128,128]{3,2,1,0:T(8,128)(2,1)S(1)} %get-tuple-element.50), channel_id=1, source_target_pairs={{0,15},{1,2},{2,1},{3,4},{4,3},{5,6},{6,5},{7,8},{8,7},{9,10},{10,... | collective-permute-start | bytes 294920 | tf_op jit(solution)/shard_map/ppermute | solution.py:333
  42.5 10.4 %collective-permute-start.8 = (bf16[2,4,128,128]{3,2,1,0:T(8,128)(2,1)S(1)}, bf16[2,4,128,128]{3,2,1,0:T(8,128)(2,1)S(1)}, u32[]{:S(2)}, u32[]{:S(2)}) collective-permute-start(bf16[2,4,128,128]{3,2,1,0:T(8,128)(2,1)S(1)} %get-tuple-element.48), channel_id=1, source_target_pairs={{0,48},{16,0},{32,16},{48,32},{1,49},{17,1},{33,17},{49,33},{2,50}... | collective-permute-start | bytes 786440 | tf_op jit(solution)/shard_map/ppermute | solution.py:331
  45.0 7.8 %collective-permute-start.11 = (bf16[2,2,128,128]{3,2,1,0:T(8,128)(2,1)S(1)}, bf16[2,2,128,128]{3,2,1,0:T(8,128)(2,1)S(1)}, u32[]{:S(2)}, u32[]{:S(2)}) collective-permute-start(bf16[2,2,128,128]{3,2,1,0:T(8,128)(2,1)S(1)} %pad_maximum_fusion), channel_id=1, source_target_pairs={{0,48},{16,0},{32,16},{48,32},{1,49},{17,1},{33,17},{49,33},{2,50}... | collective-permute-start | bytes 393224 | tf_op jit(solution)/shard_map/ppermute | solution.py:345
  49.1 8.8 %collective-permute-start.16 = (bf16[4,28,16,128]{3,2,1,0:T(8,128)(2,1)S(1)}, bf16[4,28,16,128]{3,2,1,0:T(8,128)(2,1)S(1)}, u32[]{:S(2)}, u32[]{:S(2)}) collective-permute-start(bf16[4,28,16,128]{3,2,1,0:T(8,128)(2,1)S(1)} %get-tuple-element.59), channel_id=1, source_target_pairs={{0,16},{1,17},{2,18},{3,19},{4,20},{5,21},{6,22},{7,23},{8,24},{9,... | collective-permute-start | bytes 1376264 | tf_op jit(solution)/shard_map/ppermute | solution.py:271
  57.8 6.3 %collective-permute-start.13 = (bf16[3,1,128,128]{3,2,1,0:T(8,128)(2,1)S(1)}, bf16[3,1,128,128]{3,2,1,0:T(8,128)(2,1)S(1)}, u32[]{:S(2)}, u32[]{:S(2)}) collective-permute-start(bf16[3,1,128,128]{3,2,1,0:T(8,128)(2,1)S(1)} %get-tuple-element.54), channel_id=1, source_target_pairs={{0,1},{1,0},{2,3},{3,2},{4,5},{5,4},{6,7},{7,6},{8,9},{9,8},{10,11... | collective-permute-start | bytes 294920 | tf_op jit(solution)/shard_map/ppermute | solution.py:332
  59.8 19.3 %collective-permute-start.18 = (bf16[4,2,7,16,128]{4,3,2,1,0:T(8,128)(2,1)S(1)}, bf16[4,2,7,16,128]{4,3,2,1,0:T(8,128)(2,1)S(1)}, u32[]{:S(2)}, u32[]{:S(2)}) collective-permute-start(bf16[4,2,7,16,128]{4,3,2,1,0:T(8,128)(2,1)S(1)} %get-tuple-element.62), channel_id=1, source_target_pairs={{0,2},{1,3},{2,0},{3,1},{4,6},{5,7},{6,4},{7,5},{8,10},{9,11},{10,... | collective-permute-start | bytes 688136 | tf_op jit(solution)/shard_map/ppermute | solution.py:271
  59.9 19.2 %collective-permute-start.19 = (bf16[4,2,7,16,128]{4,3,2,1,0:T(8,128)(2,1)S(1)}, bf16[4,2,7,16,128]{4,3,2,1,0:T(8,128)(2,1)S(1)}, u32[]{:S(2)}, u32[]{:S(2)}) collective-permute-start(bf16[4,2,7,16,128]{4,3,2,1,0:T(8,128)(2,1)S(1)} %get-tuple-element.63), channel_id=1, source_target_pairs={{0,1},{1,0},{2,3},{3,2},{4,5},{5,4},{6,7},{7,6},{8,9},{9,8},{10,11... | collective-permute-start | bytes 688136 | tf_op jit(solution)/shard_map/ppermute | solution.py:271
  60.0 19.1 %collective-permute-start.20 = (bf16[4,2,7,16,128]{4,3,2,1,0:T(8,128)(2,1)S(1)}, bf16[4,2,7,16,128]{4,3,2,1,0:T(8,128)(2,1)S(1)}, u32[]{:S(2)}, u32[]{:S(2)}) collective-permute-start(bf16[4,2,7,16,128]{4,3,2,1,0:T(8,128)(2,1)S(1)} %get-tuple-element.64), channel_id=1, source_target_pairs={{0,3},{1,2},{2,1},{3,0},{4,7},{5,6},{6,5},{7,4},{8,11},{9,10},{10,... | collective-permute-start | bytes 688136 | tf_op jit(solution)/shard_map/ppermute | solution.py:271
  63.1 19.4 %collective-permute-start.12 = (bf16[2,4,128,128]{3,2,1,0:T(8,128)(2,1)S(1)}, bf16[2,4,128,128]{3,2,1,0:T(8,128)(2,1)S(1)}, u32[]{:S(2)}, u32[]{:S(2)}) collective-permute-start(bf16[2,4,128,128]{3,2,1,0:T(8,128)(2,1)S(1)} %get-tuple-element.53), channel_id=1, source_target_pairs={{0,48},{16,0},{32,16},{48,32},{1,49},{17,1},{33,17},{49,33},{2,50}... | collective-permute-start | bytes 786440 | tf_op jit(solution)/shard_map/ppermute | solution.py:331
  64.1 14.4 %collective-permute-start.14 = (bf16[3,1,128,128]{3,2,1,0:T(8,128)(2,1)S(1)}, bf16[3,1,128,128]{3,2,1,0:T(8,128)(2,1)S(1)}, u32[]{:S(2)}, u32[]{:S(2)}) collective-permute-start(bf16[3,1,128,128]{3,2,1,0:T(8,128)(2,1)S(1)} %get-tuple-element.55), channel_id=1, source_target_pairs={{0,15},{1,2},{2,1},{3,4},{4,3},{5,6},{6,5},{7,8},{8,7},{9,10},{10,... | collective-permute-start | bytes 294920 | tf_op jit(solution)/shard_map/ppermute | solution.py:333
  78.5 6.3 %collective-permute-start.17 = (bf16[2,2,128,128]{3,2,1,0:T(8,128)(2,1)S(1)}, bf16[2,2,128,128]{3,2,1,0:T(8,128)(2,1)S(1)}, u32[]{:S(2)}, u32[]{:S(2)}) collective-permute-start(bf16[2,2,128,128]{3,2,1,0:T(8,128)(2,1)S(1)} %shard_map.83), channel_id=1, source_target_pairs={{0,48},{16,0},{32,16},{48,32},{1,49},{17,1},{33,17},{49,33},{2,50}... | collective-permute-start | bytes 393224 | tf_op jit(solution)/shard_map/ppermute | solution.py:345
  79.2 5.6 %collective-permute-start.21 = (bf16[2,7,16,128]{3,2,1,0:T(8,128)(2,1)S(1)}, bf16[2,7,16,128]{3,2,1,0:T(8,128)(2,1)S(1)}, u32[]{:S(2)}, u32[]{:S(2)}) collective-permute-start(bf16[2,7,16,128]{3,2,1,0:T(8,128)(2,1)S(1)} %get-tuple-element.66), channel_id=1, source_target_pairs={{0,8},{1,9},{2,10},{3,11},{4,12},{5,13},{6,14},{7,15},{8,0},{9,1},... | collective-permute-start | bytes 172040 | tf_op jit(solution)/shard_map/ppermute | solution.py:271
  79.3 5.5 %collective-permute-start.22 = (bf16[2,7,16,128]{3,2,1,0:T(8,128)(2,1)S(1)}, bf16[2,7,16,128]{3,2,1,0:T(8,128)(2,1)S(1)}, u32[]{:S(2)}, u32[]{:S(2)}) collective-permute-start(bf16[2,7,16,128]{3,2,1,0:T(8,128)(2,1)S(1)} %get-tuple-element.67), channel_id=1, source_target_pairs={{0,4},{1,5},{2,6},{3,7},{4,0},{5,1},{6,2},{7,3},{8,12},{9,13},{10,... | collective-permute-start | bytes 172040 | tf_op jit(solution)/shard_map/ppermute | solution.py:271
  79.4 6.3 %collective-permute-start.23 = (bf16[2,7,16,128]{3,2,1,0:T(8,128)(2,1)S(1)}, bf16[2,7,16,128]{3,2,1,0:T(8,128)(2,1)S(1)}, u32[]{:S(2)}, u32[]{:S(2)}) collective-permute-start(bf16[2,7,16,128]{3,2,1,0:T(8,128)(2,1)S(1)} %get-tuple-element.68), channel_id=1, source_target_pairs={{0,12},{1,13},{2,14},{3,15},{4,8},{5,9},{6,10},{7,11},{8,4},{9,5},... | collective-permute-start | bytes 172040 | tf_op jit(solution)/shard_map/ppermute | solution.py:271
  85.8 6.0 %collective-permute-start.26 = (bf16[2,7,16,128]{3,2,1,0:T(8,128)(2,1)S(1)}, bf16[2,7,16,128]{3,2,1,0:T(8,128)(2,1)S(1)}, u32[]{:S(2)}, u32[]{:S(2)}) collective-permute-start(bf16[2,7,16,128]{3,2,1,0:T(8,128)(2,1)S(1)} %shard_map.86.refs_0_), channel_id=1, source_target_pairs={{0,32},{1,33},{2,34},{3,35},{4,36},{5,37},{6,38},{7,39},{8,40},{9,... | collective-permute-start | bytes 172040 | tf_op jit(solution)/shard_map/ppermute | solution.py:271
  85.8 6.0 %collective-permute-start.25 = (bf16[2,7,16,128]{3,2,1,0:T(8,128)(2,1)S(1)}, bf16[2,7,16,128]{3,2,1,0:T(8,128)(2,1)S(1)}, u32[]{:S(2)}, u32[]{:S(2)}) collective-permute-start(bf16[2,7,16,128]{3,2,1,0:T(8,128)(2,1)S(1)} %shard_map.86.refs_0_), channel_id=1, source_target_pairs={{0,96},{1,97},{2,98},{3,99},{4,100},{5,101},{6,102},{7,103},{8,104... | collective-permute-start | bytes 172040 | tf_op jit(solution)/shard_map/ppermute | solution.py:271
  92.3 4.7 %collective-permute-start.29 = (bf16[2,7,16,128]{3,2,1,0:T(8,128)(2,1)S(1)}, bf16[2,7,16,128]{3,2,1,0:T(8,128)(2,1)S(1)}, u32[]{:S(2)}, u32[]{:S(2)}) collective-permute-start(bf16[2,7,16,128]{3,2,1,0:T(8,128)(2,1)S(1)} %shard_map.87.refs_0_), channel_id=1, source_target_pairs={{0,8},{1,9},{2,10},{3,11},{4,12},{5,13},{6,14},{7,15},{8,0},{9,1},... | collective-permute-start | bytes 172040 | tf_op jit(solution)/shard_map/ppermute | solution.py:271
  92.4 4.9 %collective-permute-start.28 = (bf16[2,7,16,128]{3,2,1,0:T(8,128)(2,1)S(1)}, bf16[2,7,16,128]{3,2,1,0:T(8,128)(2,1)S(1)}, u32[]{:S(2)}, u32[]{:S(2)}) collective-permute-start(bf16[2,7,16,128]{3,2,1,0:T(8,128)(2,1)S(1)} %shard_map.87.refs_0_), channel_id=1, source_target_pairs={{0,12},{1,13},{2,14},{3,15},{4,8},{5,9},{6,10},{7,11},{8,4},{9,5},... | collective-permute-start | bytes 172040 | tf_op jit(solution)/shard_map/ppermute | solution.py:271
  97.3 8.7 %collective-permute-start.32 = (bf16[4,2,7,16,128]{4,3,2,1,0:T(8,128)(2,1)S(1)}, bf16[4,2,7,16,128]{4,3,2,1,0:T(8,128)(2,1)S(1)}, u32[]{:S(2)}, u32[]{:S(2)}) collective-permute-start(bf16[4,2,7,16,128]{4,3,2,1,0:T(8,128)(2,1)S(1)} %shard_map.88.refs_0_), channel_id=1, source_target_pairs={{0,3},{1,2},{2,1},{3,0},{4,7},{5,6},{6,5},{7,4},{8,11},{9,10},{10,... | collective-permute-start | bytes 688136 | tf_op jit(solution)/shard_map/ppermute | solution.py:271
  99.6 11.1 %collective-permute-start.31 = (bf16[4,2,7,16,128]{4,3,2,1,0:T(8,128)(2,1)S(1)}, bf16[4,2,7,16,128]{4,3,2,1,0:T(8,128)(2,1)S(1)}, u32[]{:S(2)}, u32[]{:S(2)}) collective-permute-start(bf16[4,2,7,16,128]{4,3,2,1,0:T(8,128)(2,1)S(1)} %shard_map.88.refs_0_), channel_id=1, source_target_pairs={{0,2},{1,3},{2,0},{3,1},{4,6},{5,7},{6,4},{7,5},{8,10},{9,11},{10,... | collective-permute-start | bytes 688136 | tf_op jit(solution)/shard_map/ppermute | solution.py:271
  99.6 12.6 %collective-permute-start.30 = (bf16[4,2,7,16,128]{4,3,2,1,0:T(8,128)(2,1)S(1)}, bf16[4,2,7,16,128]{4,3,2,1,0:T(8,128)(2,1)S(1)}, u32[]{:S(2)}, u32[]{:S(2)}) collective-permute-start(bf16[4,2,7,16,128]{4,3,2,1,0:T(8,128)(2,1)S(1)} %shard_map.88.refs_0_), channel_id=1, source_target_pairs={{0,1},{1,0},{2,3},{3,2},{4,5},{5,4},{6,7},{7,6},{8,9},{9,8},{10,11... | collective-permute-start | bytes 688136 | tf_op jit(solution)/shard_map/ppermute | solution.py:271
  100.7 11.9 %collective-permute-start.33 = (bf16[4,2,7,16,128]{4,3,2,1,0:T(8,128)(2,1)S(1)}, bf16[4,2,7,16,128]{4,3,2,1,0:T(8,128)(2,1)S(1)}, u32[]{:S(2)}, u32[]{:S(2)}) collective-permute-start(bf16[4,2,7,16,128]{4,3,2,1,0:T(8,128)(2,1)S(1)} %shard_map.88.refs_0_), channel_id=1, source_target_pairs={{0,16},{1,17},{2,18},{3,19},{4,20},{5,21},{6,22},{7,23},{8,24},{9,... | collective-permute-start | bytes 688136 | tf_op jit(solution)/shard_map/ppermute | solution.py:271
  106.0 6.5 %collective-permute-start.36 = (bf16[4,2,7,16,128]{4,3,2,1,0:T(8,128)(2,1)S(1)}, bf16[4,2,7,16,128]{4,3,2,1,0:T(8,128)(2,1)S(1)}, u32[]{:S(2)}, u32[]{:S(2)}) collective-permute-start(bf16[4,2,7,16,128]{4,3,2,1,0:T(8,128)(2,1)S(1)} %collective-permute-done.32.refs_3_), channel_id=1, source_target_pairs={{0,16},{1,17},{2,18},{3,19},{4,20},{5,21},{6,22},{7,23},{8,24},{9,... | collective-permute-start | bytes 688136 | tf_op jit(solution)/shard_map/ppermute | solution.py:271
  (10 other events, 77.3 us)

commit v3 on v2

--- a/solution.py
+++ b/solution.py
@@ -141,22 +141,7 @@
 
 
 def second_kernel(
-    centre,
-    time,
-    near,
-    far,
-    corners,
-    kernel,
-    cotangent,
-    output,
-    grad,
-    last,
-    near_out,
-    far_out,
-    pad,
-    taps,
-    held,
-    sems,
+    centre, time, near, far, corners, kernel, cotangent, output, grad, last, near_out, far_out, pad, taps
 ):
     lay(pad, centre, time, near, far, corners, False)
     lay_taps(taps, kernel, False)
@@ -164,24 +149,24 @@
     for t in range(frames):
         z = convolve(pad, taps, t, rows, False)
         s = jax.nn.sigmoid(z)
-        held[t] = (z * s).astype(jnp.bfloat16).reshape(held.shape[1:])
-        pltpu.make_async_copy(held.at[t], output.at[t], sems.at[t]).start()
+        output[t] = (z * s).astype(jnp.bfloat16).reshape(output.shape[1:])
         steep = (s * (1.0 + z * (1.0 - s))).reshape(grad.shape[1:])
         grad[t] = (cotangent[t].astype(jnp.float32) * steep).astype(jnp.bfloat16)
     strips(grad, last, near_out, far_out, True)
-    for t in range(frames):
-        pltpu.make_async_copy(held.at[t], output.at[t], sems.at[t]).wait()
-
-
-def back_kernel(centre, time, near, far, corners, kernel, grad, ended, pad, taps, held, sems):
+
+
+def back_kernel(centre, time, near, far, corners, kernel, made, grad, output, ended, pad, taps, held, sems):
+    frames, rows = centre.shape[:2]
+    made_copy = pltpu.make_async_copy(made, output, sems.at[frames])
+    made_copy.start()
     lay(pad, centre, time, near, far, corners, True)
     lay_taps(taps, kernel, True)
-    frames, rows = centre.shape[:2]
     for t in range(frames):
         z = convolve(pad, taps, t, rows, True)
         held[t] = z.astype(jnp.bfloat16).reshape(held.shape[1:])
         pltpu.make_async_copy(held.at[t], grad.at[t], sems.at[t]).start()
     ended[...] = jnp.zeros_like(ended)
+    made_copy.wait()
     for t in range(frames):
         pltpu.make_async_copy(held.at[t], grad.at[t], sems.at[t]).wait()
 
@@ -222,19 +207,27 @@
         out[:, 27:] = jnp.zeros_like(out[:, 27:])
 
 
-def first_scatter_kernel(keep_one, came_one, keep_two, came_two, mine, *sent):
+def scatter_kernel(keep_one, came_one, keep_two, came_two, mine, *parts):
     x = lax.axis_index("height") % 4
-    for d, out in enumerate((mine, *sent)):
-        for k, (keep, came) in enumerate(((keep_one, came_one), (keep_two, came_two))):
+    over_one, over_three, plain_one, plain_three, later_one, later_three = parts
+    targets = ((mine.at[0], plain_one, over_one, later_three), (mine.at[1], later_one, over_three, plain_three))
+    for (keep, came), outs in zip(((keep_one, came_one), (keep_two, came_two)), targets, strict=True):
+        for d in (2, 1, 3, 0):
             total = keep[x ^ d] + came[x ^ d].astype(jnp.float32)
-            out[:, k] = total.reshape(4, -1, *total.shape[1:]).astype(out.dtype)
-
-
-def second_scatter_kernel(own, one, two, three, mine, *sent):
+            outs[d][...] = total.reshape(outs[d].shape).astype(outs[d].dtype)
+
+
+def relay_kernel(later_one, later_three, came_one, came_three, to_one, to_three):
+    to_one[...] = (later_one[...] + came_three[...].astype(jnp.float32)).astype(jnp.bfloat16)
+    to_three[...] = (later_three[...] + came_one[...].astype(jnp.float32)).astype(jnp.bfloat16)
+
+
+def second_scatter_kernel(own, one_first, three_first, one_second, three_second, mine, *sent):
     y = lax.axis_index("height") // 4
     for d, out in enumerate((mine, *sent)):
-        own_part, *parts = (ref[y ^ d].astype(jnp.float32) for ref in (own, one, two, three))
-        out[...] = ((own_part + parts[0]) + (parts[1] + parts[2])).astype(out.dtype)
+        for k, (one, three) in enumerate(((one_first, three_first), (one_second, three_second))):
+            came = one[y ^ d].astype(jnp.float32) + three[y ^ d].astype(jnp.float32)
+            out[k] = (own[k, y ^ d] + came).astype(out.dtype)
 
 
 def add_kernel(own, one, two, three, out):
@@ -245,7 +238,7 @@
 def join_kernel(own, one, three, two, out):
     y = lax.axis_index("height") // 4
     for d, part in enumerate((own, one, two, three)):
-        out[y ^ d] = part[...]
+        out[:, y ^ d] = part[...]
 
 
 def gather_kernel(scale, *refs):
@@ -258,7 +251,7 @@
             first, count = 7 * q, min(7, taps - 7 * q)
             for d in range(4):
                 for half in range(2):
-                    block = pieces[4 * half + d][q, k, :count].astype(jnp.float32) * scale
+                    block = pieces[4 * half + d][k, q, :count].astype(jnp.float32) * scale
                     held[k, pl.ds(first, count), pl.ds((core ^ half) * 4 + (x ^ d), 1)] = block[:, None]
             part = pl.ds(first, count)
             copies.append(pltpu.make_async_copy(held.at[k, part], out.at[part], sems.at[4 * k + q]))
@@ -271,44 +264,48 @@
     return lax.ppermute(value, ALL, [(i, i ^ mask) for i in range(lax.axis_size(ALL))])
 
 
-def kinds(shape):
-    return [jax.ShapeDtypeStruct(shape, jnp.float32)] + 3 * [jax.ShapeDtypeStruct(shape, jnp.bfloat16)]
-
-
 def started(one, two):
     _, taps, part, channels = one[0].shape
-    shape = (4, 2, taps // 4, part, channels)
+    shape = (4, taps // 4, part, channels)
+    f32 = jax.ShapeDtypeStruct((2, *shape), jnp.float32)
+    bf16 = jax.ShapeDtypeStruct(shape, jnp.bfloat16)
     halves = (one[0], swap(one[1], 16), two[0], swap(two[1], 16))
-    return call(first_scatter_kernel, kinds(shape), [], 8 * math.prod(shape), *halves)
-
-
-def summed(mine, sent, edged, ended):
-    quarter = mine.shape[1:]
-    size = math.prod(quarter)
+    later = jax.ShapeDtypeStruct(shape, jnp.float32)
+    return call(scatter_kernel, [f32, *4 * [bf16], later, later], [], 16 * math.prod(shape), *halves)
+
+
+def summed(quarters, scale, cornered, ended):
+    mine, over_one, over_three, plain_one, plain_three, *later = quarters
+    shape = mine.shape
+    part, channels = shape[3:]
+    size = math.prod(shape)
+    whole = jax.ShapeDtypeStruct(shape, jnp.bfloat16)
+    half = jax.ShapeDtypeStruct(shape[1:], jnp.bfloat16)
+    came = swap(over_one, 1), swap(over_three, 3)
+    one_first, three_second = swap(plain_one, 1), swap(plain_three, 3)
+    to_one, to_three = call(relay_kernel, [half, half], [], size, *later, *came)
+    one_second, three_first = swap(to_one, 1), swap(to_three, 3)
+    came = one_first, three_first, one_second, three_second
+    quarter = (shape[0], *shape[2:])
     small = jax.ShapeDtypeStruct(quarter, jnp.bfloat16)
-    one, two, three = (swap(value, d) for d, value in enumerate(sent, 1))
-    mine, *sent = call(second_scatter_kernel, kinds(quarter), [], 16 * size, mine, two, one, three)
+    exact = jax.ShapeDtypeStruct(quarter, jnp.float32)
+    mine, *sent = call(
+        second_scatter_kernel, [exact, small, small, small], [], 4 * size, mine, *came
+    )
     one, two, three = (swap(value, 4 * d) for d, value in enumerate(sent, 1))
-    (total,) = call(add_kernel, [small], [], 4 * size, mine, two, one, three, after=edged)
+    (total,) = call(add_kernel, [small], [], size, mine, two, one, three, after=cornered)
     one, two, three = (swap(total, mask) for mask in (64, 32, 96))
-    (total,) = call(add_kernel, [small], [], 4 * size, total, one, three, two, after=ended)
+    (total,) = call(add_kernel, [small], [], size, total, one, three, two, after=ended)
     one, two, three = (swap(total, 4 * d) for d in (1, 2, 3))
-    (total,) = call(
-        join_kernel, [jax.ShapeDtypeStruct((4, *quarter), jnp.bfloat16)], [], 4 * size, total, one, three, two
-    )
-    return total
-
-
-def spread(total, scale):
-    part, channels = total.shape[3:]
+    (total,) = call(join_kernel, [whole], [], size, total, one, three, two)
     pieces = [total] + [swap(total, d) for d in (1, 2, 3)]
     pieces += [swap(value, 16) for value in pieces]
-    whole = (27, 8, part, channels)
+    out_shape = (27, 8, part, channels)
     outs = call(
         functools.partial(gather_kernel, scale),
-        [jax.ShapeDtypeStruct(whole, jnp.float32)] * 2,
-        [pltpu.VMEM((2, *whole), jnp.float32), pltpu.SemaphoreType.DMA((8,))],
-        16 * total.size,
+        [jax.ShapeDtypeStruct(out_shape, jnp.float32)] * 2,
+        [pltpu.VMEM((2, *out_shape), jnp.float32), pltpu.SemaphoreType.DMA((8,))],
+        8 * size,
         *pieces,
         outside=(HBM, HBM),
     )
@@ -362,7 +359,7 @@
     taps = pltpu.VMEM((9 * channels, 3 * channels), jnp.bfloat16)
     back_taps = pltpu.VMEM((3 * channels, 9 * channels), jnp.bfloat16)
     moved = pltpu.VMEM((cells, 3 * channels), jnp.bfloat16)
-    out = pltpu.VMEM(shape, jnp.bfloat16), pltpu.SemaphoreType.DMA((frames,))
+    out = pltpu.VMEM(shape, jnp.bfloat16), pltpu.SemaphoreType.DMA((frames + 1,))
     scale = 1.0 / math.sqrt(cells * lax.axis_size(ALL))
 
     whole, *cut = call(
@@ -381,16 +378,15 @@
         first_kernel, [f32, bf16, last, line, line], [pad], flops, whole, *clip_edges, first_taps
     )
     hidden_edges = cornered(*exchanged(*cut, False), False)
-    output, grad_two, *cut = call(
+    made, grad_two, *cut = call(
         second_kernel,
         [bf16, bf16, last, line, line],
-        [pad, taps, *out],
+        [pad, taps],
         flops,
         hidden,
         *hidden_edges,
         second_weight,
         cotangent,
-        outside=(HBM,),
     )
     two_edges = cornered(*exchanged(*cut, True), True)
     second_terms = call(weight_kernel, [keep, send], [pad, moved], flops, hidden, *hidden_edges, grad_two)
@@ -406,20 +402,21 @@
     )
     one_edges = exchanged(*cut, True)
     first_terms = call(weight_kernel, [keep, send], [pad, moved], flops, whole, *clip_edges, grad_one)
-    mine, *sent = started(first_terms, second_terms)
-    one_edges = cornered(*one_edges, True, after=(mine,))
+    quarters = started(first_terms, second_terms)
+    one_edges = cornered(*one_edges, True, after=quarters[:1])
     ended = jax.ShapeDtypeStruct((8, 128), jnp.float32)
-    clip_grad, ended = call(
+    clip_grad, output, ended = call(
         back_kernel,
-        [bf16, ended],
+        [bf16, bf16, ended],
         [pad, back_taps, *out],
         flops,
         grad_one,
         *one_edges,
         first_weight,
-        outside=(HBM,),
-    )
-    first_grad, second_grad = spread(summed(mine, sent, (one_edges[0], one_edges[3]), (ended,)), scale)
+        made,
+        outside=(HBM, HBM),
+    )
+    first_grad, second_grad = summed(quarters, scale, one_edges[3:], (ended,))
     return output[None], clip_grad[None], first_grad, second_grad
 
 

time: 116 us -> 113 us (0.974)
  waiting for transfers between devices: 26.1 us -> 20.9 us
  starting transfers between devices: 68 us -> 70.9 us
    ppermute x4, waiting for transfers between devices: 11.8 us -> 1.61 us  [exchanged(): lax.ppermute(far, 'height', [(i, (i - 1 if i % 2 == 0 else i + 1) % line)...]
    ppermute x21 -> x24, waiting for transfers between devices: 6.53 us -> 13.7 us  [swap(): lax.ppermute(value, ALL, [(i, i ^ mask) for i in range(lax.axis_size(ALL))])]
    ppermute x4, waiting for transfers between devices: 7.76 us -> 5.54 us  [cornered(): return (time, near, far, lax.ppermute(rows, 'tm', time_route(ahead)))]
    ppermute x21 -> x24, starting transfers between devices: 28.2 us -> 29.7 us  [swap(): lax.ppermute(value, ALL, [(i, i ^ mask) for i in range(lax.axis_size(ALL))])]
    ppermute x4, starting transfers between devices: 2.37 us -> 3.65 us  [exchanged(): near = lax.ppermute(near, 'height', [(i, i ^ 1) for i in range(line)])]
    pallas_call x15 -> x16, Pallas kernels: 18.5 us -> 17.8 us  [call(): pl.pallas_call(run, out_shape=outs, in_specs=[inside] * len(args) + [ANY]...]
  transfers between devices with their start and end apart: 37 -> 40, of which waited for: 13 -> 16; matrix products, arithmetic and copies ran while one was open for 0% -> 0% of each run, Pallas kernels for 9% -> 9%
where the time goes in v3:
time: 113 us
  starting transfers between devices  70.9 us (63%)
  waiting for transfers between devices  20.9 us (18%)
  Pallas kernels  17.8 us (16%)
  local copies, waits for them, and re-layouts  2.17 us (2%)
    ppermute x24, starting transfers between devices, swap(): lax.ppermute(value, ALL, [(i, i ^ mask) for i in range(lax.axis_size(ALL))])  29.7 us
    pallas_call x16, Pallas kernels, call(): pl.pallas_call(run, out_shape=outs, in_specs=[inside] * len(args) + [ANY]...  17.8 us
    ppermute x4, starting transfers between devices, exchanged(): lax.ppermute(far, 'height', [(i, (i - 1 if i % 2 == 0 else i + 1) % line)...  17.2 us
    ppermute x24, waiting for transfers between devices, swap(): lax.ppermute(value, ALL, [(i, i ^ mask) for i in range(lax.axis_size(ALL))])  13.7 us
    ppermute x4, starting transfers between devices, exchanged(): time = lax.ppermute(last, 'tm', time_route(ahead))  10.9 us
    ppermute x4, starting transfers between devices, cornered(): return (time, near, far, lax.ppermute(rows, 'tm', time_route(ahead)))  9.55 us
    ppermute x4, waiting for transfers between devices, cornered(): return (time, near, far, lax.ppermute(rows, 'tm', time_route(ahead)))  5.54 us
    ppermute x4, starting transfers between devices, exchanged(): near = lax.ppermute(near, 'height', [(i, i ^ 1) for i in range(line)])  3.65 us
  transfers between devices with their start and end apart: 40, of which 16 were waited for; matrix products, arithmetic and copies ran while one was open for 0% of the time, Pallas kernels for 9%

profile of v3, /device:TPU:1, one launch (start us, length us, event | category | flops | bytes accessed | tf_op | source)
XLA Modules:
  0.0 112.9 jit_solution(9427503207733525709)
XLA Ops:
  2.0 2.1 %collective-permute-start.1 = (bf16[3,1,128,128]{3,2,1,0:T(8,128)(2,1)S(1)}, bf16[3,1,128,128]{3,2,1,0:T(8,128)(2,1)S(1)}, u32[]{:S(2)}, u32[]{:S(2)}) collective-permute-start(bf16[3,1,128,128]{3,2,1,0:T(8,128)(2,1)S(1)} %get-tuple-element.46), channel_id=1, source_target_pairs={{0,1},{1,0},{2,3},{3,2},{4,5},{5,4},{6,7},{7,6},{8,9},{9,8},{10,11... | collective-permute-start | bytes 294920 | tf_op jit(solution)/shard_map/ppermute | solution.py:329
  4.1 4.3 %collective-permute-start.2 = (bf16[3,1,128,128]{3,2,1,0:T(8,128)(2,1)S(1)}, bf16[3,1,128,128]{3,2,1,0:T(8,128)(2,1)S(1)}, u32[]{:S(2)}, u32[]{:S(2)}) collective-permute-start(bf16[3,1,128,128]{3,2,1,0:T(8,128)(2,1)S(1)} %get-tuple-element.47), channel_id=1, source_target_pairs={{0,15},{1,2},{2,1},{3,4},{4,3},{5,6},{6,5},{7,8},{8,7},{9,10},{10,... | collective-permute-start | bytes 294920 | tf_op jit(solution)/shard_map/ppermute | solution.py:330
  8.3 4.7 %collective-permute-start = (bf16[2,4,128,128]{3,2,1,0:T(8,128)(2,1)S(1)}, bf16[2,4,128,128]{3,2,1,0:T(8,128)(2,1)S(1)}, u32[]{:S(2)}, u32[]{:S(2)}) collective-permute-start(bf16[2,4,128,128]{3,2,1,0:T(8,128)(2,1)S(1)} %get-tuple-element.45), channel_id=1, source_target_pairs={{0,16},{16,32},{32,48},{48,0},{1,17},{17,33},{33,49},{49,1},{2,18}... | collective-permute-start | bytes 786440 | tf_op jit(solution)/shard_map/ppermute | solution.py:328
  13.1 3.5 %collective-permute-start.3 = (bf16[2,2,128,128]{3,2,1,0:T(8,128)(2,1)S(1)}, bf16[2,2,128,128]{3,2,1,0:T(8,128)(2,1)S(1)}, u32[]{:S(2)}, u32[]{:S(2)}) collective-permute-start(bf16[2,2,128,128]{3,2,1,0:T(8,128)(2,1)S(1)} %pad_maximum_fusion.2), channel_id=1, source_target_pairs={{0,16},{16,32},{32,48},{48,0},{1,17},{17,33},{33,49},{49,1},{2,18}... | collective-permute-start | bytes 393224 | tf_op jit(solution)/shard_map/ppermute | solution.py:342
  18.5 2.3 %shard_map.77 = (f32[3,4,128,128]{3,2,1,0:T(8,128)S(1)}, bf16[3,4,128,128]{3,2,1,0:T(8,128)(2,1)S(1)}, bf16[2,4,128,128]{3,2,1,0:T(8,128)(2,1)S(1)}, bf16[3,1,12...) custom-call(bf16[3,4,128,128]{3,2,1,0:T(8,128)(2,1)S(1)} %get-tuple-element.44.refs_0_, ...), custom_call_target="tpu_custom_call" | custom-call | flops 1358954496 | bytes 3506176 | tf_op jit(solution)/shard_map/pallas_call | solution.py:25
  20.9 4.3 %collective-permute-start.6 = (bf16[3,1,128,128]{3,2,1,0:T(8,128)(2,1)S(1)}, bf16[3,1,128,128]{3,2,1,0:T(8,128)(2,1)S(1)}, u32[]{:S(2)}, u32[]{:S(2)}) collective-permute-start(bf16[3,1,128,128]{3,2,1,0:T(8,128)(2,1)S(1)} %get-tuple-element.51), channel_id=1, source_target_pairs={{0,15},{1,2},{2,1},{3,4},{4,3},{5,6},{6,5},{7,8},{8,7},{9,10},{10,... | collective-permute-start | bytes 294920 | tf_op jit(solution)/shard_map/ppermute | solution.py:330
  25.3 4.2 %collective-permute-start.4 = (bf16[2,4,128,128]{3,2,1,0:T(8,128)(2,1)S(1)}, bf16[2,4,128,128]{3,2,1,0:T(8,128)(2,1)S(1)}, u32[]{:S(2)}, u32[]{:S(2)}) collective-permute-start(bf16[2,4,128,128]{3,2,1,0:T(8,128)(2,1)S(1)} %get-tuple-element.49), channel_id=1, source_target_pairs={{0,16},{16,32},{32,48},{48,0},{1,17},{17,33},{33,49},{49,1},{2,18}... | collective-permute-start | bytes 786440 | tf_op jit(solution)/shard_map/ppermute | solution.py:328
  29.5 3.5 %collective-permute-start.7 = (bf16[2,2,128,128]{3,2,1,0:T(8,128)(2,1)S(1)}, bf16[2,2,128,128]{3,2,1,0:T(8,128)(2,1)S(1)}, u32[]{:S(2)}, u32[]{:S(2)}) collective-permute-start(bf16[2,2,128,128]{3,2,1,0:T(8,128)(2,1)S(1)} %pad_maximum_fusion.1), channel_id=1, source_target_pairs={{0,16},{16,32},{32,48},{48,0},{1,17},{17,33},{33,49},{49,1},{2,18}... | collective-permute-start | bytes 393224 | tf_op jit(solution)/shard_map/ppermute | solution.py:342
  33.0 1.9 %collective-permute-done.7.refs_4_ = bf16[2,2,128,128]{3,2,1,0:T(8,128)(2,1)S(1)} collective-permute-done((bf16[2,2,128,128]{3,2,1,0:T(8,128)(2,1)S(1)}, bf16[2,2,128,128]{3,2,1,0:T(8,128)(2,1)S(1)}, u32[]{:S(2)}, u32[]{:S(2)}) %collective-permute-start.7) | collective-permute-done | bytes 131104 | tf_op jit(solution)/shard_map/ppermute | solution.py:342
  34.9 2.5 %shard_map.78 = (bf16[3,4,128,128]{3,2,1,0:T(8,128)(2,1)S(1)}, bf16[3,4,128,128]{3,2,1,0:T(8,128)(2,1)S(1)}, bf16[2,4,128,128]{3,2,1,0:T(8,128)(2,1)S(1)}, bf16[...) custom-call(bf16[3,4,128,128]{3,2,1,0:T(8,128)(2,1)S(1)} %get-tuple-element.48.refs_0_, ...), custom_call_target="tpu_custom_call" | custom-call | flops 1358954496 | bytes 3506176 | tf_op jit(solution)/shard_map/pallas_call | solution.py:25
  37.5 4.3 %collective-permute-start.10 = (bf16[3,1,128,128]{3,2,1,0:T(8,128)(2,1)S(1)}, bf16[3,1,128,128]{3,2,1,0:T(8,128)(2,1)S(1)}, u32[]{:S(2)}, u32[]{:S(2)}) collective-permute-start(bf16[3,1,128,128]{3,2,1,0:T(8,128)(2,1)S(1)} %get-tuple-element.55), channel_id=1, source_target_pairs={{0,15},{1,2},{2,1},{3,4},{4,3},{5,6},{6,5},{7,8},{8,7},{9,10},{10,... | collective-permute-start | bytes 294920 | tf_op jit(solution)/shard_map/ppermute | solution.py:330
  42.7 1.6 %collective-permute-done.10.refs_3_ = bf16[3,1,128,128]{3,2,1,0:T(8,128)(2,1)S(1)} collective-permute-done((bf16[3,1,128,128]{3,2,1,0:T(8,128)(2,1)S(1)}, bf16[3,1,128,128]{3,2,1,0:T(8,128)(2,1)S(1)}, u32[]{:S(2)}, u32[]{:S(2)}) %collective-permute-start.10) | collective-permute-done | bytes 98336 | tf_op jit(solution)/shard_map/ppermute | solution.py:330
  44.4 1.9 %collective-permute-start.11 = (bf16[2,2,128,128]{3,2,1,0:T(8,128)(2,1)S(1)}, bf16[2,2,128,128]{3,2,1,0:T(8,128)(2,1)S(1)}, u32[]{:S(2)}, u32[]{:S(2)}) collective-permute-start(bf16[2,2,128,128]{3,2,1,0:T(8,128)(2,1)S(1)} %pad_maximum_fusion), channel_id=1, source_target_pairs={{0,48},{16,0},{32,16},{48,32},{1,49},{17,1},{33,17},{49,33},{2,50}... | collective-permute-start | bytes 393224 | tf_op jit(solution)/shard_map/ppermute | solution.py:342
  46.2 2.3 %shard_map.81 = (f32[4,28,16,128]{3,2,1,0:T(8,128)S(1)}, bf16[4,28,16,128]{3,2,1,0:T(8,128)(2,1)S(1)}) custom-call(bf16[3,4,128,128]{3,2,1,0:T(8,128)(2,1)S(1)} %get-tuple-element.48.refs_0_, bf16[2,4,128,128]{3,2,1,0:T(8,128)(2,1)S(1)} %collective-permute-done.4.refs_1_, bf16[3,1,128,128]{3,2,1,0:T(8,128)(2,1)S(1)} %collective-permute-done.5.refs_2_, ...), custom_call_target="tpu_custom_call" | custom-call | flops 1358954496 | bytes 2752512 | tf_op jit(solution)/shard_map/pallas_call | solution.py:25
  49.0 3.1 %collective-permute-done.11.refs_4_ = bf16[2,2,128,128]{3,2,1,0:T(8,128)(2,1)S(1)} collective-permute-done((bf16[2,2,128,128]{3,2,1,0:T(8,128)(2,1)S(1)}, bf16[2,2,128,128]{3,2,1,0:T(8,128)(2,1)S(1)}, u32[]{:S(2)}, u32[]{:S(2)}) %collective-permute-start.11) | collective-permute-done | bytes 131104 | tf_op jit(solution)/shard_map/ppermute | solution.py:342
  52.2 2.6 %shard_map.79 = (bf16[3,4,128,128]{3,2,1,0:T(8,128)(2,1)S(1)}, bf16[2,4,128,128]{3,2,1,0:T(8,128)(2,1)S(1)}, bf16[3,1,128,128]{3,2,1,0:T(8,128)(2,1)S(1)}, bf16[3,1,128,128]{3,2,1,0:T(8,128)(2,1)S(1)}) custom-call(bf16[3,4,128,128]{3,2,1,0:T(8,128)(2,1)S(1)} %get-tuple-element.52.refs_0_.refs_5_, ...), custom_call_target="tpu_custom_call" | custom-call | flops 1358954496 | bytes 3506176 | tf_op jit(solution)/shard_map/pallas_call | solution.py:25
  54.8 2.3 %shard_map.80 = (f32[4,28,16,128]{3,2,1,0:T(8,128)S(1)}, bf16[4,28,16,128]{3,2,1,0:T(8,128)(2,1)S(1)}) custom-call(bf16[3,4,128,128]{3,2,1,0:T(8,128)(2,1)S(1)} %get-tuple-element.44.refs_0_, bf16[2,4,128,128]{3,2,1,0:T(8,128)(2,1)S(1)} %collective-permute-done.refs_1_, bf16[3,1,128,128]{3,2,1,0:T(8,128)(2,1)S(1)} %collective-permute-done.1.refs_2_, ...), custom_call_target="tpu_custom_call" | custom-call | flops 1358954496 | bytes 2752512 | tf_op jit(solution)/shard_map/pallas_call | solution.py:25
  57.1 1.8 %collective-permute-done.15.refs_1_ = bf16[4,28,16,128]{3,2,1,0:T(8,128)(2,1)S(1)} collective-permute-done((bf16[4,28,16,128]{3,2,1,0:T(8,128)(2,1)S(1)}, bf16[4,28,16,128]{3,2,1,0:T(8,128)(2,1)S(1)}, u32[]{:S(2)}, u32[]{:S(2)}) %collective-permute-start.15) | collective-permute-done | bytes 458784 | tf_op jit(solution)/shard_map/ppermute | solution.py:264
  60.6 4.2 %collective-permute-start.14 = (bf16[3,1,128,128]{3,2,1,0:T(8,128)(2,1)S(1)}, bf16[3,1,128,128]{3,2,1,0:T(8,128)(2,1)S(1)}, u32[]{:S(2)}, u32[]{:S(2)}) collective-permute-start(bf16[3,1,128,128]{3,2,1,0:T(8,128)(2,1)S(1)} %get-tuple-element.60), channel_id=1, source_target_pairs={{0,15},{1,2},{2,1},{3,4},{4,3},{5,6},{6,5},{7,8},{8,7},{9,10},{10,... | collective-permute-start | bytes 294920 | tf_op jit(solution)/shard_map/ppermute | solution.py:330
  66.0 2.7 %collective-permute-start.21 = (bf16[4,7,16,128]{3,2,1,0:T(8,128)(2,1)S(1)}, bf16[4,7,16,128]{3,2,1,0:T(8,128)(2,1)S(1)}, u32[]{:S(2)}, u32[]{:S(2)}) collective-permute-start(bf16[4,7,16,128]{3,2,1,0:T(8,128)(2,1)S(1)} %get-tuple-element.74), channel_id=1, source_target_pairs={{0,3},{1,2},{2,1},{3,0},{4,7},{5,6},{6,5},{7,4},{8,11},{9,10},{10,... | collective-permute-start | bytes 344072 | tf_op jit(solution)/shard_map/ppermute | solution.py:264
  69.0 1.7 %collective-permute-done.18.refs_1_ = bf16[4,7,16,128]{3,2,1,0:T(8,128)(2,1)S(1)} collective-permute-done((bf16[4,7,16,128]{3,2,1,0:T(8,128)(2,1)S(1)}, bf16[4,7,16,128]{3,2,1,0:T(8,128)(2,1)S(1)}, u32[]{:S(2)}, u32[]{:S(2)}) %collective-permute-start.18) | collective-permute-done | bytes 114720 | tf_op jit(solution)/shard_map/ppermute | solution.py:264
  71.4 2.3 %collective-permute-done.21.refs_2_ = bf16[4,7,16,128]{3,2,1,0:T(8,128)(2,1)S(1)} collective-permute-done((bf16[4,7,16,128]{3,2,1,0:T(8,128)(2,1)S(1)}, bf16[4,7,16,128]{3,2,1,0:T(8,128)(2,1)S(1)}, u32[]{:S(2)}, u32[]{:S(2)}) %collective-permute-start.21) | collective-permute-done | bytes 114720 | tf_op jit(solution)/shard_map/ppermute | solution.py:264
  73.8 2.4 %collective-permute-start.24 = (bf16[2,7,16,128]{3,2,1,0:T(8,128)(2,1)S(1)}, bf16[2,7,16,128]{3,2,1,0:T(8,128)(2,1)S(1)}, u32[]{:S(2)}, u32[]{:S(2)}) collective-permute-start(bf16[2,7,16,128]{3,2,1,0:T(8,128)(2,1)S(1)} %get-tuple-element.78), channel_id=1, source_target_pairs={{0,8},{1,9},{2,10},{3,11},{4,12},{5,13},{6,14},{7,15},{8,0},{9,1},... | collective-permute-start | bytes 172040 | tf_op jit(solution)/shard_map/ppermute | solution.py:264
  79.3 1.7 %collective-permute-done.26.refs_3_ = bf16[2,7,16,128]{3,2,1,0:T(8,128)(2,1)S(1)} collective-permute-done((bf16[2,7,16,128]{3,2,1,0:T(8,128)(2,1)S(1)}, bf16[2,7,16,128]{3,2,1,0:T(8,128)(2,1)S(1)}, u32[]{:S(2)}, u32[]{:S(2)}) %collective-permute-start.26) | collective-permute-done | bytes 57376 | tf_op jit(solution)/shard_map/ppermute | solution.py:264
  81.1 3.1 %collective-permute-start.28 = (bf16[2,7,16,128]{3,2,1,0:T(8,128)(2,1)S(1)}, bf16[2,7,16,128]{3,2,1,0:T(8,128)(2,1)S(1)}, u32[]{:S(2)}, u32[]{:S(2)}) collective-permute-start(bf16[2,7,16,128]{3,2,1,0:T(8,128)(2,1)S(1)} %shard_map.87.refs_0_), channel_id=1, source_target_pairs={{0,96},{1,97},{2,98},{3,99},{4,100},{5,101},{6,102},{7,103},{8,104... | collective-permute-start | bytes 172040 | tf_op jit(solution)/shard_map/ppermute | solution.py:264
  84.2 3.0 %shard_map.84 = (bf16[3,4,128,128]{3,2,1,0:T(8,128)(2,1)}, bf16[3,4,128,128]{3,2,1,0:T(8,128)(2,1)}, f32[8,128]{1,0:T(8,128)S(1)}) custom-call(bf16[3,4,128,128]{3,2,1,0:T(8,128)(2,1)S(1)} %get-tuple-element.57.refs_5_.refs_0_, bf16[2,4,128,128]{3,2,1,0:T(8,128)(2,1)S(1)} %collective-permute-done.12.refs_1_, ...), custom_call_target="tpu_custom_call" | custom-call | flops 1358954496 | bytes 3051520 | tf_op jit(solution)/shard_map/pallas_call | solution.py:25
  88.1 2.6 %collective-permute-start.31 = (bf16[2,7,16,128]{3,2,1,0:T(8,128)(2,1)S(1)}, bf16[2,7,16,128]{3,2,1,0:T(8,128)(2,1)S(1)}, u32[]{:S(2)}, u32[]{:S(2)}) collective-permute-start(bf16[2,7,16,128]{3,2,1,0:T(8,128)(2,1)S(1)} %shard_map.88.refs_0_), channel_id=1, source_target_pairs={{0,12},{1,13},{2,14},{3,15},{4,8},{5,9},{6,10},{7,11},{8,4},{9,5},... | collective-permute-start | bytes 172040 | tf_op jit(solution)/shard_map/ppermute | solution.py:264
  93.7 1.8 %collective-permute-start.35 = (bf16[2,4,7,16,128]{4,3,2,1,0:T(8,128)(2,1)S(1)}, bf16[2,4,7,16,128]{4,3,2,1,0:T(8,128)(2,1)S(1)}, u32[]{:S(2)}, u32[]{:S(2)}) collective-permute-start(bf16[2,4,7,16,128]{4,3,2,1,0:T(8,128)(2,1)S(1)} %shard_map.89.refs_0_), channel_id=1, source_target_pairs={{0,3},{1,2},{2,1},{3,0},{4,7},{5,6},{6,5},{7,4},{8,11},{9,10},{10,... | collective-permute-start | bytes 688136 | tf_op jit(solution)/shard_map/ppermute | solution.py:264
  95.6 1.5 %collective-permute-start.33 = (bf16[2,4,7,16,128]{4,3,2,1,0:T(8,128)(2,1)S(1)}, bf16[2,4,7,16,128]{4,3,2,1,0:T(8,128)(2,1)S(1)}, u32[]{:S(2)}, u32[]{:S(2)}) collective-permute-start(bf16[2,4,7,16,128]{4,3,2,1,0:T(8,128)(2,1)S(1)} %shard_map.89.refs_0_), channel_id=1, source_target_pairs={{0,1},{1,0},{2,3},{3,2},{4,5},{5,4},{6,7},{7,6},{8,9},{9,8},{10,11... | collective-permute-start | bytes 688136 | tf_op jit(solution)/shard_map/ppermute | solution.py:264
  97.1 6.1 %collective-permute-start.36 = (bf16[2,4,7,16,128]{4,3,2,1,0:T(8,128)(2,1)S(1)}, bf16[2,4,7,16,128]{4,3,2,1,0:T(8,128)(2,1)S(1)}, u32[]{:S(2)}, u32[]{:S(2)}) collective-permute-start(bf16[2,4,7,16,128]{4,3,2,1,0:T(8,128)(2,1)S(1)} %shard_map.89.refs_0_), channel_id=1, source_target_pairs={{0,16},{1,17},{2,18},{3,19},{4,20},{5,21},{6,22},{7,23},{8,24},{9,... | collective-permute-start | bytes 688136 | tf_op jit(solution)/shard_map/ppermute | solution.py:264
  103.2 5.6 %collective-permute-start.39 = (bf16[2,4,7,16,128]{4,3,2,1,0:T(8,128)(2,1)S(1)}, bf16[2,4,7,16,128]{4,3,2,1,0:T(8,128)(2,1)S(1)}, u32[]{:S(2)}, u32[]{:S(2)}) collective-permute-start(bf16[2,4,7,16,128]{4,3,2,1,0:T(8,128)(2,1)S(1)} %collective-permute-done.35.refs_3_), channel_id=1, source_target_pairs={{0,16},{1,17},{2,18},{3,19},{4,20},{5,21},{6,22},{7,23},{8,24},{9,... | collective-permute-start | bytes 688136 | tf_op jit(solution)/shard_map/ppermute | solution.py:264
  110.8 1.9 %shard_map.90 = (f32[27,8,16,128]{3,2,1,0:T(8,128)}, f32[27,8,16,128]{3,2,1,0:T(8,128)}) custom-call(bf16[2,4,7,16,128]{4,3,2,1,0:T(8,128)(2,1)S(1)} %shard_map.89.refs_0_, bf16[2,4,7,16,128]{4,3,2,1,0:T(8,128)(2,1)S(1)} %collective-permute-done.33.refs_1_, bf16[2,4,7,16,128]{4,3,2,1,0:T(8,128)(2,1)S(1)} %collective-permute-done.34.refs_2_, ...), custom_call_target="tpu_custom_call" | custom-call | flops 917504 | bytes 5373952 | tf_op jit(solution)/shard_map/pallas_call | solution.py:25
  (77 shorter events, 17.9 us)
Async XLA Ops:
  2.0 11.1 %collective-permute-start.1 = (bf16[3,1,128,128]{3,2,1,0:T(8,128)(2,1)S(1)}, bf16[3,1,128,128]{3,2,1,0:T(8,128)(2,1)S(1)}, u32[]{:S(2)}, u32[]{:S(2)}) collective-permute-start(bf16[3,1,128,128]{3,2,1,0:T(8,128)(2,1)S(1)} %get-tuple-element.46), channel_id=1, source_target_pairs={{0,1},{1,0},{2,3},{3,2},{4,5},{5,4},{6,7},{7,6},{8,9},{9,8},{10,11... | collective-permute-start | bytes 294920 | tf_op jit(solution)/shard_map/ppermute | solution.py:329
  4.1 9.0 %collective-permute-start.2 = (bf16[3,1,128,128]{3,2,1,0:T(8,128)(2,1)S(1)}, bf16[3,1,128,128]{3,2,1,0:T(8,128)(2,1)S(1)}, u32[]{:S(2)}, u32[]{:S(2)}) collective-permute-start(bf16[3,1,128,128]{3,2,1,0:T(8,128)(2,1)S(1)} %get-tuple-element.47), channel_id=1, source_target_pairs={{0,15},{1,2},{2,1},{3,4},{4,3},{5,6},{6,5},{7,8},{8,7},{9,10},{10,... | collective-permute-start | bytes 294920 | tf_op jit(solution)/shard_map/ppermute | solution.py:330
  8.3 10.1 %collective-permute-start = (bf16[2,4,128,128]{3,2,1,0:T(8,128)(2,1)S(1)}, bf16[2,4,128,128]{3,2,1,0:T(8,128)(2,1)S(1)}, u32[]{:S(2)}, u32[]{:S(2)}) collective-permute-start(bf16[2,4,128,128]{3,2,1,0:T(8,128)(2,1)S(1)} %get-tuple-element.45), channel_id=1, source_target_pairs={{0,16},{16,32},{32,48},{48,0},{1,17},{17,33},{33,49},{49,1},{2,18}... | collective-permute-start | bytes 786440 | tf_op jit(solution)/shard_map/ppermute | solution.py:328
  13.1 5.4 %collective-permute-start.3 = (bf16[2,2,128,128]{3,2,1,0:T(8,128)(2,1)S(1)}, bf16[2,2,128,128]{3,2,1,0:T(8,128)(2,1)S(1)}, u32[]{:S(2)}, u32[]{:S(2)}) collective-permute-start(bf16[2,2,128,128]{3,2,1,0:T(8,128)(2,1)S(1)} %pad_maximum_fusion.2), channel_id=1, source_target_pairs={{0,16},{16,32},{32,48},{48,0},{1,17},{17,33},{33,49},{49,1},{2,18}... | collective-permute-start | bytes 393224 | tf_op jit(solution)/shard_map/ppermute | solution.py:342
  20.8 8.7 %collective-permute-start.5 = (bf16[3,1,128,128]{3,2,1,0:T(8,128)(2,1)S(1)}, bf16[3,1,128,128]{3,2,1,0:T(8,128)(2,1)S(1)}, u32[]{:S(2)}, u32[]{:S(2)}) collective-permute-start(bf16[3,1,128,128]{3,2,1,0:T(8,128)(2,1)S(1)} %get-tuple-element.50), channel_id=1, source_target_pairs={{0,1},{1,0},{2,3},{3,2},{4,5},{5,4},{6,7},{7,6},{8,9},{9,8},{10,11... | collective-permute-start | bytes 294920 | tf_op jit(solution)/shard_map/ppermute | solution.py:329
  20.9 8.6 %collective-permute-start.6 = (bf16[3,1,128,128]{3,2,1,0:T(8,128)(2,1)S(1)}, bf16[3,1,128,128]{3,2,1,0:T(8,128)(2,1)S(1)}, u32[]{:S(2)}, u32[]{:S(2)}) collective-permute-start(bf16[3,1,128,128]{3,2,1,0:T(8,128)(2,1)S(1)} %get-tuple-element.51), channel_id=1, source_target_pairs={{0,15},{1,2},{2,1},{3,4},{4,3},{5,6},{6,5},{7,8},{8,7},{9,10},{10,... | collective-permute-start | bytes 294920 | tf_op jit(solution)/shard_map/ppermute | solution.py:330
  25.3 9.7 %collective-permute-start.4 = (bf16[2,4,128,128]{3,2,1,0:T(8,128)(2,1)S(1)}, bf16[2,4,128,128]{3,2,1,0:T(8,128)(2,1)S(1)}, u32[]{:S(2)}, u32[]{:S(2)}) collective-permute-start(bf16[2,4,128,128]{3,2,1,0:T(8,128)(2,1)S(1)} %get-tuple-element.49), channel_id=1, source_target_pairs={{0,16},{16,32},{32,48},{48,0},{1,17},{17,33},{33,49},{49,1},{2,18}... | collective-permute-start | bytes 786440 | tf_op jit(solution)/shard_map/ppermute | solution.py:328
  29.5 5.4 %collective-permute-start.7 = (bf16[2,2,128,128]{3,2,1,0:T(8,128)(2,1)S(1)}, bf16[2,2,128,128]{3,2,1,0:T(8,128)(2,1)S(1)}, u32[]{:S(2)}, u32[]{:S(2)}) collective-permute-start(bf16[2,2,128,128]{3,2,1,0:T(8,128)(2,1)S(1)} %pad_maximum_fusion.1), channel_id=1, source_target_pairs={{0,16},{16,32},{32,48},{48,0},{1,17},{17,33},{33,49},{49,1},{2,18}... | collective-permute-start | bytes 393224 | tf_op jit(solution)/shard_map/ppermute | solution.py:342
  37.4 5.4 %collective-permute-start.9 = (bf16[3,1,128,128]{3,2,1,0:T(8,128)(2,1)S(1)}, bf16[3,1,128,128]{3,2,1,0:T(8,128)(2,1)S(1)}, u32[]{:S(2)}, u32[]{:S(2)}) collective-permute-start(bf16[3,1,128,128]{3,2,1,0:T(8,128)(2,1)S(1)} %get-tuple-element.54), channel_id=1, source_target_pairs={{0,1},{1,0},{2,3},{3,2},{4,5},{5,4},{6,7},{7,6},{8,9},{9,8},{10,11... | collective-permute-start | bytes 294920 | tf_op jit(solution)/shard_map/ppermute | solution.py:329
  37.5 6.9 %collective-permute-start.10 = (bf16[3,1,128,128]{3,2,1,0:T(8,128)(2,1)S(1)}, bf16[3,1,128,128]{3,2,1,0:T(8,128)(2,1)S(1)}, u32[]{:S(2)}, u32[]{:S(2)}) collective-permute-start(bf16[3,1,128,128]{3,2,1,0:T(8,128)(2,1)S(1)} %get-tuple-element.55), channel_id=1, source_target_pairs={{0,15},{1,2},{2,1},{3,4},{4,3},{5,6},{6,5},{7,8},{8,7},{9,10},{10,... | collective-permute-start | bytes 294920 | tf_op jit(solution)/shard_map/ppermute | solution.py:330
  41.8 10.4 %collective-permute-start.8 = (bf16[2,4,128,128]{3,2,1,0:T(8,128)(2,1)S(1)}, bf16[2,4,128,128]{3,2,1,0:T(8,128)(2,1)S(1)}, u32[]{:S(2)}, u32[]{:S(2)}) collective-permute-start(bf16[2,4,128,128]{3,2,1,0:T(8,128)(2,1)S(1)} %get-tuple-element.53), channel_id=1, source_target_pairs={{0,48},{16,0},{32,16},{48,32},{1,49},{17,1},{33,17},{49,33},{2,50}... | collective-permute-start | bytes 786440 | tf_op jit(solution)/shard_map/ppermute | solution.py:328
  44.4 7.8 %collective-permute-start.11 = (bf16[2,2,128,128]{3,2,1,0:T(8,128)(2,1)S(1)}, bf16[2,2,128,128]{3,2,1,0:T(8,128)(2,1)S(1)}, u32[]{:S(2)}, u32[]{:S(2)}) collective-permute-start(bf16[2,2,128,128]{3,2,1,0:T(8,128)(2,1)S(1)} %pad_maximum_fusion), channel_id=1, source_target_pairs={{0,48},{16,0},{32,16},{48,32},{1,49},{17,1},{33,17},{49,33},{2,50}... | collective-permute-start | bytes 393224 | tf_op jit(solution)/shard_map/ppermute | solution.py:342
  48.5 8.7 %collective-permute-start.16 = (bf16[4,28,16,128]{3,2,1,0:T(8,128)(2,1)S(1)}, bf16[4,28,16,128]{3,2,1,0:T(8,128)(2,1)S(1)}, u32[]{:S(2)}, u32[]{:S(2)}) collective-permute-start(bf16[4,28,16,128]{3,2,1,0:T(8,128)(2,1)S(1)} %get-tuple-element.64), channel_id=1, source_target_pairs={{0,16},{1,17},{2,18},{3,19},{4,20},{5,21},{6,22},{7,23},{8,24},{9,... | collective-permute-start | bytes 1376264 | tf_op jit(solution)/shard_map/ppermute | solution.py:264
  59.1 6.8 %collective-permute-start.19 = (bf16[4,7,16,128]{3,2,1,0:T(8,128)(2,1)S(1)}, bf16[4,7,16,128]{3,2,1,0:T(8,128)(2,1)S(1)}, u32[]{:S(2)}, u32[]{:S(2)}) collective-permute-start(bf16[4,7,16,128]{3,2,1,0:T(8,128)(2,1)S(1)} %get-tuple-element.72), channel_id=1, source_target_pairs={{0,1},{1,0},{2,3},{3,2},{4,5},{5,4},{6,7},{7,6},{8,9},{9,8},{10,11... | collective-permute-start | bytes 344072 | tf_op jit(solution)/shard_map/ppermute | solution.py:264
  59.2 6.7 %collective-permute-start.20 = (bf16[4,7,16,128]{3,2,1,0:T(8,128)(2,1)S(1)}, bf16[4,7,16,128]{3,2,1,0:T(8,128)(2,1)S(1)}, u32[]{:S(2)}, u32[]{:S(2)}) collective-permute-start(bf16[4,7,16,128]{3,2,1,0:T(8,128)(2,1)S(1)} %get-tuple-element.73), channel_id=1, source_target_pairs={{0,3},{1,2},{2,1},{3,0},{4,7},{5,6},{6,5},{7,4},{8,11},{9,10},{10,... | collective-permute-start | bytes 344072 | tf_op jit(solution)/shard_map/ppermute | solution.py:264
  59.3 6.8 %collective-permute-start.13 = (bf16[3,1,128,128]{3,2,1,0:T(8,128)(2,1)S(1)}, bf16[3,1,128,128]{3,2,1,0:T(8,128)(2,1)S(1)}, u32[]{:S(2)}, u32[]{:S(2)}) collective-permute-start(bf16[3,1,128,128]{3,2,1,0:T(8,128)(2,1)S(1)} %get-tuple-element.59), channel_id=1, source_target_pairs={{0,1},{1,0},{2,3},{3,2},{4,5},{5,4},{6,7},{7,6},{8,9},{9,8},{10,11... | collective-permute-start | bytes 294920 | tf_op jit(solution)/shard_map/ppermute | solution.py:329
  60.6 8.1 %collective-permute-start.14 = (bf16[3,1,128,128]{3,2,1,0:T(8,128)(2,1)S(1)}, bf16[3,1,128,128]{3,2,1,0:T(8,128)(2,1)S(1)}, u32[]{:S(2)}, u32[]{:S(2)}) collective-permute-start(bf16[3,1,128,128]{3,2,1,0:T(8,128)(2,1)S(1)} %get-tuple-element.60), channel_id=1, source_target_pairs={{0,15},{1,2},{2,1},{3,4},{4,3},{5,6},{6,5},{7,8},{8,7},{9,10},{10,... | collective-permute-start | bytes 294920 | tf_op jit(solution)/shard_map/ppermute | solution.py:330
  64.9 19.3 %collective-permute-start.12 = (bf16[2,4,128,128]{3,2,1,0:T(8,128)(2,1)S(1)}, bf16[2,4,128,128]{3,2,1,0:T(8,128)(2,1)S(1)}, u32[]{:S(2)}, u32[]{:S(2)}) collective-permute-start(bf16[2,4,128,128]{3,2,1,0:T(8,128)(2,1)S(1)} %get-tuple-element.58), channel_id=1, source_target_pairs={{0,48},{16,0},{32,16},{48,32},{1,49},{17,1},{33,17},{49,33},{2,50}... | collective-permute-start | bytes 786440 | tf_op jit(solution)/shard_map/ppermute | solution.py:328
  65.9 4.8 %collective-permute-start.18 = (bf16[4,7,16,128]{3,2,1,0:T(8,128)(2,1)S(1)}, bf16[4,7,16,128]{3,2,1,0:T(8,128)(2,1)S(1)}, u32[]{:S(2)}, u32[]{:S(2)}) collective-permute-start(bf16[4,7,16,128]{3,2,1,0:T(8,128)(2,1)S(1)} %get-tuple-element.69), channel_id=1, source_target_pairs={{0,1},{1,0},{2,3},{3,2},{4,5},{5,4},{6,7},{7,6},{8,9},{9,8},{10,11... | collective-permute-start | bytes 344072 | tf_op jit(solution)/shard_map/ppermute | solution.py:264
  65.9 5.6 %collective-permute-start.23 = (bf16[4,7,16,128]{3,2,1,0:T(8,128)(2,1)S(1)}, bf16[4,7,16,128]{3,2,1,0:T(8,128)(2,1)S(1)}, u32[]{:S(2)}, u32[]{:S(2)}) collective-permute-start(bf16[4,7,16,128]{3,2,1,0:T(8,128)(2,1)S(1)} %get-tuple-element.76), channel_id=1, source_target_pairs={{0,3},{1,2},{2,1},{3,0},{4,7},{5,6},{6,5},{7,4},{8,11},{9,10},{10,... | collective-permute-start | bytes 344072 | tf_op jit(solution)/shard_map/ppermute | solution.py:264
  66.0 7.7 %collective-permute-start.21 = (bf16[4,7,16,128]{3,2,1,0:T(8,128)(2,1)S(1)}, bf16[4,7,16,128]{3,2,1,0:T(8,128)(2,1)S(1)}, u32[]{:S(2)}, u32[]{:S(2)}) collective-permute-start(bf16[4,7,16,128]{3,2,1,0:T(8,128)(2,1)S(1)} %get-tuple-element.74), channel_id=1, source_target_pairs={{0,3},{1,2},{2,1},{3,0},{4,7},{5,6},{6,5},{7,4},{8,11},{9,10},{10,... | collective-permute-start | bytes 344072 | tf_op jit(solution)/shard_map/ppermute | solution.py:264
  68.8 4.9 %collective-permute-start.22 = (bf16[4,7,16,128]{3,2,1,0:T(8,128)(2,1)S(1)}, bf16[4,7,16,128]{3,2,1,0:T(8,128)(2,1)S(1)}, u32[]{:S(2)}, u32[]{:S(2)}) collective-permute-start(bf16[4,7,16,128]{3,2,1,0:T(8,128)(2,1)S(1)} %get-tuple-element.75), channel_id=1, source_target_pairs={{0,1},{1,0},{2,3},{3,2},{4,5},{5,4},{6,7},{7,6},{8,9},{9,8},{10,11... | collective-permute-start | bytes 344072 | tf_op jit(solution)/shard_map/ppermute | solution.py:264
  70.7 6.5 %collective-permute-start.17 = (bf16[2,2,128,128]{3,2,1,0:T(8,128)(2,1)S(1)}, bf16[2,2,128,128]{3,2,1,0:T(8,128)(2,1)S(1)}, u32[]{:S(2)}, u32[]{:S(2)}) collective-permute-start(bf16[2,2,128,128]{3,2,1,0:T(8,128)(2,1)S(1)} %shard_map.83), channel_id=1, source_target_pairs={{0,48},{16,0},{32,16},{48,32},{1,49},{17,1},{33,17},{49,33},{2,50}... | collective-permute-start | bytes 393224 | tf_op jit(solution)/shard_map/ppermute | solution.py:342
  76.3 4.7 %collective-permute-start.26 = (bf16[2,7,16,128]{3,2,1,0:T(8,128)(2,1)S(1)}, bf16[2,7,16,128]{3,2,1,0:T(8,128)(2,1)S(1)}, u32[]{:S(2)}, u32[]{:S(2)}) collective-permute-start(bf16[2,7,16,128]{3,2,1,0:T(8,128)(2,1)S(1)} %get-tuple-element.80), channel_id=1, source_target_pairs={{0,12},{1,13},{2,14},{3,15},{4,8},{5,9},{6,10},{7,11},{8,4},{9,5},... | collective-permute-start | bytes 172040 | tf_op jit(solution)/shard_map/ppermute | solution.py:264
  81.0 6.2 %collective-permute-start.29 = (bf16[2,7,16,128]{3,2,1,0:T(8,128)(2,1)S(1)}, bf16[2,7,16,128]{3,2,1,0:T(8,128)(2,1)S(1)}, u32[]{:S(2)}, u32[]{:S(2)}) collective-permute-start(bf16[2,7,16,128]{3,2,1,0:T(8,128)(2,1)S(1)} %shard_map.87.refs_0_), channel_id=1, source_target_pairs={{0,32},{1,33},{2,34},{3,35},{4,36},{5,37},{6,38},{7,39},{8,40},{9,... | collective-permute-start | bytes 172040 | tf_op jit(solution)/shard_map/ppermute | solution.py:264
  81.1 6.2 %collective-permute-start.28 = (bf16[2,7,16,128]{3,2,1,0:T(8,128)(2,1)S(1)}, bf16[2,7,16,128]{3,2,1,0:T(8,128)(2,1)S(1)}, u32[]{:S(2)}, u32[]{:S(2)}) collective-permute-start(bf16[2,7,16,128]{3,2,1,0:T(8,128)(2,1)S(1)} %shard_map.87.refs_0_), channel_id=1, source_target_pairs={{0,96},{1,97},{2,98},{3,99},{4,100},{5,101},{6,102},{7,103},{8,104... | collective-permute-start | bytes 172040 | tf_op jit(solution)/shard_map/ppermute | solution.py:264
  87.3 4.6 %collective-permute-start.32 = (bf16[2,7,16,128]{3,2,1,0:T(8,128)(2,1)S(1)}, bf16[2,7,16,128]{3,2,1,0:T(8,128)(2,1)S(1)}, u32[]{:S(2)}, u32[]{:S(2)}) collective-permute-start(bf16[2,7,16,128]{3,2,1,0:T(8,128)(2,1)S(1)} %shard_map.88.refs_0_), channel_id=1, source_target_pairs={{0,8},{1,9},{2,10},{3,11},{4,12},{5,13},{6,14},{7,15},{8,0},{9,1},... | collective-permute-start | bytes 172040 | tf_op jit(solution)/shard_map/ppermute | solution.py:264
  93.7 9.5 %collective-permute-start.35 = (bf16[2,4,7,16,128]{4,3,2,1,0:T(8,128)(2,1)S(1)}, bf16[2,4,7,16,128]{4,3,2,1,0:T(8,128)(2,1)S(1)}, u32[]{:S(2)}, u32[]{:S(2)}) collective-permute-start(bf16[2,4,7,16,128]{4,3,2,1,0:T(8,128)(2,1)S(1)} %shard_map.89.refs_0_), channel_id=1, source_target_pairs={{0,3},{1,2},{2,1},{3,0},{4,7},{5,6},{6,5},{7,4},{8,11},{9,10},{10,... | collective-permute-start | bytes 688136 | tf_op jit(solution)/shard_map/ppermute | solution.py:264
  95.6 13.2 %collective-permute-start.34 = (bf16[2,4,7,16,128]{4,3,2,1,0:T(8,128)(2,1)S(1)}, bf16[2,4,7,16,128]{4,3,2,1,0:T(8,128)(2,1)S(1)}, u32[]{:S(2)}, u32[]{:S(2)}) collective-permute-start(bf16[2,4,7,16,128]{4,3,2,1,0:T(8,128)(2,1)S(1)} %shard_map.89.refs_0_), channel_id=1, source_target_pairs={{0,2},{1,3},{2,0},{3,1},{4,6},{5,7},{6,4},{7,5},{8,10},{9,11},{10,... | collective-permute-start | bytes 688136 | tf_op jit(solution)/shard_map/ppermute | solution.py:264
  95.6 13.3 %collective-permute-start.33 = (bf16[2,4,7,16,128]{4,3,2,1,0:T(8,128)(2,1)S(1)}, bf16[2,4,7,16,128]{4,3,2,1,0:T(8,128)(2,1)S(1)}, u32[]{:S(2)}, u32[]{:S(2)}) collective-permute-start(bf16[2,4,7,16,128]{4,3,2,1,0:T(8,128)(2,1)S(1)} %shard_map.89.refs_0_), channel_id=1, source_target_pairs={{0,1},{1,0},{2,3},{3,2},{4,5},{5,4},{6,7},{7,6},{8,9},{9,8},{10,11... | collective-permute-start | bytes 688136 | tf_op jit(solution)/shard_map/ppermute | solution.py:264
  97.1 12.6 %collective-permute-start.36 = (bf16[2,4,7,16,128]{4,3,2,1,0:T(8,128)(2,1)S(1)}, bf16[2,4,7,16,128]{4,3,2,1,0:T(8,128)(2,1)S(1)}, u32[]{:S(2)}, u32[]{:S(2)}) collective-permute-start(bf16[2,4,7,16,128]{4,3,2,1,0:T(8,128)(2,1)S(1)} %shard_map.89.refs_0_), channel_id=1, source_target_pairs={{0,16},{1,17},{2,18},{3,19},{4,20},{5,21},{6,22},{7,23},{8,24},{9,... | collective-permute-start | bytes 688136 | tf_op jit(solution)/shard_map/ppermute | solution.py:264
  103.2 6.7 %collective-permute-start.39 = (bf16[2,4,7,16,128]{4,3,2,1,0:T(8,128)(2,1)S(1)}, bf16[2,4,7,16,128]{4,3,2,1,0:T(8,128)(2,1)S(1)}, u32[]{:S(2)}, u32[]{:S(2)}) collective-permute-start(bf16[2,4,7,16,128]{4,3,2,1,0:T(8,128)(2,1)S(1)} %collective-permute-done.35.refs_3_), channel_id=1, source_target_pairs={{0,16},{1,17},{2,18},{3,19},{4,20},{5,21},{6,22},{7,23},{8,24},{9,... | collective-permute-start | bytes 688136 | tf_op jit(solution)/shard_map/ppermute | solution.py:264
  (13 other events, 83.8 us)

commit v4 on v3

--- a/solution.py
+++ b/solution.py
@@ -155,20 +155,17 @@
     strips(grad, last, near_out, far_out, True)
 
 
-def back_kernel(centre, time, near, far, corners, kernel, made, grad, output, ended, pad, taps, held, sems):
-    frames, rows = centre.shape[:2]
-    made_copy = pltpu.make_async_copy(made, output, sems.at[frames])
-    made_copy.start()
+def back_kernel(centre, time, near, far, corners, kernel, made, output, grad, ended, pad, taps, sems):
+    copy = pltpu.make_async_copy(made, output, sems.at[0])
+    copy.start()
     lay(pad, centre, time, near, far, corners, True)
     lay_taps(taps, kernel, True)
+    frames, rows = centre.shape[:2]
     for t in range(frames):
         z = convolve(pad, taps, t, rows, True)
-        held[t] = z.astype(jnp.bfloat16).reshape(held.shape[1:])
-        pltpu.make_async_copy(held.at[t], grad.at[t], sems.at[t]).start()
+        grad[t] = z.astype(jnp.bfloat16).reshape(grad.shape[1:])
     ended[...] = jnp.zeros_like(ended)
-    made_copy.wait()
-    for t in range(frames):
-        pltpu.make_async_copy(held.at[t], grad.at[t], sems.at[t]).wait()
+    copy.wait()
 
 
 def back_slope_kernel(
@@ -242,10 +239,11 @@
 
 
 def gather_kernel(scale, *refs):
-    pieces, outs, (held, sems) = refs[:8], refs[8:10], refs[10:]
+    pieces, made, outs, clip_grad, (held, sems) = refs[:8], refs[8], refs[9:11], refs[11], refs[12:]
     x, core = lax.axis_index("height") % 4, lax.axis_index("tm") % 2
     taps = outs[0].shape[0]
-    copies = []
+    copies = [pltpu.make_async_copy(made, clip_grad, sems.at[8])]
+    copies[0].start()
     for k, out in enumerate(outs):
         for q in range(4):
             first, count = 7 * q, min(7, taps - 7 * q)
@@ -274,7 +272,7 @@
     return call(scatter_kernel, [f32, *4 * [bf16], later, later], [], 16 * math.prod(shape), *halves)
 
 
-def summed(quarters, scale, cornered, ended):
+def summed(quarters, scale, cornered, ended, made):
     mine, over_one, over_three, plain_one, plain_three, *later = quarters
     shape = mine.shape
     part, channels = shape[3:]
@@ -303,13 +301,14 @@
     out_shape = (27, 8, part, channels)
     outs = call(
         functools.partial(gather_kernel, scale),
-        [jax.ShapeDtypeStruct(out_shape, jnp.float32)] * 2,
-        [pltpu.VMEM((2, *out_shape), jnp.float32), pltpu.SemaphoreType.DMA((8,))],
+        [jax.ShapeDtypeStruct(out_shape, jnp.float32)] * 2 + [jax.ShapeDtypeStruct(made.shape, made.dtype)],
+        [pltpu.VMEM((2, *out_shape), jnp.float32), pltpu.SemaphoreType.DMA((9,))],
         8 * size,
         *pieces,
-        outside=(HBM, HBM),
-    )
-    return [out.reshape(3, 3, 3, channels, channels) for out in outs]
+        made,
+        outside=(HBM, HBM, HBM),
+    )
+    return [out.reshape(3, 3, 3, channels, channels) for out in outs[:2]] + list(outs[2:])
 
 
 def time_route(ahead):
@@ -359,7 +358,6 @@
     taps = pltpu.VMEM((9 * channels, 3 * channels), jnp.bfloat16)
     back_taps = pltpu.VMEM((3 * channels, 9 * channels), jnp.bfloat16)
     moved = pltpu.VMEM((cells, 3 * channels), jnp.bfloat16)
-    out = pltpu.VMEM(shape, jnp.bfloat16), pltpu.SemaphoreType.DMA((frames + 1,))
     scale = 1.0 / math.sqrt(cells * lax.axis_size(ALL))
 
     whole, *cut = call(
@@ -405,18 +403,18 @@
     quarters = started(first_terms, second_terms)
     one_edges = cornered(*one_edges, True, after=quarters[:1])
     ended = jax.ShapeDtypeStruct((8, 128), jnp.float32)
-    clip_grad, output, ended = call(
+    output, grad, ended = call(
         back_kernel,
         [bf16, bf16, ended],
-        [pad, back_taps, *out],
+        [pad, back_taps, pltpu.SemaphoreType.DMA((1,))],
         flops,
         grad_one,
         *one_edges,
         first_weight,
         made,
-        outside=(HBM, HBM),
-    )
-    first_grad, second_grad = summed(quarters, scale, one_edges[3:], (ended,))
+        outside=(HBM,),
+    )
+    first_grad, second_grad, clip_grad = summed(quarters, scale, one_edges[3:], (ended,), grad)
     return output[None], clip_grad[None], first_grad, second_grad
 
 

time: 113 us -> 113 us (level)
  transfers between devices with their start and end apart: 40 -> 40, of which waited for: 16 -> 17; matrix products, arithmetic and copies ran while one was open for 0% -> 0% of each run, Pallas kernels for 9% -> 9%
where the time goes in v4:
time: 113 us
  starting transfers between devices  71 us (63%)
  waiting for transfers between devices  21.6 us (19%)
  Pallas kernels  17.2 us (15%)
  local copies, waits for them, and re-layouts  2.17 us (2%)
    ppermute x24, starting transfers between devices, swap(): lax.ppermute(value, ALL, [(i, i ^ mask) for i in range(lax.axis_size(ALL))])  29.7 us
    pallas_call x16, Pallas kernels, call(): pl.pallas_call(run, out_shape=outs, in_specs=[inside] * len(args) + [ANY]...  17.2 us
    ppermute x4, starting transfers between devices, exchanged(): lax.ppermute(far, 'height', [(i, (i - 1 if i % 2 == 0 else i + 1) % line)...  17.2 us
    ppermute x24, waiting for transfers between devices, swap(): lax.ppermute(value, ALL, [(i, i ^ mask) for i in range(lax.axis_size(ALL))])  14.4 us
    ppermute x4, starting transfers between devices, exchanged(): time = lax.ppermute(last, 'tm', time_route(ahead))  10.9 us
    ppermute x4, starting transfers between devices, cornered(): return (time, near, far, lax.ppermute(rows, 'tm', time_route(ahead)))  9.55 us
    ppermute x4, waiting for transfers between devices, cornered(): return (time, near, far, lax.ppermute(rows, 'tm', time_route(ahead)))  5.54 us
    ppermute x4, starting transfers between devices, exchanged(): near = lax.ppermute(near, 'height', [(i, i ^ 1) for i in range(line)])  3.65 us
  transfers between devices with their start and end apart: 40, of which 17 were waited for; matrix products, arithmetic and copies ran while one was open for 0% of the time, Pallas kernels for 9%

profile of v4, /device:TPU:1, one launch (start us, length us, event | category | flops | bytes accessed | tf_op | source)
XLA Modules:
  0.0 113.0 jit_solution(8563625428204333779)
XLA Ops:
  2.0 2.1 %collective-permute-start.1 = (bf16[3,1,128,128]{3,2,1,0:T(8,128)(2,1)S(1)}, bf16[3,1,128,128]{3,2,1,0:T(8,128)(2,1)S(1)}, u32[]{:S(2)}, u32[]{:S(2)}) collective-permute-start(bf16[3,1,128,128]{3,2,1,0:T(8,128)(2,1)S(1)} %get-tuple-element.47), channel_id=1, source_target_pairs={{0,1},{1,0},{2,3},{3,2},{4,5},{5,4},{6,7},{7,6},{8,9},{9,8},{10,11... | collective-permute-start | bytes 294920 | tf_op jit(solution)/shard_map/ppermute | solution.py:328
  4.1 4.3 %collective-permute-start.2 = (bf16[3,1,128,128]{3,2,1,0:T(8,128)(2,1)S(1)}, bf16[3,1,128,128]{3,2,1,0:T(8,128)(2,1)S(1)}, u32[]{:S(2)}, u32[]{:S(2)}) collective-permute-start(bf16[3,1,128,128]{3,2,1,0:T(8,128)(2,1)S(1)} %get-tuple-element.48), channel_id=1, source_target_pairs={{0,15},{1,2},{2,1},{3,4},{4,3},{5,6},{6,5},{7,8},{8,7},{9,10},{10,... | collective-permute-start | bytes 294920 | tf_op jit(solution)/shard_map/ppermute | solution.py:329
  8.3 4.7 %collective-permute-start = (bf16[2,4,128,128]{3,2,1,0:T(8,128)(2,1)S(1)}, bf16[2,4,128,128]{3,2,1,0:T(8,128)(2,1)S(1)}, u32[]{:S(2)}, u32[]{:S(2)}) collective-permute-start(bf16[2,4,128,128]{3,2,1,0:T(8,128)(2,1)S(1)} %get-tuple-element.46), channel_id=1, source_target_pairs={{0,16},{16,32},{32,48},{48,0},{1,17},{17,33},{33,49},{49,1},{2,18}... | collective-permute-start | bytes 786440 | tf_op jit(solution)/shard_map/ppermute | solution.py:327
  13.1 3.5 %collective-permute-start.3 = (bf16[2,2,128,128]{3,2,1,0:T(8,128)(2,1)S(1)}, bf16[2,2,128,128]{3,2,1,0:T(8,128)(2,1)S(1)}, u32[]{:S(2)}, u32[]{:S(2)}) collective-permute-start(bf16[2,2,128,128]{3,2,1,0:T(8,128)(2,1)S(1)} %pad_maximum_fusion.2), channel_id=1, source_target_pairs={{0,16},{16,32},{32,48},{48,0},{1,17},{17,33},{33,49},{49,1},{2,18}... | collective-permute-start | bytes 393224 | tf_op jit(solution)/shard_map/ppermute | solution.py:341
  18.5 2.3 %shard_map.77 = (f32[3,4,128,128]{3,2,1,0:T(8,128)S(1)}, bf16[3,4,128,128]{3,2,1,0:T(8,128)(2,1)S(1)}, bf16[2,4,128,128]{3,2,1,0:T(8,128)(2,1)S(1)}, bf16[3,1,12...) custom-call(bf16[3,4,128,128]{3,2,1,0:T(8,128)(2,1)S(1)} %get-tuple-element.45.refs_0_, ...), custom_call_target="tpu_custom_call" | custom-call | flops 1358954496 | bytes 3506176 | tf_op jit(solution)/shard_map/pallas_call | solution.py:25
  20.9 4.3 %collective-permute-start.6 = (bf16[3,1,128,128]{3,2,1,0:T(8,128)(2,1)S(1)}, bf16[3,1,128,128]{3,2,1,0:T(8,128)(2,1)S(1)}, u32[]{:S(2)}, u32[]{:S(2)}) collective-permute-start(bf16[3,1,128,128]{3,2,1,0:T(8,128)(2,1)S(1)} %get-tuple-element.52), channel_id=1, source_target_pairs={{0,15},{1,2},{2,1},{3,4},{4,3},{5,6},{6,5},{7,8},{8,7},{9,10},{10,... | collective-permute-start | bytes 294920 | tf_op jit(solution)/shard_map/ppermute | solution.py:329
  25.3 4.2 %collective-permute-start.4 = (bf16[2,4,128,128]{3,2,1,0:T(8,128)(2,1)S(1)}, bf16[2,4,128,128]{3,2,1,0:T(8,128)(2,1)S(1)}, u32[]{:S(2)}, u32[]{:S(2)}) collective-permute-start(bf16[2,4,128,128]{3,2,1,0:T(8,128)(2,1)S(1)} %get-tuple-element.50), channel_id=1, source_target_pairs={{0,16},{16,32},{32,48},{48,0},{1,17},{17,33},{33,49},{49,1},{2,18}... | collective-permute-start | bytes 786440 | tf_op jit(solution)/shard_map/ppermute | solution.py:327
  29.5 3.5 %collective-permute-start.7 = (bf16[2,2,128,128]{3,2,1,0:T(8,128)(2,1)S(1)}, bf16[2,2,128,128]{3,2,1,0:T(8,128)(2,1)S(1)}, u32[]{:S(2)}, u32[]{:S(2)}) collective-permute-start(bf16[2,2,128,128]{3,2,1,0:T(8,128)(2,1)S(1)} %pad_maximum_fusion.1), channel_id=1, source_target_pairs={{0,16},{16,32},{32,48},{48,0},{1,17},{17,33},{33,49},{49,1},{2,18}... | collective-permute-start | bytes 393224 | tf_op jit(solution)/shard_map/ppermute | solution.py:341
  33.0 1.9 %collective-permute-done.7.refs_4_ = bf16[2,2,128,128]{3,2,1,0:T(8,128)(2,1)S(1)} collective-permute-done((bf16[2,2,128,128]{3,2,1,0:T(8,128)(2,1)S(1)}, bf16[2,2,128,128]{3,2,1,0:T(8,128)(2,1)S(1)}, u32[]{:S(2)}, u32[]{:S(2)}) %collective-permute-start.7) | collective-permute-done | bytes 131104 | tf_op jit(solution)/shard_map/ppermute | solution.py:341
  34.9 2.5 %shard_map.78 = (bf16[3,4,128,128]{3,2,1,0:T(8,128)(2,1)S(1)}, bf16[3,4,128,128]{3,2,1,0:T(8,128)(2,1)S(1)}, bf16[2,4,128,128]{3,2,1,0:T(8,128)(2,1)S(1)}, bf16[...) custom-call(bf16[3,4,128,128]{3,2,1,0:T(8,128)(2,1)S(1)} %get-tuple-element.49.refs_0_, ...), custom_call_target="tpu_custom_call" | custom-call | flops 1358954496 | bytes 3506176 | tf_op jit(solution)/shard_map/pallas_call | solution.py:25
  37.5 4.3 %collective-permute-start.10 = (bf16[3,1,128,128]{3,2,1,0:T(8,128)(2,1)S(1)}, bf16[3,1,128,128]{3,2,1,0:T(8,128)(2,1)S(1)}, u32[]{:S(2)}, u32[]{:S(2)}) collective-permute-start(bf16[3,1,128,128]{3,2,1,0:T(8,128)(2,1)S(1)} %get-tuple-element.56), channel_id=1, source_target_pairs={{0,15},{1,2},{2,1},{3,4},{4,3},{5,6},{6,5},{7,8},{8,7},{9,10},{10,... | collective-permute-start | bytes 294920 | tf_op jit(solution)/shard_map/ppermute | solution.py:329
  42.7 1.6 %collective-permute-done.10.refs_3_ = bf16[3,1,128,128]{3,2,1,0:T(8,128)(2,1)S(1)} collective-permute-done((bf16[3,1,128,128]{3,2,1,0:T(8,128)(2,1)S(1)}, bf16[3,1,128,128]{3,2,1,0:T(8,128)(2,1)S(1)}, u32[]{:S(2)}, u32[]{:S(2)}) %collective-permute-start.10) | collective-permute-done | bytes 98336 | tf_op jit(solution)/shard_map/ppermute | solution.py:329
  44.4 1.9 %collective-permute-start.11 = (bf16[2,2,128,128]{3,2,1,0:T(8,128)(2,1)S(1)}, bf16[2,2,128,128]{3,2,1,0:T(8,128)(2,1)S(1)}, u32[]{:S(2)}, u32[]{:S(2)}) collective-permute-start(bf16[2,2,128,128]{3,2,1,0:T(8,128)(2,1)S(1)} %pad_maximum_fusion), channel_id=1, source_target_pairs={{0,48},{16,0},{32,16},{48,32},{1,49},{17,1},{33,17},{49,33},{2,50}... | collective-permute-start | bytes 393224 | tf_op jit(solution)/shard_map/ppermute | solution.py:341
  46.2 2.3 %shard_map.81 = (f32[4,28,16,128]{3,2,1,0:T(8,128)S(1)}, bf16[4,28,16,128]{3,2,1,0:T(8,128)(2,1)S(1)}) custom-call(bf16[3,4,128,128]{3,2,1,0:T(8,128)(2,1)S(1)} %get-tuple-element.49.refs_0_, bf16[2,4,128,128]{3,2,1,0:T(8,128)(2,1)S(1)} %collective-permute-done.4.refs_1_, bf16[3,1,128,128]{3,2,1,0:T(8,128)(2,1)S(1)} %collective-permute-done.5.refs_2_, ...), custom_call_target="tpu_custom_call" | custom-call | flops 1358954496 | bytes 2752512 | tf_op jit(solution)/shard_map/pallas_call | solution.py:25
  49.0 3.1 %collective-permute-done.11.refs_4_ = bf16[2,2,128,128]{3,2,1,0:T(8,128)(2,1)S(1)} collective-permute-done((bf16[2,2,128,128]{3,2,1,0:T(8,128)(2,1)S(1)}, bf16[2,2,128,128]{3,2,1,0:T(8,128)(2,1)S(1)}, u32[]{:S(2)}, u32[]{:S(2)}) %collective-permute-start.11) | collective-permute-done | bytes 131104 | tf_op jit(solution)/shard_map/ppermute | solution.py:341
  52.2 2.6 %shard_map.79 = (bf16[3,4,128,128]{3,2,1,0:T(8,128)(2,1)S(1)}, bf16[2,4,128,128]{3,2,1,0:T(8,128)(2,1)S(1)}, bf16[3,1,128,128]{3,2,1,0:T(8,128)(2,1)S(1)}, bf16[3,1,128,128]{3,2,1,0:T(8,128)(2,1)S(1)}) custom-call(bf16[3,4,128,128]{3,2,1,0:T(8,128)(2,1)S(1)} %get-tuple-element.53.refs_0_.refs_5_, ...), custom_call_target="tpu_custom_call" | custom-call | flops 1358954496 | bytes 3506176 | tf_op jit(solution)/shard_map/pallas_call | solution.py:25
  54.8 2.3 %shard_map.80 = (f32[4,28,16,128]{3,2,1,0:T(8,128)S(1)}, bf16[4,28,16,128]{3,2,1,0:T(8,128)(2,1)S(1)}) custom-call(bf16[3,4,128,128]{3,2,1,0:T(8,128)(2,1)S(1)} %get-tuple-element.45.refs_0_, bf16[2,4,128,128]{3,2,1,0:T(8,128)(2,1)S(1)} %collective-permute-done.refs_1_, bf16[3,1,128,128]{3,2,1,0:T(8,128)(2,1)S(1)} %collective-permute-done.1.refs_2_, ...), custom_call_target="tpu_custom_call" | custom-call | flops 1358954496 | bytes 2752512 | tf_op jit(solution)/shard_map/pallas_call | solution.py:25
  57.1 1.8 %collective-permute-done.15.refs_1_ = bf16[4,28,16,128]{3,2,1,0:T(8,128)(2,1)S(1)} collective-permute-done((bf16[4,28,16,128]{3,2,1,0:T(8,128)(2,1)S(1)}, bf16[4,28,16,128]{3,2,1,0:T(8,128)(2,1)S(1)}, u32[]{:S(2)}, u32[]{:S(2)}) %collective-permute-start.15) | collective-permute-done | bytes 458784 | tf_op jit(solution)/shard_map/ppermute | solution.py:262
  60.6 4.2 %collective-permute-start.14 = (bf16[3,1,128,128]{3,2,1,0:T(8,128)(2,1)S(1)}, bf16[3,1,128,128]{3,2,1,0:T(8,128)(2,1)S(1)}, u32[]{:S(2)}, u32[]{:S(2)}) collective-permute-start(bf16[3,1,128,128]{3,2,1,0:T(8,128)(2,1)S(1)} %get-tuple-element.61), channel_id=1, source_target_pairs={{0,15},{1,2},{2,1},{3,4},{4,3},{5,6},{6,5},{7,8},{8,7},{9,10},{10,... | collective-permute-start | bytes 294920 | tf_op jit(solution)/shard_map/ppermute | solution.py:329
  66.0 2.7 %collective-permute-start.21 = (bf16[4,7,16,128]{3,2,1,0:T(8,128)(2,1)S(1)}, bf16[4,7,16,128]{3,2,1,0:T(8,128)(2,1)S(1)}, u32[]{:S(2)}, u32[]{:S(2)}) collective-permute-start(bf16[4,7,16,128]{3,2,1,0:T(8,128)(2,1)S(1)} %get-tuple-element.74), channel_id=1, source_target_pairs={{0,3},{1,2},{2,1},{3,0},{4,7},{5,6},{6,5},{7,4},{8,11},{9,10},{10,... | collective-permute-start | bytes 344072 | tf_op jit(solution)/shard_map/ppermute | solution.py:262
  69.0 1.7 %collective-permute-done.18.refs_1_ = bf16[4,7,16,128]{3,2,1,0:T(8,128)(2,1)S(1)} collective-permute-done((bf16[4,7,16,128]{3,2,1,0:T(8,128)(2,1)S(1)}, bf16[4,7,16,128]{3,2,1,0:T(8,128)(2,1)S(1)}, u32[]{:S(2)}, u32[]{:S(2)}) %collective-permute-start.18) | collective-permute-done | bytes 114720 | tf_op jit(solution)/shard_map/ppermute | solution.py:262
  71.4 2.3 %collective-permute-done.21.refs_2_ = bf16[4,7,16,128]{3,2,1,0:T(8,128)(2,1)S(1)} collective-permute-done((bf16[4,7,16,128]{3,2,1,0:T(8,128)(2,1)S(1)}, bf16[4,7,16,128]{3,2,1,0:T(8,128)(2,1)S(1)}, u32[]{:S(2)}, u32[]{:S(2)}) %collective-permute-start.21) | collective-permute-done | bytes 114720 | tf_op jit(solution)/shard_map/ppermute | solution.py:262
  73.8 2.4 %collective-permute-start.24 = (bf16[2,7,16,128]{3,2,1,0:T(8,128)(2,1)S(1)}, bf16[2,7,16,128]{3,2,1,0:T(8,128)(2,1)S(1)}, u32[]{:S(2)}, u32[]{:S(2)}) collective-permute-start(bf16[2,7,16,128]{3,2,1,0:T(8,128)(2,1)S(1)} %get-tuple-element.78), channel_id=1, source_target_pairs={{0,8},{1,9},{2,10},{3,11},{4,12},{5,13},{6,14},{7,15},{8,0},{9,1},... | collective-permute-start | bytes 172040 | tf_op jit(solution)/shard_map/ppermute | solution.py:262
  79.3 1.7 %collective-permute-done.26.refs_3_ = bf16[2,7,16,128]{3,2,1,0:T(8,128)(2,1)S(1)} collective-permute-done((bf16[2,7,16,128]{3,2,1,0:T(8,128)(2,1)S(1)}, bf16[2,7,16,128]{3,2,1,0:T(8,128)(2,1)S(1)}, u32[]{:S(2)}, u32[]{:S(2)}) %collective-permute-start.26) | collective-permute-done | bytes 57376 | tf_op jit(solution)/shard_map/ppermute | solution.py:262
  81.1 3.1 %collective-permute-start.28 = (bf16[2,7,16,128]{3,2,1,0:T(8,128)(2,1)S(1)}, bf16[2,7,16,128]{3,2,1,0:T(8,128)(2,1)S(1)}, u32[]{:S(2)}, u32[]{:S(2)}) collective-permute-start(bf16[2,7,16,128]{3,2,1,0:T(8,128)(2,1)S(1)} %shard_map.87.refs_0_), channel_id=1, source_target_pairs={{0,96},{1,97},{2,98},{3,99},{4,100},{5,101},{6,102},{7,103},{8,104... | collective-permute-start | bytes 172040 | tf_op jit(solution)/shard_map/ppermute | solution.py:262
  84.2 2.3 %shard_map.84 = (bf16[3,4,128,128]{3,2,1,0:T(8,128)(2,1)}, bf16[3,4,128,128]{3,2,1,0:T(8,128)(2,1)S(1)}, f32[8,128]{1,0:T(8,128)S(1)}) custom-call(bf16[3,4,128,128]{3,2,1,0:T(8,128)(2,1)S(1)} %get-tuple-element.58.refs_5_.refs_0_, bf16[2,4,128,128]{3,2,1,0:T(8,128)(2,1)S(1)} %collective-permute-done.12.refs_1_, ...), custom_call_target="tpu_custom_call" | custom-call | flops 1358954496 | bytes 3051520 | tf_op jit(solution)/shard_map/pallas_call | solution.py:25
  88.1 2.6 %collective-permute-start.31 = (bf16[2,7,16,128]{3,2,1,0:T(8,128)(2,1)S(1)}, bf16[2,7,16,128]{3,2,1,0:T(8,128)(2,1)S(1)}, u32[]{:S(2)}, u32[]{:S(2)}) collective-permute-start(bf16[2,7,16,128]{3,2,1,0:T(8,128)(2,1)S(1)} %shard_map.88.refs_0_), channel_id=1, source_target_pairs={{0,12},{1,13},{2,14},{3,15},{4,8},{5,9},{6,10},{7,11},{8,4},{9,5},... | collective-permute-start | bytes 172040 | tf_op jit(solution)/shard_map/ppermute | solution.py:262
  93.7 1.8 %collective-permute-start.35 = (bf16[2,4,7,16,128]{4,3,2,1,0:T(8,128)(2,1)S(1)}, bf16[2,4,7,16,128]{4,3,2,1,0:T(8,128)(2,1)S(1)}, u32[]{:S(2)}, u32[]{:S(2)}) collective-permute-start(bf16[2,4,7,16,128]{4,3,2,1,0:T(8,128)(2,1)S(1)} %shard_map.89.refs_0_), channel_id=1, source_target_pairs={{0,3},{1,2},{2,1},{3,0},{4,7},{5,6},{6,5},{7,4},{8,11},{9,10},{10,... | collective-permute-start | bytes 688136 | tf_op jit(solution)/shard_map/ppermute | solution.py:262
  95.6 1.5 %collective-permute-start.33 = (bf16[2,4,7,16,128]{4,3,2,1,0:T(8,128)(2,1)S(1)}, bf16[2,4,7,16,128]{4,3,2,1,0:T(8,128)(2,1)S(1)}, u32[]{:S(2)}, u32[]{:S(2)}) collective-permute-start(bf16[2,4,7,16,128]{4,3,2,1,0:T(8,128)(2,1)S(1)} %shard_map.89.refs_0_), channel_id=1, source_target_pairs={{0,1},{1,0},{2,3},{3,2},{4,5},{5,4},{6,7},{7,6},{8,9},{9,8},{10,11... | collective-permute-start | bytes 688136 | tf_op jit(solution)/shard_map/ppermute | solution.py:262
  97.1 6.1 %collective-permute-start.36 = (bf16[2,4,7,16,128]{4,3,2,1,0:T(8,128)(2,1)S(1)}, bf16[2,4,7,16,128]{4,3,2,1,0:T(8,128)(2,1)S(1)}, u32[]{:S(2)}, u32[]{:S(2)}) collective-permute-start(bf16[2,4,7,16,128]{4,3,2,1,0:T(8,128)(2,1)S(1)} %shard_map.89.refs_0_), channel_id=1, source_target_pairs={{0,16},{1,17},{2,18},{3,19},{4,20},{5,21},{6,22},{7,23},{8,24},{9,... | collective-permute-start | bytes 688136 | tf_op jit(solution)/shard_map/ppermute | solution.py:262
  103.2 5.6 %collective-permute-start.39 = (bf16[2,4,7,16,128]{4,3,2,1,0:T(8,128)(2,1)S(1)}, bf16[2,4,7,16,128]{4,3,2,1,0:T(8,128)(2,1)S(1)}, u32[]{:S(2)}, u32[]{:S(2)}) collective-permute-start(bf16[2,4,7,16,128]{4,3,2,1,0:T(8,128)(2,1)S(1)} %collective-permute-done.35.refs_3_), channel_id=1, source_target_pairs={{0,16},{1,17},{2,18},{3,19},{4,20},{5,21},{6,22},{7,23},{8,24},{9,... | collective-permute-start | bytes 688136 | tf_op jit(solution)/shard_map/ppermute | solution.py:262
  110.8 2.0 %shard_map.90 = (f32[27,8,16,128]{3,2,1,0:T(8,128)}, f32[27,8,16,128]{3,2,1,0:T(8,128)}, bf16[3,4,128,128]{3,2,1,0:T(8,128)(2,1)}) custom-call(bf16[2,4,7,16,128]{4,3,2,1,0:T(8,128)(2,1)S(1)} %shard_map.89.refs_0_, bf16[2,4,7,16,128]{4,3,2,1,0:T(8,128)(2,1)S(1)} %collective-permute-done.33.refs_1_, ...), custom_call_target="tpu_custom_call" | custom-call | flops 917504 | bytes 6160384 | tf_op jit(solution)/shard_map/pallas_call | solution.py:25
  (77 shorter events, 18.6 us)
Async XLA Ops:
  2.0 11.1 %collective-permute-start.1 = (bf16[3,1,128,128]{3,2,1,0:T(8,128)(2,1)S(1)}, bf16[3,1,128,128]{3,2,1,0:T(8,128)(2,1)S(1)}, u32[]{:S(2)}, u32[]{:S(2)}) collective-permute-start(bf16[3,1,128,128]{3,2,1,0:T(8,128)(2,1)S(1)} %get-tuple-element.47), channel_id=1, source_target_pairs={{0,1},{1,0},{2,3},{3,2},{4,5},{5,4},{6,7},{7,6},{8,9},{9,8},{10,11... | collective-permute-start | bytes 294920 | tf_op jit(solution)/shard_map/ppermute | solution.py:328
  4.1 9.0 %collective-permute-start.2 = (bf16[3,1,128,128]{3,2,1,0:T(8,128)(2,1)S(1)}, bf16[3,1,128,128]{3,2,1,0:T(8,128)(2,1)S(1)}, u32[]{:S(2)}, u32[]{:S(2)}) collective-permute-start(bf16[3,1,128,128]{3,2,1,0:T(8,128)(2,1)S(1)} %get-tuple-element.48), channel_id=1, source_target_pairs={{0,15},{1,2},{2,1},{3,4},{4,3},{5,6},{6,5},{7,8},{8,7},{9,10},{10,... | collective-permute-start | bytes 294920 | tf_op jit(solution)/shard_map/ppermute | solution.py:329
  8.3 10.1 %collective-permute-start = (bf16[2,4,128,128]{3,2,1,0:T(8,128)(2,1)S(1)}, bf16[2,4,128,128]{3,2,1,0:T(8,128)(2,1)S(1)}, u32[]{:S(2)}, u32[]{:S(2)}) collective-permute-start(bf16[2,4,128,128]{3,2,1,0:T(8,128)(2,1)S(1)} %get-tuple-element.46), channel_id=1, source_target_pairs={{0,16},{16,32},{32,48},{48,0},{1,17},{17,33},{33,49},{49,1},{2,18}... | collective-permute-start | bytes 786440 | tf_op jit(solution)/shard_map/ppermute | solution.py:327
  13.1 5.4 %collective-permute-start.3 = (bf16[2,2,128,128]{3,2,1,0:T(8,128)(2,1)S(1)}, bf16[2,2,128,128]{3,2,1,0:T(8,128)(2,1)S(1)}, u32[]{:S(2)}, u32[]{:S(2)}) collective-permute-start(bf16[2,2,128,128]{3,2,1,0:T(8,128)(2,1)S(1)} %pad_maximum_fusion.2), channel_id=1, source_target_pairs={{0,16},{16,32},{32,48},{48,0},{1,17},{17,33},{33,49},{49,1},{2,18}... | collective-permute-start | bytes 393224 | tf_op jit(solution)/shard_map/ppermute | solution.py:341
  20.8 8.7 %collective-permute-start.5 = (bf16[3,1,128,128]{3,2,1,0:T(8,128)(2,1)S(1)}, bf16[3,1,128,128]{3,2,1,0:T(8,128)(2,1)S(1)}, u32[]{:S(2)}, u32[]{:S(2)}) collective-permute-start(bf16[3,1,128,128]{3,2,1,0:T(8,128)(2,1)S(1)} %get-tuple-element.51), channel_id=1, source_target_pairs={{0,1},{1,0},{2,3},{3,2},{4,5},{5,4},{6,7},{7,6},{8,9},{9,8},{10,11... | collective-permute-start | bytes 294920 | tf_op jit(solution)/shard_map/ppermute | solution.py:328
  20.9 8.6 %collective-permute-start.6 = (bf16[3,1,128,128]{3,2,1,0:T(8,128)(2,1)S(1)}, bf16[3,1,128,128]{3,2,1,0:T(8,128)(2,1)S(1)}, u32[]{:S(2)}, u32[]{:S(2)}) collective-permute-start(bf16[3,1,128,128]{3,2,1,0:T(8,128)(2,1)S(1)} %get-tuple-element.52), channel_id=1, source_target_pairs={{0,15},{1,2},{2,1},{3,4},{4,3},{5,6},{6,5},{7,8},{8,7},{9,10},{10,... | collective-permute-start | bytes 294920 | tf_op jit(solution)/shard_map/ppermute | solution.py:329
  25.3 9.7 %collective-permute-start.4 = (bf16[2,4,128,128]{3,2,1,0:T(8,128)(2,1)S(1)}, bf16[2,4,128,128]{3,2,1,0:T(8,128)(2,1)S(1)}, u32[]{:S(2)}, u32[]{:S(2)}) collective-permute-start(bf16[2,4,128,128]{3,2,1,0:T(8,128)(2,1)S(1)} %get-tuple-element.50), channel_id=1, source_target_pairs={{0,16},{16,32},{32,48},{48,0},{1,17},{17,33},{33,49},{49,1},{2,18}... | collective-permute-start | bytes 786440 | tf_op jit(solution)/shard_map/ppermute | solution.py:327
  29.5 5.4 %collective-permute-start.7 = (bf16[2,2,128,128]{3,2,1,0:T(8,128)(2,1)S(1)}, bf16[2,2,128,128]{3,2,1,0:T(8,128)(2,1)S(1)}, u32[]{:S(2)}, u32[]{:S(2)}) collective-permute-start(bf16[2,2,128,128]{3,2,1,0:T(8,128)(2,1)S(1)} %pad_maximum_fusion.1), channel_id=1, source_target_pairs={{0,16},{16,32},{32,48},{48,0},{1,17},{17,33},{33,49},{49,1},{2,18}... | collective-permute-start | bytes 393224 | tf_op jit(solution)/shard_map/ppermute | solution.py:341
  37.4 5.4 %collective-permute-start.9 = (bf16[3,1,128,128]{3,2,1,0:T(8,128)(2,1)S(1)}, bf16[3,1,128,128]{3,2,1,0:T(8,128)(2,1)S(1)}, u32[]{:S(2)}, u32[]{:S(2)}) collective-permute-start(bf16[3,1,128,128]{3,2,1,0:T(8,128)(2,1)S(1)} %get-tuple-element.55), channel_id=1, source_target_pairs={{0,1},{1,0},{2,3},{3,2},{4,5},{5,4},{6,7},{7,6},{8,9},{9,8},{10,11... | collective-permute-start | bytes 294920 | tf_op jit(solution)/shard_map/ppermute | solution.py:328
  37.5 6.9 %collective-permute-start.10 = (bf16[3,1,128,128]{3,2,1,0:T(8,128)(2,1)S(1)}, bf16[3,1,128,128]{3,2,1,0:T(8,128)(2,1)S(1)}, u32[]{:S(2)}, u32[]{:S(2)}) collective-permute-start(bf16[3,1,128,128]{3,2,1,0:T(8,128)(2,1)S(1)} %get-tuple-element.56), channel_id=1, source_target_pairs={{0,15},{1,2},{2,1},{3,4},{4,3},{5,6},{6,5},{7,8},{8,7},{9,10},{10,... | collective-permute-start | bytes 294920 | tf_op jit(solution)/shard_map/ppermute | solution.py:329
  41.8 10.4 %collective-permute-start.8 = (bf16[2,4,128,128]{3,2,1,0:T(8,128)(2,1)S(1)}, bf16[2,4,128,128]{3,2,1,0:T(8,128)(2,1)S(1)}, u32[]{:S(2)}, u32[]{:S(2)}) collective-permute-start(bf16[2,4,128,128]{3,2,1,0:T(8,128)(2,1)S(1)} %get-tuple-element.54), channel_id=1, source_target_pairs={{0,48},{16,0},{32,16},{48,32},{1,49},{17,1},{33,17},{49,33},{2,50}... | collective-permute-start | bytes 786440 | tf_op jit(solution)/shard_map/ppermute | solution.py:327
  44.4 7.8 %collective-permute-start.11 = (bf16[2,2,128,128]{3,2,1,0:T(8,128)(2,1)S(1)}, bf16[2,2,128,128]{3,2,1,0:T(8,128)(2,1)S(1)}, u32[]{:S(2)}, u32[]{:S(2)}) collective-permute-start(bf16[2,2,128,128]{3,2,1,0:T(8,128)(2,1)S(1)} %pad_maximum_fusion), channel_id=1, source_target_pairs={{0,48},{16,0},{32,16},{48,32},{1,49},{17,1},{33,17},{49,33},{2,50}... | collective-permute-start | bytes 393224 | tf_op jit(solution)/shard_map/ppermute | solution.py:341
  48.5 8.7 %collective-permute-start.16 = (bf16[4,28,16,128]{3,2,1,0:T(8,128)(2,1)S(1)}, bf16[4,28,16,128]{3,2,1,0:T(8,128)(2,1)S(1)}, u32[]{:S(2)}, u32[]{:S(2)}) collective-permute-start(bf16[4,28,16,128]{3,2,1,0:T(8,128)(2,1)S(1)} %get-tuple-element.65), channel_id=1, source_target_pairs={{0,16},{1,17},{2,18},{3,19},{4,20},{5,21},{6,22},{7,23},{8,24},{9,... | collective-permute-start | bytes 1376264 | tf_op jit(solution)/shard_map/ppermute | solution.py:262
  59.1 6.8 %collective-permute-start.19 = (bf16[4,7,16,128]{3,2,1,0:T(8,128)(2,1)S(1)}, bf16[4,7,16,128]{3,2,1,0:T(8,128)(2,1)S(1)}, u32[]{:S(2)}, u32[]{:S(2)}) collective-permute-start(bf16[4,7,16,128]{3,2,1,0:T(8,128)(2,1)S(1)} %get-tuple-element.72), channel_id=1, source_target_pairs={{0,1},{1,0},{2,3},{3,2},{4,5},{5,4},{6,7},{7,6},{8,9},{9,8},{10,11... | collective-permute-start | bytes 344072 | tf_op jit(solution)/shard_map/ppermute | solution.py:262
  59.2 6.7 %collective-permute-start.20 = (bf16[4,7,16,128]{3,2,1,0:T(8,128)(2,1)S(1)}, bf16[4,7,16,128]{3,2,1,0:T(8,128)(2,1)S(1)}, u32[]{:S(2)}, u32[]{:S(2)}) collective-permute-start(bf16[4,7,16,128]{3,2,1,0:T(8,128)(2,1)S(1)} %get-tuple-element.73), channel_id=1, source_target_pairs={{0,3},{1,2},{2,1},{3,0},{4,7},{5,6},{6,5},{7,4},{8,11},{9,10},{10,... | collective-permute-start | bytes 344072 | tf_op jit(solution)/shard_map/ppermute | solution.py:262
  59.3 6.8 %collective-permute-start.13 = (bf16[3,1,128,128]{3,2,1,0:T(8,128)(2,1)S(1)}, bf16[3,1,128,128]{3,2,1,0:T(8,128)(2,1)S(1)}, u32[]{:S(2)}, u32[]{:S(2)}) collective-permute-start(bf16[3,1,128,128]{3,2,1,0:T(8,128)(2,1)S(1)} %get-tuple-element.60), channel_id=1, source_target_pairs={{0,1},{1,0},{2,3},{3,2},{4,5},{5,4},{6,7},{7,6},{8,9},{9,8},{10,11... | collective-permute-start | bytes 294920 | tf_op jit(solution)/shard_map/ppermute | solution.py:328
  60.6 8.1 %collective-permute-start.14 = (bf16[3,1,128,128]{3,2,1,0:T(8,128)(2,1)S(1)}, bf16[3,1,128,128]{3,2,1,0:T(8,128)(2,1)S(1)}, u32[]{:S(2)}, u32[]{:S(2)}) collective-permute-start(bf16[3,1,128,128]{3,2,1,0:T(8,128)(2,1)S(1)} %get-tuple-element.61), channel_id=1, source_target_pairs={{0,15},{1,2},{2,1},{3,4},{4,3},{5,6},{6,5},{7,8},{8,7},{9,10},{10,... | collective-permute-start | bytes 294920 | tf_op jit(solution)/shard_map/ppermute | solution.py:329
  64.9 19.3 %collective-permute-start.12 = (bf16[2,4,128,128]{3,2,1,0:T(8,128)(2,1)S(1)}, bf16[2,4,128,128]{3,2,1,0:T(8,128)(2,1)S(1)}, u32[]{:S(2)}, u32[]{:S(2)}) collective-permute-start(bf16[2,4,128,128]{3,2,1,0:T(8,128)(2,1)S(1)} %get-tuple-element.59), channel_id=1, source_target_pairs={{0,48},{16,0},{32,16},{48,32},{1,49},{17,1},{33,17},{49,33},{2,50}... | collective-permute-start | bytes 786440 | tf_op jit(solution)/shard_map/ppermute | solution.py:327
  65.9 4.8 %collective-permute-start.18 = (bf16[4,7,16,128]{3,2,1,0:T(8,128)(2,1)S(1)}, bf16[4,7,16,128]{3,2,1,0:T(8,128)(2,1)S(1)}, u32[]{:S(2)}, u32[]{:S(2)}) collective-permute-start(bf16[4,7,16,128]{3,2,1,0:T(8,128)(2,1)S(1)} %get-tuple-element.69), channel_id=1, source_target_pairs={{0,1},{1,0},{2,3},{3,2},{4,5},{5,4},{6,7},{7,6},{8,9},{9,8},{10,11... | collective-permute-start | bytes 344072 | tf_op jit(solution)/shard_map/ppermute | solution.py:262
  65.9 5.6 %collective-permute-start.23 = (bf16[4,7,16,128]{3,2,1,0:T(8,128)(2,1)S(1)}, bf16[4,7,16,128]{3,2,1,0:T(8,128)(2,1)S(1)}, u32[]{:S(2)}, u32[]{:S(2)}) collective-permute-start(bf16[4,7,16,128]{3,2,1,0:T(8,128)(2,1)S(1)} %get-tuple-element.76), channel_id=1, source_target_pairs={{0,3},{1,2},{2,1},{3,0},{4,7},{5,6},{6,5},{7,4},{8,11},{9,10},{10,... | collective-permute-start | bytes 344072 | tf_op jit(solution)/shard_map/ppermute | solution.py:262
  66.0 7.7 %collective-permute-start.21 = (bf16[4,7,16,128]{3,2,1,0:T(8,128)(2,1)S(1)}, bf16[4,7,16,128]{3,2,1,0:T(8,128)(2,1)S(1)}, u32[]{:S(2)}, u32[]{:S(2)}) collective-permute-start(bf16[4,7,16,128]{3,2,1,0:T(8,128)(2,1)S(1)} %get-tuple-element.74), channel_id=1, source_target_pairs={{0,3},{1,2},{2,1},{3,0},{4,7},{5,6},{6,5},{7,4},{8,11},{9,10},{10,... | collective-permute-start | bytes 344072 | tf_op jit(solution)/shard_map/ppermute | solution.py:262
  68.8 4.9 %collective-permute-start.22 = (bf16[4,7,16,128]{3,2,1,0:T(8,128)(2,1)S(1)}, bf16[4,7,16,128]{3,2,1,0:T(8,128)(2,1)S(1)}, u32[]{:S(2)}, u32[]{:S(2)}) collective-permute-start(bf16[4,7,16,128]{3,2,1,0:T(8,128)(2,1)S(1)} %get-tuple-element.75), channel_id=1, source_target_pairs={{0,1},{1,0},{2,3},{3,2},{4,5},{5,4},{6,7},{7,6},{8,9},{9,8},{10,11... | collective-permute-start | bytes 344072 | tf_op jit(solution)/shard_map/ppermute | solution.py:262
  70.7 6.5 %collective-permute-start.17 = (bf16[2,2,128,128]{3,2,1,0:T(8,128)(2,1)S(1)}, bf16[2,2,128,128]{3,2,1,0:T(8,128)(2,1)S(1)}, u32[]{:S(2)}, u32[]{:S(2)}) collective-permute-start(bf16[2,2,128,128]{3,2,1,0:T(8,128)(2,1)S(1)} %shard_map.83), channel_id=1, source_target_pairs={{0,48},{16,0},{32,16},{48,32},{1,49},{17,1},{33,17},{49,33},{2,50}... | collective-permute-start | bytes 393224 | tf_op jit(solution)/shard_map/ppermute | solution.py:341
  76.3 4.7 %collective-permute-start.26 = (bf16[2,7,16,128]{3,2,1,0:T(8,128)(2,1)S(1)}, bf16[2,7,16,128]{3,2,1,0:T(8,128)(2,1)S(1)}, u32[]{:S(2)}, u32[]{:S(2)}) collective-permute-start(bf16[2,7,16,128]{3,2,1,0:T(8,128)(2,1)S(1)} %get-tuple-element.80), channel_id=1, source_target_pairs={{0,12},{1,13},{2,14},{3,15},{4,8},{5,9},{6,10},{7,11},{8,4},{9,5},... | collective-permute-start | bytes 172040 | tf_op jit(solution)/shard_map/ppermute | solution.py:262
  81.0 5.6 %collective-permute-start.29 = (bf16[2,7,16,128]{3,2,1,0:T(8,128)(2,1)S(1)}, bf16[2,7,16,128]{3,2,1,0:T(8,128)(2,1)S(1)}, u32[]{:S(2)}, u32[]{:S(2)}) collective-permute-start(bf16[2,7,16,128]{3,2,1,0:T(8,128)(2,1)S(1)} %shard_map.87.refs_0_), channel_id=1, source_target_pairs={{0,32},{1,33},{2,34},{3,35},{4,36},{5,37},{6,38},{7,39},{8,40},{9,... | collective-permute-start | bytes 172040 | tf_op jit(solution)/shard_map/ppermute | solution.py:262
  81.1 5.5 %collective-permute-start.28 = (bf16[2,7,16,128]{3,2,1,0:T(8,128)(2,1)S(1)}, bf16[2,7,16,128]{3,2,1,0:T(8,128)(2,1)S(1)}, u32[]{:S(2)}, u32[]{:S(2)}) collective-permute-start(bf16[2,7,16,128]{3,2,1,0:T(8,128)(2,1)S(1)} %shard_map.87.refs_0_), channel_id=1, source_target_pairs={{0,96},{1,97},{2,98},{3,99},{4,100},{5,101},{6,102},{7,103},{8,104... | collective-permute-start | bytes 172040 | tf_op jit(solution)/shard_map/ppermute | solution.py:262
  87.3 4.6 %collective-permute-start.32 = (bf16[2,7,16,128]{3,2,1,0:T(8,128)(2,1)S(1)}, bf16[2,7,16,128]{3,2,1,0:T(8,128)(2,1)S(1)}, u32[]{:S(2)}, u32[]{:S(2)}) collective-permute-start(bf16[2,7,16,128]{3,2,1,0:T(8,128)(2,1)S(1)} %shard_map.88.refs_0_), channel_id=1, source_target_pairs={{0,8},{1,9},{2,10},{3,11},{4,12},{5,13},{6,14},{7,15},{8,0},{9,1},... | collective-permute-start | bytes 172040 | tf_op jit(solution)/shard_map/ppermute | solution.py:262
  93.7 9.5 %collective-permute-start.35 = (bf16[2,4,7,16,128]{4,3,2,1,0:T(8,128)(2,1)S(1)}, bf16[2,4,7,16,128]{4,3,2,1,0:T(8,128)(2,1)S(1)}, u32[]{:S(2)}, u32[]{:S(2)}) collective-permute-start(bf16[2,4,7,16,128]{4,3,2,1,0:T(8,128)(2,1)S(1)} %shard_map.89.refs_0_), channel_id=1, source_target_pairs={{0,3},{1,2},{2,1},{3,0},{4,7},{5,6},{6,5},{7,4},{8,11},{9,10},{10,... | collective-permute-start | bytes 688136 | tf_op jit(solution)/shard_map/ppermute | solution.py:262
  95.6 13.2 %collective-permute-start.34 = (bf16[2,4,7,16,128]{4,3,2,1,0:T(8,128)(2,1)S(1)}, bf16[2,4,7,16,128]{4,3,2,1,0:T(8,128)(2,1)S(1)}, u32[]{:S(2)}, u32[]{:S(2)}) collective-permute-start(bf16[2,4,7,16,128]{4,3,2,1,0:T(8,128)(2,1)S(1)} %shard_map.89.refs_0_), channel_id=1, source_target_pairs={{0,2},{1,3},{2,0},{3,1},{4,6},{5,7},{6,4},{7,5},{8,10},{9,11},{10,... | collective-permute-start | bytes 688136 | tf_op jit(solution)/shard_map/ppermute | solution.py:262
  95.6 13.3 %collective-permute-start.33 = (bf16[2,4,7,16,128]{4,3,2,1,0:T(8,128)(2,1)S(1)}, bf16[2,4,7,16,128]{4,3,2,1,0:T(8,128)(2,1)S(1)}, u32[]{:S(2)}, u32[]{:S(2)}) collective-permute-start(bf16[2,4,7,16,128]{4,3,2,1,0:T(8,128)(2,1)S(1)} %shard_map.89.refs_0_), channel_id=1, source_target_pairs={{0,1},{1,0},{2,3},{3,2},{4,5},{5,4},{6,7},{7,6},{8,9},{9,8},{10,11... | collective-permute-start | bytes 688136 | tf_op jit(solution)/shard_map/ppermute | solution.py:262
  97.1 12.6 %collective-permute-start.36 = (bf16[2,4,7,16,128]{4,3,2,1,0:T(8,128)(2,1)S(1)}, bf16[2,4,7,16,128]{4,3,2,1,0:T(8,128)(2,1)S(1)}, u32[]{:S(2)}, u32[]{:S(2)}) collective-permute-start(bf16[2,4,7,16,128]{4,3,2,1,0:T(8,128)(2,1)S(1)} %shard_map.89.refs_0_), channel_id=1, source_target_pairs={{0,16},{1,17},{2,18},{3,19},{4,20},{5,21},{6,22},{7,23},{8,24},{9,... | collective-permute-start | bytes 688136 | tf_op jit(solution)/shard_map/ppermute | solution.py:262
  103.2 6.7 %collective-permute-start.39 = (bf16[2,4,7,16,128]{4,3,2,1,0:T(8,128)(2,1)S(1)}, bf16[2,4,7,16,128]{4,3,2,1,0:T(8,128)(2,1)S(1)}, u32[]{:S(2)}, u32[]{:S(2)}) collective-permute-start(bf16[2,4,7,16,128]{4,3,2,1,0:T(8,128)(2,1)S(1)} %collective-permute-done.35.refs_3_), channel_id=1, source_target_pairs={{0,16},{1,17},{2,18},{3,19},{4,20},{5,21},{6,22},{7,23},{8,24},{9,... | collective-permute-start | bytes 688136 | tf_op jit(solution)/shard_map/ppermute | solution.py:262
  (13 other events, 83.7 us)

commit v5 on v4

--- a/solution.py
+++ b/solution.py
@@ -104,11 +104,11 @@
     return jnp.where(row == columns - 1, 0.0, pltpu.roll(value, value.shape[0] - 1, 0))
 
 
-def convolve(pad, taps, frame, rows, transposed):
+def convolve(pad, taps, frame, row, rows, transposed):
     columns, channels = pad.shape[2:]
     parts = []
     for a, b in TAPS:
-        t, h = (frame + 2 - a, 2 - b) if transposed else (frame + a, b)
+        t, h = (frame + 2 - a, row + 2 - b) if transposed else (frame + a, row + b)
         parts.append(pad[t, h : h + rows].reshape(rows * columns, channels))
     stacked = jnp.concatenate(parts, axis=1)
     dims = (((1,), (1 if transposed else 0,)), ((), ()))
@@ -129,14 +129,18 @@
                 taps[place * c_in : (place + 1) * c_in, c * c_out : (c + 1) * c_out] = kernel[a, b, c]
 
 
+def blocks(frames, rows):
+    return [(t, slice(h, h + 2)) for t in range(frames) for h in range(0, rows, 2)]
+
+
 def first_kernel(centre, time, near, far, corners, taps, slope, hidden, last, near_out, far_out, pad):
     lay(pad, centre, time, near, far, corners, False)
     frames, rows = centre.shape[:2]
-    for t in range(frames):
-        z = convolve(pad, taps, t, rows, False)
+    for t, rows in blocks(frames, rows):
+        z = convolve(pad, taps, t, rows.start, 2, False)
         s = jax.nn.sigmoid(z)
-        slope[t] = (s * (1.0 + z * (1.0 - s))).reshape(slope.shape[1:])
-        hidden[t] = (z * s).astype(jnp.bfloat16).reshape(hidden.shape[1:])
+        slope[t, rows] = (s * (1.0 + z * (1.0 - s))).reshape(2, *slope.shape[2:])
+        hidden[t, rows] = (z * s).astype(jnp.bfloat16).reshape(2, *hidden.shape[2:])
     strips(hidden, last, near_out, far_out, False)
 
 
@@ -146,12 +150,12 @@
     lay(pad, centre, time, near, far, corners, False)
     lay_taps(taps, kernel, False)
     frames, rows = centre.shape[:2]
-    for t in range(frames):
-        z = convolve(pad, taps, t, rows, False)
+    for t, rows in blocks(frames, rows):
+        z = convolve(pad, taps, t, rows.start, 2, False)
         s = jax.nn.sigmoid(z)
-        output[t] = (z * s).astype(jnp.bfloat16).reshape(output.shape[1:])
-        steep = (s * (1.0 + z * (1.0 - s))).reshape(grad.shape[1:])
-        grad[t] = (cotangent[t].astype(jnp.float32) * steep).astype(jnp.bfloat16)
+        output[t, rows] = (z * s).astype(jnp.bfloat16).reshape(2, *output.shape[2:])
+        steep = (s * (1.0 + z * (1.0 - s))).reshape(2, *grad.shape[2:])
+        grad[t, rows] = (cotangent[t, rows].astype(jnp.float32) * steep).astype(jnp.bfloat16)
     strips(grad, last, near_out, far_out, True)
 
 
@@ -161,9 +165,9 @@
     lay(pad, centre, time, near, far, corners, True)
     lay_taps(taps, kernel, True)
     frames, rows = centre.shape[:2]
-    for t in range(frames):
-        z = convolve(pad, taps, t, rows, True)
-        grad[t] = z.astype(jnp.bfloat16).reshape(grad.shape[1:])
+    for t, rows in blocks(frames, rows):
+        z = convolve(pad, taps, t, rows.start, 2, True)
+        grad[t, rows] = z.astype(jnp.bfloat16).reshape(2, *grad.shape[2:])
     ended[...] = jnp.zeros_like(ended)
     copy.wait()
 
@@ -174,9 +178,9 @@
     lay(pad, centre, time, near, far, corners, True)
     lay_taps(taps, kernel, True)
     frames, rows = centre.shape[:2]
-    for t in range(frames):
-        z = convolve(pad, taps, t, rows, True).reshape(grad.shape[1:])
-        grad[t] = (z * slope[t]).astype(jnp.bfloat16)
+    for t, rows in blocks(frames, rows):
+        z = convolve(pad, taps, t, rows.start, 2, True).reshape(2, *grad.shape[2:])
+        grad[t, rows] = (z * slope[t, rows]).astype(jnp.bfloat16)
     strips(grad, last, near_out, far_out, True)
 
 
@@ -247,9 +251,9 @@
     for k, out in enumerate(outs):
         for q in range(4):
             first, count = 7 * q, min(7, taps - 7 * q)
-            for d in range(4):
+            for place, d in enumerate((0, 1, 3, 2)):
                 for half in range(2):
-                    block = pieces[4 * half + d][k, q, :count].astype(jnp.float32) * scale
+                    block = pieces[4 * half + place][k, q, :count].astype(jnp.float32) * scale
                     held[k, pl.ds(first, count), pl.ds((core ^ half) * 4 + (x ^ d), 1)] = block[:, None]
             part = pl.ds(first, count)
             copies.append(pltpu.make_async_copy(held.at[k, part], out.at[part], sems.at[4 * k + q]))
@@ -296,7 +300,7 @@
     (total,) = call(add_kernel, [small], [], size, total, one, three, two, after=ended)
     one, two, three = (swap(total, 4 * d) for d in (1, 2, 3))
     (total,) = call(join_kernel, [whole], [], size, total, one, three, two)
-    pieces = [total] + [swap(total, d) for d in (1, 2, 3)]
+    pieces = [total] + [swap(total, d) for d in (1, 3, 2)]
     pieces += [swap(value, 16) for value in pieces]
     out_shape = (27, 8, part, channels)
     outs = call(

time: 113 us -> 113 us (level)
  transfers between devices with their start and end apart: 40 -> 40, of which waited for: 17 -> 16; matrix products, arithmetic and copies ran while one was open for 0% -> 0% of each run, Pallas kernels for 9% -> 9%
where the time goes in v5:
time: 113 us
  starting transfers between devices  70.4 us (62%)
  waiting for transfers between devices  21.9 us (19%)
  Pallas kernels  17.1 us (15%)
  local copies, waits for them, and re-layouts  2.17 us (2%)
    ppermute x24, starting transfers between devices, swap(): lax.ppermute(value, ALL, [(i, i ^ mask) for i in range(lax.axis_size(ALL))])  29.1 us
    ppermute x4, starting transfers between devices, exchanged(): lax.ppermute(far, 'height', [(i, (i - 1 if i % 2 == 0 else i + 1) % line)...  17.2 us
    pallas_call x16, Pallas kernels, call(): pl.pallas_call(run, out_shape=outs, in_specs=[inside] * len(args) + [ANY]...  17.1 us
    ppermute x24, waiting for transfers between devices, swap(): lax.ppermute(value, ALL, [(i, i ^ mask) for i in range(lax.axis_size(ALL))])  14.8 us
    ppermute x4, starting transfers between devices, exchanged(): time = lax.ppermute(last, 'tm', time_route(ahead))  10.9 us
    ppermute x4, starting transfers between devices, cornered(): return (time, near, far, lax.ppermute(rows, 'tm', time_route(ahead)))  9.55 us
    ppermute x4, waiting for transfers between devices, cornered(): return (time, near, far, lax.ppermute(rows, 'tm', time_route(ahead)))  5.54 us
    ppermute x4, starting transfers between devices, exchanged(): near = lax.ppermute(near, 'height', [(i, i ^ 1) for i in range(line)])  3.65 us
  transfers between devices with their start and end apart: 40, of which 16 were waited for; matrix products, arithmetic and copies ran while one was open for 0% of the time, Pallas kernels for 9%

profile of v5, /device:TPU:1, one launch (start us, length us, event | category | flops | bytes accessed | tf_op | source)
XLA Modules:
  0.0 112.6 jit_solution(8048082488365532161)
XLA Ops:
  2.0 2.1 %collective-permute-start.1 = (bf16[3,1,128,128]{3,2,1,0:T(8,128)(2,1)S(1)}, bf16[3,1,128,128]{3,2,1,0:T(8,128)(2,1)S(1)}, u32[]{:S(2)}, u32[]{:S(2)}) collective-permute-start(bf16[3,1,128,128]{3,2,1,0:T(8,128)(2,1)S(1)} %get-tuple-element.47), channel_id=1, source_target_pairs={{0,1},{1,0},{2,3},{3,2},{4,5},{5,4},{6,7},{7,6},{8,9},{9,8},{10,11... | collective-permute-start | bytes 294920 | tf_op jit(solution)/shard_map/ppermute | solution.py:332
  4.1 4.3 %collective-permute-start.2 = (bf16[3,1,128,128]{3,2,1,0:T(8,128)(2,1)S(1)}, bf16[3,1,128,128]{3,2,1,0:T(8,128)(2,1)S(1)}, u32[]{:S(2)}, u32[]{:S(2)}) collective-permute-start(bf16[3,1,128,128]{3,2,1,0:T(8,128)(2,1)S(1)} %get-tuple-element.48), channel_id=1, source_target_pairs={{0,15},{1,2},{2,1},{3,4},{4,3},{5,6},{6,5},{7,8},{8,7},{9,10},{10,... | collective-permute-start | bytes 294920 | tf_op jit(solution)/shard_map/ppermute | solution.py:333
  8.3 4.7 %collective-permute-start = (bf16[2,4,128,128]{3,2,1,0:T(8,128)(2,1)S(1)}, bf16[2,4,128,128]{3,2,1,0:T(8,128)(2,1)S(1)}, u32[]{:S(2)}, u32[]{:S(2)}) collective-permute-start(bf16[2,4,128,128]{3,2,1,0:T(8,128)(2,1)S(1)} %get-tuple-element.46), channel_id=1, source_target_pairs={{0,16},{16,32},{32,48},{48,0},{1,17},{17,33},{33,49},{49,1},{2,18}... | collective-permute-start | bytes 786440 | tf_op jit(solution)/shard_map/ppermute | solution.py:331
  13.1 3.5 %collective-permute-start.3 = (bf16[2,2,128,128]{3,2,1,0:T(8,128)(2,1)S(1)}, bf16[2,2,128,128]{3,2,1,0:T(8,128)(2,1)S(1)}, u32[]{:S(2)}, u32[]{:S(2)}) collective-permute-start(bf16[2,2,128,128]{3,2,1,0:T(8,128)(2,1)S(1)} %pad_maximum_fusion.2), channel_id=1, source_target_pairs={{0,16},{16,32},{32,48},{48,0},{1,17},{17,33},{33,49},{49,1},{2,18}... | collective-permute-start | bytes 393224 | tf_op jit(solution)/shard_map/ppermute | solution.py:345
  18.5 2.3 %shard_map.77 = (f32[3,4,128,128]{3,2,1,0:T(8,128)S(1)}, bf16[3,4,128,128]{3,2,1,0:T(8,128)(2,1)S(1)}, bf16[2,4,128,128]{3,2,1,0:T(8,128)(2,1)S(1)}, bf16[3,1,12...) custom-call(bf16[3,4,128,128]{3,2,1,0:T(8,128)(2,1)S(1)} %get-tuple-element.45.refs_0_, ...), custom_call_target="tpu_custom_call" | custom-call | flops 1358954496 | bytes 3506176 | tf_op jit(solution)/shard_map/pallas_call | solution.py:25
  20.9 4.3 %collective-permute-start.6 = (bf16[3,1,128,128]{3,2,1,0:T(8,128)(2,1)S(1)}, bf16[3,1,128,128]{3,2,1,0:T(8,128)(2,1)S(1)}, u32[]{:S(2)}, u32[]{:S(2)}) collective-permute-start(bf16[3,1,128,128]{3,2,1,0:T(8,128)(2,1)S(1)} %get-tuple-element.52), channel_id=1, source_target_pairs={{0,15},{1,2},{2,1},{3,4},{4,3},{5,6},{6,5},{7,8},{8,7},{9,10},{10,... | collective-permute-start | bytes 294920 | tf_op jit(solution)/shard_map/ppermute | solution.py:333
  25.2 4.2 %collective-permute-start.4 = (bf16[2,4,128,128]{3,2,1,0:T(8,128)(2,1)S(1)}, bf16[2,4,128,128]{3,2,1,0:T(8,128)(2,1)S(1)}, u32[]{:S(2)}, u32[]{:S(2)}) collective-permute-start(bf16[2,4,128,128]{3,2,1,0:T(8,128)(2,1)S(1)} %get-tuple-element.50), channel_id=1, source_target_pairs={{0,16},{16,32},{32,48},{48,0},{1,17},{17,33},{33,49},{49,1},{2,18}... | collective-permute-start | bytes 786440 | tf_op jit(solution)/shard_map/ppermute | solution.py:331
  29.5 3.5 %collective-permute-start.7 = (bf16[2,2,128,128]{3,2,1,0:T(8,128)(2,1)S(1)}, bf16[2,2,128,128]{3,2,1,0:T(8,128)(2,1)S(1)}, u32[]{:S(2)}, u32[]{:S(2)}) collective-permute-start(bf16[2,2,128,128]{3,2,1,0:T(8,128)(2,1)S(1)} %pad_maximum_fusion.1), channel_id=1, source_target_pairs={{0,16},{16,32},{32,48},{48,0},{1,17},{17,33},{33,49},{49,1},{2,18}... | collective-permute-start | bytes 393224 | tf_op jit(solution)/shard_map/ppermute | solution.py:345
  32.9 1.9 %collective-permute-done.7.refs_4_ = bf16[2,2,128,128]{3,2,1,0:T(8,128)(2,1)S(1)} collective-permute-done((bf16[2,2,128,128]{3,2,1,0:T(8,128)(2,1)S(1)}, bf16[2,2,128,128]{3,2,1,0:T(8,128)(2,1)S(1)}, u32[]{:S(2)}, u32[]{:S(2)}) %collective-permute-start.7) | collective-permute-done | bytes 131104 | tf_op jit(solution)/shard_map/ppermute | solution.py:345
  34.9 2.4 %shard_map.78 = (bf16[3,4,128,128]{3,2,1,0:T(8,128)(2,1)S(1)}, bf16[3,4,128,128]{3,2,1,0:T(8,128)(2,1)S(1)}, bf16[2,4,128,128]{3,2,1,0:T(8,128)(2,1)S(1)}, bf16[...) custom-call(bf16[3,4,128,128]{3,2,1,0:T(8,128)(2,1)S(1)} %get-tuple-element.49.refs_0_, ...), custom_call_target="tpu_custom_call" | custom-call | flops 1358954496 | bytes 3506176 | tf_op jit(solution)/shard_map/pallas_call | solution.py:25
  37.4 4.3 %collective-permute-start.10 = (bf16[3,1,128,128]{3,2,1,0:T(8,128)(2,1)S(1)}, bf16[3,1,128,128]{3,2,1,0:T(8,128)(2,1)S(1)}, u32[]{:S(2)}, u32[]{:S(2)}) collective-permute-start(bf16[3,1,128,128]{3,2,1,0:T(8,128)(2,1)S(1)} %get-tuple-element.56), channel_id=1, source_target_pairs={{0,15},{1,2},{2,1},{3,4},{4,3},{5,6},{6,5},{7,8},{8,7},{9,10},{10,... | collective-permute-start | bytes 294920 | tf_op jit(solution)/shard_map/ppermute | solution.py:333
  42.6 1.6 %collective-permute-done.10.refs_3_ = bf16[3,1,128,128]{3,2,1,0:T(8,128)(2,1)S(1)} collective-permute-done((bf16[3,1,128,128]{3,2,1,0:T(8,128)(2,1)S(1)}, bf16[3,1,128,128]{3,2,1,0:T(8,128)(2,1)S(1)}, u32[]{:S(2)}, u32[]{:S(2)}) %collective-permute-start.10) | collective-permute-done | bytes 98336 | tf_op jit(solution)/shard_map/ppermute | solution.py:333
  44.2 1.9 %collective-permute-start.11 = (bf16[2,2,128,128]{3,2,1,0:T(8,128)(2,1)S(1)}, bf16[2,2,128,128]{3,2,1,0:T(8,128)(2,1)S(1)}, u32[]{:S(2)}, u32[]{:S(2)}) collective-permute-start(bf16[2,2,128,128]{3,2,1,0:T(8,128)(2,1)S(1)} %pad_maximum_fusion), channel_id=1, source_target_pairs={{0,48},{16,0},{32,16},{48,32},{1,49},{17,1},{33,17},{49,33},{2,50}... | collective-permute-start | bytes 393224 | tf_op jit(solution)/shard_map/ppermute | solution.py:345
  46.1 2.3 %shard_map.81 = (f32[4,28,16,128]{3,2,1,0:T(8,128)S(1)}, bf16[4,28,16,128]{3,2,1,0:T(8,128)(2,1)S(1)}) custom-call(bf16[3,4,128,128]{3,2,1,0:T(8,128)(2,1)S(1)} %get-tuple-element.49.refs_0_, bf16[2,4,128,128]{3,2,1,0:T(8,128)(2,1)S(1)} %collective-permute-done.4.refs_1_, bf16[3,1,128,128]{3,2,1,0:T(8,128)(2,1)S(1)} %collective-permute-done.5.refs_2_, ...), custom_call_target="tpu_custom_call" | custom-call | flops 1358954496 | bytes 2752512 | tf_op jit(solution)/shard_map/pallas_call | solution.py:25
  48.9 3.1 %collective-permute-done.11.refs_4_ = bf16[2,2,128,128]{3,2,1,0:T(8,128)(2,1)S(1)} collective-permute-done((bf16[2,2,128,128]{3,2,1,0:T(8,128)(2,1)S(1)}, bf16[2,2,128,128]{3,2,1,0:T(8,128)(2,1)S(1)}, u32[]{:S(2)}, u32[]{:S(2)}) %collective-permute-start.11) | collective-permute-done | bytes 131104 | tf_op jit(solution)/shard_map/ppermute | solution.py:345
  52.1 2.6 %shard_map.79 = (bf16[3,4,128,128]{3,2,1,0:T(8,128)(2,1)S(1)}, bf16[2,4,128,128]{3,2,1,0:T(8,128)(2,1)S(1)}, bf16[3,1,128,128]{3,2,1,0:T(8,128)(2,1)S(1)}, bf16[3,1,128,128]{3,2,1,0:T(8,128)(2,1)S(1)}) custom-call(bf16[3,4,128,128]{3,2,1,0:T(8,128)(2,1)S(1)} %get-tuple-element.53.refs_0_.refs_5_, ...), custom_call_target="tpu_custom_call" | custom-call | flops 1358954496 | bytes 3506176 | tf_op jit(solution)/shard_map/pallas_call | solution.py:25
  54.7 2.3 %shard_map.80 = (f32[4,28,16,128]{3,2,1,0:T(8,128)S(1)}, bf16[4,28,16,128]{3,2,1,0:T(8,128)(2,1)S(1)}) custom-call(bf16[3,4,128,128]{3,2,1,0:T(8,128)(2,1)S(1)} %get-tuple-element.45.refs_0_, bf16[2,4,128,128]{3,2,1,0:T(8,128)(2,1)S(1)} %collective-permute-done.refs_1_, bf16[3,1,128,128]{3,2,1,0:T(8,128)(2,1)S(1)} %collective-permute-done.1.refs_2_, ...), custom_call_target="tpu_custom_call" | custom-call | flops 1358954496 | bytes 2752512 | tf_op jit(solution)/shard_map/pallas_call | solution.py:25
  57.0 1.8 %collective-permute-done.15.refs_1_ = bf16[4,28,16,128]{3,2,1,0:T(8,128)(2,1)S(1)} collective-permute-done((bf16[4,28,16,128]{3,2,1,0:T(8,128)(2,1)S(1)}, bf16[4,28,16,128]{3,2,1,0:T(8,128)(2,1)S(1)}, u32[]{:S(2)}, u32[]{:S(2)}) %collective-permute-start.15) | collective-permute-done | bytes 458784 | tf_op jit(solution)/shard_map/ppermute | solution.py:266
  60.5 4.2 %collective-permute-start.14 = (bf16[3,1,128,128]{3,2,1,0:T(8,128)(2,1)S(1)}, bf16[3,1,128,128]{3,2,1,0:T(8,128)(2,1)S(1)}, u32[]{:S(2)}, u32[]{:S(2)}) collective-permute-start(bf16[3,1,128,128]{3,2,1,0:T(8,128)(2,1)S(1)} %get-tuple-element.61), channel_id=1, source_target_pairs={{0,15},{1,2},{2,1},{3,4},{4,3},{5,6},{6,5},{7,8},{8,7},{9,10},{10,... | collective-permute-start | bytes 294920 | tf_op jit(solution)/shard_map/ppermute | solution.py:333
  65.9 2.7 %collective-permute-start.21 = (bf16[4,7,16,128]{3,2,1,0:T(8,128)(2,1)S(1)}, bf16[4,7,16,128]{3,2,1,0:T(8,128)(2,1)S(1)}, u32[]{:S(2)}, u32[]{:S(2)}) collective-permute-start(bf16[4,7,16,128]{3,2,1,0:T(8,128)(2,1)S(1)} %get-tuple-element.74), channel_id=1, source_target_pairs={{0,3},{1,2},{2,1},{3,0},{4,7},{5,6},{6,5},{7,4},{8,11},{9,10},{10,... | collective-permute-start | bytes 344072 | tf_op jit(solution)/shard_map/ppermute | solution.py:266
  68.9 1.7 %collective-permute-done.18.refs_1_ = bf16[4,7,16,128]{3,2,1,0:T(8,128)(2,1)S(1)} collective-permute-done((bf16[4,7,16,128]{3,2,1,0:T(8,128)(2,1)S(1)}, bf16[4,7,16,128]{3,2,1,0:T(8,128)(2,1)S(1)}, u32[]{:S(2)}, u32[]{:S(2)}) %collective-permute-start.18) | collective-permute-done | bytes 114720 | tf_op jit(solution)/shard_map/ppermute | solution.py:266
  71.3 2.3 %collective-permute-done.21.refs_2_ = bf16[4,7,16,128]{3,2,1,0:T(8,128)(2,1)S(1)} collective-permute-done((bf16[4,7,16,128]{3,2,1,0:T(8,128)(2,1)S(1)}, bf16[4,7,16,128]{3,2,1,0:T(8,128)(2,1)S(1)}, u32[]{:S(2)}, u32[]{:S(2)}) %collective-permute-start.21) | collective-permute-done | bytes 114720 | tf_op jit(solution)/shard_map/ppermute | solution.py:266
  73.7 2.4 %collective-permute-start.24 = (bf16[2,7,16,128]{3,2,1,0:T(8,128)(2,1)S(1)}, bf16[2,7,16,128]{3,2,1,0:T(8,128)(2,1)S(1)}, u32[]{:S(2)}, u32[]{:S(2)}) collective-permute-start(bf16[2,7,16,128]{3,2,1,0:T(8,128)(2,1)S(1)} %get-tuple-element.78), channel_id=1, source_target_pairs={{0,8},{1,9},{2,10},{3,11},{4,12},{5,13},{6,14},{7,15},{8,0},{9,1},... | collective-permute-start | bytes 172040 | tf_op jit(solution)/shard_map/ppermute | solution.py:266
  79.2 1.7 %collective-permute-done.26.refs_3_ = bf16[2,7,16,128]{3,2,1,0:T(8,128)(2,1)S(1)} collective-permute-done((bf16[2,7,16,128]{3,2,1,0:T(8,128)(2,1)S(1)}, bf16[2,7,16,128]{3,2,1,0:T(8,128)(2,1)S(1)}, u32[]{:S(2)}, u32[]{:S(2)}) %collective-permute-start.26) | collective-permute-done | bytes 57376 | tf_op jit(solution)/shard_map/ppermute | solution.py:266
  81.0 3.1 %collective-permute-start.28 = (bf16[2,7,16,128]{3,2,1,0:T(8,128)(2,1)S(1)}, bf16[2,7,16,128]{3,2,1,0:T(8,128)(2,1)S(1)}, u32[]{:S(2)}, u32[]{:S(2)}) collective-permute-start(bf16[2,7,16,128]{3,2,1,0:T(8,128)(2,1)S(1)} %shard_map.87.refs_0_), channel_id=1, source_target_pairs={{0,96},{1,97},{2,98},{3,99},{4,100},{5,101},{6,102},{7,103},{8,104... | collective-permute-start | bytes 172040 | tf_op jit(solution)/shard_map/ppermute | solution.py:266
  84.1 2.3 %shard_map.84 = (bf16[3,4,128,128]{3,2,1,0:T(8,128)(2,1)}, bf16[3,4,128,128]{3,2,1,0:T(8,128)(2,1)S(1)}, f32[8,128]{1,0:T(8,128)S(1)}) custom-call(bf16[3,4,128,128]{3,2,1,0:T(8,128)(2,1)S(1)} %get-tuple-element.58.refs_5_.refs_0_, bf16[2,4,128,128]{3,2,1,0:T(8,128)(2,1)S(1)} %collective-permute-done.12.refs_1_, ...), custom_call_target="tpu_custom_call" | custom-call | flops 1358954496 | bytes 3051520 | tf_op jit(solution)/shard_map/pallas_call | solution.py:25
  88.0 2.6 %collective-permute-start.31 = (bf16[2,7,16,128]{3,2,1,0:T(8,128)(2,1)S(1)}, bf16[2,7,16,128]{3,2,1,0:T(8,128)(2,1)S(1)}, u32[]{:S(2)}, u32[]{:S(2)}) collective-permute-start(bf16[2,7,16,128]{3,2,1,0:T(8,128)(2,1)S(1)} %shard_map.88.refs_0_), channel_id=1, source_target_pairs={{0,12},{1,13},{2,14},{3,15},{4,8},{5,9},{6,10},{7,11},{8,4},{9,5},... | collective-permute-start | bytes 172040 | tf_op jit(solution)/shard_map/ppermute | solution.py:266
  94.5 1.5 %collective-permute-start.34 = (bf16[2,4,7,16,128]{4,3,2,1,0:T(8,128)(2,1)S(1)}, bf16[2,4,7,16,128]{4,3,2,1,0:T(8,128)(2,1)S(1)}, u32[]{:S(2)}, u32[]{:S(2)}) collective-permute-start(bf16[2,4,7,16,128]{4,3,2,1,0:T(8,128)(2,1)S(1)} %shard_map.89.refs_0_), channel_id=1, source_target_pairs={{0,3},{1,2},{2,1},{3,0},{4,7},{5,6},{6,5},{7,4},{8,11},{9,10},{10,... | collective-permute-start | bytes 688136 | tf_op jit(solution)/shard_map/ppermute | solution.py:266
  96.3 6.1 %collective-permute-start.36 = (bf16[2,4,7,16,128]{4,3,2,1,0:T(8,128)(2,1)S(1)}, bf16[2,4,7,16,128]{4,3,2,1,0:T(8,128)(2,1)S(1)}, u32[]{:S(2)}, u32[]{:S(2)}) collective-permute-start(bf16[2,4,7,16,128]{4,3,2,1,0:T(8,128)(2,1)S(1)} %shard_map.89.refs_0_), channel_id=1, source_target_pairs={{0,16},{1,17},{2,18},{3,19},{4,20},{5,21},{6,22},{7,23},{8,24},{9,... | collective-permute-start | bytes 688136 | tf_op jit(solution)/shard_map/ppermute | solution.py:266
  102.5 4.1 %collective-permute-start.39 = (bf16[2,4,7,16,128]{4,3,2,1,0:T(8,128)(2,1)S(1)}, bf16[2,4,7,16,128]{4,3,2,1,0:T(8,128)(2,1)S(1)}, u32[]{:S(2)}, u32[]{:S(2)}) collective-permute-start(bf16[2,4,7,16,128]{4,3,2,1,0:T(8,128)(2,1)S(1)} %collective-permute-done.35.refs_3_), channel_id=1, source_target_pairs={{0,16},{1,17},{2,18},{3,19},{4,20},{5,21},{6,22},{7,23},{8,24},{9,... | collective-permute-start | bytes 688136 | tf_op jit(solution)/shard_map/ppermute | solution.py:266
  106.6 2.4 %collective-permute-start.38 = (bf16[2,4,7,16,128]{4,3,2,1,0:T(8,128)(2,1)S(1)}, bf16[2,4,7,16,128]{4,3,2,1,0:T(8,128)(2,1)S(1)}, u32[]{:S(2)}, u32[]{:S(2)}) collective-permute-start(bf16[2,4,7,16,128]{4,3,2,1,0:T(8,128)(2,1)S(1)} %collective-permute-done.34.refs_2_), channel_id=1, source_target_pairs={{0,16},{1,17},{2,18},{3,19},{4,20},{5,21},{6,22},{7,23},{8,24},{9,... | collective-permute-start | bytes 688136 | tf_op jit(solution)/shard_map/ppermute | solution.py:266
  110.5 2.0 %shard_map.90 = (f32[27,8,16,128]{3,2,1,0:T(8,128)}, f32[27,8,16,128]{3,2,1,0:T(8,128)}, bf16[3,4,128,128]{3,2,1,0:T(8,128)(2,1)}) custom-call(bf16[2,4,7,16,128]{4,3,2,1,0:T(8,128)(2,1)S(1)} %shard_map.89.refs_0_, bf16[2,4,7,16,128]{4,3,2,1,0:T(8,128)(2,1)S(1)} %collective-permute-done.33.refs_1_, ...), custom_call_target="tpu_custom_call" | custom-call | flops 917504 | bytes 6160384 | tf_op jit(solution)/shard_map/pallas_call | solution.py:25
  (77 shorter events, 19.3 us)
Async XLA Ops:
  2.0 11.1 %collective-permute-start.1 = (bf16[3,1,128,128]{3,2,1,0:T(8,128)(2,1)S(1)}, bf16[3,1,128,128]{3,2,1,0:T(8,128)(2,1)S(1)}, u32[]{:S(2)}, u32[]{:S(2)}) collective-permute-start(bf16[3,1,128,128]{3,2,1,0:T(8,128)(2,1)S(1)} %get-tuple-element.47), channel_id=1, source_target_pairs={{0,1},{1,0},{2,3},{3,2},{4,5},{5,4},{6,7},{7,6},{8,9},{9,8},{10,11... | collective-permute-start | bytes 294920 | tf_op jit(solution)/shard_map/ppermute | solution.py:332
  4.1 9.0 %collective-permute-start.2 = (bf16[3,1,128,128]{3,2,1,0:T(8,128)(2,1)S(1)}, bf16[3,1,128,128]{3,2,1,0:T(8,128)(2,1)S(1)}, u32[]{:S(2)}, u32[]{:S(2)}) collective-permute-start(bf16[3,1,128,128]{3,2,1,0:T(8,128)(2,1)S(1)} %get-tuple-element.48), channel_id=1, source_target_pairs={{0,15},{1,2},{2,1},{3,4},{4,3},{5,6},{6,5},{7,8},{8,7},{9,10},{10,... | collective-permute-start | bytes 294920 | tf_op jit(solution)/shard_map/ppermute | solution.py:333
  8.3 10.1 %collective-permute-start = (bf16[2,4,128,128]{3,2,1,0:T(8,128)(2,1)S(1)}, bf16[2,4,128,128]{3,2,1,0:T(8,128)(2,1)S(1)}, u32[]{:S(2)}, u32[]{:S(2)}) collective-permute-start(bf16[2,4,128,128]{3,2,1,0:T(8,128)(2,1)S(1)} %get-tuple-element.46), channel_id=1, source_target_pairs={{0,16},{16,32},{32,48},{48,0},{1,17},{17,33},{33,49},{49,1},{2,18}... | collective-permute-start | bytes 786440 | tf_op jit(solution)/shard_map/ppermute | solution.py:331
  13.1 5.4 %collective-permute-start.3 = (bf16[2,2,128,128]{3,2,1,0:T(8,128)(2,1)S(1)}, bf16[2,2,128,128]{3,2,1,0:T(8,128)(2,1)S(1)}, u32[]{:S(2)}, u32[]{:S(2)}) collective-permute-start(bf16[2,2,128,128]{3,2,1,0:T(8,128)(2,1)S(1)} %pad_maximum_fusion.2), channel_id=1, source_target_pairs={{0,16},{16,32},{32,48},{48,0},{1,17},{17,33},{33,49},{49,1},{2,18}... | collective-permute-start | bytes 393224 | tf_op jit(solution)/shard_map/ppermute | solution.py:345
  20.8 8.7 %collective-permute-start.5 = (bf16[3,1,128,128]{3,2,1,0:T(8,128)(2,1)S(1)}, bf16[3,1,128,128]{3,2,1,0:T(8,128)(2,1)S(1)}, u32[]{:S(2)}, u32[]{:S(2)}) collective-permute-start(bf16[3,1,128,128]{3,2,1,0:T(8,128)(2,1)S(1)} %get-tuple-element.51), channel_id=1, source_target_pairs={{0,1},{1,0},{2,3},{3,2},{4,5},{5,4},{6,7},{7,6},{8,9},{9,8},{10,11... | collective-permute-start | bytes 294920 | tf_op jit(solution)/shard_map/ppermute | solution.py:332
  20.9 8.6 %collective-permute-start.6 = (bf16[3,1,128,128]{3,2,1,0:T(8,128)(2,1)S(1)}, bf16[3,1,128,128]{3,2,1,0:T(8,128)(2,1)S(1)}, u32[]{:S(2)}, u32[]{:S(2)}) collective-permute-start(bf16[3,1,128,128]{3,2,1,0:T(8,128)(2,1)S(1)} %get-tuple-element.52), channel_id=1, source_target_pairs={{0,15},{1,2},{2,1},{3,4},{4,3},{5,6},{6,5},{7,8},{8,7},{9,10},{10,... | collective-permute-start | bytes 294920 | tf_op jit(solution)/shard_map/ppermute | solution.py:333
  25.2 9.7 %collective-permute-start.4 = (bf16[2,4,128,128]{3,2,1,0:T(8,128)(2,1)S(1)}, bf16[2,4,128,128]{3,2,1,0:T(8,128)(2,1)S(1)}, u32[]{:S(2)}, u32[]{:S(2)}) collective-permute-start(bf16[2,4,128,128]{3,2,1,0:T(8,128)(2,1)S(1)} %get-tuple-element.50), channel_id=1, source_target_pairs={{0,16},{16,32},{32,48},{48,0},{1,17},{17,33},{33,49},{49,1},{2,18}... | collective-permute-start | bytes 786440 | tf_op jit(solution)/shard_map/ppermute | solution.py:331
  29.5 5.4 %collective-permute-start.7 = (bf16[2,2,128,128]{3,2,1,0:T(8,128)(2,1)S(1)}, bf16[2,2,128,128]{3,2,1,0:T(8,128)(2,1)S(1)}, u32[]{:S(2)}, u32[]{:S(2)}) collective-permute-start(bf16[2,2,128,128]{3,2,1,0:T(8,128)(2,1)S(1)} %pad_maximum_fusion.1), channel_id=1, source_target_pairs={{0,16},{16,32},{32,48},{48,0},{1,17},{17,33},{33,49},{49,1},{2,18}... | collective-permute-start | bytes 393224 | tf_op jit(solution)/shard_map/ppermute | solution.py:345
  37.3 5.4 %collective-permute-start.9 = (bf16[3,1,128,128]{3,2,1,0:T(8,128)(2,1)S(1)}, bf16[3,1,128,128]{3,2,1,0:T(8,128)(2,1)S(1)}, u32[]{:S(2)}, u32[]{:S(2)}) collective-permute-start(bf16[3,1,128,128]{3,2,1,0:T(8,128)(2,1)S(1)} %get-tuple-element.55), channel_id=1, source_target_pairs={{0,1},{1,0},{2,3},{3,2},{4,5},{5,4},{6,7},{7,6},{8,9},{9,8},{10,11... | collective-permute-start | bytes 294920 | tf_op jit(solution)/shard_map/ppermute | solution.py:332
  37.4 6.9 %collective-permute-start.10 = (bf16[3,1,128,128]{3,2,1,0:T(8,128)(2,1)S(1)}, bf16[3,1,128,128]{3,2,1,0:T(8,128)(2,1)S(1)}, u32[]{:S(2)}, u32[]{:S(2)}) collective-permute-start(bf16[3,1,128,128]{3,2,1,0:T(8,128)(2,1)S(1)} %get-tuple-element.56), channel_id=1, source_target_pairs={{0,15},{1,2},{2,1},{3,4},{4,3},{5,6},{6,5},{7,8},{8,7},{9,10},{10,... | collective-permute-start | bytes 294920 | tf_op jit(solution)/shard_map/ppermute | solution.py:333
  41.7 10.4 %collective-permute-start.8 = (bf16[2,4,128,128]{3,2,1,0:T(8,128)(2,1)S(1)}, bf16[2,4,128,128]{3,2,1,0:T(8,128)(2,1)S(1)}, u32[]{:S(2)}, u32[]{:S(2)}) collective-permute-start(bf16[2,4,128,128]{3,2,1,0:T(8,128)(2,1)S(1)} %get-tuple-element.54), channel_id=1, source_target_pairs={{0,48},{16,0},{32,16},{48,32},{1,49},{17,1},{33,17},{49,33},{2,50}... | collective-permute-start | bytes 786440 | tf_op jit(solution)/shard_map/ppermute | solution.py:331
  44.2 7.8 %collective-permute-start.11 = (bf16[2,2,128,128]{3,2,1,0:T(8,128)(2,1)S(1)}, bf16[2,2,128,128]{3,2,1,0:T(8,128)(2,1)S(1)}, u32[]{:S(2)}, u32[]{:S(2)}) collective-permute-start(bf16[2,2,128,128]{3,2,1,0:T(8,128)(2,1)S(1)} %pad_maximum_fusion), channel_id=1, source_target_pairs={{0,48},{16,0},{32,16},{48,32},{1,49},{17,1},{33,17},{49,33},{2,50}... | collective-permute-start | bytes 393224 | tf_op jit(solution)/shard_map/ppermute | solution.py:345
  48.4 8.6 %collective-permute-start.16 = (bf16[4,28,16,128]{3,2,1,0:T(8,128)(2,1)S(1)}, bf16[4,28,16,128]{3,2,1,0:T(8,128)(2,1)S(1)}, u32[]{:S(2)}, u32[]{:S(2)}) collective-permute-start(bf16[4,28,16,128]{3,2,1,0:T(8,128)(2,1)S(1)} %get-tuple-element.65), channel_id=1, source_target_pairs={{0,16},{1,17},{2,18},{3,19},{4,20},{5,21},{6,22},{7,23},{8,24},{9,... | collective-permute-start | bytes 1376264 | tf_op jit(solution)/shard_map/ppermute | solution.py:266
  59.0 6.8 %collective-permute-start.19 = (bf16[4,7,16,128]{3,2,1,0:T(8,128)(2,1)S(1)}, bf16[4,7,16,128]{3,2,1,0:T(8,128)(2,1)S(1)}, u32[]{:S(2)}, u32[]{:S(2)}) collective-permute-start(bf16[4,7,16,128]{3,2,1,0:T(8,128)(2,1)S(1)} %get-tuple-element.72), channel_id=1, source_target_pairs={{0,1},{1,0},{2,3},{3,2},{4,5},{5,4},{6,7},{7,6},{8,9},{9,8},{10,11... | collective-permute-start | bytes 344072 | tf_op jit(solution)/shard_map/ppermute | solution.py:266
  59.1 6.7 %collective-permute-start.20 = (bf16[4,7,16,128]{3,2,1,0:T(8,128)(2,1)S(1)}, bf16[4,7,16,128]{3,2,1,0:T(8,128)(2,1)S(1)}, u32[]{:S(2)}, u32[]{:S(2)}) collective-permute-start(bf16[4,7,16,128]{3,2,1,0:T(8,128)(2,1)S(1)} %get-tuple-element.73), channel_id=1, source_target_pairs={{0,3},{1,2},{2,1},{3,0},{4,7},{5,6},{6,5},{7,4},{8,11},{9,10},{10,... | collective-permute-start | bytes 344072 | tf_op jit(solution)/shard_map/ppermute | solution.py:266
  59.2 6.8 %collective-permute-start.13 = (bf16[3,1,128,128]{3,2,1,0:T(8,128)(2,1)S(1)}, bf16[3,1,128,128]{3,2,1,0:T(8,128)(2,1)S(1)}, u32[]{:S(2)}, u32[]{:S(2)}) collective-permute-start(bf16[3,1,128,128]{3,2,1,0:T(8,128)(2,1)S(1)} %get-tuple-element.60), channel_id=1, source_target_pairs={{0,1},{1,0},{2,3},{3,2},{4,5},{5,4},{6,7},{7,6},{8,9},{9,8},{10,11... | collective-permute-start | bytes 294920 | tf_op jit(solution)/shard_map/ppermute | solution.py:332
  60.5 8.1 %collective-permute-start.14 = (bf16[3,1,128,128]{3,2,1,0:T(8,128)(2,1)S(1)}, bf16[3,1,128,128]{3,2,1,0:T(8,128)(2,1)S(1)}, u32[]{:S(2)}, u32[]{:S(2)}) collective-permute-start(bf16[3,1,128,128]{3,2,1,0:T(8,128)(2,1)S(1)} %get-tuple-element.61), channel_id=1, source_target_pairs={{0,15},{1,2},{2,1},{3,4},{4,3},{5,6},{6,5},{7,8},{8,7},{9,10},{10,... | collective-permute-start | bytes 294920 | tf_op jit(solution)/shard_map/ppermute | solution.py:333
  64.8 19.3 %collective-permute-start.12 = (bf16[2,4,128,128]{3,2,1,0:T(8,128)(2,1)S(1)}, bf16[2,4,128,128]{3,2,1,0:T(8,128)(2,1)S(1)}, u32[]{:S(2)}, u32[]{:S(2)}) collective-permute-start(bf16[2,4,128,128]{3,2,1,0:T(8,128)(2,1)S(1)} %get-tuple-element.59), channel_id=1, source_target_pairs={{0,48},{16,0},{32,16},{48,32},{1,49},{17,1},{33,17},{49,33},{2,50}... | collective-permute-start | bytes 786440 | tf_op jit(solution)/shard_map/ppermute | solution.py:331
  65.8 4.8 %collective-permute-start.18 = (bf16[4,7,16,128]{3,2,1,0:T(8,128)(2,1)S(1)}, bf16[4,7,16,128]{3,2,1,0:T(8,128)(2,1)S(1)}, u32[]{:S(2)}, u32[]{:S(2)}) collective-permute-start(bf16[4,7,16,128]{3,2,1,0:T(8,128)(2,1)S(1)} %get-tuple-element.69), channel_id=1, source_target_pairs={{0,1},{1,0},{2,3},{3,2},{4,5},{5,4},{6,7},{7,6},{8,9},{9,8},{10,11... | collective-permute-start | bytes 344072 | tf_op jit(solution)/shard_map/ppermute | solution.py:266
  65.8 5.6 %collective-permute-start.23 = (bf16[4,7,16,128]{3,2,1,0:T(8,128)(2,1)S(1)}, bf16[4,7,16,128]{3,2,1,0:T(8,128)(2,1)S(1)}, u32[]{:S(2)}, u32[]{:S(2)}) collective-permute-start(bf16[4,7,16,128]{3,2,1,0:T(8,128)(2,1)S(1)} %get-tuple-element.76), channel_id=1, source_target_pairs={{0,3},{1,2},{2,1},{3,0},{4,7},{5,6},{6,5},{7,4},{8,11},{9,10},{10,... | collective-permute-start | bytes 344072 | tf_op jit(solution)/shard_map/ppermute | solution.py:266
  65.9 7.7 %collective-permute-start.21 = (bf16[4,7,16,128]{3,2,1,0:T(8,128)(2,1)S(1)}, bf16[4,7,16,128]{3,2,1,0:T(8,128)(2,1)S(1)}, u32[]{:S(2)}, u32[]{:S(2)}) collective-permute-start(bf16[4,7,16,128]{3,2,1,0:T(8,128)(2,1)S(1)} %get-tuple-element.74), channel_id=1, source_target_pairs={{0,3},{1,2},{2,1},{3,0},{4,7},{5,6},{6,5},{7,4},{8,11},{9,10},{10,... | collective-permute-start | bytes 344072 | tf_op jit(solution)/shard_map/ppermute | solution.py:266
  68.7 4.9 %collective-permute-start.22 = (bf16[4,7,16,128]{3,2,1,0:T(8,128)(2,1)S(1)}, bf16[4,7,16,128]{3,2,1,0:T(8,128)(2,1)S(1)}, u32[]{:S(2)}, u32[]{:S(2)}) collective-permute-start(bf16[4,7,16,128]{3,2,1,0:T(8,128)(2,1)S(1)} %get-tuple-element.75), channel_id=1, source_target_pairs={{0,1},{1,0},{2,3},{3,2},{4,5},{5,4},{6,7},{7,6},{8,9},{9,8},{10,11... | collective-permute-start | bytes 344072 | tf_op jit(solution)/shard_map/ppermute | solution.py:266
  70.5 6.5 %collective-permute-start.17 = (bf16[2,2,128,128]{3,2,1,0:T(8,128)(2,1)S(1)}, bf16[2,2,128,128]{3,2,1,0:T(8,128)(2,1)S(1)}, u32[]{:S(2)}, u32[]{:S(2)}) collective-permute-start(bf16[2,2,128,128]{3,2,1,0:T(8,128)(2,1)S(1)} %shard_map.83), channel_id=1, source_target_pairs={{0,48},{16,0},{32,16},{48,32},{1,49},{17,1},{33,17},{49,33},{2,50}... | collective-permute-start | bytes 393224 | tf_op jit(solution)/shard_map/ppermute | solution.py:345
  76.1 4.7 %collective-permute-start.26 = (bf16[2,7,16,128]{3,2,1,0:T(8,128)(2,1)S(1)}, bf16[2,7,16,128]{3,2,1,0:T(8,128)(2,1)S(1)}, u32[]{:S(2)}, u32[]{:S(2)}) collective-permute-start(bf16[2,7,16,128]{3,2,1,0:T(8,128)(2,1)S(1)} %get-tuple-element.80), channel_id=1, source_target_pairs={{0,12},{1,13},{2,14},{3,15},{4,8},{5,9},{6,10},{7,11},{8,4},{9,5},... | collective-permute-start | bytes 172040 | tf_op jit(solution)/shard_map/ppermute | solution.py:266
  80.9 5.5 %collective-permute-start.29 = (bf16[2,7,16,128]{3,2,1,0:T(8,128)(2,1)S(1)}, bf16[2,7,16,128]{3,2,1,0:T(8,128)(2,1)S(1)}, u32[]{:S(2)}, u32[]{:S(2)}) collective-permute-start(bf16[2,7,16,128]{3,2,1,0:T(8,128)(2,1)S(1)} %shard_map.87.refs_0_), channel_id=1, source_target_pairs={{0,32},{1,33},{2,34},{3,35},{4,36},{5,37},{6,38},{7,39},{8,40},{9,... | collective-permute-start | bytes 172040 | tf_op jit(solution)/shard_map/ppermute | solution.py:266
  81.0 5.5 %collective-permute-start.28 = (bf16[2,7,16,128]{3,2,1,0:T(8,128)(2,1)S(1)}, bf16[2,7,16,128]{3,2,1,0:T(8,128)(2,1)S(1)}, u32[]{:S(2)}, u32[]{:S(2)}) collective-permute-start(bf16[2,7,16,128]{3,2,1,0:T(8,128)(2,1)S(1)} %shard_map.87.refs_0_), channel_id=1, source_target_pairs={{0,96},{1,97},{2,98},{3,99},{4,100},{5,101},{6,102},{7,103},{8,104... | collective-permute-start | bytes 172040 | tf_op jit(solution)/shard_map/ppermute | solution.py:266
  87.2 4.6 %collective-permute-start.32 = (bf16[2,7,16,128]{3,2,1,0:T(8,128)(2,1)S(1)}, bf16[2,7,16,128]{3,2,1,0:T(8,128)(2,1)S(1)}, u32[]{:S(2)}, u32[]{:S(2)}) collective-permute-start(bf16[2,7,16,128]{3,2,1,0:T(8,128)(2,1)S(1)} %shard_map.88.refs_0_), channel_id=1, source_target_pairs={{0,8},{1,9},{2,10},{3,11},{4,12},{5,13},{6,14},{7,15},{8,0},{9,1},... | collective-permute-start | bytes 172040 | tf_op jit(solution)/shard_map/ppermute | solution.py:266
  93.6 8.9 %collective-permute-start.35 = (bf16[2,4,7,16,128]{4,3,2,1,0:T(8,128)(2,1)S(1)}, bf16[2,4,7,16,128]{4,3,2,1,0:T(8,128)(2,1)S(1)}, u32[]{:S(2)}, u32[]{:S(2)}) collective-permute-start(bf16[2,4,7,16,128]{4,3,2,1,0:T(8,128)(2,1)S(1)} %shard_map.89.refs_0_), channel_id=1, source_target_pairs={{0,2},{1,3},{2,0},{3,1},{4,6},{5,7},{6,4},{7,5},{8,10},{9,11},{10,... | collective-permute-start | bytes 688136 | tf_op jit(solution)/shard_map/ppermute | solution.py:266
  94.5 12.1 %collective-permute-start.34 = (bf16[2,4,7,16,128]{4,3,2,1,0:T(8,128)(2,1)S(1)}, bf16[2,4,7,16,128]{4,3,2,1,0:T(8,128)(2,1)S(1)}, u32[]{:S(2)}, u32[]{:S(2)}) collective-permute-start(bf16[2,4,7,16,128]{4,3,2,1,0:T(8,128)(2,1)S(1)} %shard_map.89.refs_0_), channel_id=1, source_target_pairs={{0,3},{1,2},{2,1},{3,0},{4,7},{5,6},{6,5},{7,4},{8,11},{9,10},{10,... | collective-permute-start | bytes 688136 | tf_op jit(solution)/shard_map/ppermute | solution.py:266
  96.0 12.9 %collective-permute-start.33 = (bf16[2,4,7,16,128]{4,3,2,1,0:T(8,128)(2,1)S(1)}, bf16[2,4,7,16,128]{4,3,2,1,0:T(8,128)(2,1)S(1)}, u32[]{:S(2)}, u32[]{:S(2)}) collective-permute-start(bf16[2,4,7,16,128]{4,3,2,1,0:T(8,128)(2,1)S(1)} %shard_map.89.refs_0_), channel_id=1, source_target_pairs={{0,1},{1,0},{2,3},{3,2},{4,5},{5,4},{6,7},{7,6},{8,9},{9,8},{10,11... | collective-permute-start | bytes 688136 | tf_op jit(solution)/shard_map/ppermute | solution.py:266
  96.3 12.6 %collective-permute-start.36 = (bf16[2,4,7,16,128]{4,3,2,1,0:T(8,128)(2,1)S(1)}, bf16[2,4,7,16,128]{4,3,2,1,0:T(8,128)(2,1)S(1)}, u32[]{:S(2)}, u32[]{:S(2)}) collective-permute-start(bf16[2,4,7,16,128]{4,3,2,1,0:T(8,128)(2,1)S(1)} %shard_map.89.refs_0_), channel_id=1, source_target_pairs={{0,16},{1,17},{2,18},{3,19},{4,20},{5,21},{6,22},{7,23},{8,24},{9,... | collective-permute-start | bytes 688136 | tf_op jit(solution)/shard_map/ppermute | solution.py:266
  102.5 6.5 %collective-permute-start.39 = (bf16[2,4,7,16,128]{4,3,2,1,0:T(8,128)(2,1)S(1)}, bf16[2,4,7,16,128]{4,3,2,1,0:T(8,128)(2,1)S(1)}, u32[]{:S(2)}, u32[]{:S(2)}) collective-permute-start(bf16[2,4,7,16,128]{4,3,2,1,0:T(8,128)(2,1)S(1)} %collective-permute-done.35.refs_3_), channel_id=1, source_target_pairs={{0,16},{1,17},{2,18},{3,19},{4,20},{5,21},{6,22},{7,23},{8,24},{9,... | collective-permute-start | bytes 688136 | tf_op jit(solution)/shard_map/ppermute | solution.py:266
  (13 other events, 85.1 us)

commit v6 on v5

--- a/solution.py
+++ b/solution.py
@@ -52,10 +52,11 @@
         copy.wait()
 
 
-def taps_kernel(kernel, taps, held, sems):
+def taps_kernel(kernel, taps, back_taps, held, sems):
     (copy,) = copied([(kernel, held)], sems)
     copy.wait()
     lay_taps(taps, held, False)
+    lay_taps(back_taps, held, True)
 
 
 def lay(pad, centre, time, near, far, corners, ahead):
@@ -111,8 +112,7 @@
         t, h = (frame + 2 - a, row + 2 - b) if transposed else (frame + a, row + b)
         parts.append(pad[t, h : h + rows].reshape(rows * columns, channels))
     stacked = jnp.concatenate(parts, axis=1)
-    dims = (((1,), (1 if transposed else 0,)), ((), ()))
-    product = lax.dot_general(stacked, taps[...], dims, preferred_element_type=jnp.float32)
+    product = jnp.dot(stacked, taps[...], preferred_element_type=jnp.float32)
     left, middle, right = (product[:, c * channels : (c + 1) * channels] for c in range(3))
     if transposed:
         left, right = right, left
@@ -123,10 +123,8 @@
     c_in, c_out = kernel.shape[3:]
     for place, (a, b) in enumerate(TAPS):
         for c in range(3):
-            if transposed:
-                taps[c * c_in : (c + 1) * c_in, place * c_out : (place + 1) * c_out] = kernel[a, b, c]
-            else:
-                taps[place * c_in : (place + 1) * c_in, c * c_out : (c + 1) * c_out] = kernel[a, b, c]
+            tap = kernel[a, b, c].T if transposed else kernel[a, b, c]
+            taps[place * c_in : (place + 1) * c_in, c * c_out : (c + 1) * c_out] = tap
 
 
 def blocks(frames, rows):
@@ -145,10 +143,9 @@
 
 
 def second_kernel(
-    centre, time, near, far, corners, kernel, cotangent, output, grad, last, near_out, far_out, pad, taps
+    centre, time, near, far, corners, taps, cotangent, output, grad, last, near_out, far_out, pad
 ):
     lay(pad, centre, time, near, far, corners, False)
-    lay_taps(taps, kernel, False)
     frames, rows = centre.shape[:2]
     for t, rows in blocks(frames, rows):
         z = convolve(pad, taps, t, rows.start, 2, False)
@@ -159,11 +156,10 @@
     strips(grad, last, near_out, far_out, True)
 
 
-def back_kernel(centre, time, near, far, corners, kernel, made, output, grad, ended, pad, taps, sems):
+def back_kernel(centre, time, near, far, corners, taps, made, output, grad, ended, pad, sems):
     copy = pltpu.make_async_copy(made, output, sems.at[0])
     copy.start()
     lay(pad, centre, time, near, far, corners, True)
-    lay_taps(taps, kernel, True)
     frames, rows = centre.shape[:2]
     for t, rows in blocks(frames, rows):
         z = convolve(pad, taps, t, rows.start, 2, True)
@@ -173,10 +169,9 @@
 
 
 def back_slope_kernel(
-    centre, time, near, far, corners, kernel, slope, grad, last, near_out, far_out, pad, taps
+    centre, time, near, far, corners, taps, slope, grad, last, near_out, far_out, pad
 ):
     lay(pad, centre, time, near, far, corners, True)
-    lay_taps(taps, kernel, True)
     frames, rows = centre.shape[:2]
     for t, rows in blocks(frames, rows):
         z = convolve(pad, taps, t, rows.start, 2, True).reshape(2, *grad.shape[2:])
@@ -368,26 +363,22 @@
         cut_kernel, [bf16, last, line, line], [pltpu.SemaphoreType.DMA((4,))], 0, clip, inside=HBM
     )
     clip_edges = cornered(*exchanged(*cut, False), False)
-    (first_taps,) = call(
-        taps_kernel,
-        [jax.ShapeDtypeStruct(taps.shape, taps.dtype)],
-        [pltpu.VMEM(first_weight.shape, first_weight.dtype), pltpu.SemaphoreType.DMA((1,))],
-        0,
-        first_weight,
-        inside=HBM,
-    )
+    layout = jax.ShapeDtypeStruct(taps.shape, taps.dtype)
+    held = [pltpu.VMEM(first_weight.shape, first_weight.dtype), pltpu.SemaphoreType.DMA((1,))]
+    first_taps, first_back = call(taps_kernel, [layout, layout], held, 0, first_weight, inside=HBM)
     slope, hidden, *cut = call(
         first_kernel, [f32, bf16, last, line, line], [pad], flops, whole, *clip_edges, first_taps
     )
     hidden_edges = cornered(*exchanged(*cut, False), False)
+    second_taps, second_back = call(taps_kernel, [layout, layout], held, 0, second_weight, after=cut[1:2], inside=HBM)
     made, grad_two, *cut = call(
         second_kernel,
         [bf16, bf16, last, line, line],
-        [pad, taps],
+        [pad],
         flops,
         hidden,
         *hidden_edges,
-        second_weight,
+        second_taps,
         cotangent,
     )
     two_edges = cornered(*exchanged(*cut, True), True)
@@ -395,11 +386,11 @@
     grad_one, *cut = call(
         back_slope_kernel,
         [bf16, last, line, line],
-        [pad, back_taps],
+        [pad],
         flops,
         grad_two,
         *two_edges,
-        second_weight,
+        second_back,
         slope,
     )
     one_edges = exchanged(*cut, True)
@@ -410,11 +401,11 @@
     output, grad, ended = call(
         back_kernel,
         [bf16, bf16, ended],
-        [pad, back_taps, pltpu.SemaphoreType.DMA((1,))],
+        [pad, pltpu.SemaphoreType.DMA((1,))],
         flops,
         grad_one,
         *one_edges,
-        first_weight,
+        first_back,
         made,
         outside=(HBM,),
     )

time: 113 us -> 112 us (level)
    ppermute x4, starting transfers between devices: 17.2 us -> 14.7 us  [exchanged(): lax.ppermute(far, 'height', [(i, (i - 1 if i % 2 == 0 else i + 1) % line)...]
    ppermute x24, waiting for transfers between devices: 14.8 us -> 13 us  [swap(): lax.ppermute(value, ALL, [(i, i ^ mask) for i in range(lax.axis_size(ALL))])]
    ppermute x4, starting transfers between devices: 9.55 us -> 11.1 us  [cornered(): return (time, near, far, lax.ppermute(rows, 'tm', time_route(ahead)))]
    ppermute x4, waiting for transfers between devices: 1.61 us -> 3.13 us  [exchanged(): lax.ppermute(far, 'height', [(i, (i - 1 if i % 2 == 0 else i + 1) % line)...]
    pallas_call x16 -> x17, Pallas kernels: 17.1 us -> 17.7 us  [call(): pl.pallas_call(run, out_shape=outs, in_specs=[inside] * len(args) + [ANY]...]
  transfers between devices with their start and end apart: 40 -> 40, of which waited for: 16 -> 18; matrix products, arithmetic and copies ran while one was open for 0% -> 0% of each run, Pallas kernels for 9% -> 9%
where the time goes in v6:
time: 112 us
  starting transfers between devices  69.7 us (62%)
  waiting for transfers between devices  21.6 us (19%)
  Pallas kernels  17.7 us (16%)
  local copies, waits for them, and re-layouts  2.16 us (2%)
    ppermute x24, starting transfers between devices, swap(): lax.ppermute(value, ALL, [(i, i ^ mask) for i in range(lax.axis_size(ALL))])  29.4 us
    pallas_call x17, Pallas kernels, call(): pl.pallas_call(run, out_shape=outs, in_specs=[inside] * len(args) + [ANY]...  17.7 us
    ppermute x4, starting transfers between devices, exchanged(): lax.ppermute(far, 'height', [(i, (i - 1 if i % 2 == 0 else i + 1) % line)...  14.7 us
    ppermute x24, waiting for transfers between devices, swap(): lax.ppermute(value, ALL, [(i, i ^ mask) for i in range(lax.axis_size(ALL))])  13 us
    ppermute x4, starting transfers between devices, cornered(): return (time, near, far, lax.ppermute(rows, 'tm', time_route(ahead)))  11.1 us
    ppermute x4, starting transfers between devices, exchanged(): time = lax.ppermute(last, 'tm', time_route(ahead))  10.9 us
    ppermute x4, waiting for transfers between devices, cornered(): return (time, near, far, lax.ppermute(rows, 'tm', time_route(ahead)))  4.91 us
    ppermute x4, starting transfers between devices, exchanged(): near = lax.ppermute(near, 'height', [(i, i ^ 1) for i in range(line)])  3.57 us
  transfers between devices with their start and end apart: 40, of which 18 were waited for; matrix products, arithmetic and copies ran while one was open for 0% of the time, Pallas kernels for 9%

profile of v6, /device:TPU:1, one launch (start us, length us, event | category | flops | bytes accessed | tf_op | source)
XLA Modules:
  0.0 112.2 jit_solution(1835432203365174311)
XLA Ops:
  2.0 2.1 %collective-permute-start.1 = (bf16[3,1,128,128]{3,2,1,0:T(8,128)(2,1)S(1)}, bf16[3,1,128,128]{3,2,1,0:T(8,128)(2,1)S(1)}, u32[]{:S(2)}, u32[]{:S(2)}) collective-permute-start(bf16[3,1,128,128]{3,2,1,0:T(8,128)(2,1)S(1)} %get-tuple-element.51), channel_id=1, source_target_pairs={{0,1},{1,0},{2,3},{3,2},{4,5},{5,4},{6,7},{7,6},{8,9},{9,8},{10,11... | collective-permute-start | bytes 294920 | tf_op jit(solution)/shard_map/ppermute | solution.py:327
  4.1 4.3 %collective-permute-start.2 = (bf16[3,1,128,128]{3,2,1,0:T(8,128)(2,1)S(1)}, bf16[3,1,128,128]{3,2,1,0:T(8,128)(2,1)S(1)}, u32[]{:S(2)}, u32[]{:S(2)}) collective-permute-start(bf16[3,1,128,128]{3,2,1,0:T(8,128)(2,1)S(1)} %get-tuple-element.52), channel_id=1, source_target_pairs={{0,15},{1,2},{2,1},{3,4},{4,3},{5,6},{6,5},{7,8},{8,7},{9,10},{10,... | collective-permute-start | bytes 294920 | tf_op jit(solution)/shard_map/ppermute | solution.py:328
  8.3 4.7 %collective-permute-start = (bf16[2,4,128,128]{3,2,1,0:T(8,128)(2,1)S(1)}, bf16[2,4,128,128]{3,2,1,0:T(8,128)(2,1)S(1)}, u32[]{:S(2)}, u32[]{:S(2)}) collective-permute-start(bf16[2,4,128,128]{3,2,1,0:T(8,128)(2,1)S(1)} %get-tuple-element.50), channel_id=1, source_target_pairs={{0,16},{16,32},{32,48},{48,0},{1,17},{17,33},{33,49},{49,1},{2,18}... | collective-permute-start | bytes 786440 | tf_op jit(solution)/shard_map/ppermute | solution.py:326
  13.1 3.5 %collective-permute-start.3 = (bf16[2,2,128,128]{3,2,1,0:T(8,128)(2,1)S(1)}, bf16[2,2,128,128]{3,2,1,0:T(8,128)(2,1)S(1)}, u32[]{:S(2)}, u32[]{:S(2)}) collective-permute-start(bf16[2,2,128,128]{3,2,1,0:T(8,128)(2,1)S(1)} %pad_maximum_fusion.2), channel_id=1, source_target_pairs={{0,16},{16,32},{32,48},{48,0},{1,17},{17,33},{33,49},{49,1},{2,18}... | collective-permute-start | bytes 393224 | tf_op jit(solution)/shard_map/ppermute | solution.py:340
  18.5 2.3 %shard_map.77 = (f32[3,4,128,128]{3,2,1,0:T(8,128)S(1)}, bf16[3,4,128,128]{3,2,1,0:T(8,128)(2,1)S(1)}, bf16[2,4,128,128]{3,2,1,0:T(8,128)(2,1)S(1)}, bf16[3,1,12...) custom-call(bf16[3,4,128,128]{3,2,1,0:T(8,128)(2,1)S(1)} %get-tuple-element.49.refs_0_, ...), custom_call_target="tpu_custom_call" | custom-call | flops 1358954496 | bytes 3506176 | tf_op jit(solution)/shard_map/pallas_call | solution.py:25
  20.8 4.3 %collective-permute-start.6 = (bf16[3,1,128,128]{3,2,1,0:T(8,128)(2,1)S(1)}, bf16[3,1,128,128]{3,2,1,0:T(8,128)(2,1)S(1)}, u32[]{:S(2)}, u32[]{:S(2)}) collective-permute-start(bf16[3,1,128,128]{3,2,1,0:T(8,128)(2,1)S(1)} %get-tuple-element.57), channel_id=1, source_target_pairs={{0,15},{1,2},{2,1},{3,4},{4,3},{5,6},{6,5},{7,8},{8,7},{9,10},{10,... | collective-permute-start | bytes 294920 | tf_op jit(solution)/shard_map/ppermute | solution.py:328
  25.1 4.2 %collective-permute-start.4 = (bf16[2,4,128,128]{3,2,1,0:T(8,128)(2,1)S(1)}, bf16[2,4,128,128]{3,2,1,0:T(8,128)(2,1)S(1)}, u32[]{:S(2)}, u32[]{:S(2)}) collective-permute-start(bf16[2,4,128,128]{3,2,1,0:T(8,128)(2,1)S(1)} %get-tuple-element.55), channel_id=1, source_target_pairs={{0,16},{16,32},{32,48},{48,0},{1,17},{17,33},{33,49},{49,1},{2,18}... | collective-permute-start | bytes 786440 | tf_op jit(solution)/shard_map/ppermute | solution.py:326
  29.4 4.7 %collective-permute-start.7 = (bf16[2,2,128,128]{3,2,1,0:T(8,128)(2,1)S(1)}, bf16[2,2,128,128]{3,2,1,0:T(8,128)(2,1)S(1)}, u32[]{:S(2)}, u32[]{:S(2)}) collective-permute-start(bf16[2,2,128,128]{3,2,1,0:T(8,128)(2,1)S(1)} %pad_maximum_fusion.1), channel_id=1, source_target_pairs={{0,16},{16,32},{32,48},{48,0},{1,17},{17,33},{33,49},{49,1},{2,18}... | collective-permute-start | bytes 393224 | tf_op jit(solution)/shard_map/ppermute | solution.py:340
  36.0 2.3 %shard_map.79 = (bf16[3,4,128,128]{3,2,1,0:T(8,128)(2,1)S(1)}, bf16[3,4,128,128]{3,2,1,0:T(8,128)(2,1)S(1)}, bf16[2,4,128,128]{3,2,1,0:T(8,128)(2,1)S(1)}, bf16[...) custom-call(bf16[3,4,128,128]{3,2,1,0:T(8,128)(2,1)S(1)} %get-tuple-element.54.refs_0_, ...), custom_call_target="tpu_custom_call" | custom-call | flops 1358954496 | bytes 3506176 | tf_op jit(solution)/shard_map/pallas_call | solution.py:25
  38.4 3.1 %collective-permute-start.10 = (bf16[3,1,128,128]{3,2,1,0:T(8,128)(2,1)S(1)}, bf16[3,1,128,128]{3,2,1,0:T(8,128)(2,1)S(1)}, u32[]{:S(2)}, u32[]{:S(2)}) collective-permute-start(bf16[3,1,128,128]{3,2,1,0:T(8,128)(2,1)S(1)} %get-tuple-element.62), channel_id=1, source_target_pairs={{0,15},{1,2},{2,1},{3,4},{4,3},{5,6},{6,5},{7,8},{8,7},{9,10},{10,... | collective-permute-start | bytes 294920 | tf_op jit(solution)/shard_map/ppermute | solution.py:328
  42.5 3.1 %collective-permute-done.10.refs_3_ = bf16[3,1,128,128]{3,2,1,0:T(8,128)(2,1)S(1)} collective-permute-done((bf16[3,1,128,128]{3,2,1,0:T(8,128)(2,1)S(1)}, bf16[3,1,128,128]{3,2,1,0:T(8,128)(2,1)S(1)}, u32[]{:S(2)}, u32[]{:S(2)}) %collective-permute-start.10) | collective-permute-done | bytes 98336 | tf_op jit(solution)/shard_map/ppermute | solution.py:328
  45.6 1.5 %collective-permute-start.11 = (bf16[2,2,128,128]{3,2,1,0:T(8,128)(2,1)S(1)}, bf16[2,2,128,128]{3,2,1,0:T(8,128)(2,1)S(1)}, u32[]{:S(2)}, u32[]{:S(2)}) collective-permute-start(bf16[2,2,128,128]{3,2,1,0:T(8,128)(2,1)S(1)} %pad_maximum_fusion), channel_id=1, source_target_pairs={{0,48},{16,0},{32,16},{48,32},{1,49},{17,1},{33,17},{49,33},{2,50}... | collective-permute-start | bytes 393224 | tf_op jit(solution)/shard_map/ppermute | solution.py:340
  47.1 2.4 %shard_map.82 = (f32[4,28,16,128]{3,2,1,0:T(8,128)S(1)}, bf16[4,28,16,128]{3,2,1,0:T(8,128)(2,1)S(1)}) custom-call(bf16[3,4,128,128]{3,2,1,0:T(8,128)(2,1)S(1)} %get-tuple-element.54.refs_0_, bf16[2,4,128,128]{3,2,1,0:T(8,128)(2,1)S(1)} %collective-permute-done.4.refs_1_, bf16[3,1,128,128]{3,2,1,0:T(8,128)(2,1)S(1)} %collective-permute-done.5.refs_2_, ...), custom_call_target="tpu_custom_call" | custom-call | flops 1358954496 | bytes 2752512 | tf_op jit(solution)/shard_map/pallas_call | solution.py:25
  49.7 3.4 %collective-permute-done.11.refs_4_ = bf16[2,2,128,128]{3,2,1,0:T(8,128)(2,1)S(1)} collective-permute-done((bf16[2,2,128,128]{3,2,1,0:T(8,128)(2,1)S(1)}, bf16[2,2,128,128]{3,2,1,0:T(8,128)(2,1)S(1)}, u32[]{:S(2)}, u32[]{:S(2)}) %collective-permute-start.11) | collective-permute-done | bytes 131104 | tf_op jit(solution)/shard_map/ppermute | solution.py:340
  53.2 2.3 %shard_map.80 = (bf16[3,4,128,128]{3,2,1,0:T(8,128)(2,1)S(1)}, bf16[2,4,128,128]{3,2,1,0:T(8,128)(2,1)S(1)}, bf16[3,1,128,128]{3,2,1,0:T(8,128)(2,1)S(1)}, bf16[3,1,128,128]{3,2,1,0:T(8,128)(2,1)S(1)}) custom-call(bf16[3,4,128,128]{3,2,1,0:T(8,128)(2,1)S(1)} %get-tuple-element.59.refs_0_.refs_5_, ...), custom_call_target="tpu_custom_call" | custom-call | flops 1358954496 | bytes 3506176 | tf_op jit(solution)/shard_map/pallas_call | solution.py:25
  55.5 2.3 %shard_map.81 = (f32[4,28,16,128]{3,2,1,0:T(8,128)S(1)}, bf16[4,28,16,128]{3,2,1,0:T(8,128)(2,1)S(1)}) custom-call(bf16[3,4,128,128]{3,2,1,0:T(8,128)(2,1)S(1)} %get-tuple-element.49.refs_0_, bf16[2,4,128,128]{3,2,1,0:T(8,128)(2,1)S(1)} %collective-permute-done.refs_1_, bf16[3,1,128,128]{3,2,1,0:T(8,128)(2,1)S(1)} %collective-permute-done.1.refs_2_, ...), custom_call_target="tpu_custom_call" | custom-call | flops 1358954496 | bytes 2752512 | tf_op jit(solution)/shard_map/pallas_call | solution.py:25
  57.8 1.8 %collective-permute-done.15.refs_1_ = bf16[4,28,16,128]{3,2,1,0:T(8,128)(2,1)S(1)} collective-permute-done((bf16[4,28,16,128]{3,2,1,0:T(8,128)(2,1)S(1)}, bf16[4,28,16,128]{3,2,1,0:T(8,128)(2,1)S(1)}, u32[]{:S(2)}, u32[]{:S(2)}) %collective-permute-start.15) | collective-permute-done | bytes 458784 | tf_op jit(solution)/shard_map/ppermute | solution.py:261
  61.3 3.0 %collective-permute-start.14 = (bf16[3,1,128,128]{3,2,1,0:T(8,128)(2,1)S(1)}, bf16[3,1,128,128]{3,2,1,0:T(8,128)(2,1)S(1)}, u32[]{:S(2)}, u32[]{:S(2)}) collective-permute-start(bf16[3,1,128,128]{3,2,1,0:T(8,128)(2,1)S(1)} %get-tuple-element.68), channel_id=1, source_target_pairs={{0,15},{1,2},{2,1},{3,4},{4,3},{5,6},{6,5},{7,8},{8,7},{9,10},{10,... | collective-permute-start | bytes 294920 | tf_op jit(solution)/shard_map/ppermute | solution.py:328
  66.6 2.0 %collective-permute-start.21 = (bf16[4,7,16,128]{3,2,1,0:T(8,128)(2,1)S(1)}, bf16[4,7,16,128]{3,2,1,0:T(8,128)(2,1)S(1)}, u32[]{:S(2)}, u32[]{:S(2)}) collective-permute-start(bf16[4,7,16,128]{3,2,1,0:T(8,128)(2,1)S(1)} %get-tuple-element.82), channel_id=1, source_target_pairs={{0,3},{1,2},{2,1},{3,0},{4,7},{5,6},{6,5},{7,4},{8,11},{9,10},{10,... | collective-permute-start | bytes 344072 | tf_op jit(solution)/shard_map/ppermute | solution.py:261
  69.4 1.5 %collective-permute-start.17 = (bf16[2,2,128,128]{3,2,1,0:T(8,128)(2,1)S(1)}, bf16[2,2,128,128]{3,2,1,0:T(8,128)(2,1)S(1)}, u32[]{:S(2)}, u32[]{:S(2)}) collective-permute-start(bf16[2,2,128,128]{3,2,1,0:T(8,128)(2,1)S(1)} %shard_map.84), channel_id=1, source_target_pairs={{0,48},{16,0},{32,16},{48,32},{1,49},{17,1},{33,17},{49,33},{2,50}... | collective-permute-start | bytes 393224 | tf_op jit(solution)/shard_map/ppermute | solution.py:340
  70.9 1.7 %collective-permute-done.21.refs_2_ = bf16[4,7,16,128]{3,2,1,0:T(8,128)(2,1)S(1)} collective-permute-done((bf16[4,7,16,128]{3,2,1,0:T(8,128)(2,1)S(1)}, bf16[4,7,16,128]{3,2,1,0:T(8,128)(2,1)S(1)}, u32[]{:S(2)}, u32[]{:S(2)}) %collective-permute-start.21) | collective-permute-done | bytes 114720 | tf_op jit(solution)/shard_map/ppermute | solution.py:261
  72.6 3.0 %collective-permute-start.24 = (bf16[2,7,16,128]{3,2,1,0:T(8,128)(2,1)S(1)}, bf16[2,7,16,128]{3,2,1,0:T(8,128)(2,1)S(1)}, u32[]{:S(2)}, u32[]{:S(2)}) collective-permute-start(bf16[2,7,16,128]{3,2,1,0:T(8,128)(2,1)S(1)} %get-tuple-element.86), channel_id=1, source_target_pairs={{0,8},{1,9},{2,10},{3,11},{4,12},{5,13},{6,14},{7,15},{8,0},{9,1},... | collective-permute-start | bytes 172040 | tf_op jit(solution)/shard_map/ppermute | solution.py:261
  80.1 3.1 %collective-permute-start.28 = (bf16[2,7,16,128]{3,2,1,0:T(8,128)(2,1)S(1)}, bf16[2,7,16,128]{3,2,1,0:T(8,128)(2,1)S(1)}, u32[]{:S(2)}, u32[]{:S(2)}) collective-permute-start(bf16[2,7,16,128]{3,2,1,0:T(8,128)(2,1)S(1)} %shard_map.88.refs_0_), channel_id=1, source_target_pairs={{0,96},{1,97},{2,98},{3,99},{4,100},{5,101},{6,102},{7,103},{8,104... | collective-permute-start | bytes 172040 | tf_op jit(solution)/shard_map/ppermute | solution.py:261
  83.2 2.2 %shard_map.85 = (bf16[3,4,128,128]{3,2,1,0:T(8,128)(2,1)}, bf16[3,4,128,128]{3,2,1,0:T(8,128)(2,1)S(1)}, f32[8,128]{1,0:T(8,128)S(1)}) custom-call(bf16[3,4,128,128]{3,2,1,0:T(8,128)(2,1)S(1)} %get-tuple-element.65.refs_5_.refs_0_, bf16[2,4,128,128]{3,2,1,0:T(8,128)(2,1)S(1)} %collective-permute-done.12.refs_1_, ...), custom_call_target="tpu_custom_call" | custom-call | flops 1358954496 | bytes 3051520 | tf_op jit(solution)/shard_map/pallas_call | solution.py:25
  86.2 2.3 %collective-permute-start.32 = (bf16[2,7,16,128]{3,2,1,0:T(8,128)(2,1)S(1)}, bf16[2,7,16,128]{3,2,1,0:T(8,128)(2,1)S(1)}, u32[]{:S(2)}, u32[]{:S(2)}) collective-permute-start(bf16[2,7,16,128]{3,2,1,0:T(8,128)(2,1)S(1)} %shard_map.89.refs_0_), channel_id=1, source_target_pairs={{0,8},{1,9},{2,10},{3,11},{4,12},{5,13},{6,14},{7,15},{8,0},{9,1},... | collective-permute-start | bytes 172040 | tf_op jit(solution)/shard_map/ppermute | solution.py:261
  88.6 1.6 %collective-permute-start.31 = (bf16[2,7,16,128]{3,2,1,0:T(8,128)(2,1)S(1)}, bf16[2,7,16,128]{3,2,1,0:T(8,128)(2,1)S(1)}, u32[]{:S(2)}, u32[]{:S(2)}) collective-permute-start(bf16[2,7,16,128]{3,2,1,0:T(8,128)(2,1)S(1)} %shard_map.89.refs_0_), channel_id=1, source_target_pairs={{0,12},{1,13},{2,14},{3,15},{4,8},{5,9},{6,10},{7,11},{8,4},{9,5},... | collective-permute-start | bytes 172040 | tf_op jit(solution)/shard_map/ppermute | solution.py:261
  90.8 2.0 %collective-permute-done.31.refs_2_ = bf16[2,7,16,128]{3,2,1,0:T(8,128)(2,1)S(1)} collective-permute-done((bf16[2,7,16,128]{3,2,1,0:T(8,128)(2,1)S(1)}, bf16[2,7,16,128]{3,2,1,0:T(8,128)(2,1)S(1)}, u32[]{:S(2)}, u32[]{:S(2)}) %collective-permute-start.31) | collective-permute-done | bytes 57376 | tf_op jit(solution)/shard_map/ppermute | solution.py:261
  94.1 1.6 %collective-permute-start.34 = (bf16[2,4,7,16,128]{4,3,2,1,0:T(8,128)(2,1)S(1)}, bf16[2,4,7,16,128]{4,3,2,1,0:T(8,128)(2,1)S(1)}, u32[]{:S(2)}, u32[]{:S(2)}) collective-permute-start(bf16[2,4,7,16,128]{4,3,2,1,0:T(8,128)(2,1)S(1)} %shard_map.90.refs_0_), channel_id=1, source_target_pairs={{0,3},{1,2},{2,1},{3,0},{4,7},{5,6},{6,5},{7,4},{8,11},{9,10},{10,... | collective-permute-start | bytes 688136 | tf_op jit(solution)/shard_map/ppermute | solution.py:261
  95.9 6.1 %collective-permute-start.36 = (bf16[2,4,7,16,128]{4,3,2,1,0:T(8,128)(2,1)S(1)}, bf16[2,4,7,16,128]{4,3,2,1,0:T(8,128)(2,1)S(1)}, u32[]{:S(2)}, u32[]{:S(2)}) collective-permute-start(bf16[2,4,7,16,128]{4,3,2,1,0:T(8,128)(2,1)S(1)} %shard_map.90.refs_0_), channel_id=1, source_target_pairs={{0,16},{1,17},{2,18},{3,19},{4,20},{5,21},{6,22},{7,23},{8,24},{9,... | collective-permute-start | bytes 688136 | tf_op jit(solution)/shard_map/ppermute | solution.py:261
  102.1 4.1 %collective-permute-start.39 = (bf16[2,4,7,16,128]{4,3,2,1,0:T(8,128)(2,1)S(1)}, bf16[2,4,7,16,128]{4,3,2,1,0:T(8,128)(2,1)S(1)}, u32[]{:S(2)}, u32[]{:S(2)}) collective-permute-start(bf16[2,4,7,16,128]{4,3,2,1,0:T(8,128)(2,1)S(1)} %collective-permute-done.35.refs_3_), channel_id=1, source_target_pairs={{0,16},{1,17},{2,18},{3,19},{4,20},{5,21},{6,22},{7,23},{8,24},{9,... | collective-permute-start | bytes 688136 | tf_op jit(solution)/shard_map/ppermute | solution.py:261
  106.2 2.4 %collective-permute-start.38 = (bf16[2,4,7,16,128]{4,3,2,1,0:T(8,128)(2,1)S(1)}, bf16[2,4,7,16,128]{4,3,2,1,0:T(8,128)(2,1)S(1)}, u32[]{:S(2)}, u32[]{:S(2)}) collective-permute-start(bf16[2,4,7,16,128]{4,3,2,1,0:T(8,128)(2,1)S(1)} %collective-permute-done.34.refs_2_), channel_id=1, source_target_pairs={{0,16},{1,17},{2,18},{3,19},{4,20},{5,21},{6,22},{7,23},{8,24},{9,... | collective-permute-start | bytes 688136 | tf_op jit(solution)/shard_map/ppermute | solution.py:261
  110.0 2.0 %shard_map.91 = (f32[27,8,16,128]{3,2,1,0:T(8,128)}, f32[27,8,16,128]{3,2,1,0:T(8,128)}, bf16[3,4,128,128]{3,2,1,0:T(8,128)(2,1)}) custom-call(bf16[2,4,7,16,128]{4,3,2,1,0:T(8,128)(2,1)S(1)} %shard_map.90.refs_0_, bf16[2,4,7,16,128]{4,3,2,1,0:T(8,128)(2,1)S(1)} %collective-permute-done.33.refs_1_, ...), custom_call_target="tpu_custom_call" | custom-call | flops 917504 | bytes 6160384 | tf_op jit(solution)/shard_map/pallas_call | solution.py:25
  (76 shorter events, 20.2 us)
Async XLA Ops:
  2.0 11.1 %collective-permute-start.1 = (bf16[3,1,128,128]{3,2,1,0:T(8,128)(2,1)S(1)}, bf16[3,1,128,128]{3,2,1,0:T(8,128)(2,1)S(1)}, u32[]{:S(2)}, u32[]{:S(2)}) collective-permute-start(bf16[3,1,128,128]{3,2,1,0:T(8,128)(2,1)S(1)} %get-tuple-element.51), channel_id=1, source_target_pairs={{0,1},{1,0},{2,3},{3,2},{4,5},{5,4},{6,7},{7,6},{8,9},{9,8},{10,11... | collective-permute-start | bytes 294920 | tf_op jit(solution)/shard_map/ppermute | solution.py:327
  4.1 9.0 %collective-permute-start.2 = (bf16[3,1,128,128]{3,2,1,0:T(8,128)(2,1)S(1)}, bf16[3,1,128,128]{3,2,1,0:T(8,128)(2,1)S(1)}, u32[]{:S(2)}, u32[]{:S(2)}) collective-permute-start(bf16[3,1,128,128]{3,2,1,0:T(8,128)(2,1)S(1)} %get-tuple-element.52), channel_id=1, source_target_pairs={{0,15},{1,2},{2,1},{3,4},{4,3},{5,6},{6,5},{7,8},{8,7},{9,10},{10,... | collective-permute-start | bytes 294920 | tf_op jit(solution)/shard_map/ppermute | solution.py:328
  8.3 10.1 %collective-permute-start = (bf16[2,4,128,128]{3,2,1,0:T(8,128)(2,1)S(1)}, bf16[2,4,128,128]{3,2,1,0:T(8,128)(2,1)S(1)}, u32[]{:S(2)}, u32[]{:S(2)}) collective-permute-start(bf16[2,4,128,128]{3,2,1,0:T(8,128)(2,1)S(1)} %get-tuple-element.50), channel_id=1, source_target_pairs={{0,16},{16,32},{32,48},{48,0},{1,17},{17,33},{33,49},{49,1},{2,18}... | collective-permute-start | bytes 786440 | tf_op jit(solution)/shard_map/ppermute | solution.py:326
  13.1 5.4 %collective-permute-start.3 = (bf16[2,2,128,128]{3,2,1,0:T(8,128)(2,1)S(1)}, bf16[2,2,128,128]{3,2,1,0:T(8,128)(2,1)S(1)}, u32[]{:S(2)}, u32[]{:S(2)}) collective-permute-start(bf16[2,2,128,128]{3,2,1,0:T(8,128)(2,1)S(1)} %pad_maximum_fusion.2), channel_id=1, source_target_pairs={{0,16},{16,32},{32,48},{48,0},{1,17},{17,33},{33,49},{49,1},{2,18}... | collective-permute-start | bytes 393224 | tf_op jit(solution)/shard_map/ppermute | solution.py:340
  20.8 8.6 %collective-permute-start.6 = (bf16[3,1,128,128]{3,2,1,0:T(8,128)(2,1)S(1)}, bf16[3,1,128,128]{3,2,1,0:T(8,128)(2,1)S(1)}, u32[]{:S(2)}, u32[]{:S(2)}) collective-permute-start(bf16[3,1,128,128]{3,2,1,0:T(8,128)(2,1)S(1)} %get-tuple-element.57), channel_id=1, source_target_pairs={{0,15},{1,2},{2,1},{3,4},{4,3},{5,6},{6,5},{7,8},{8,7},{9,10},{10,... | collective-permute-start | bytes 294920 | tf_op jit(solution)/shard_map/ppermute | solution.py:328
  25.1 4.2 %collective-permute-start.5 = (bf16[3,1,128,128]{3,2,1,0:T(8,128)(2,1)S(1)}, bf16[3,1,128,128]{3,2,1,0:T(8,128)(2,1)S(1)}, u32[]{:S(2)}, u32[]{:S(2)}) collective-permute-start(bf16[3,1,128,128]{3,2,1,0:T(8,128)(2,1)S(1)} %get-tuple-element.56.refs_1_), channel_id=1, source_target_pairs={{0,1},{1,0},{2,3},{3,2},{4,5},{5,4},{6,7},{7,6},{8,9},{9,8},{10,11... | collective-permute-start | bytes 294920 | tf_op jit(solution)/shard_map/ppermute | solution.py:327
  25.1 10.9 %collective-permute-start.4 = (bf16[2,4,128,128]{3,2,1,0:T(8,128)(2,1)S(1)}, bf16[2,4,128,128]{3,2,1,0:T(8,128)(2,1)S(1)}, u32[]{:S(2)}, u32[]{:S(2)}) collective-permute-start(bf16[2,4,128,128]{3,2,1,0:T(8,128)(2,1)S(1)} %get-tuple-element.55), channel_id=1, source_target_pairs={{0,16},{16,32},{32,48},{48,0},{1,17},{17,33},{33,49},{49,1},{2,18}... | collective-permute-start | bytes 786440 | tf_op jit(solution)/shard_map/ppermute | solution.py:326
  29.4 6.6 %collective-permute-start.7 = (bf16[2,2,128,128]{3,2,1,0:T(8,128)(2,1)S(1)}, bf16[2,2,128,128]{3,2,1,0:T(8,128)(2,1)S(1)}, u32[]{:S(2)}, u32[]{:S(2)}) collective-permute-start(bf16[2,2,128,128]{3,2,1,0:T(8,128)(2,1)S(1)} %pad_maximum_fusion.1), channel_id=1, source_target_pairs={{0,16},{16,32},{32,48},{48,0},{1,17},{17,33},{33,49},{49,1},{2,18}... | collective-permute-start | bytes 393224 | tf_op jit(solution)/shard_map/ppermute | solution.py:340
  38.4 4.1 %collective-permute-start.9 = (bf16[3,1,128,128]{3,2,1,0:T(8,128)(2,1)S(1)}, bf16[3,1,128,128]{3,2,1,0:T(8,128)(2,1)S(1)}, u32[]{:S(2)}, u32[]{:S(2)}) collective-permute-start(bf16[3,1,128,128]{3,2,1,0:T(8,128)(2,1)S(1)} %get-tuple-element.61), channel_id=1, source_target_pairs={{0,1},{1,0},{2,3},{3,2},{4,5},{5,4},{6,7},{7,6},{8,9},{9,8},{10,11... | collective-permute-start | bytes 294920 | tf_op jit(solution)/shard_map/ppermute | solution.py:327
  38.4 7.2 %collective-permute-start.10 = (bf16[3,1,128,128]{3,2,1,0:T(8,128)(2,1)S(1)}, bf16[3,1,128,128]{3,2,1,0:T(8,128)(2,1)S(1)}, u32[]{:S(2)}, u32[]{:S(2)}) collective-permute-start(bf16[3,1,128,128]{3,2,1,0:T(8,128)(2,1)S(1)} %get-tuple-element.62), channel_id=1, source_target_pairs={{0,15},{1,2},{2,1},{3,4},{4,3},{5,6},{6,5},{7,8},{8,7},{9,10},{10,... | collective-permute-start | bytes 294920 | tf_op jit(solution)/shard_map/ppermute | solution.py:328
  41.6 11.6 %collective-permute-start.8 = (bf16[2,4,128,128]{3,2,1,0:T(8,128)(2,1)S(1)}, bf16[2,4,128,128]{3,2,1,0:T(8,128)(2,1)S(1)}, u32[]{:S(2)}, u32[]{:S(2)}) collective-permute-start(bf16[2,4,128,128]{3,2,1,0:T(8,128)(2,1)S(1)} %get-tuple-element.60), channel_id=1, source_target_pairs={{0,48},{16,0},{32,16},{48,32},{1,49},{17,1},{33,17},{49,33},{2,50}... | collective-permute-start | bytes 786440 | tf_op jit(solution)/shard_map/ppermute | solution.py:326
  45.6 7.5 %collective-permute-start.11 = (bf16[2,2,128,128]{3,2,1,0:T(8,128)(2,1)S(1)}, bf16[2,2,128,128]{3,2,1,0:T(8,128)(2,1)S(1)}, u32[]{:S(2)}, u32[]{:S(2)}) collective-permute-start(bf16[2,2,128,128]{3,2,1,0:T(8,128)(2,1)S(1)} %pad_maximum_fusion), channel_id=1, source_target_pairs={{0,48},{16,0},{32,16},{48,32},{1,49},{17,1},{33,17},{49,33},{2,50}... | collective-permute-start | bytes 393224 | tf_op jit(solution)/shard_map/ppermute | solution.py:340
  49.6 8.2 %collective-permute-start.16 = (bf16[4,28,16,128]{3,2,1,0:T(8,128)(2,1)S(1)}, bf16[4,28,16,128]{3,2,1,0:T(8,128)(2,1)S(1)}, u32[]{:S(2)}, u32[]{:S(2)}) collective-permute-start(bf16[4,28,16,128]{3,2,1,0:T(8,128)(2,1)S(1)} %get-tuple-element.72), channel_id=1, source_target_pairs={{0,16},{1,17},{2,18},{3,19},{4,20},{5,21},{6,22},{7,23},{8,24},{9,... | collective-permute-start | bytes 1376264 | tf_op jit(solution)/shard_map/ppermute | solution.py:261
  59.8 5.6 %collective-permute-start.19 = (bf16[4,7,16,128]{3,2,1,0:T(8,128)(2,1)S(1)}, bf16[4,7,16,128]{3,2,1,0:T(8,128)(2,1)S(1)}, u32[]{:S(2)}, u32[]{:S(2)}) collective-permute-start(bf16[4,7,16,128]{3,2,1,0:T(8,128)(2,1)S(1)} %get-tuple-element.80), channel_id=1, source_target_pairs={{0,1},{1,0},{2,3},{3,2},{4,5},{5,4},{6,7},{7,6},{8,9},{9,8},{10,11... | collective-permute-start | bytes 344072 | tf_op jit(solution)/shard_map/ppermute | solution.py:261
  59.9 5.9 %collective-permute-start.20 = (bf16[4,7,16,128]{3,2,1,0:T(8,128)(2,1)S(1)}, bf16[4,7,16,128]{3,2,1,0:T(8,128)(2,1)S(1)}, u32[]{:S(2)}, u32[]{:S(2)}) collective-permute-start(bf16[4,7,16,128]{3,2,1,0:T(8,128)(2,1)S(1)} %get-tuple-element.81), channel_id=1, source_target_pairs={{0,3},{1,2},{2,1},{3,0},{4,7},{5,6},{6,5},{7,4},{8,11},{9,10},{10,... | collective-permute-start | bytes 344072 | tf_op jit(solution)/shard_map/ppermute | solution.py:261
  59.9 6.6 %collective-permute-start.13 = (bf16[3,1,128,128]{3,2,1,0:T(8,128)(2,1)S(1)}, bf16[3,1,128,128]{3,2,1,0:T(8,128)(2,1)S(1)}, u32[]{:S(2)}, u32[]{:S(2)}) collective-permute-start(bf16[3,1,128,128]{3,2,1,0:T(8,128)(2,1)S(1)} %get-tuple-element.67), channel_id=1, source_target_pairs={{0,1},{1,0},{2,3},{3,2},{4,5},{5,4},{6,7},{7,6},{8,9},{9,8},{10,11... | collective-permute-start | bytes 294920 | tf_op jit(solution)/shard_map/ppermute | solution.py:327
  61.3 7.3 %collective-permute-start.14 = (bf16[3,1,128,128]{3,2,1,0:T(8,128)(2,1)S(1)}, bf16[3,1,128,128]{3,2,1,0:T(8,128)(2,1)S(1)}, u32[]{:S(2)}, u32[]{:S(2)}) collective-permute-start(bf16[3,1,128,128]{3,2,1,0:T(8,128)(2,1)S(1)} %get-tuple-element.68), channel_id=1, source_target_pairs={{0,15},{1,2},{2,1},{3,4},{4,3},{5,6},{6,5},{7,8},{8,7},{9,10},{10,... | collective-permute-start | bytes 294920 | tf_op jit(solution)/shard_map/ppermute | solution.py:328
  64.3 18.9 %collective-permute-start.12 = (bf16[2,4,128,128]{3,2,1,0:T(8,128)(2,1)S(1)}, bf16[2,4,128,128]{3,2,1,0:T(8,128)(2,1)S(1)}, u32[]{:S(2)}, u32[]{:S(2)}) collective-permute-start(bf16[2,4,128,128]{3,2,1,0:T(8,128)(2,1)S(1)} %get-tuple-element.66), channel_id=1, source_target_pairs={{0,48},{16,0},{32,16},{48,32},{1,49},{17,1},{33,17},{49,33},{2,50}... | collective-permute-start | bytes 786440 | tf_op jit(solution)/shard_map/ppermute | solution.py:326
  65.8 5.1 %collective-permute-start.23 = (bf16[4,7,16,128]{3,2,1,0:T(8,128)(2,1)S(1)}, bf16[4,7,16,128]{3,2,1,0:T(8,128)(2,1)S(1)}, u32[]{:S(2)}, u32[]{:S(2)}) collective-permute-start(bf16[4,7,16,128]{3,2,1,0:T(8,128)(2,1)S(1)} %get-tuple-element.84), channel_id=1, source_target_pairs={{0,3},{1,2},{2,1},{3,0},{4,7},{5,6},{6,5},{7,4},{8,11},{9,10},{10,... | collective-permute-start | bytes 344072 | tf_op jit(solution)/shard_map/ppermute | solution.py:261
  66.6 6.0 %collective-permute-start.21 = (bf16[4,7,16,128]{3,2,1,0:T(8,128)(2,1)S(1)}, bf16[4,7,16,128]{3,2,1,0:T(8,128)(2,1)S(1)}, u32[]{:S(2)}, u32[]{:S(2)}) collective-permute-start(bf16[4,7,16,128]{3,2,1,0:T(8,128)(2,1)S(1)} %get-tuple-element.82), channel_id=1, source_target_pairs={{0,3},{1,2},{2,1},{3,0},{4,7},{5,6},{6,5},{7,4},{8,11},{9,10},{10,... | collective-permute-start | bytes 344072 | tf_op jit(solution)/shard_map/ppermute | solution.py:261
  69.4 7.5 %collective-permute-start.17 = (bf16[2,2,128,128]{3,2,1,0:T(8,128)(2,1)S(1)}, bf16[2,2,128,128]{3,2,1,0:T(8,128)(2,1)S(1)}, u32[]{:S(2)}, u32[]{:S(2)}) collective-permute-start(bf16[2,2,128,128]{3,2,1,0:T(8,128)(2,1)S(1)} %shard_map.84), channel_id=1, source_target_pairs={{0,48},{16,0},{32,16},{48,32},{1,49},{17,1},{33,17},{49,33},{2,50}... | collective-permute-start | bytes 393224 | tf_op jit(solution)/shard_map/ppermute | solution.py:340
  72.6 4.6 %collective-permute-start.24 = (bf16[2,7,16,128]{3,2,1,0:T(8,128)(2,1)S(1)}, bf16[2,7,16,128]{3,2,1,0:T(8,128)(2,1)S(1)}, u32[]{:S(2)}, u32[]{:S(2)}) collective-permute-start(bf16[2,7,16,128]{3,2,1,0:T(8,128)(2,1)S(1)} %get-tuple-element.86), channel_id=1, source_target_pairs={{0,8},{1,9},{2,10},{3,11},{4,12},{5,13},{6,14},{7,15},{8,0},{9,1},... | collective-permute-start | bytes 172040 | tf_op jit(solution)/shard_map/ppermute | solution.py:261
  75.7 4.2 %collective-permute-start.26 = (bf16[2,7,16,128]{3,2,1,0:T(8,128)(2,1)S(1)}, bf16[2,7,16,128]{3,2,1,0:T(8,128)(2,1)S(1)}, u32[]{:S(2)}, u32[]{:S(2)}) collective-permute-start(bf16[2,7,16,128]{3,2,1,0:T(8,128)(2,1)S(1)} %get-tuple-element.88), channel_id=1, source_target_pairs={{0,12},{1,13},{2,14},{3,15},{4,8},{5,9},{6,10},{7,11},{8,4},{9,5},... | collective-permute-start | bytes 172040 | tf_op jit(solution)/shard_map/ppermute | solution.py:261
  80.0 5.4 %collective-permute-start.29 = (bf16[2,7,16,128]{3,2,1,0:T(8,128)(2,1)S(1)}, bf16[2,7,16,128]{3,2,1,0:T(8,128)(2,1)S(1)}, u32[]{:S(2)}, u32[]{:S(2)}) collective-permute-start(bf16[2,7,16,128]{3,2,1,0:T(8,128)(2,1)S(1)} %shard_map.88.refs_0_), channel_id=1, source_target_pairs={{0,32},{1,33},{2,34},{3,35},{4,36},{5,37},{6,38},{7,39},{8,40},{9,... | collective-permute-start | bytes 172040 | tf_op jit(solution)/shard_map/ppermute | solution.py:261
  80.1 5.4 %collective-permute-start.28 = (bf16[2,7,16,128]{3,2,1,0:T(8,128)(2,1)S(1)}, bf16[2,7,16,128]{3,2,1,0:T(8,128)(2,1)S(1)}, u32[]{:S(2)}, u32[]{:S(2)}) collective-permute-start(bf16[2,7,16,128]{3,2,1,0:T(8,128)(2,1)S(1)} %shard_map.88.refs_0_), channel_id=1, source_target_pairs={{0,96},{1,97},{2,98},{3,99},{4,100},{5,101},{6,102},{7,103},{8,104... | collective-permute-start | bytes 172040 | tf_op jit(solution)/shard_map/ppermute | solution.py:261
  86.2 4.6 %collective-permute-start.32 = (bf16[2,7,16,128]{3,2,1,0:T(8,128)(2,1)S(1)}, bf16[2,7,16,128]{3,2,1,0:T(8,128)(2,1)S(1)}, u32[]{:S(2)}, u32[]{:S(2)}) collective-permute-start(bf16[2,7,16,128]{3,2,1,0:T(8,128)(2,1)S(1)} %shard_map.89.refs_0_), channel_id=1, source_target_pairs={{0,8},{1,9},{2,10},{3,11},{4,12},{5,13},{6,14},{7,15},{8,0},{9,1},... | collective-permute-start | bytes 172040 | tf_op jit(solution)/shard_map/ppermute | solution.py:261
  88.6 4.2 %collective-permute-start.31 = (bf16[2,7,16,128]{3,2,1,0:T(8,128)(2,1)S(1)}, bf16[2,7,16,128]{3,2,1,0:T(8,128)(2,1)S(1)}, u32[]{:S(2)}, u32[]{:S(2)}) collective-permute-start(bf16[2,7,16,128]{3,2,1,0:T(8,128)(2,1)S(1)} %shard_map.89.refs_0_), channel_id=1, source_target_pairs={{0,12},{1,13},{2,14},{3,15},{4,8},{5,9},{6,10},{7,11},{8,4},{9,5},... | collective-permute-start | bytes 172040 | tf_op jit(solution)/shard_map/ppermute | solution.py:261
  93.2 8.9 %collective-permute-start.35 = (bf16[2,4,7,16,128]{4,3,2,1,0:T(8,128)(2,1)S(1)}, bf16[2,4,7,16,128]{4,3,2,1,0:T(8,128)(2,1)S(1)}, u32[]{:S(2)}, u32[]{:S(2)}) collective-permute-start(bf16[2,4,7,16,128]{4,3,2,1,0:T(8,128)(2,1)S(1)} %shard_map.90.refs_0_), channel_id=1, source_target_pairs={{0,2},{1,3},{2,0},{3,1},{4,6},{5,7},{6,4},{7,5},{8,10},{9,11},{10,... | collective-permute-start | bytes 688136 | tf_op jit(solution)/shard_map/ppermute | solution.py:261
  94.1 12.1 %collective-permute-start.34 = (bf16[2,4,7,16,128]{4,3,2,1,0:T(8,128)(2,1)S(1)}, bf16[2,4,7,16,128]{4,3,2,1,0:T(8,128)(2,1)S(1)}, u32[]{:S(2)}, u32[]{:S(2)}) collective-permute-start(bf16[2,4,7,16,128]{4,3,2,1,0:T(8,128)(2,1)S(1)} %shard_map.90.refs_0_), channel_id=1, source_target_pairs={{0,3},{1,2},{2,1},{3,0},{4,7},{5,6},{6,5},{7,4},{8,11},{9,10},{10,... | collective-permute-start | bytes 688136 | tf_op jit(solution)/shard_map/ppermute | solution.py:261
  95.8 12.8 %collective-permute-start.33 = (bf16[2,4,7,16,128]{4,3,2,1,0:T(8,128)(2,1)S(1)}, bf16[2,4,7,16,128]{4,3,2,1,0:T(8,128)(2,1)S(1)}, u32[]{:S(2)}, u32[]{:S(2)}) collective-permute-start(bf16[2,4,7,16,128]{4,3,2,1,0:T(8,128)(2,1)S(1)} %shard_map.90.refs_0_), channel_id=1, source_target_pairs={{0,1},{1,0},{2,3},{3,2},{4,5},{5,4},{6,7},{7,6},{8,9},{9,8},{10,11... | collective-permute-start | bytes 688136 | tf_op jit(solution)/shard_map/ppermute | solution.py:261
  95.9 12.6 %collective-permute-start.36 = (bf16[2,4,7,16,128]{4,3,2,1,0:T(8,128)(2,1)S(1)}, bf16[2,4,7,16,128]{4,3,2,1,0:T(8,128)(2,1)S(1)}, u32[]{:S(2)}, u32[]{:S(2)}) collective-permute-start(bf16[2,4,7,16,128]{4,3,2,1,0:T(8,128)(2,1)S(1)} %shard_map.90.refs_0_), channel_id=1, source_target_pairs={{0,16},{1,17},{2,18},{3,19},{4,20},{5,21},{6,22},{7,23},{8,24},{9,... | collective-permute-start | bytes 688136 | tf_op jit(solution)/shard_map/ppermute | solution.py:261
  102.1 6.5 %collective-permute-start.39 = (bf16[2,4,7,16,128]{4,3,2,1,0:T(8,128)(2,1)S(1)}, bf16[2,4,7,16,128]{4,3,2,1,0:T(8,128)(2,1)S(1)}, u32[]{:S(2)}, u32[]{:S(2)}) collective-permute-start(bf16[2,4,7,16,128]{4,3,2,1,0:T(8,128)(2,1)S(1)} %collective-permute-done.35.refs_3_), channel_id=1, source_target_pairs={{0,16},{1,17},{2,18},{3,19},{4,20},{5,21},{6,22},{7,23},{8,24},{9,... | collective-permute-start | bytes 688136 | tf_op jit(solution)/shard_map/ppermute | solution.py:261
  (12 other events, 59.3 us)

commit v7 on v6

--- a/solution.py
+++ b/solution.py
@@ -128,17 +128,17 @@
 
 
 def blocks(frames, rows):
-    return [(t, slice(h, h + 2)) for t in range(frames) for h in range(0, rows, 2)]
+    return [(t, slice(h, h + 1)) for t in range(frames) for h in range(rows)]
 
 
 def first_kernel(centre, time, near, far, corners, taps, slope, hidden, last, near_out, far_out, pad):
     lay(pad, centre, time, near, far, corners, False)
     frames, rows = centre.shape[:2]
     for t, rows in blocks(frames, rows):
-        z = convolve(pad, taps, t, rows.start, 2, False)
+        z = convolve(pad, taps, t, rows.start, 1, False)
         s = jax.nn.sigmoid(z)
-        slope[t, rows] = (s * (1.0 + z * (1.0 - s))).reshape(2, *slope.shape[2:])
-        hidden[t, rows] = (z * s).astype(jnp.bfloat16).reshape(2, *hidden.shape[2:])
+        slope[t, rows] = (s * (1.0 + z * (1.0 - s))).reshape(1, *slope.shape[2:])
+        hidden[t, rows] = (z * s).astype(jnp.bfloat16).reshape(1, *hidden.shape[2:])
     strips(hidden, last, near_out, far_out, False)
 
 
@@ -148,10 +148,10 @@
     lay(pad, centre, time, near, far, corners, False)
     frames, rows = centre.shape[:2]
     for t, rows in blocks(frames, rows):
-        z = convolve(pad, taps, t, rows.start, 2, False)
+        z = convolve(pad, taps, t, rows.start, 1, False)
         s = jax.nn.sigmoid(z)
-        output[t, rows] = (z * s).astype(jnp.bfloat16).reshape(2, *output.shape[2:])
-        steep = (s * (1.0 + z * (1.0 - s))).reshape(2, *grad.shape[2:])
+        output[t, rows] = (z * s).astype(jnp.bfloat16).reshape(1, *output.shape[2:])
+        steep = (s * (1.0 + z * (1.0 - s))).reshape(1, *grad.shape[2:])
         grad[t, rows] = (cotangent[t, rows].astype(jnp.float32) * steep).astype(jnp.bfloat16)
     strips(grad, last, near_out, far_out, True)
 
@@ -162,8 +162,8 @@
     lay(pad, centre, time, near, far, corners, True)
     frames, rows = centre.shape[:2]
     for t, rows in blocks(frames, rows):
-        z = convolve(pad, taps, t, rows.start, 2, True)
-        grad[t, rows] = z.astype(jnp.bfloat16).reshape(2, *grad.shape[2:])
+        z = convolve(pad, taps, t, rows.start, 1, True)
+        grad[t, rows] = z.astype(jnp.bfloat16).reshape(1, *grad.shape[2:])
     ended[...] = jnp.zeros_like(ended)
     copy.wait()
 
@@ -174,7 +174,7 @@
     lay(pad, centre, time, near, far, corners, True)
     frames, rows = centre.shape[:2]
     for t, rows in blocks(frames, rows):
-        z = convolve(pad, taps, t, rows.start, 2, True).reshape(2, *grad.shape[2:])
+        z = convolve(pad, taps, t, rows.start, 1, True).reshape(1, *grad.shape[2:])
         grad[t, rows] = (z * slope[t, rows]).astype(jnp.bfloat16)
     strips(grad, last, near_out, far_out, True)
 

time: 112 us -> 113 us (level)
  transfers between devices with their start and end apart: 40 -> 40, of which waited for: 18 -> 18; matrix products, arithmetic and copies ran while one was open for 0% -> 0% of each run, Pallas kernels for 9% -> 10%
where the time goes in v7:
time: 113 us; the launch traced here: 112 us
  starting transfers between devices  69.7 us (62%)
  waiting for transfers between devices  21.5 us (19%)
  Pallas kernels  18 us (16%)
  local copies, waits for them, and re-layouts  2.16 us (2%)
    ppermute x24, starting transfers between devices, swap(): lax.ppermute(value, ALL, [(i, i ^ mask) for i in range(lax.axis_size(ALL))])  29.4 us
    pallas_call x17, Pallas kernels, call(): pl.pallas_call(run, out_shape=outs, in_specs=[inside] * len(args) + [ANY]...  18 us
    ppermute x4, starting transfers between devices, exchanged(): lax.ppermute(far, 'height', [(i, (i - 1 if i % 2 == 0 else i + 1) % line)...  14.7 us
    ppermute x24, waiting for transfers between devices, swap(): lax.ppermute(value, ALL, [(i, i ^ mask) for i in range(lax.axis_size(ALL))])  12.9 us
    ppermute x4, starting transfers between devices, cornered(): return (time, near, far, lax.ppermute(rows, 'tm', time_route(ahead)))  11.1 us
    ppermute x4, starting transfers between devices, exchanged(): time = lax.ppermute(last, 'tm', time_route(ahead))  10.9 us
    ppermute x4, waiting for transfers between devices, cornered(): return (time, near, far, lax.ppermute(rows, 'tm', time_route(ahead)))  4.92 us
    ppermute x4, starting transfers between devices, exchanged(): near = lax.ppermute(near, 'height', [(i, i ^ 1) for i in range(line)])  3.57 us
  transfers between devices with their start and end apart: 40, of which 18 were waited for; matrix products, arithmetic and copies ran while one was open for 0% of the time, Pallas kernels for 10%

profile of v7, /device:TPU:1, one launch (start us, length us, event | category | flops | bytes accessed | tf_op | source)
XLA Modules:
  0.0 112.4 jit_solution(16791228982847460466)
XLA Ops:
  2.0 2.1 %collective-permute-start.1 = (bf16[3,1,128,128]{3,2,1,0:T(8,128)(2,1)S(1)}, bf16[3,1,128,128]{3,2,1,0:T(8,128)(2,1)S(1)}, u32[]{:S(2)}, u32[]{:S(2)}) collective-permute-start(bf16[3,1,128,128]{3,2,1,0:T(8,128)(2,1)S(1)} %get-tuple-element.51), channel_id=1, source_target_pairs={{0,1},{1,0},{2,3},{3,2},{4,5},{5,4},{6,7},{7,6},{8,9},{9,8},{10,11... | collective-permute-start | bytes 294920 | tf_op jit(solution)/shard_map/ppermute | solution.py:327
  4.1 4.3 %collective-permute-start.2 = (bf16[3,1,128,128]{3,2,1,0:T(8,128)(2,1)S(1)}, bf16[3,1,128,128]{3,2,1,0:T(8,128)(2,1)S(1)}, u32[]{:S(2)}, u32[]{:S(2)}) collective-permute-start(bf16[3,1,128,128]{3,2,1,0:T(8,128)(2,1)S(1)} %get-tuple-element.52), channel_id=1, source_target_pairs={{0,15},{1,2},{2,1},{3,4},{4,3},{5,6},{6,5},{7,8},{8,7},{9,10},{10,... | collective-permute-start | bytes 294920 | tf_op jit(solution)/shard_map/ppermute | solution.py:328
  8.3 4.7 %collective-permute-start = (bf16[2,4,128,128]{3,2,1,0:T(8,128)(2,1)S(1)}, bf16[2,4,128,128]{3,2,1,0:T(8,128)(2,1)S(1)}, u32[]{:S(2)}, u32[]{:S(2)}) collective-permute-start(bf16[2,4,128,128]{3,2,1,0:T(8,128)(2,1)S(1)} %get-tuple-element.50), channel_id=1, source_target_pairs={{0,16},{16,32},{32,48},{48,0},{1,17},{17,33},{33,49},{49,1},{2,18}... | collective-permute-start | bytes 786440 | tf_op jit(solution)/shard_map/ppermute | solution.py:326
  13.1 3.5 %collective-permute-start.3 = (bf16[2,2,128,128]{3,2,1,0:T(8,128)(2,1)S(1)}, bf16[2,2,128,128]{3,2,1,0:T(8,128)(2,1)S(1)}, u32[]{:S(2)}, u32[]{:S(2)}) collective-permute-start(bf16[2,2,128,128]{3,2,1,0:T(8,128)(2,1)S(1)} %pad_maximum_fusion.2), channel_id=1, source_target_pairs={{0,16},{16,32},{32,48},{48,0},{1,17},{17,33},{33,49},{49,1},{2,18}... | collective-permute-start | bytes 393224 | tf_op jit(solution)/shard_map/ppermute | solution.py:340
  18.5 2.4 %shard_map.77 = (f32[3,4,128,128]{3,2,1,0:T(8,128)S(1)}, bf16[3,4,128,128]{3,2,1,0:T(8,128)(2,1)S(1)}, bf16[2,4,128,128]{3,2,1,0:T(8,128)(2,1)S(1)}, bf16[3,1,12...) custom-call(bf16[3,4,128,128]{3,2,1,0:T(8,128)(2,1)S(1)} %get-tuple-element.49.refs_0_, ...), custom_call_target="tpu_custom_call" | custom-call | flops 1358954496 | bytes 3506176 | tf_op jit(solution)/shard_map/pallas_call | solution.py:25
  20.9 4.3 %collective-permute-start.6 = (bf16[3,1,128,128]{3,2,1,0:T(8,128)(2,1)S(1)}, bf16[3,1,128,128]{3,2,1,0:T(8,128)(2,1)S(1)}, u32[]{:S(2)}, u32[]{:S(2)}) collective-permute-start(bf16[3,1,128,128]{3,2,1,0:T(8,128)(2,1)S(1)} %get-tuple-element.57), channel_id=1, source_target_pairs={{0,15},{1,2},{2,1},{3,4},{4,3},{5,6},{6,5},{7,8},{8,7},{9,10},{10,... | collective-permute-start | bytes 294920 | tf_op jit(solution)/shard_map/ppermute | solution.py:328
  25.2 4.2 %collective-permute-start.4 = (bf16[2,4,128,128]{3,2,1,0:T(8,128)(2,1)S(1)}, bf16[2,4,128,128]{3,2,1,0:T(8,128)(2,1)S(1)}, u32[]{:S(2)}, u32[]{:S(2)}) collective-permute-start(bf16[2,4,128,128]{3,2,1,0:T(8,128)(2,1)S(1)} %get-tuple-element.55), channel_id=1, source_target_pairs={{0,16},{16,32},{32,48},{48,0},{1,17},{17,33},{33,49},{49,1},{2,18}... | collective-permute-start | bytes 786440 | tf_op jit(solution)/shard_map/ppermute | solution.py:326
  29.5 4.7 %collective-permute-start.7 = (bf16[2,2,128,128]{3,2,1,0:T(8,128)(2,1)S(1)}, bf16[2,2,128,128]{3,2,1,0:T(8,128)(2,1)S(1)}, u32[]{:S(2)}, u32[]{:S(2)}) collective-permute-start(bf16[2,2,128,128]{3,2,1,0:T(8,128)(2,1)S(1)} %pad_maximum_fusion.1), channel_id=1, source_target_pairs={{0,16},{16,32},{32,48},{48,0},{1,17},{17,33},{33,49},{49,1},{2,18}... | collective-permute-start | bytes 393224 | tf_op jit(solution)/shard_map/ppermute | solution.py:340
  36.1 2.4 %shard_map.79 = (bf16[3,4,128,128]{3,2,1,0:T(8,128)(2,1)S(1)}, bf16[3,4,128,128]{3,2,1,0:T(8,128)(2,1)S(1)}, bf16[2,4,128,128]{3,2,1,0:T(8,128)(2,1)S(1)}, bf16[...) custom-call(bf16[3,4,128,128]{3,2,1,0:T(8,128)(2,1)S(1)} %get-tuple-element.54.refs_0_, ...), custom_call_target="tpu_custom_call" | custom-call | flops 1358954496 | bytes 3506176 | tf_op jit(solution)/shard_map/pallas_call | solution.py:25
  38.6 3.1 %collective-permute-start.10 = (bf16[3,1,128,128]{3,2,1,0:T(8,128)(2,1)S(1)}, bf16[3,1,128,128]{3,2,1,0:T(8,128)(2,1)S(1)}, u32[]{:S(2)}, u32[]{:S(2)}) collective-permute-start(bf16[3,1,128,128]{3,2,1,0:T(8,128)(2,1)S(1)} %get-tuple-element.62), channel_id=1, source_target_pairs={{0,15},{1,2},{2,1},{3,4},{4,3},{5,6},{6,5},{7,8},{8,7},{9,10},{10,... | collective-permute-start | bytes 294920 | tf_op jit(solution)/shard_map/ppermute | solution.py:328
  42.6 3.1 %collective-permute-done.10.refs_3_ = bf16[3,1,128,128]{3,2,1,0:T(8,128)(2,1)S(1)} collective-permute-done((bf16[3,1,128,128]{3,2,1,0:T(8,128)(2,1)S(1)}, bf16[3,1,128,128]{3,2,1,0:T(8,128)(2,1)S(1)}, u32[]{:S(2)}, u32[]{:S(2)}) %collective-permute-start.10) | collective-permute-done | bytes 98336 | tf_op jit(solution)/shard_map/ppermute | solution.py:328
  45.8 1.5 %collective-permute-start.11 = (bf16[2,2,128,128]{3,2,1,0:T(8,128)(2,1)S(1)}, bf16[2,2,128,128]{3,2,1,0:T(8,128)(2,1)S(1)}, u32[]{:S(2)}, u32[]{:S(2)}) collective-permute-start(bf16[2,2,128,128]{3,2,1,0:T(8,128)(2,1)S(1)} %pad_maximum_fusion), channel_id=1, source_target_pairs={{0,48},{16,0},{32,16},{48,32},{1,49},{17,1},{33,17},{49,33},{2,50}... | collective-permute-start | bytes 393224 | tf_op jit(solution)/shard_map/ppermute | solution.py:340
  47.3 2.4 %shard_map.82 = (f32[4,28,16,128]{3,2,1,0:T(8,128)S(1)}, bf16[4,28,16,128]{3,2,1,0:T(8,128)(2,1)S(1)}) custom-call(bf16[3,4,128,128]{3,2,1,0:T(8,128)(2,1)S(1)} %get-tuple-element.54.refs_0_, bf16[2,4,128,128]{3,2,1,0:T(8,128)(2,1)S(1)} %collective-permute-done.4.refs_1_, bf16[3,1,128,128]{3,2,1,0:T(8,128)(2,1)S(1)} %collective-permute-done.5.refs_2_, ...), custom_call_target="tpu_custom_call" | custom-call | flops 1358954496 | bytes 2752512 | tf_op jit(solution)/shard_map/pallas_call | solution.py:25
  49.9 3.4 %collective-permute-done.11.refs_4_ = bf16[2,2,128,128]{3,2,1,0:T(8,128)(2,1)S(1)} collective-permute-done((bf16[2,2,128,128]{3,2,1,0:T(8,128)(2,1)S(1)}, bf16[2,2,128,128]{3,2,1,0:T(8,128)(2,1)S(1)}, u32[]{:S(2)}, u32[]{:S(2)}) %collective-permute-start.11) | collective-permute-done | bytes 131104 | tf_op jit(solution)/shard_map/ppermute | solution.py:340
  53.3 2.4 %shard_map.80 = (bf16[3,4,128,128]{3,2,1,0:T(8,128)(2,1)S(1)}, bf16[2,4,128,128]{3,2,1,0:T(8,128)(2,1)S(1)}, bf16[3,1,128,128]{3,2,1,0:T(8,128)(2,1)S(1)}, bf16[3,1,128,128]{3,2,1,0:T(8,128)(2,1)S(1)}) custom-call(bf16[3,4,128,128]{3,2,1,0:T(8,128)(2,1)S(1)} %get-tuple-element.59.refs_0_.refs_5_, ...), custom_call_target="tpu_custom_call" | custom-call | flops 1358954496 | bytes 3506176 | tf_op jit(solution)/shard_map/pallas_call | solution.py:25
  55.7 2.3 %shard_map.81 = (f32[4,28,16,128]{3,2,1,0:T(8,128)S(1)}, bf16[4,28,16,128]{3,2,1,0:T(8,128)(2,1)S(1)}) custom-call(bf16[3,4,128,128]{3,2,1,0:T(8,128)(2,1)S(1)} %get-tuple-element.49.refs_0_, bf16[2,4,128,128]{3,2,1,0:T(8,128)(2,1)S(1)} %collective-permute-done.refs_1_, bf16[3,1,128,128]{3,2,1,0:T(8,128)(2,1)S(1)} %collective-permute-done.1.refs_2_, ...), custom_call_target="tpu_custom_call" | custom-call | flops 1358954496 | bytes 2752512 | tf_op jit(solution)/shard_map/pallas_call | solution.py:25
  58.0 1.8 %collective-permute-done.15.refs_1_ = bf16[4,28,16,128]{3,2,1,0:T(8,128)(2,1)S(1)} collective-permute-done((bf16[4,28,16,128]{3,2,1,0:T(8,128)(2,1)S(1)}, bf16[4,28,16,128]{3,2,1,0:T(8,128)(2,1)S(1)}, u32[]{:S(2)}, u32[]{:S(2)}) %collective-permute-start.15) | collective-permute-done | bytes 458784 | tf_op jit(solution)/shard_map/ppermute | solution.py:261
  61.5 3.0 %collective-permute-start.14 = (bf16[3,1,128,128]{3,2,1,0:T(8,128)(2,1)S(1)}, bf16[3,1,128,128]{3,2,1,0:T(8,128)(2,1)S(1)}, u32[]{:S(2)}, u32[]{:S(2)}) collective-permute-start(bf16[3,1,128,128]{3,2,1,0:T(8,128)(2,1)S(1)} %get-tuple-element.68), channel_id=1, source_target_pairs={{0,15},{1,2},{2,1},{3,4},{4,3},{5,6},{6,5},{7,8},{8,7},{9,10},{10,... | collective-permute-start | bytes 294920 | tf_op jit(solution)/shard_map/ppermute | solution.py:328
  66.8 2.0 %collective-permute-start.21 = (bf16[4,7,16,128]{3,2,1,0:T(8,128)(2,1)S(1)}, bf16[4,7,16,128]{3,2,1,0:T(8,128)(2,1)S(1)}, u32[]{:S(2)}, u32[]{:S(2)}) collective-permute-start(bf16[4,7,16,128]{3,2,1,0:T(8,128)(2,1)S(1)} %get-tuple-element.82), channel_id=1, source_target_pairs={{0,3},{1,2},{2,1},{3,0},{4,7},{5,6},{6,5},{7,4},{8,11},{9,10},{10,... | collective-permute-start | bytes 344072 | tf_op jit(solution)/shard_map/ppermute | solution.py:261
  69.6 1.5 %collective-permute-start.17 = (bf16[2,2,128,128]{3,2,1,0:T(8,128)(2,1)S(1)}, bf16[2,2,128,128]{3,2,1,0:T(8,128)(2,1)S(1)}, u32[]{:S(2)}, u32[]{:S(2)}) collective-permute-start(bf16[2,2,128,128]{3,2,1,0:T(8,128)(2,1)S(1)} %shard_map.84), channel_id=1, source_target_pairs={{0,48},{16,0},{32,16},{48,32},{1,49},{17,1},{33,17},{49,33},{2,50}... | collective-permute-start | bytes 393224 | tf_op jit(solution)/shard_map/ppermute | solution.py:340
  71.1 1.7 %collective-permute-done.21.refs_2_ = bf16[4,7,16,128]{3,2,1,0:T(8,128)(2,1)S(1)} collective-permute-done((bf16[4,7,16,128]{3,2,1,0:T(8,128)(2,1)S(1)}, bf16[4,7,16,128]{3,2,1,0:T(8,128)(2,1)S(1)}, u32[]{:S(2)}, u32[]{:S(2)}) %collective-permute-start.21) | collective-permute-done | bytes 114720 | tf_op jit(solution)/shard_map/ppermute | solution.py:261
  72.8 3.0 %collective-permute-start.24 = (bf16[2,7,16,128]{3,2,1,0:T(8,128)(2,1)S(1)}, bf16[2,7,16,128]{3,2,1,0:T(8,128)(2,1)S(1)}, u32[]{:S(2)}, u32[]{:S(2)}) collective-permute-start(bf16[2,7,16,128]{3,2,1,0:T(8,128)(2,1)S(1)} %get-tuple-element.86), channel_id=1, source_target_pairs={{0,8},{1,9},{2,10},{3,11},{4,12},{5,13},{6,14},{7,15},{8,0},{9,1},... | collective-permute-start | bytes 172040 | tf_op jit(solution)/shard_map/ppermute | solution.py:261
  80.3 3.1 %collective-permute-start.28 = (bf16[2,7,16,128]{3,2,1,0:T(8,128)(2,1)S(1)}, bf16[2,7,16,128]{3,2,1,0:T(8,128)(2,1)S(1)}, u32[]{:S(2)}, u32[]{:S(2)}) collective-permute-start(bf16[2,7,16,128]{3,2,1,0:T(8,128)(2,1)S(1)} %shard_map.88.refs_0_), channel_id=1, source_target_pairs={{0,96},{1,97},{2,98},{3,99},{4,100},{5,101},{6,102},{7,103},{8,104... | collective-permute-start | bytes 172040 | tf_op jit(solution)/shard_map/ppermute | solution.py:261
  83.4 2.3 %shard_map.85 = (bf16[3,4,128,128]{3,2,1,0:T(8,128)(2,1)}, bf16[3,4,128,128]{3,2,1,0:T(8,128)(2,1)S(1)}, f32[8,128]{1,0:T(8,128)S(1)}) custom-call(bf16[3,4,128,128]{3,2,1,0:T(8,128)(2,1)S(1)} %get-tuple-element.65.refs_5_.refs_0_, bf16[2,4,128,128]{3,2,1,0:T(8,128)(2,1)S(1)} %collective-permute-done.12.refs_1_, ...), custom_call_target="tpu_custom_call" | custom-call | flops 1358954496 | bytes 3051520 | tf_op jit(solution)/shard_map/pallas_call | solution.py:25
  86.4 2.3 %collective-permute-start.32 = (bf16[2,7,16,128]{3,2,1,0:T(8,128)(2,1)S(1)}, bf16[2,7,16,128]{3,2,1,0:T(8,128)(2,1)S(1)}, u32[]{:S(2)}, u32[]{:S(2)}) collective-permute-start(bf16[2,7,16,128]{3,2,1,0:T(8,128)(2,1)S(1)} %shard_map.89.refs_0_), channel_id=1, source_target_pairs={{0,8},{1,9},{2,10},{3,11},{4,12},{5,13},{6,14},{7,15},{8,0},{9,1},... | collective-permute-start | bytes 172040 | tf_op jit(solution)/shard_map/ppermute | solution.py:261
  88.8 1.6 %collective-permute-start.31 = (bf16[2,7,16,128]{3,2,1,0:T(8,128)(2,1)S(1)}, bf16[2,7,16,128]{3,2,1,0:T(8,128)(2,1)S(1)}, u32[]{:S(2)}, u32[]{:S(2)}) collective-permute-start(bf16[2,7,16,128]{3,2,1,0:T(8,128)(2,1)S(1)} %shard_map.89.refs_0_), channel_id=1, source_target_pairs={{0,12},{1,13},{2,14},{3,15},{4,8},{5,9},{6,10},{7,11},{8,4},{9,5},... | collective-permute-start | bytes 172040 | tf_op jit(solution)/shard_map/ppermute | solution.py:261
  91.0 2.0 %collective-permute-done.31.refs_2_ = bf16[2,7,16,128]{3,2,1,0:T(8,128)(2,1)S(1)} collective-permute-done((bf16[2,7,16,128]{3,2,1,0:T(8,128)(2,1)S(1)}, bf16[2,7,16,128]{3,2,1,0:T(8,128)(2,1)S(1)}, u32[]{:S(2)}, u32[]{:S(2)}) %collective-permute-start.31) | collective-permute-done | bytes 57376 | tf_op jit(solution)/shard_map/ppermute | solution.py:261
  94.3 1.6 %collective-permute-start.34 = (bf16[2,4,7,16,128]{4,3,2,1,0:T(8,128)(2,1)S(1)}, bf16[2,4,7,16,128]{4,3,2,1,0:T(8,128)(2,1)S(1)}, u32[]{:S(2)}, u32[]{:S(2)}) collective-permute-start(bf16[2,4,7,16,128]{4,3,2,1,0:T(8,128)(2,1)S(1)} %shard_map.90.refs_0_), channel_id=1, source_target_pairs={{0,3},{1,2},{2,1},{3,0},{4,7},{5,6},{6,5},{7,4},{8,11},{9,10},{10,... | collective-permute-start | bytes 688136 | tf_op jit(solution)/shard_map/ppermute | solution.py:261
  96.1 6.1 %collective-permute-start.36 = (bf16[2,4,7,16,128]{4,3,2,1,0:T(8,128)(2,1)S(1)}, bf16[2,4,7,16,128]{4,3,2,1,0:T(8,128)(2,1)S(1)}, u32[]{:S(2)}, u32[]{:S(2)}) collective-permute-start(bf16[2,4,7,16,128]{4,3,2,1,0:T(8,128)(2,1)S(1)} %shard_map.90.refs_0_), channel_id=1, source_target_pairs={{0,16},{1,17},{2,18},{3,19},{4,20},{5,21},{6,22},{7,23},{8,24},{9,... | collective-permute-start | bytes 688136 | tf_op jit(solution)/shard_map/ppermute | solution.py:261
  102.3 4.1 %collective-permute-start.39 = (bf16[2,4,7,16,128]{4,3,2,1,0:T(8,128)(2,1)S(1)}, bf16[2,4,7,16,128]{4,3,2,1,0:T(8,128)(2,1)S(1)}, u32[]{:S(2)}, u32[]{:S(2)}) collective-permute-start(bf16[2,4,7,16,128]{4,3,2,1,0:T(8,128)(2,1)S(1)} %collective-permute-done.35.refs_3_), channel_id=1, source_target_pairs={{0,16},{1,17},{2,18},{3,19},{4,20},{5,21},{6,22},{7,23},{8,24},{9,... | collective-permute-start | bytes 688136 | tf_op jit(solution)/shard_map/ppermute | solution.py:261
  106.4 2.4 %collective-permute-start.38 = (bf16[2,4,7,16,128]{4,3,2,1,0:T(8,128)(2,1)S(1)}, bf16[2,4,7,16,128]{4,3,2,1,0:T(8,128)(2,1)S(1)}, u32[]{:S(2)}, u32[]{:S(2)}) collective-permute-start(bf16[2,4,7,16,128]{4,3,2,1,0:T(8,128)(2,1)S(1)} %collective-permute-done.34.refs_2_), channel_id=1, source_target_pairs={{0,16},{1,17},{2,18},{3,19},{4,20},{5,21},{6,22},{7,23},{8,24},{9,... | collective-permute-start | bytes 688136 | tf_op jit(solution)/shard_map/ppermute | solution.py:261
  110.2 2.0 %shard_map.91 = (f32[27,8,16,128]{3,2,1,0:T(8,128)}, f32[27,8,16,128]{3,2,1,0:T(8,128)}, bf16[3,4,128,128]{3,2,1,0:T(8,128)(2,1)}) custom-call(bf16[2,4,7,16,128]{4,3,2,1,0:T(8,128)(2,1)S(1)} %shard_map.90.refs_0_, bf16[2,4,7,16,128]{4,3,2,1,0:T(8,128)(2,1)S(1)} %collective-permute-done.33.refs_1_, ...), custom_call_target="tpu_custom_call" | custom-call | flops 917504 | bytes 6160384 | tf_op jit(solution)/shard_map/pallas_call | solution.py:25
  (76 shorter events, 20.1 us)
Async XLA Ops:
  2.0 11.1 %collective-permute-start.1 = (bf16[3,1,128,128]{3,2,1,0:T(8,128)(2,1)S(1)}, bf16[3,1,128,128]{3,2,1,0:T(8,128)(2,1)S(1)}, u32[]{:S(2)}, u32[]{:S(2)}) collective-permute-start(bf16[3,1,128,128]{3,2,1,0:T(8,128)(2,1)S(1)} %get-tuple-element.51), channel_id=1, source_target_pairs={{0,1},{1,0},{2,3},{3,2},{4,5},{5,4},{6,7},{7,6},{8,9},{9,8},{10,11... | collective-permute-start | bytes 294920 | tf_op jit(solution)/shard_map/ppermute | solution.py:327
  4.1 9.0 %collective-permute-start.2 = (bf16[3,1,128,128]{3,2,1,0:T(8,128)(2,1)S(1)}, bf16[3,1,128,128]{3,2,1,0:T(8,128)(2,1)S(1)}, u32[]{:S(2)}, u32[]{:S(2)}) collective-permute-start(bf16[3,1,128,128]{3,2,1,0:T(8,128)(2,1)S(1)} %get-tuple-element.52), channel_id=1, source_target_pairs={{0,15},{1,2},{2,1},{3,4},{4,3},{5,6},{6,5},{7,8},{8,7},{9,10},{10,... | collective-permute-start | bytes 294920 | tf_op jit(solution)/shard_map/ppermute | solution.py:328
  8.3 10.1 %collective-permute-start = (bf16[2,4,128,128]{3,2,1,0:T(8,128)(2,1)S(1)}, bf16[2,4,128,128]{3,2,1,0:T(8,128)(2,1)S(1)}, u32[]{:S(2)}, u32[]{:S(2)}) collective-permute-start(bf16[2,4,128,128]{3,2,1,0:T(8,128)(2,1)S(1)} %get-tuple-element.50), channel_id=1, source_target_pairs={{0,16},{16,32},{32,48},{48,0},{1,17},{17,33},{33,49},{49,1},{2,18}... | collective-permute-start | bytes 786440 | tf_op jit(solution)/shard_map/ppermute | solution.py:326
  13.1 5.4 %collective-permute-start.3 = (bf16[2,2,128,128]{3,2,1,0:T(8,128)(2,1)S(1)}, bf16[2,2,128,128]{3,2,1,0:T(8,128)(2,1)S(1)}, u32[]{:S(2)}, u32[]{:S(2)}) collective-permute-start(bf16[2,2,128,128]{3,2,1,0:T(8,128)(2,1)S(1)} %pad_maximum_fusion.2), channel_id=1, source_target_pairs={{0,16},{16,32},{32,48},{48,0},{1,17},{17,33},{33,49},{49,1},{2,18}... | collective-permute-start | bytes 393224 | tf_op jit(solution)/shard_map/ppermute | solution.py:340
  20.9 8.6 %collective-permute-start.6 = (bf16[3,1,128,128]{3,2,1,0:T(8,128)(2,1)S(1)}, bf16[3,1,128,128]{3,2,1,0:T(8,128)(2,1)S(1)}, u32[]{:S(2)}, u32[]{:S(2)}) collective-permute-start(bf16[3,1,128,128]{3,2,1,0:T(8,128)(2,1)S(1)} %get-tuple-element.57), channel_id=1, source_target_pairs={{0,15},{1,2},{2,1},{3,4},{4,3},{5,6},{6,5},{7,8},{8,7},{9,10},{10,... | collective-permute-start | bytes 294920 | tf_op jit(solution)/shard_map/ppermute | solution.py:328
  25.2 4.2 %collective-permute-start.5 = (bf16[3,1,128,128]{3,2,1,0:T(8,128)(2,1)S(1)}, bf16[3,1,128,128]{3,2,1,0:T(8,128)(2,1)S(1)}, u32[]{:S(2)}, u32[]{:S(2)}) collective-permute-start(bf16[3,1,128,128]{3,2,1,0:T(8,128)(2,1)S(1)} %get-tuple-element.56.refs_1_), channel_id=1, source_target_pairs={{0,1},{1,0},{2,3},{3,2},{4,5},{5,4},{6,7},{7,6},{8,9},{9,8},{10,11... | collective-permute-start | bytes 294920 | tf_op jit(solution)/shard_map/ppermute | solution.py:327
  25.2 10.9 %collective-permute-start.4 = (bf16[2,4,128,128]{3,2,1,0:T(8,128)(2,1)S(1)}, bf16[2,4,128,128]{3,2,1,0:T(8,128)(2,1)S(1)}, u32[]{:S(2)}, u32[]{:S(2)}) collective-permute-start(bf16[2,4,128,128]{3,2,1,0:T(8,128)(2,1)S(1)} %get-tuple-element.55), channel_id=1, source_target_pairs={{0,16},{16,32},{32,48},{48,0},{1,17},{17,33},{33,49},{49,1},{2,18}... | collective-permute-start | bytes 786440 | tf_op jit(solution)/shard_map/ppermute | solution.py:326
  29.5 6.6 %collective-permute-start.7 = (bf16[2,2,128,128]{3,2,1,0:T(8,128)(2,1)S(1)}, bf16[2,2,128,128]{3,2,1,0:T(8,128)(2,1)S(1)}, u32[]{:S(2)}, u32[]{:S(2)}) collective-permute-start(bf16[2,2,128,128]{3,2,1,0:T(8,128)(2,1)S(1)} %pad_maximum_fusion.1), channel_id=1, source_target_pairs={{0,16},{16,32},{32,48},{48,0},{1,17},{17,33},{33,49},{49,1},{2,18}... | collective-permute-start | bytes 393224 | tf_op jit(solution)/shard_map/ppermute | solution.py:340
  38.5 4.1 %collective-permute-start.9 = (bf16[3,1,128,128]{3,2,1,0:T(8,128)(2,1)S(1)}, bf16[3,1,128,128]{3,2,1,0:T(8,128)(2,1)S(1)}, u32[]{:S(2)}, u32[]{:S(2)}) collective-permute-start(bf16[3,1,128,128]{3,2,1,0:T(8,128)(2,1)S(1)} %get-tuple-element.61), channel_id=1, source_target_pairs={{0,1},{1,0},{2,3},{3,2},{4,5},{5,4},{6,7},{7,6},{8,9},{9,8},{10,11... | collective-permute-start | bytes 294920 | tf_op jit(solution)/shard_map/ppermute | solution.py:327
  38.6 7.2 %collective-permute-start.10 = (bf16[3,1,128,128]{3,2,1,0:T(8,128)(2,1)S(1)}, bf16[3,1,128,128]{3,2,1,0:T(8,128)(2,1)S(1)}, u32[]{:S(2)}, u32[]{:S(2)}) collective-permute-start(bf16[3,1,128,128]{3,2,1,0:T(8,128)(2,1)S(1)} %get-tuple-element.62), channel_id=1, source_target_pairs={{0,15},{1,2},{2,1},{3,4},{4,3},{5,6},{6,5},{7,8},{8,7},{9,10},{10,... | collective-permute-start | bytes 294920 | tf_op jit(solution)/shard_map/ppermute | solution.py:328
  41.7 11.6 %collective-permute-start.8 = (bf16[2,4,128,128]{3,2,1,0:T(8,128)(2,1)S(1)}, bf16[2,4,128,128]{3,2,1,0:T(8,128)(2,1)S(1)}, u32[]{:S(2)}, u32[]{:S(2)}) collective-permute-start(bf16[2,4,128,128]{3,2,1,0:T(8,128)(2,1)S(1)} %get-tuple-element.60), channel_id=1, source_target_pairs={{0,48},{16,0},{32,16},{48,32},{1,49},{17,1},{33,17},{49,33},{2,50}... | collective-permute-start | bytes 786440 | tf_op jit(solution)/shard_map/ppermute | solution.py:326
  45.8 7.5 %collective-permute-start.11 = (bf16[2,2,128,128]{3,2,1,0:T(8,128)(2,1)S(1)}, bf16[2,2,128,128]{3,2,1,0:T(8,128)(2,1)S(1)}, u32[]{:S(2)}, u32[]{:S(2)}) collective-permute-start(bf16[2,2,128,128]{3,2,1,0:T(8,128)(2,1)S(1)} %pad_maximum_fusion), channel_id=1, source_target_pairs={{0,48},{16,0},{32,16},{48,32},{1,49},{17,1},{33,17},{49,33},{2,50}... | collective-permute-start | bytes 393224 | tf_op jit(solution)/shard_map/ppermute | solution.py:340
  49.7 8.3 %collective-permute-start.16 = (bf16[4,28,16,128]{3,2,1,0:T(8,128)(2,1)S(1)}, bf16[4,28,16,128]{3,2,1,0:T(8,128)(2,1)S(1)}, u32[]{:S(2)}, u32[]{:S(2)}) collective-permute-start(bf16[4,28,16,128]{3,2,1,0:T(8,128)(2,1)S(1)} %get-tuple-element.72), channel_id=1, source_target_pairs={{0,16},{1,17},{2,18},{3,19},{4,20},{5,21},{6,22},{7,23},{8,24},{9,... | collective-permute-start | bytes 1376264 | tf_op jit(solution)/shard_map/ppermute | solution.py:261
  60.0 5.6 %collective-permute-start.19 = (bf16[4,7,16,128]{3,2,1,0:T(8,128)(2,1)S(1)}, bf16[4,7,16,128]{3,2,1,0:T(8,128)(2,1)S(1)}, u32[]{:S(2)}, u32[]{:S(2)}) collective-permute-start(bf16[4,7,16,128]{3,2,1,0:T(8,128)(2,1)S(1)} %get-tuple-element.80), channel_id=1, source_target_pairs={{0,1},{1,0},{2,3},{3,2},{4,5},{5,4},{6,7},{7,6},{8,9},{9,8},{10,11... | collective-permute-start | bytes 344072 | tf_op jit(solution)/shard_map/ppermute | solution.py:261
  60.1 5.9 %collective-permute-start.20 = (bf16[4,7,16,128]{3,2,1,0:T(8,128)(2,1)S(1)}, bf16[4,7,16,128]{3,2,1,0:T(8,128)(2,1)S(1)}, u32[]{:S(2)}, u32[]{:S(2)}) collective-permute-start(bf16[4,7,16,128]{3,2,1,0:T(8,128)(2,1)S(1)} %get-tuple-element.81), channel_id=1, source_target_pairs={{0,3},{1,2},{2,1},{3,0},{4,7},{5,6},{6,5},{7,4},{8,11},{9,10},{10,... | collective-permute-start | bytes 344072 | tf_op jit(solution)/shard_map/ppermute | solution.py:261
  60.2 6.6 %collective-permute-start.13 = (bf16[3,1,128,128]{3,2,1,0:T(8,128)(2,1)S(1)}, bf16[3,1,128,128]{3,2,1,0:T(8,128)(2,1)S(1)}, u32[]{:S(2)}, u32[]{:S(2)}) collective-permute-start(bf16[3,1,128,128]{3,2,1,0:T(8,128)(2,1)S(1)} %get-tuple-element.67), channel_id=1, source_target_pairs={{0,1},{1,0},{2,3},{3,2},{4,5},{5,4},{6,7},{7,6},{8,9},{9,8},{10,11... | collective-permute-start | bytes 294920 | tf_op jit(solution)/shard_map/ppermute | solution.py:327
  61.5 7.3 %collective-permute-start.14 = (bf16[3,1,128,128]{3,2,1,0:T(8,128)(2,1)S(1)}, bf16[3,1,128,128]{3,2,1,0:T(8,128)(2,1)S(1)}, u32[]{:S(2)}, u32[]{:S(2)}) collective-permute-start(bf16[3,1,128,128]{3,2,1,0:T(8,128)(2,1)S(1)} %get-tuple-element.68), channel_id=1, source_target_pairs={{0,15},{1,2},{2,1},{3,4},{4,3},{5,6},{6,5},{7,8},{8,7},{9,10},{10,... | collective-permute-start | bytes 294920 | tf_op jit(solution)/shard_map/ppermute | solution.py:328
  64.5 18.8 %collective-permute-start.12 = (bf16[2,4,128,128]{3,2,1,0:T(8,128)(2,1)S(1)}, bf16[2,4,128,128]{3,2,1,0:T(8,128)(2,1)S(1)}, u32[]{:S(2)}, u32[]{:S(2)}) collective-permute-start(bf16[2,4,128,128]{3,2,1,0:T(8,128)(2,1)S(1)} %get-tuple-element.66), channel_id=1, source_target_pairs={{0,48},{16,0},{32,16},{48,32},{1,49},{17,1},{33,17},{49,33},{2,50}... | collective-permute-start | bytes 786440 | tf_op jit(solution)/shard_map/ppermute | solution.py:326
  66.0 5.1 %collective-permute-start.23 = (bf16[4,7,16,128]{3,2,1,0:T(8,128)(2,1)S(1)}, bf16[4,7,16,128]{3,2,1,0:T(8,128)(2,1)S(1)}, u32[]{:S(2)}, u32[]{:S(2)}) collective-permute-start(bf16[4,7,16,128]{3,2,1,0:T(8,128)(2,1)S(1)} %get-tuple-element.84), channel_id=1, source_target_pairs={{0,3},{1,2},{2,1},{3,0},{4,7},{5,6},{6,5},{7,4},{8,11},{9,10},{10,... | collective-permute-start | bytes 344072 | tf_op jit(solution)/shard_map/ppermute | solution.py:261
  66.8 6.0 %collective-permute-start.21 = (bf16[4,7,16,128]{3,2,1,0:T(8,128)(2,1)S(1)}, bf16[4,7,16,128]{3,2,1,0:T(8,128)(2,1)S(1)}, u32[]{:S(2)}, u32[]{:S(2)}) collective-permute-start(bf16[4,7,16,128]{3,2,1,0:T(8,128)(2,1)S(1)} %get-tuple-element.82), channel_id=1, source_target_pairs={{0,3},{1,2},{2,1},{3,0},{4,7},{5,6},{6,5},{7,4},{8,11},{9,10},{10,... | collective-permute-start | bytes 344072 | tf_op jit(solution)/shard_map/ppermute | solution.py:261
  69.6 7.5 %collective-permute-start.17 = (bf16[2,2,128,128]{3,2,1,0:T(8,128)(2,1)S(1)}, bf16[2,2,128,128]{3,2,1,0:T(8,128)(2,1)S(1)}, u32[]{:S(2)}, u32[]{:S(2)}) collective-permute-start(bf16[2,2,128,128]{3,2,1,0:T(8,128)(2,1)S(1)} %shard_map.84), channel_id=1, source_target_pairs={{0,48},{16,0},{32,16},{48,32},{1,49},{17,1},{33,17},{49,33},{2,50}... | collective-permute-start | bytes 393224 | tf_op jit(solution)/shard_map/ppermute | solution.py:340
  72.8 4.6 %collective-permute-start.24 = (bf16[2,7,16,128]{3,2,1,0:T(8,128)(2,1)S(1)}, bf16[2,7,16,128]{3,2,1,0:T(8,128)(2,1)S(1)}, u32[]{:S(2)}, u32[]{:S(2)}) collective-permute-start(bf16[2,7,16,128]{3,2,1,0:T(8,128)(2,1)S(1)} %get-tuple-element.86), channel_id=1, source_target_pairs={{0,8},{1,9},{2,10},{3,11},{4,12},{5,13},{6,14},{7,15},{8,0},{9,1},... | collective-permute-start | bytes 172040 | tf_op jit(solution)/shard_map/ppermute | solution.py:261
  75.9 4.2 %collective-permute-start.26 = (bf16[2,7,16,128]{3,2,1,0:T(8,128)(2,1)S(1)}, bf16[2,7,16,128]{3,2,1,0:T(8,128)(2,1)S(1)}, u32[]{:S(2)}, u32[]{:S(2)}) collective-permute-start(bf16[2,7,16,128]{3,2,1,0:T(8,128)(2,1)S(1)} %get-tuple-element.88), channel_id=1, source_target_pairs={{0,12},{1,13},{2,14},{3,15},{4,8},{5,9},{6,10},{7,11},{8,4},{9,5},... | collective-permute-start | bytes 172040 | tf_op jit(solution)/shard_map/ppermute | solution.py:261
  80.2 5.5 %collective-permute-start.29 = (bf16[2,7,16,128]{3,2,1,0:T(8,128)(2,1)S(1)}, bf16[2,7,16,128]{3,2,1,0:T(8,128)(2,1)S(1)}, u32[]{:S(2)}, u32[]{:S(2)}) collective-permute-start(bf16[2,7,16,128]{3,2,1,0:T(8,128)(2,1)S(1)} %shard_map.88.refs_0_), channel_id=1, source_target_pairs={{0,32},{1,33},{2,34},{3,35},{4,36},{5,37},{6,38},{7,39},{8,40},{9,... | collective-permute-start | bytes 172040 | tf_op jit(solution)/shard_map/ppermute | solution.py:261
  80.3 5.4 %collective-permute-start.28 = (bf16[2,7,16,128]{3,2,1,0:T(8,128)(2,1)S(1)}, bf16[2,7,16,128]{3,2,1,0:T(8,128)(2,1)S(1)}, u32[]{:S(2)}, u32[]{:S(2)}) collective-permute-start(bf16[2,7,16,128]{3,2,1,0:T(8,128)(2,1)S(1)} %shard_map.88.refs_0_), channel_id=1, source_target_pairs={{0,96},{1,97},{2,98},{3,99},{4,100},{5,101},{6,102},{7,103},{8,104... | collective-permute-start | bytes 172040 | tf_op jit(solution)/shard_map/ppermute | solution.py:261
  86.4 4.6 %collective-permute-start.32 = (bf16[2,7,16,128]{3,2,1,0:T(8,128)(2,1)S(1)}, bf16[2,7,16,128]{3,2,1,0:T(8,128)(2,1)S(1)}, u32[]{:S(2)}, u32[]{:S(2)}) collective-permute-start(bf16[2,7,16,128]{3,2,1,0:T(8,128)(2,1)S(1)} %shard_map.89.refs_0_), channel_id=1, source_target_pairs={{0,8},{1,9},{2,10},{3,11},{4,12},{5,13},{6,14},{7,15},{8,0},{9,1},... | collective-permute-start | bytes 172040 | tf_op jit(solution)/shard_map/ppermute | solution.py:261
  88.8 4.2 %collective-permute-start.31 = (bf16[2,7,16,128]{3,2,1,0:T(8,128)(2,1)S(1)}, bf16[2,7,16,128]{3,2,1,0:T(8,128)(2,1)S(1)}, u32[]{:S(2)}, u32[]{:S(2)}) collective-permute-start(bf16[2,7,16,128]{3,2,1,0:T(8,128)(2,1)S(1)} %shard_map.89.refs_0_), channel_id=1, source_target_pairs={{0,12},{1,13},{2,14},{3,15},{4,8},{5,9},{6,10},{7,11},{8,4},{9,5},... | collective-permute-start | bytes 172040 | tf_op jit(solution)/shard_map/ppermute | solution.py:261
  93.4 8.9 %collective-permute-start.35 = (bf16[2,4,7,16,128]{4,3,2,1,0:T(8,128)(2,1)S(1)}, bf16[2,4,7,16,128]{4,3,2,1,0:T(8,128)(2,1)S(1)}, u32[]{:S(2)}, u32[]{:S(2)}) collective-permute-start(bf16[2,4,7,16,128]{4,3,2,1,0:T(8,128)(2,1)S(1)} %shard_map.90.refs_0_), channel_id=1, source_target_pairs={{0,2},{1,3},{2,0},{3,1},{4,6},{5,7},{6,4},{7,5},{8,10},{9,11},{10,... | collective-permute-start | bytes 688136 | tf_op jit(solution)/shard_map/ppermute | solution.py:261
  94.3 12.0 %collective-permute-start.34 = (bf16[2,4,7,16,128]{4,3,2,1,0:T(8,128)(2,1)S(1)}, bf16[2,4,7,16,128]{4,3,2,1,0:T(8,128)(2,1)S(1)}, u32[]{:S(2)}, u32[]{:S(2)}) collective-permute-start(bf16[2,4,7,16,128]{4,3,2,1,0:T(8,128)(2,1)S(1)} %shard_map.90.refs_0_), channel_id=1, source_target_pairs={{0,3},{1,2},{2,1},{3,0},{4,7},{5,6},{6,5},{7,4},{8,11},{9,10},{10,... | collective-permute-start | bytes 688136 | tf_op jit(solution)/shard_map/ppermute | solution.py:261
  96.0 12.8 %collective-permute-start.33 = (bf16[2,4,7,16,128]{4,3,2,1,0:T(8,128)(2,1)S(1)}, bf16[2,4,7,16,128]{4,3,2,1,0:T(8,128)(2,1)S(1)}, u32[]{:S(2)}, u32[]{:S(2)}) collective-permute-start(bf16[2,4,7,16,128]{4,3,2,1,0:T(8,128)(2,1)S(1)} %shard_map.90.refs_0_), channel_id=1, source_target_pairs={{0,1},{1,0},{2,3},{3,2},{4,5},{5,4},{6,7},{7,6},{8,9},{9,8},{10,11... | collective-permute-start | bytes 688136 | tf_op jit(solution)/shard_map/ppermute | solution.py:261
  96.1 12.6 %collective-permute-start.36 = (bf16[2,4,7,16,128]{4,3,2,1,0:T(8,128)(2,1)S(1)}, bf16[2,4,7,16,128]{4,3,2,1,0:T(8,128)(2,1)S(1)}, u32[]{:S(2)}, u32[]{:S(2)}) collective-permute-start(bf16[2,4,7,16,128]{4,3,2,1,0:T(8,128)(2,1)S(1)} %shard_map.90.refs_0_), channel_id=1, source_target_pairs={{0,16},{1,17},{2,18},{3,19},{4,20},{5,21},{6,22},{7,23},{8,24},{9,... | collective-permute-start | bytes 688136 | tf_op jit(solution)/shard_map/ppermute | solution.py:261
  102.3 6.5 %collective-permute-start.39 = (bf16[2,4,7,16,128]{4,3,2,1,0:T(8,128)(2,1)S(1)}, bf16[2,4,7,16,128]{4,3,2,1,0:T(8,128)(2,1)S(1)}, u32[]{:S(2)}, u32[]{:S(2)}) collective-permute-start(bf16[2,4,7,16,128]{4,3,2,1,0:T(8,128)(2,1)S(1)} %collective-permute-done.35.refs_3_), channel_id=1, source_target_pairs={{0,16},{1,17},{2,18},{3,19},{4,20},{5,21},{6,22},{7,23},{8,24},{9,... | collective-permute-start | bytes 688136 | tf_op jit(solution)/shard_map/ppermute | solution.py:261
  (12 other events, 59.4 us)
